TPU v7x, 32 devices: a whole 2x2x4 slice. The times are simulated.
32 devices in a mesh: ctx: 8 (over z, y), head: 4 (over x, core).
Axes of the slice: x: 2, y: 2, z: 4, core: 2. Of those that a mesh axis runs over, the one named last changes fastest.
Arguments:
- queries: bfloat16 [8192, 32, 128], P('ctx', 'head'), may hold values from -6 to 6
- keys: bfloat16 [8192, 32, 128], P('ctx', 'head'), may hold values from -6 to 6
- values: bfloat16 [8192, 32, 128], P('ctx', 'head'), may hold values from -6 to 6
- d_layer: bfloat16 [8192, 4096], P('ctx', 'head'), may hold values from -6 to 6
- out_weight: bfloat16 [4096, 4096], P('head'), may hold values from -0.09375 to 0.09375
Outputs:
- d_queries: bfloat16 [8192, 32, 128], P('ctx', 'head')
- d_keys: bfloat16 [8192, 32, 128], P('ctx', 'head')
- d_values: bfloat16 [8192, 32, 128], P('ctx', 'head')
All inputs are finite; a program needn't handle non-finite values.
Results may differ from a plain program's by a relative error of at most 0.0071.
Values may be sent and summed in bfloat16 or wider, within the bound.
No kernel may reach another device: no remote copies, remote signals or barrier semaphores. Data moves between devices by JAX's collectives and lax.ppermute only.
A program may use at most 192 MiB of HBM per device.

v0:
```python
import jax
import jax.numpy as jnp
from jax import lax
from jax.sharding import PartitionSpec as P


def body(queries, keys, values, d_layer, out_weight):
    tokens, heads_local, head_dim = queries.shape
    flat = lax.dot_general(
        lax.all_gather(d_layer, "head", axis=1, tiled=True),
        out_weight,
        (((1,), (1,)), ((), ())),
        preferred_element_type=jnp.float32,
    )
    d_heads = flat.astype(jnp.bfloat16).reshape(tokens, heads_local, head_dim)
    block_index = lax.axis_index("ctx")
    position = block_index * tokens + jnp.arange(tokens, dtype=jnp.int32)
    scale = lax.rsqrt((head_dim * (position + 1)).astype(jnp.float32))
    grad_scaled = (d_heads.astype(jnp.float32) * scale[:, None, None]).astype(jnp.bfloat16)
    key_state = jnp.einsum("thd,the->hde", keys, values, preferred_element_type=jnp.float32).astype(
        jnp.bfloat16
    )
    query_state = jnp.einsum(
        "thd,the->hde", queries, grad_scaled, preferred_element_type=jnp.float32
    ).astype(jnp.bfloat16)
    every_key, every_query = (
        lax.all_gather(key_state[None], "ctx", axis=0, tiled=True),
        lax.all_gather(query_state[None], "ctx", axis=0, tiled=True),
    )
    order = jnp.arange(every_key.shape[0], dtype=jnp.int32)
    before = (order < block_index)[:, None, None, None]
    after = (order > block_index)[:, None, None, None]
    prefix = jnp.sum(jnp.where(before, every_key.astype(jnp.float32), 0.0), axis=0)
    suffix = jnp.sum(jnp.where(after, every_query.astype(jnp.float32), 0.0), axis=0)
    prefix_low = prefix.astype(jnp.bfloat16)
    suffix_low = suffix.astype(jnp.bfloat16)
    lower = jnp.tril(jnp.ones((tokens, tokens), dtype=bool))[None]
    score_grad = jnp.where(
        lower,
        jnp.einsum("thd,shd->hts", grad_scaled, values, preferred_element_type=jnp.float32),
        0.0,
    ).astype(jnp.bfloat16)
    score_keys = jnp.where(
        lower, jnp.einsum("thd,shd->hts", queries, keys, preferred_element_type=jnp.float32), 0.0
    ).astype(jnp.bfloat16)
    d_queries = scale[:, None, None] * jnp.einsum(
        "the,hde->thd", d_heads, prefix_low, preferred_element_type=jnp.float32
    )
    d_queries = d_queries + jnp.einsum(
        "hts,shd->thd", score_grad, keys, preferred_element_type=jnp.float32
    )
    d_keys = jnp.einsum("hts,thd->shd", score_grad, queries, preferred_element_type=jnp.float32)
    d_keys = d_keys + jnp.einsum(
        "she,hde->shd", values, suffix_low, preferred_element_type=jnp.float32
    )
    d_values = jnp.einsum(
        "hts,the->she", score_keys, grad_scaled, preferred_element_type=jnp.float32
    )
    d_values = d_values + jnp.einsum(
        "shd,hde->she", keys, suffix_low, preferred_element_type=jnp.float32
    )
    return (
        d_queries.astype(jnp.bfloat16),
        d_keys.astype(jnp.bfloat16),
        d_values.astype(jnp.bfloat16),
    )


def solution(mesh):
    in_specs = (
        P("ctx", "head", None),
        P("ctx", "head", None),
        P("ctx", "head", None),
        P("ctx", "head"),
        P("head", None),
    )
    out_specs = (P("ctx", "head", None), P("ctx", "head", None), P("ctx", "head", None))
    return jax.shard_map(body, mesh=mesh, in_specs=in_specs, out_specs=out_specs, check_vma=False)
```

profile of v0, /device:TPU:0, one launch (start us, length us, event | category | flops | bytes accessed | tf_op | source)
XLA Modules:
  0.0 217.0 jit_solution(12946771182350368306)
XLA Ops:
  7.2 0.0 copy-start
  7.2 0.0 all-gather.8.cloned.1.call-start
  7.2 4.2 %copy.26 = bf16[1024,8,128]{0,2,1:T(8,128)(2,1)} copy(bf16[1024,8,128]{2,1,0:T(8,128)(2,1)} %param.6) | data formatting | bytes 4194304 | tf_op args[1]
  11.5 0.0 copy-done
  11.5 3.3 %fusion.24 = bf16[8,128,128]{2,1,0:T(8,128)(2,1)} fusion(bf16[1024,8,128]{0,2,1:T(8,128)(2,1)} %copy.26, bf16[1024,8,128]{2,1,0:T(8,128)(2,1)S(1)} %copy-done), kind=kOutput, calls=%fused_computation.30 | convolution fusion | flops 268566528 | bytes 4456448 | tf_op jit(solution)/shard_map/thd,the->hde/dot_general | solution.py:20
  14.8 0.0 all-gather.8.cloned.1.call-update
  14.8 0.0 all-gather.6.cloned.1.call-start
  14.8 0.7 all-gather.6.cloned.1.call-update
  15.5 0.0 all-gather.10.cloned.1.call-start
  15.6 1.3 iota_compare_fusion
  16.9 50.0 %all-gather.8.cloned.1.call-done = bf16[64,128,128]{2,1,0:T(8,128)(2,1)} async-done(((bf16[8,128,128]{2,1,0:T(8,128)(2,1)}), bf16[64,128,128]{2,1,0:T(8,128)(2,1)}) %all-gather.8.cloned.1.call-update) | async-done | bytes 2097168 | tf_op jit(solution)/shard_map/all_gather | solution.py:27
  66.9 2.1 fusion.6
  69.0 56.3 %all-gather.6.cloned.1.call-done = bf16[1024,4096]{1,0:T(8,128)(2,1)} async-done(((bf16[1024,1024]{1,0:T(8,128)(2,1)}), bf16[1024,4096]{1,0:T(8,128)(2,1)}) %all-gather.6.cloned.1.call-update) | async-done | bytes 8388624 | tf_op jit(solution)/shard_map/all_gather | solution.py:10
  125.3 13.9 %convolution_convert_fusion = bf16[1024,1024]{0,1:T(8,128)(2,1)S(1)} fusion(bf16[1024,4096]{1,0:T(8,128)(2,1)} %all-gather.6.cloned.1.call-done, bf16[1024,4096]{1,0:T(8,128)(2,1)} %param.9), kind=kOutput, calls=%fused_computation.17 | convolution fusion | flops 8590983168 | bytes 18874368 | tf_op jit(solution)/shard_map/dot_general | solution.py:9
  139.2 0.0 copy-start.3
  139.2 1.3 copy-done.3
  140.5 0.9 fusion.30
  141.4 0.9 copy.36
  142.3 0.0 all-gather.10.cloned.1.call-update
  142.3 0.0 copy-start.4
  142.3 4.4 %fusion.38 = f32[8,128,1024]{2,1,0:T(8,128)} fusion(bf16[8,128,128]{2,1,0:T(8,128)(2,1)S(1)} %fusion.6, bf16[1024,8,128]{0,2,1:T(8,128)(2,1)} %bitcast.32), kind=kOutput, calls=%fused_computation.41 | convolution fusion | flops 268435456 | bytes 6553600 | tf_op jit(solution)/shard_map/the,hde->thd/dot_general | solution.py:46
  146.7 10.2 %select_convert_fusion.1 = bf16[8,1024,1024]{2,1,0:T(8,128)(2,1)} fusion(pred[1024,1024]{1,0:T(8,128)(4,1)} %iota_compare_fusion, bf16[1024,8,128]{2,1,0:T(8,128)(2,1)S(1)} %copy-done, bf16[1024,8,128]{0,2,1:T(8,128)(2,1)S(1)} %bitcast.34, f32[1024]{0:T(1024)S(1)} %convert_rsqrt_fusion), kind=kOutput, calls=%fused_computation.1 | convolution fusion | flops 2167406592 | bytes 22024192 | tf_op jit(solution)/shard_map/thd,shd->hts/dot_general | solution.py:40
  156.9 10.9 %fusion.8 = bf16[1024,8,128]{0,2,1:T(8,128)(2,1)} fusion(f32[8,128,1024]{2,1,0:T(8,128)} %fusion.38, bf16[8,1024,1024]{2,1,0:T(8,128)(2,1)} %select_convert_fusion.1, f32[1024]{0:T(1024)S(1)} %convert_rsqrt_fusion, bf16[1024,8,128]{2,1,0:T(8,128)(2,1)S(1)} %copy-done.1), kind=kOutput, calls=%fused_computation.13 | convolution fusion | flops 2150629376 | bytes 25169920 | tf_op jit(solution)/shard_map/hts,shd->thd/dot_general | solution.py:49
  167.8 4.2 %copy.41 = bf16[1024,8,128]{2,1,0:T(8,128)(2,1)} copy(bf16[1024,8,128]{0,2,1:T(8,128)(2,1)} %fusion.8) | data formatting | bytes 4194304
  172.0 11.4 %fusion = f32[8,128,1024]{2,1,0:T(8,128)} fusion(pred[1024,1024]{1,0:T(8,128)(4,1)S(1)} %copy-done.5, bf16[1024,8,128]{0,2,1:T(8,128)(2,1)} %copy.26, bf16[1024,8,128]{2,1,0:T(8,128)(2,1)} %param.5, bf16[1024,8,128]{0,2,1:T(8,128)(2,1)} %bitcast.33, f32[1024]{0:T(1024)S(1)} %convert_rsqrt_fusion), kind=kOutput, calls=%fused_computation.2 | convolution fusion | flops 4314890240 | bytes 11538432 | tf_op jit(solution)/shard_map/hts,the->she/dot_general | solution.py:56
  183.5 10.7 %fusion.18 = f32[8,1024,128]{2,1,0:T(8,128)} fusion(bf16[8,1024,1024]{2,1,0:T(8,128)(2,1)} %select_convert_fusion.1, bf16[1024,8,128]{2,1,0:T(8,128)(2,1)} %param.5), kind=kOutput, calls=%fused_computation.24 | convolution fusion | flops 2147483648 | bytes 23068672 | tf_op jit(solution)/shard_map/hts,thd->shd/dot_general | solution.py:52
  194.1 2.2 %fusion.5 = bf16[8,128,128]{2,1,0:T(8,128)(2,1)S(1)} fusion(bf16[8,8,128,128]{3,2,1,0:T(8,128)(2,1)} %bitcast.36, pred[8]{0:T(512)(128)(4,1)S(1)} %iota_compare_fusion.1), kind=kLoop, calls=%fused_computation.7 | loop fusion | flops 3014656 | bytes 2359304 | tf_op jit(solution)/shard_map/reduce_sum | solution.py:34
  196.4 0.0 copy-done.2
  196.4 4.4 %fusion.11 = bf16[1024,8,128]{0,2,1:T(8,128)(2,1)} fusion(f32[8,128,1024]{2,1,0:T(8,128)} %fusion, bf16[1024,8,128]{2,1,0:T(8,128)(2,1)S(1)} %copy-done.2, bf16[8,128,128]{2,1,0:T(8,128)(2,1)S(1)} %fusion.5), kind=kOutput, calls=%fused_computation.20 | convolution fusion | flops 270532608 | bytes 8650752 | tf_op jit(solution)/shard_map/shd,hde->she/dot_general | solution.py:59
  200.8 4.1 %copy.43 = bf16[1024,8,128]{2,1,0:T(8,128)(2,1)} copy(bf16[1024,8,128]{0,2,1:T(8,128)(2,1)} %fusion.11) | data formatting | bytes 4194304
  204.9 2.9 %fusion.7 = bf16[1024,8,128]{2,0,1:T(8,128)(2,1)S(1)} fusion(f32[8,1024,128]{2,1,0:T(8,128)} %fusion.18, bf16[1024,8,128]{2,1,0:T(8,128)(2,1)S(1)} %copy-done, bf16[8,128,128]{2,1,0:T(8,128)(2,1)S(1)} %fusion.5), kind=kOutput, calls=%fused_computation.11 | convolution fusion | flops 270532608 | bytes 8650752 | tf_op jit(solution)/shard_map/she,hde->shd/dot_general | solution.py:53
  207.8 2.7 %copy.42 = bf16[1024,8,128]{2,1,0:T(8,128)(2,1)} copy(bf16[1024,8,128]{2,0,1:T(8,128)(2,1)S(1)} %fusion.7) | data formatting | bytes 4194304
  (12 shorter events, 0.0 us)
Async XLA Ops:
  7.2 4.3 %copy-start = (bf16[1024,8,128]{2,1,0:T(8,128)(2,1)S(1)}, bf16[1024,8,128]{2,1,0:T(8,128)(2,1)}, u32[]{:S(2)}) copy-start(bf16[1024,8,128]{2,1,0:T(8,128)(2,1)} %param.7) | copy-start | bytes 6291460
  7.2 59.7 %all-gather.8.cloned.1.call-start = ((), (), s32[]{:S(2)}) async-start(), calls=%async_computation.1 | async-start | bytes 2359296 | tf_op jit(solution)/shard_map/all_gather | solution.py:27
  14.8 110.5 %all-gather.6.cloned.1.call-start = ((), (), s32[]{:S(2)}) async-start(), calls=%async_computation | async-start | bytes 10485760 | tf_op jit(solution)/shard_map/all_gather | solution.py:10
  15.5 178.6 %all-gather.10.cloned.1.call-start = ((), (), s32[]{:S(2)}) async-start(), calls=%async_computation.2 | async-start | bytes 2359296 | tf_op jit(solution)/shard_map/all_gather | solution.py:28
  125.3 15.2 %copy-start.6 = (bf16[1024,8,128]{2,1,0:T(8,128)(2,1)S(1)}, bf16[1024,8,128]{2,1,0:T(8,128)(2,1)}, u32[]{:S(2)}) copy-start(bf16[1024,8,128]{2,1,0:T(8,128)(2,1)} %param.5) | copy-start | bytes 6291460
  139.2 1.3 copy-start.3
  142.3 4.4 %copy-start.4 = (bf16[1024,1024]{0,1:T(8,128)(2,1)S(1)}, bf16[1024,1024]{0,1:T(8,128)(2,1)}, u32[]{:S(2)}) copy-start(bf16[1024,1024]{0,1:T(8,128)(2,1)} %copy-done.3) | copy-start | bytes 6291460
  146.7 10.2 %copy-start.1 = (bf16[1024,8,128]{2,1,0:T(8,128)(2,1)S(1)}, bf16[1024,8,128]{2,1,0:T(8,128)(2,1)}, u32[]{:S(2)}) copy-start(bf16[1024,8,128]{2,1,0:T(8,128)(2,1)} %param.6) | copy-start | bytes 6291460
  167.8 4.2 %copy-start.5 = (pred[1024,1024]{1,0:T(8,128)(4,1)S(1)}, pred[1024,1024]{1,0:T(8,128)(4,1)}, u32[]{:S(2)}) copy-start(pred[1024,1024]{1,0:T(8,128)(4,1)} %iota_compare_fusion) | copy-start | bytes 3145732
  194.1 2.2 %copy-start.2 = (bf16[1024,8,128]{2,1,0:T(8,128)(2,1)S(1)}, bf16[1024,8,128]{2,1,0:T(8,128)(2,1)}, u32[]{:S(2)}) copy-start(bf16[1024,8,128]{2,1,0:T(8,128)(2,1)} %param.6) | copy-start | bytes 6291460
Sparse Core Ops, SparseCore 0:
  14.9 51.9 all-gather.7
  68.5 56.7 all-gather.5
  142.4 49.2 all-gather.9
where the time goes:
time: 217 us
  waiting for transfers between devices  107 us (49%)
  matrix products  72.9 us (34%)
  local copies, waits for them, and re-layouts  17.5 us (8%)
  between operations  13.8 us (6%)
  other arithmetic  5.61 us (3%)
    all_gather x1, waiting for transfers between devices, body(): lax.all_gather(d_layer, 'head', axis=1, tiled=True)  56.3 us
    all_gather x1, waiting for transfers between devices, body(): lax.all_gather(key_state[None], 'ctx', axis=0, tiled=True)  50 us
    unnamed x18, local copies, waits for them, and re-layouts  16.6 us
    dot_general x1, matrix products, body(): lax.dot_general(lax.all_gather(d_layer, 'head', axis=1, tiled=True), out_...  13.9 us
    dot_general x1, matrix products, body(): jnp.einsum('hts,the->she', score_keys, grad_scaled, preferred_element_typ...  11.4 us
    dot_general x1, matrix products, body(): jnp.einsum('hts,shd->thd', score_grad, keys, preferred_element_type=jnp.f...  10.9 us
    dot_general x1, matrix products, body(): jnp.einsum('hts,thd->shd', score_grad, queries, preferred_element_type=jn...  10.7 us
    dot_general x1, matrix products, body(): jnp.einsum('thd,shd->hts', grad_scaled, values, preferred_element_type=jn...  10.2 us
  transfers between devices with their start and end apart: 3, of which 2 were waited for; matrix products, arithmetic and copies ran while one was open for 25% of the time, Pallas kernels for 0%

commit v1 on v0

v1 whole, which is shorter than its diff:
```python
import jax
import jax.numpy as jnp
from jax import lax
from jax.sharding import PartitionSpec as P

ROW_CHUNKS = 4


def swap(array, axis, size, bit):
    return lax.ppermute(array, axis, [(i, i ^ bit) for i in range(size)])


def gather_features(d_layer, size):
    rows = d_layer.shape[0] // ROW_CHUNKS
    held = [[d_layer[i * rows : (i + 1) * rows] for i in range(ROW_CHUNKS)]]
    bits = []
    bit = 1
    while bit < size:
        bits.append(bit)
        bit *= 2
    order = [0]
    top = bits[-1]
    across = [swap(c, "head", size, top) for c in held[0]]
    own = {0: held[0], top: across}
    for bit in bits[:-1]:
        for offset in list(own):
            own[offset ^ bit] = [swap(c, "head", size, bit) for c in own[offset]]
    return own


def shifted(array, size, step):
    return lax.ppermute(array, "ctx", [(i, i + step) for i in range(size) if 0 <= i + step < size])


def scan_states(state, size, direction):
    total = state.astype(jnp.float32)
    exclusive = jnp.zeros_like(total)
    step = 1
    while step < size:
        came = shifted(total.astype(jnp.bfloat16), size, direction * step).astype(jnp.float32)
        exclusive = exclusive + came
        total = total + came
        step *= 2
    return exclusive.astype(jnp.bfloat16)


def body(n_ctx, n_head, queries, keys, values, d_layer, out_weight):
    tokens, heads_local, head_dim = queries.shape
    features = d_layer.shape[1]
    mine = lax.axis_index("head")
    pieces = gather_features(d_layer, n_head)

    key_state = jnp.einsum("thd,the->hde", keys, values, preferred_element_type=jnp.float32).astype(
        jnp.bfloat16
    )
    prefix_low = scan_states(key_state, n_ctx, 1)

    def weight_of(offset):
        return lax.dynamic_slice_in_dim(out_weight, (mine ^ offset) * features, features, axis=1)

    weights = {offset: weight_of(offset) for offset in pieces}
    flat = []
    for i in range(ROW_CHUNKS):
        total = None
        for offset in pieces:
            part = lax.dot_general(
                pieces[offset][i], weights[offset], (((1,), (1,)), ((), ())), preferred_element_type=jnp.float32
            )
            total = part if total is None else total + part
        flat.append(total.astype(jnp.bfloat16))
    d_heads = jnp.concatenate(flat, axis=0).reshape(tokens, heads_local, head_dim)
    block_index = lax.axis_index("ctx")
    position = block_index * tokens + jnp.arange(tokens, dtype=jnp.int32)
    scale = lax.rsqrt((head_dim * (position + 1)).astype(jnp.float32))
    grad_scaled = (d_heads.astype(jnp.float32) * scale[:, None, None]).astype(jnp.bfloat16)
    query_state = jnp.einsum(
        "thd,the->hde", queries, grad_scaled, preferred_element_type=jnp.float32
    ).astype(jnp.bfloat16)
    suffix_low = scan_states(query_state, n_ctx, -1)
    lower = jnp.tril(jnp.ones((tokens, tokens), dtype=bool))[None]
    score_grad = jnp.where(
        lower,
        jnp.einsum("thd,shd->hts", grad_scaled, values, preferred_element_type=jnp.float32),
        0.0,
    ).astype(jnp.bfloat16)
    score_keys = jnp.where(
        lower, jnp.einsum("thd,shd->hts", queries, keys, preferred_element_type=jnp.float32), 0.0
    ).astype(jnp.bfloat16)
    d_queries = scale[:, None, None] * jnp.einsum(
        "the,hde->thd", d_heads, prefix_low, preferred_element_type=jnp.float32
    )
    d_queries = d_queries + jnp.einsum(
        "hts,shd->thd", score_grad, keys, preferred_element_type=jnp.float32
    )
    d_keys = jnp.einsum("hts,thd->shd", score_grad, queries, preferred_element_type=jnp.float32)
    d_keys = d_keys + jnp.einsum(
        "she,hde->shd", values, suffix_low, preferred_element_type=jnp.float32
    )
    d_values = jnp.einsum(
        "hts,the->she", score_keys, grad_scaled, preferred_element_type=jnp.float32
    )
    d_values = d_values + jnp.einsum(
        "shd,hde->she", keys, suffix_low, preferred_element_type=jnp.float32
    )
    return (
        d_queries.astype(jnp.bfloat16),
        d_keys.astype(jnp.bfloat16),
        d_values.astype(jnp.bfloat16),
    )


def solution(mesh):
    in_specs = (
        P("ctx", "head", None),
        P("ctx", "head", None),
        P("ctx", "head", None),
        P("ctx", "head"),
        P("head", None),
    )
    out_specs = (P("ctx", "head", None), P("ctx", "head", None), P("ctx", "head", None))

    def program(queries, keys, values, d_layer, out_weight):
        return body(mesh.shape["ctx"], mesh.shape["head"], queries, keys, values, d_layer, out_weight)

    return jax.shard_map(program, mesh=mesh, in_specs=in_specs, out_specs=out_specs, check_vma=False)
```

time: 217 us -> 149 us (0.69)
  waiting for transfers between devices: 107 us -> 11.9 us
  starting transfers between devices: 0.12 us -> 24.2 us
  matrix products: 72.9 us -> 87.9 us
  between operations: 13.8 us -> 1.02 us
  local copies, waits for them, and re-layouts: 17.5 us -> 19.7 us
    all_gather x3 -> x0, waiting for transfers between devices: 106 us -> none  [the longest x1 56.3 us: body(): lax.all_gather(d_layer, 'head', axis=1, tiled=True)]
    ppermute x0 -> x18, starting transfers between devices: none -> 24.2 us  [the longest x6 17.3 us: shifted(): lax.ppermute(array, 'ctx', [(i, i + step) for i in range(size) if 0 <= i...]
    dot_general x1 -> x16, matrix products: 13.9 us -> 27.9 us  [body(): lax.dot_general(pieces[offset][i], weights[offset], (((1,), (1,)), ((), (...]
    ppermute x0 -> x18, waiting for transfers between devices: none -> 11.9 us  [the longest x6 11.8 us: shifted(): lax.ppermute(array, 'ctx', [(i, i + step) for i in range(size) if 0 <= i...]
    reduce_sum x2 -> x0, other arithmetic: 4.28 us -> none  [the longest x1 2.22 us: body(): jnp.sum(jnp.where(after, every_query.astype(jnp.float32), 0.0), axis=0)]
    slice x0 -> x1, local copies, waits for them, and re-layouts: none -> 3.03 us  [gather_features(): held = [[d_layer[i * rows:(i + 1) * rows] for i in range(ROW_CHUNKS)]]]
    reshape x0 -> x1, local copies, waits for them, and re-layouts: none -> 2.78 us  [body(): jnp.concatenate(flat, axis=0).reshape(tokens, heads_local, head_dim)]
    unnamed x18 -> x30, local copies, waits for them, and re-layouts: 16.6 us -> 13.9 us
  transfers between devices with their start and end apart: 3 -> 18, of which waited for: 2 -> 2; matrix products, arithmetic and copies ran while one was open for 25% -> 64% of each run, Pallas kernels for 0% -> 0%
where the time goes in v1:
time: 149 us
  matrix products  87.9 us (59%)
  starting transfers between devices  24.2 us (16%)
  local copies, waits for them, and re-layouts  19.7 us (13%)
  waiting for transfers between devices  11.9 us (8%)
  other arithmetic  3.93 us (3%)
    dot_general x16, matrix products, body(): lax.dot_general(pieces[offset][i], weights[offset], (((1,), (1,)), ((), (...  27.9 us
    ppermute x6, starting transfers between devices, shifted(): lax.ppermute(array, 'ctx', [(i, i + step) for i in range(size) if 0 <= i...  17.3 us
    unnamed x30, local copies, waits for them, and re-layouts  13.9 us
    dot_general x1, matrix products, body(): jnp.einsum('hts,the->she', score_keys, grad_scaled, preferred_element_typ...  12 us
    ppermute x6, waiting for transfers between devices, shifted(): lax.ppermute(array, 'ctx', [(i, i + step) for i in range(size) if 0 <= i...  11.8 us
    dot_general x1, matrix products, body(): jnp.einsum('hts,shd->thd', score_grad, keys, preferred_element_type=jnp.f...  11.5 us
    dot_general x1, matrix products, body(): jnp.einsum('thd,shd->hts', grad_scaled, values, preferred_element_type=jn...  10.8 us
    dot_general x1, matrix products, body(): jnp.einsum('hts,thd->shd', score_grad, queries, preferred_element_type=jn...  10.8 us
  transfers between devices with their start and end apart: 18, of which 2 were waited for; matrix products, arithmetic and copies ran while one was open for 64% of the time, Pallas kernels for 0%

profile of v1, /device:TPU:0, one launch (start us, length us, event | category | flops | bytes accessed | tf_op | source)
XLA Modules:
  0.0 148.7 jit_solution(16487063146189839091)
XLA Ops:
  0.6 3.0 %fusion.108 = (bf16[256,1024]{1,0:T(8,128)(2,1)}, bf16[256,1024]{1,0:T(8,128)(2,1)}, bf16[256,1024]{1,0:T(8,128)(2,1)}, bf16[256,1024]{1,0:T(8,128)(2,1)}) fusion(bf16[1024,1024]{1,0:T(8,128)(2,1)} %param.8), kind=kLoop, calls=%fused_computation.106 | loop fusion | bytes 4194304 | tf_op jit(solution)/shard_map/slice | solution.py:15
  3.7 2.9 %collective-permute-start.12 = (bf16[256,1024]{1,0:T(8,128)(2,1)}, bf16[256,1024]{1,0:T(8,128)(2,1)S(1)}, u32[]{:S(2)}, u32[]{:S(2)}) collective-permute-start(bf16[256,1024]{1,0:T(8,128)(2,1)} %get-tuple-element.8), channel_id=1, source_target_pairs={{0,2},{1,3},{2,0},{3,1},{4,6},{5,7},{6,4},{7,5},{8,10},{9,11},{10,... | collective-permute-start | bytes 1572872 | tf_op jit(solution)/shard_map/ppermute | solution.py:10
  7.1 2.8 %copy.8 = bf16[1024,8,128]{0,2,1:T(8,128)(2,1)} copy(bf16[1024,8,128]{2,1,0:T(8,128)(2,1)S(1)} %copy-done) | data formatting | bytes 4194304 | tf_op args[1]
  10.0 3.3 %fusion.67 = bf16[8,128,128]{2,1,0:T(8,128)(2,1)S(1)} fusion(bf16[1024,8,128]{0,2,1:T(8,128)(2,1)} %copy.8, bf16[1024,8,128]{2,1,0:T(8,128)(2,1)} %param.7), kind=kOutput, calls=%fused_computation.67 | convolution fusion | flops 268566528 | bytes 4456448 | tf_op jit(solution)/shard_map/thd,the->hde/dot_general | solution.py:53
  13.3 3.7 %collective-permute-start = (bf16[8,128,128]{2,1,0:T(8,128)(2,1)S(1)}, bf16[8,128,128]{2,1,0:T(8,128)(2,1)S(1)}, u32[]{:S(2)}, u32[]{:S(2)}) collective-permute-start(bf16[8,128,128]{2,1,0:T(8,128)(2,1)S(1)} %fusion.67), channel_id=1, source_target_pairs={{0,4},{4,8},{8,12},{12,16},{16,20},{20,24},{24,28},{1,5},{5,9},{9,... | collective-permute-start | bytes 786440 | tf_op jit(solution)/shard_map/ppermute | solution.py:32
  18.3 3.3 %fusion.35 = f32[1024,256]{0,1:T(8,128)} fusion(bf16[1024,4096]{1,0:T(8,128)(2,1)} %param.9, s32[]{:T(128)S(6)} %select_n.21, bf16[1024,1024]{1,0:T(8,128)(2,1)S(1)} %copy-done.4), kind=kOutput, calls=%fused_computation.51 | convolution fusion | flops 536870912 | bytes 3670020 | tf_op jit(solution)/shard_map/dot_general | solution.py:66
  21.6 3.3 %fusion.37 = f32[1024,256]{0,1:T(8,128)} fusion(bf16[1024,4096]{1,0:T(8,128)(2,1)} %param.9, s32[]{:T(128)S(6)} %select_n.21, bf16[1024,1024]{1,0:T(8,128)(2,1)S(1)} %copy-done.4), kind=kOutput, calls=%fused_computation.53 | convolution fusion | flops 536870912 | bytes 3670020 | tf_op jit(solution)/shard_map/dot_general | solution.py:66
  24.9 3.3 %fusion.39 = f32[1024,256]{0,1:T(8,128)} fusion(bf16[1024,4096]{1,0:T(8,128)(2,1)} %param.9, s32[]{:T(128)S(6)} %select_n.21, bf16[1024,1024]{1,0:T(8,128)(2,1)S(1)} %copy-done.4), kind=kOutput, calls=%fused_computation.55 | convolution fusion | flops 536870912 | bytes 3670020 | tf_op jit(solution)/shard_map/dot_general | solution.py:66
  28.2 2.5 %fusion.41 = f32[1024,256]{0,1:T(8,128)S(1)} fusion(bf16[1024,4096]{1,0:T(8,128)(2,1)} %param.9, s32[]{:T(128)S(6)} %select_n.21, bf16[1024,1024]{1,0:T(8,128)(2,1)S(1)} %copy-done.4), kind=kOutput, calls=%fused_computation.57 | convolution fusion | flops 536870912 | bytes 3670020 | tf_op jit(solution)/shard_map/dot_general | solution.py:66
  30.7 1.6 %collective-permute-start.6 = (bf16[256,1024]{1,0:T(8,128)(2,1)S(1)}, bf16[256,1024]{1,0:T(8,128)(2,1)S(1)}, u32[]{:S(2)}, u32[]{:S(2)}) collective-permute-start(bf16[256,1024]{1,0:T(8,128)(2,1)S(1)} %copy-done.9), channel_id=1, source_target_pairs={{0,2},{1,3},{2,0},{3,1},{4,6},{5,7},{6,4},{7,5},{8,10},{9,11},{10,... | collective-permute-start | bytes 1572872 | tf_op jit(solution)/shard_map/ppermute | solution.py:10
  32.5 2.5 %convolution_add_fusion.2 = f32[1024,256]{0,1:T(8,128)S(1)} fusion(f32[1024,256]{0,1:T(8,128)S(1)} %copy-done.7, bf16[256,1024]{1,0:T(8,128)(2,1)S(1)} %collective-permute-done.12, bf16[1024,4096]{1,0:T(8,128)(2,1)} %param.9, s32[]{:T(128)S(6)} %select_n.22), kind=kOutput, calls=%fused_computation.29 | convolution fusion | flops 537133056 | bytes 4718596 | tf_op jit(solution)/shard_map/dot_general | solution.py:66
  35.6 2.7 %convolution_add_fusion.5 = f32[1024,256]{0,1:T(8,128)S(1)} fusion(f32[1024,256]{0,1:T(8,128)S(1)} %copy-done.6, bf16[256,1024]{1,0:T(8,128)(2,1)} %collective-permute-done.9, bf16[1024,4096]{1,0:T(8,128)(2,1)} %param.9, s32[]{:T(128)S(6)} %select_n.22), kind=kOutput, calls=%fused_computation.32 | convolution fusion | flops 537133056 | bytes 4718596 | tf_op jit(solution)/shard_map/dot_general | solution.py:66
  38.3 3.5 %collective-permute-start.1 = (bf16[8,128,128]{2,1,0:T(8,128)(2,1)S(1)}, bf16[8,128,128]{2,1,0:T(8,128)(2,1)S(1)}, u32[]{:S(2)}, u32[]{:S(2)}) collective-permute-start(bf16[8,128,128]{2,1,0:T(8,128)(2,1)S(1)} %fusion.82), channel_id=1, source_target_pairs={{0,8},{4,12},{8,16},{12,20},{16,24},{20,28},{1,9},{5,13},{9,17},{1... | collective-permute-start | bytes 786440 | tf_op jit(solution)/shard_map/ppermute | solution.py:32
  41.8 2.4 %convolution_add_fusion.1 = f32[1024,256]{0,1:T(8,128)S(1)} fusion(f32[1024,256]{0,1:T(8,128)S(1)} %convolution_add_fusion.2, bf16[256,1024]{1,0:T(8,128)(2,1)} %collective-permute-done.13, bf16[1024,4096]{1,0:T(8,128)(2,1)} %param.9, s32[]{:T(128)S(6)} %select_n.23), kind=kOutput, calls=%fused_computation.28 | convolution fusion | flops 537133056 | bytes 4718596 | tf_op jit(solution)/shard_map/dot_general | solution.py:66
  44.3 3.3 %collective-permute-done.1 = bf16[8,128,128]{2,1,0:T(8,128)(2,1)S(1)} collective-permute-done((bf16[8,128,128]{2,1,0:T(8,128)(2,1)S(1)}, bf16[8,128,128]{2,1,0:T(8,128)(2,1)S(1)}, u32[]{:S(2)}, u32[]{:S(2)}) %collective-permute-start.1) | collective-permute-done | bytes 262176 | tf_op jit(solution)/shard_map/ppermute | solution.py:32
  48.4 6.2 %collective-permute-start.2 = (bf16[8,128,128]{2,1,0:T(8,128)(2,1)}, bf16[8,128,128]{2,1,0:T(8,128)(2,1)}, u32[]{:S(2)}, u32[]{:S(2)}) collective-permute-start(bf16[8,128,128]{2,1,0:T(8,128)(2,1)} %fusion.78), channel_id=1, source_target_pairs={{0,16},{4,20},{8,24},{12,28},{1,17},{5,21},{9,25},{13,29},{2,18},{... | collective-permute-start | bytes 786440 | tf_op jit(solution)/shard_map/ppermute | solution.py:32
  54.7 1.8 %convolution_add_fusion.4 = f32[1024,256]{0,1:T(8,128)S(1)} fusion(f32[1024,256]{0,1:T(8,128)S(1)} %convolution_add_fusion.5, bf16[256,1024]{1,0:T(8,128)(2,1)} %collective-permute-done.10, bf16[1024,4096]{1,0:T(8,128)(2,1)S(1)} %bitcast.43, s32[]{:T(128)S(6)} %select_n.23), kind=kOutput, calls=%fused_computation.31 | convolution fusion | flops 537133056 | bytes 4718596 | tf_op jit(solution)/shard_map/dot_general | solution.py:66
  64.2 2.8 %copy.31 = bf16[1024,1024]{0,1:T(8,128)(2,1)} copy(bf16[1024,1024]{1,0:T(8,128)(2,1)S(1)} %pad_maximum_fusion) | data formatting | bytes 4194304 | tf_op jit(solution)/shard_map/reshape | solution.py:71
  67.0 10.8 %select_convert_fusion.1 = bf16[8,1024,1024]{2,1,0:T(8,128)(2,1)} fusion(pred[1024,1024]{1,0:T(8,128)(4,1)} %iota_compare_fusion, bf16[1024,8,128]{2,1,0:T(8,128)(2,1)} %param.7, bf16[1024,8,128]{0,2,1:T(8,128)(2,1)} %bitcast.44, f32[1024]{0:T(1024)S(1)} %convert_rsqrt_fusion), kind=kOutput, calls=%fused_computation.1 | convolution fusion | flops 2167406592 | bytes 22024192 | tf_op jit(solution)/shard_map/thd,shd->hts/dot_general | solution.py:83
  77.8 11.5 %fusion.8 = f32[8,1024,128]{1,2,0:T(8,128)} fusion(bf16[8,1024,1024]{2,1,0:T(8,128)(2,1)} %select_convert_fusion.1, bf16[1024,8,128]{2,1,0:T(8,128)(2,1)S(1)} %copy-done.1), kind=kOutput, calls=%fused_computation.15 | convolution fusion | flops 2147483648 | bytes 23068672 | tf_op jit(solution)/shard_map/hts,shd->thd/dot_general | solution.py:92
  90.2 1.3 collective-permute-start.15
  91.5 10.8 %fusion.17 = f32[8,1024,128]{2,1,0:T(8,128)} fusion(bf16[8,1024,1024]{2,1,0:T(8,128)(2,1)} %select_convert_fusion.1, bf16[1024,8,128]{2,1,0:T(8,128)(2,1)S(1)} %copy-done.10), kind=kOutput, calls=%fused_computation.21 | convolution fusion | flops 2147483648 | bytes 23068672 | tf_op jit(solution)/shard_map/hts,thd->shd/dot_general | solution.py:95
  103.0 1.3 collective-permute-start.16
  104.3 12.0 %fusion = f32[8,128,1024]{2,1,0:T(8,128)} fusion(pred[1024,1024]{1,0:T(8,128)(4,1)} %iota_compare_fusion, bf16[1024,8,128]{0,2,1:T(8,128)(2,1)} %copy.8, bf16[1024,8,128]{2,1,0:T(8,128)(2,1)} %param.5, bf16[1024,8,128]{0,2,1:T(8,128)(2,1)} %bitcast.45, f32[1024]{0:T(1024)S(1)} %convert_rsqrt_fusion), kind=kOutput, calls=%fused_computation.2 | convolution fusion | flops 4314890240 | bytes 11538432 | tf_op jit(solution)/shard_map/hts,the->she/dot_general | solution.py:99
  117.1 1.3 collective-permute-start.17
  118.4 4.9 %fusion.6 = bf16[1024,8,128]{0,2,1:T(8,128)(2,1)} fusion(f32[8,1024,128]{1,2,0:T(8,128)} %fusion.8, bf16[1024,8,128]{0,2,1:T(8,128)(2,1)} %bitcast.46, f32[1024]{0:T(1024)S(1)} %convert_rsqrt_fusion, bf16[8,128,128]{2,1,0:T(8,128)(2,1)S(1)} %collective-permute-done.1, bf16[8,128,128]{2,1,0:T(8,128)(2,1)S(1)} %collective-permute-done, ...), kind=kOutput, calls=%fused_computation.9 | convolution fusion | flops 272367616 | bytes 9179136 | tf_op jit(solution)/shard_map/the,hde->thd/dot_general | solution.py:89
  123.4 4.1 %copy.23 = bf16[1024,8,128]{2,1,0:T(8,128)(2,1)} copy(bf16[1024,8,128]{0,2,1:T(8,128)(2,1)} %fusion.6) | data formatting | bytes 4194304
  127.5 8.5 %collective-permute-done.17 = bf16[8,128,128]{1,2,0:T(8,128)(2,1)S(1)} collective-permute-done((bf16[8,128,128]{1,2,0:T(8,128)(2,1)}, bf16[8,128,128]{1,2,0:T(8,128)(2,1)S(1)}, u32[]{:S(2)}, u32[]{:S(2)}) %collective-permute-start.17) | collective-permute-done | bytes 262176 | tf_op jit(solution)/shard_map/ppermute | solution.py:32
  136.0 3.5 %fusion.5 = bf16[1024,8,128]{2,0,1:T(8,128)(2,1)S(1)} fusion(f32[8,1024,128]{2,1,0:T(8,128)} %fusion.17, bf16[1024,8,128]{2,1,0:T(8,128)(2,1)} %param.7, bf16[8,128,128]{1,2,0:T(8,128)(2,1)S(1)} %collective-permute-done.16, bf16[8,128,128]{1,2,0:T(8,128)(2,1)S(1)} %collective-permute-done.15, bf16[8,128,128]{1,2,0:T(8,128)(2,1)S(1)} %collective-permute-done.17), kind=kOutput, calls=%fused_computation.7 | convolution fusion | flops 271319040 | bytes 9175040 | tf_op jit(solution)/shard_map/she,hde->shd/dot_general | solution.py:96
  139.6 2.7 %copy.24 = bf16[1024,8,128]{2,1,0:T(8,128)(2,1)} copy(bf16[1024,8,128]{2,0,1:T(8,128)(2,1)S(1)} %fusion.5) | data formatting | bytes 4194304
  142.2 2.3 %fusion.10 = bf16[1024,8,128]{0,2,1:T(8,128)(2,1)} fusion(f32[8,128,1024]{2,1,0:T(8,128)S(1)} %copy-done.3, bf16[1024,8,128]{2,1,0:T(8,128)(2,1)S(1)} %copy-done.1, bf16[8,128,128]{1,2,0:T(8,128)(2,1)S(1)} %collective-permute-done.16, bf16[8,128,128]{1,2,0:T(8,128)(2,1)S(1)} %collective-permute-done.15, bf16[8,128,128]{1,2,0:T(8,128)(2,1)S(1)} %collective-permute-done.17), kind=kOutput, calls=%fused_computation.17 | convolution fusion | flops 271319040 | bytes 9175040 | tf_op jit(solution)/shard_map/shd,hde->she/dot_general | solution.py:102
  144.5 4.1 %copy.25 = bf16[1024,8,128]{2,1,0:T(8,128)(2,1)} copy(bf16[1024,8,128]{0,2,1:T(8,128)(2,1)} %fusion.10) | data formatting | bytes 4194304
  (69 shorter events, 13.4 us)
Async XLA Ops:
  0.6 6.5 %copy-start = (bf16[1024,8,128]{2,1,0:T(8,128)(2,1)S(1)}, bf16[1024,8,128]{2,1,0:T(8,128)(2,1)}, u32[]{:S(2)}) copy-start(bf16[1024,8,128]{2,1,0:T(8,128)(2,1)} %param.6) | copy-start | bytes 6291460
  3.7 28.7 %collective-permute-start.12 = (bf16[256,1024]{1,0:T(8,128)(2,1)}, bf16[256,1024]{1,0:T(8,128)(2,1)S(1)}, u32[]{:S(2)}, u32[]{:S(2)}) collective-permute-start(bf16[256,1024]{1,0:T(8,128)(2,1)} %get-tuple-element.8), channel_id=1, source_target_pairs={{0,2},{1,3},{2,0},{3,1},{4,6},{5,7},{6,4},{7,5},{8,10},{9,11},{10,... | collective-permute-start | bytes 1572872 | tf_op jit(solution)/shard_map/ppermute | solution.py:10
  6.6 31.7 %collective-permute-start.13 = (bf16[256,1024]{1,0:T(8,128)(2,1)}, bf16[256,1024]{1,0:T(8,128)(2,1)}, u32[]{:S(2)}, u32[]{:S(2)}) collective-permute-start(bf16[256,1024]{1,0:T(8,128)(2,1)} %get-tuple-element.8), channel_id=1, source_target_pairs={{0,1},{1,0},{2,3},{3,2},{4,5},{5,4},{6,7},{7,6},{8,9},{9,8},{10,11... | collective-permute-start | bytes 1572872 | tf_op jit(solution)/shard_map/ppermute | solution.py:10
  6.6 28.4 %collective-permute-start.9 = (bf16[256,1024]{1,0:T(8,128)(2,1)}, bf16[256,1024]{1,0:T(8,128)(2,1)}, u32[]{:S(2)}, u32[]{:S(2)}) collective-permute-start(bf16[256,1024]{1,0:T(8,128)(2,1)} %get-tuple-element.9), channel_id=1, source_target_pairs={{0,2},{1,3},{2,0},{3,1},{4,6},{5,7},{6,4},{7,5},{8,10},{9,11},{10,... | collective-permute-start | bytes 1572872 | tf_op jit(solution)/shard_map/ppermute | solution.py:10
  6.7 41.8 %collective-permute-start.10 = (bf16[256,1024]{1,0:T(8,128)(2,1)}, bf16[256,1024]{1,0:T(8,128)(2,1)}, u32[]{:S(2)}, u32[]{:S(2)}) collective-permute-start(bf16[256,1024]{1,0:T(8,128)(2,1)} %get-tuple-element.9), channel_id=1, source_target_pairs={{0,1},{1,0},{2,3},{3,2},{4,5},{5,4},{6,7},{7,6},{8,9},{9,8},{10,11... | collective-permute-start | bytes 1572872 | tf_op jit(solution)/shard_map/ppermute | solution.py:10
  10.0 8.3 %copy-start.4 = (bf16[1024,1024]{1,0:T(8,128)(2,1)S(1)}, bf16[1024,1024]{1,0:T(8,128)(2,1)}, u32[]{:S(2)}) copy-start(bf16[1024,1024]{1,0:T(8,128)(2,1)} %param.8) | copy-start | bytes 6291460
  13.3 17.4 %collective-permute-start = (bf16[8,128,128]{2,1,0:T(8,128)(2,1)S(1)}, bf16[8,128,128]{2,1,0:T(8,128)(2,1)S(1)}, u32[]{:S(2)}, u32[]{:S(2)}) collective-permute-start(bf16[8,128,128]{2,1,0:T(8,128)(2,1)S(1)} %fusion.67), channel_id=1, source_target_pairs={{0,4},{4,8},{8,12},{12,16},{16,20},{20,24},{24,28},{1,5},{5,9},{9,... | collective-permute-start | bytes 786440 | tf_op jit(solution)/shard_map/ppermute | solution.py:32
  28.2 2.5 %copy-start.9 = (bf16[256,1024]{1,0:T(8,128)(2,1)S(1)}, bf16[256,1024]{1,0:T(8,128)(2,1)}, u32[]{:S(2)}) copy-start(bf16[256,1024]{1,0:T(8,128)(2,1)} %get-tuple-element.7) | copy-start | bytes 1572868
  28.2 4.2 %copy-start.7 = (f32[1024,256]{0,1:T(8,128)S(1)}, f32[1024,256]{0,1:T(8,128)}, u32[]{:S(2)}) copy-start(f32[1024,256]{0,1:T(8,128)} %fusion.35) | copy-start | bytes 3145732
  30.7 25.8 %collective-permute-start.6 = (bf16[256,1024]{1,0:T(8,128)(2,1)S(1)}, bf16[256,1024]{1,0:T(8,128)(2,1)S(1)}, u32[]{:S(2)}, u32[]{:S(2)}) collective-permute-start(bf16[256,1024]{1,0:T(8,128)(2,1)S(1)} %copy-done.9), channel_id=1, source_target_pairs={{0,2},{1,3},{2,0},{3,1},{4,6},{5,7},{6,4},{7,5},{8,10},{9,11},{10,... | collective-permute-start | bytes 1572872 | tf_op jit(solution)/shard_map/ppermute | solution.py:10
  32.3 2.7 %copy-start.8 = (bf16[256,1024]{1,0:T(8,128)(2,1)S(1)}, bf16[256,1024]{1,0:T(8,128)(2,1)}, u32[]{:S(2)}) copy-start(bf16[256,1024]{1,0:T(8,128)(2,1)} %get-tuple-element.6) | copy-start | bytes 1572868
  32.4 3.3 %copy-start.6 = (f32[1024,256]{0,1:T(8,128)S(1)}, f32[1024,256]{0,1:T(8,128)}, u32[]{:S(2)}) copy-start(f32[1024,256]{0,1:T(8,128)} %fusion.37) | copy-start | bytes 3145732
  32.4 25.2 %collective-permute-start.7 = (bf16[256,1024]{1,0:T(8,128)(2,1)S(1)}, bf16[256,1024]{1,0:T(8,128)(2,1)S(1)}, u32[]{:S(2)}, u32[]{:S(2)}) collective-permute-start(bf16[256,1024]{1,0:T(8,128)(2,1)S(1)} %copy-done.9), channel_id=1, source_target_pairs={{0,1},{1,0},{2,3},{3,2},{4,5},{5,4},{6,7},{7,6},{8,9},{9,8},{10,11... | collective-permute-start | bytes 1572872 | tf_op jit(solution)/shard_map/ppermute | solution.py:10
  32.5 22.2 %slice-start = ((s8[8388608]{0:T(1024)(128)(4,1)}), s8[4194304]{0:T(1024)(128)(4,1)S(1)}, s32[]{:S(2)}) async-start(s8[8388608]{0:T(1024)(128)(4,1)} %bitcast.42), calls=%async_computation | async-start | bytes 8388608
  35.0 19.7 %slice-start.1 = ((s8[8388608]{0:T(1024)(128)(4,1)}), s8[4194304]{0:T(1024)(128)(4,1)S(1)}, s32[]{:S(2)}) async-start(s8[8388608]{0:T(1024)(128)(4,1)} %bitcast.42), calls=%async_computation.1 | async-start | bytes 8388608
  35.0 23.7 %collective-permute-start.3 = (bf16[256,1024]{1,0:T(8,128)(2,1)S(1)}, bf16[256,1024]{1,0:T(8,128)(2,1)S(1)}, u32[]{:S(2)}, u32[]{:S(2)}) collective-permute-start(bf16[256,1024]{1,0:T(8,128)(2,1)S(1)} %copy-done.8), channel_id=1, source_target_pairs={{0,2},{1,3},{2,0},{3,1},{4,6},{5,7},{6,4},{7,5},{8,10},{9,11},{10,... | collective-permute-start | bytes 1572872 | tf_op jit(solution)/shard_map/ppermute | solution.py:10
  38.3 9.3 %collective-permute-start.1 = (bf16[8,128,128]{2,1,0:T(8,128)(2,1)S(1)}, bf16[8,128,128]{2,1,0:T(8,128)(2,1)S(1)}, u32[]{:S(2)}, u32[]{:S(2)}) collective-permute-start(bf16[8,128,128]{2,1,0:T(8,128)(2,1)S(1)} %fusion.82), channel_id=1, source_target_pairs={{0,8},{4,12},{8,16},{12,20},{16,24},{20,28},{1,9},{5,13},{9,17},{1... | collective-permute-start | bytes 786440 | tf_op jit(solution)/shard_map/ppermute | solution.py:32
  47.6 12.2 %collective-permute-start.4 = (bf16[256,1024]{1,0:T(8,128)(2,1)S(1)}, bf16[256,1024]{1,0:T(8,128)(2,1)S(1)}, u32[]{:S(2)}, u32[]{:S(2)}) collective-permute-start(bf16[256,1024]{1,0:T(8,128)(2,1)S(1)} %copy-done.8), channel_id=1, source_target_pairs={{0,1},{1,0},{2,3},{3,2},{4,5},{5,4},{6,7},{7,6},{8,9},{9,8},{10,11... | collective-permute-start | bytes 1572872 | tf_op jit(solution)/shard_map/ppermute | solution.py:10
  48.4 8.4 %copy-start.5 = (f32[1024,256]{0,1:T(8,128)S(1)}, f32[1024,256]{0,1:T(8,128)}, u32[]{:S(2)}) copy-start(f32[1024,256]{0,1:T(8,128)} %fusion.39) | copy-start | bytes 3145732
  48.4 70.0 %collective-permute-start.2 = (bf16[8,128,128]{2,1,0:T(8,128)(2,1)}, bf16[8,128,128]{2,1,0:T(8,128)(2,1)}, u32[]{:S(2)}, u32[]{:S(2)}) collective-permute-start(bf16[8,128,128]{2,1,0:T(8,128)(2,1)} %fusion.78), channel_id=1, source_target_pairs={{0,16},{4,20},{8,24},{12,28},{1,17},{5,21},{9,25},{13,29},{2,18},{... | collective-permute-start | bytes 786440 | tf_op jit(solution)/shard_map/ppermute | solution.py:32
  56.6 4.4 %collective-permute-start.14 = (bf16[256,1024]{1,0:T(8,128)(2,1)S(1)}, bf16[256,1024]{1,0:T(8,128)(2,1)S(1)}, u32[]{:S(2)}, u32[]{:S(2)}) collective-permute-start(bf16[256,1024]{1,0:T(8,128)(2,1)S(1)} %collective-permute-done.12), channel_id=1, source_target_pairs={{0,1},{1,0},{2,3},{3,2},{4,5},{5,4},{6,7},{7,6},{8,9},{9,8},{10,11... | collective-permute-start | bytes 1572872 | tf_op jit(solution)/shard_map/ppermute | solution.py:10
  57.6 4.1 %collective-permute-start.11 = (bf16[256,1024]{1,0:T(8,128)(2,1)}, bf16[256,1024]{1,0:T(8,128)(2,1)S(1)}, u32[]{:S(2)}, u32[]{:S(2)}) collective-permute-start(bf16[256,1024]{1,0:T(8,128)(2,1)} %collective-permute-done.9), channel_id=1, source_target_pairs={{0,1},{1,0},{2,3},{3,2},{4,5},{5,4},{6,7},{7,6},{8,9},{9,8},{10,11... | collective-permute-start | bytes 1572872 | tf_op jit(solution)/shard_map/ppermute | solution.py:10
  58.8 3.7 %collective-permute-start.8 = (bf16[256,1024]{1,0:T(8,128)(2,1)S(1)}, bf16[256,1024]{1,0:T(8,128)(2,1)S(1)}, u32[]{:S(2)}, u32[]{:S(2)}) collective-permute-start(bf16[256,1024]{1,0:T(8,128)(2,1)S(1)} %collective-permute-done.6), channel_id=1, source_target_pairs={{0,1},{1,0},{2,3},{3,2},{4,5},{5,4},{6,7},{7,6},{8,9},{9,8},{10,11... | collective-permute-start | bytes 1572872 | tf_op jit(solution)/shard_map/ppermute | solution.py:10
  59.8 3.4 %collective-permute-start.5 = (bf16[256,1024]{1,0:T(8,128)(2,1)S(1)}, bf16[256,1024]{1,0:T(8,128)(2,1)S(1)}, u32[]{:S(2)}, u32[]{:S(2)}) collective-permute-start(bf16[256,1024]{1,0:T(8,128)(2,1)S(1)} %collective-permute-done.3), channel_id=1, source_target_pairs={{0,1},{1,0},{2,3},{3,2},{4,5},{5,4},{6,7},{7,6},{8,9},{9,8},{10,11... | collective-permute-start | bytes 1572872 | tf_op jit(solution)/shard_map/ppermute | solution.py:10
  67.0 10.9 %copy-start.1 = (bf16[1024,8,128]{2,1,0:T(8,128)(2,1)S(1)}, bf16[1024,8,128]{2,1,0:T(8,128)(2,1)}, u32[]{:S(2)}) copy-start(bf16[1024,8,128]{2,1,0:T(8,128)(2,1)} %param.6) | copy-start | bytes 6291460
  77.8 11.5 %copy-start.2 = (bf16[1024,1024]{0,1:T(8,128)(2,1)S(1)}, bf16[1024,1024]{0,1:T(8,128)(2,1)}, u32[]{:S(2)}) copy-start(bf16[1024,1024]{0,1:T(8,128)(2,1)} %copy.31) | copy-start | bytes 6291460
  77.8 11.5 %copy-start.10 = (bf16[1024,8,128]{2,1,0:T(8,128)(2,1)S(1)}, bf16[1024,8,128]{2,1,0:T(8,128)(2,1)}, u32[]{:S(2)}) copy-start(bf16[1024,8,128]{2,1,0:T(8,128)(2,1)} %param.5) | copy-start | bytes 6291460
  90.2 12.1 %collective-permute-start.15 = (bf16[8,128,128]{1,2,0:T(8,128)(2,1)S(1)}, bf16[8,128,128]{1,2,0:T(8,128)(2,1)S(1)}, u32[]{:S(2)}, u32[]{:S(2)}) collective-permute-start(bf16[8,128,128]{1,2,0:T(8,128)(2,1)S(1)} %fusion.73), channel_id=1, source_target_pairs={{4,0},{8,4},{12,8},{16,12},{20,16},{24,20},{28,24},{5,1},{9,5},{13... | collective-permute-start | bytes 786440 | tf_op jit(solution)/shard_map/ppermute | solution.py:32
  103.0 13.3 %collective-permute-start.16 = (bf16[8,128,128]{1,2,0:T(8,128)(2,1)}, bf16[8,128,128]{1,2,0:T(8,128)(2,1)S(1)}, u32[]{:S(2)}, u32[]{:S(2)}) collective-permute-start(bf16[8,128,128]{1,2,0:T(8,128)(2,1)} %fusion.83), channel_id=1, source_target_pairs={{8,0},{12,4},{16,8},{20,12},{24,16},{28,20},{9,1},{13,5},{17,9},{2... | collective-permute-start | bytes 786440 | tf_op jit(solution)/shard_map/ppermute | solution.py:32
  117.1 18.9 %collective-permute-start.17 = (bf16[8,128,128]{1,2,0:T(8,128)(2,1)}, bf16[8,128,128]{1,2,0:T(8,128)(2,1)S(1)}, u32[]{:S(2)}, u32[]{:S(2)}) collective-permute-start(bf16[8,128,128]{1,2,0:T(8,128)(2,1)} %fusion.81), channel_id=1, source_target_pairs={{16,0},{20,4},{24,8},{28,12},{17,1},{21,5},{25,9},{29,13},{18,2},{... | collective-permute-start | bytes 786440 | tf_op jit(solution)/shard_map/ppermute | solution.py:32
  139.6 2.7 %copy-start.3 = (f32[8,128,1024]{2,1,0:T(8,128)S(1)}, f32[8,128,1024]{2,1,0:T(8,128)}, u32[]{:S(2)}) copy-start(f32[8,128,1024]{2,1,0:T(8,128)} %fusion) | copy-start | bytes 12582916

commit v2 on v0

v2 whole, which is shorter than its diff:
```python
import functools

import jax
import jax.numpy as jnp
from jax import lax
from jax.experimental import pallas as pl
from jax.experimental.pallas import tpu as pltpu
from jax.sharding import PartitionSpec as P

CHUNK = 256
PAIR = 2
F32 = jnp.float32
BF16 = jnp.bfloat16
NT = (((1,), (1,)), ((), ()))
NN = (((1,), (0,)), ((), ()))
TN = (((0,), (0,)), ((), ()))
VMEM_LIMIT = 40 * 1024 * 1024


def dot(a, b, dims):
    return lax.dot_general(a, b, dims, preferred_element_type=F32)


def params():
    return pltpu.CompilerParams(vmem_limit_bytes=VMEM_LIMIT)


def shape(dims, dtype):
    return jax.ShapeDtypeStruct(dims, dtype)


def prepare_kernel(heads, dk, half_ref, q_ref, k_ref, v_ref, qf_ref, kf_ref, vf_ref, before_ref, keep_ref, send_ref, wide, acc):
    step = pl.program_id(0)
    rows = qf_ref.shape[0]

    @pl.when(step == 0)
    def _():
        acc[...] = jnp.zeros_like(acc)

    for source, target in ((q_ref, qf_ref), (k_ref, kf_ref), (v_ref, vf_ref)):
        wide[...] = source[...].astype(F32)
        for h in range(heads):
            target[:, h * dk : (h + 1) * dk] = wide[pl.ds(h, rows, stride=heads), :].astype(BF16)
    before_ref[0] = acc[...]
    for h in range(heads):
        cols = slice(h * dk, (h + 1) * dk)
        acc[h] += dot(kf_ref[:, cols], vf_ref[:, cols], TN)

    @pl.when(step == pl.num_programs(0) - 1)
    def _():
        low, high = acc[: heads // 2].astype(BF16), acc[heads // 2 :].astype(BF16)
        first = half_ref[0] == 0
        keep_ref[...] = jnp.where(first, low, high)
        send_ref[...] = jnp.where(first, high, low)


def prepare(half, q, k, v, tokens, heads, dk):
    n = tokens // CHUNK
    raw = pl.BlockSpec((CHUNK * heads, dk), lambda i, s: (i, 0))
    flat = pl.BlockSpec((CHUNK, heads * dk), lambda i, s: (i, 0))
    part = pl.BlockSpec((heads // 2, dk, dk), lambda i, s: (0, 0, 0))
    width = heads * dk
    return pl.pallas_call(
        functools.partial(prepare_kernel, heads, dk),
        grid_spec=pltpu.PrefetchScalarGridSpec(
            num_scalar_prefetch=1,
            grid=(n,),
            in_specs=[raw] * 3,
            out_specs=[flat] * 3 + [pl.BlockSpec((1, heads, dk, dk), lambda i, s: (i, 0, 0, 0)), part, part],
            scratch_shapes=[pltpu.VMEM((CHUNK * heads, dk), F32), pltpu.VMEM((heads, dk, dk), F32)],
        ),
        out_shape=[shape((tokens, width), BF16)] * 3
        + [shape((n, heads, dk, dk), F32)]
        + [shape((heads // 2, dk, dk), BF16)] * 2,
        compiler_params=params(),
        cost_estimate=pl.CostEstimate(
            flops=4 * tokens * width * dk, bytes_accessed=12 * tokens * width + 4 * n * width * dk, transcendentals=0
        ),
        name="prepare",
    )(half, q, k, v)


def early_kernel(index_ref, a_ref, b_ref, wa_ref, wb_ref, out_ref):
    out_ref[...] = dot(a_ref[...], wa_ref[...], NT) + dot(b_ref[...], wb_ref[...], NT)


def early(index, a, b, weight):
    tokens, features = a.shape
    width = weight.shape[0]
    tile = 256
    whole = pl.BlockSpec((tokens, features), lambda j, s: (0, 0))
    return pl.pallas_call(
        early_kernel,
        grid_spec=pltpu.PrefetchScalarGridSpec(
            num_scalar_prefetch=1,
            grid=(width // tile,),
            in_specs=[
                whole,
                whole,
                pl.BlockSpec((tile, features), lambda j, s: (j, s[0])),
                pl.BlockSpec((tile, features), lambda j, s: (j, s[1])),
            ],
            out_specs=pl.BlockSpec((tokens, tile), lambda j, s: (0, j)),
        ),
        out_shape=shape((tokens, width), F32),
        compiler_params=params(),
        cost_estimate=pl.CostEstimate(
            flops=4 * tokens * features * width,
            bytes_accessed=4 * tokens * features + 4 * features * width + 4 * tokens * width,
            transcendentals=0,
        ),
        name="early",
    )(index, a, b, weight, weight)


def late_kernel(last, dk, index_ref, a_ref, b_ref, wa_ref, wb_ref, part_ref, scale_ref, q_ref, *refs):
    j = pl.program_id(0)
    state_ref, refs = (refs[0], refs[1:]) if len(refs) == (4 if last else 3) else (None, refs)
    d_ref = refs[0]
    full = part_ref[...] + dot(a_ref[...], wa_ref[...], NT) + dot(b_ref[...], wb_ref[...], NT)
    low = full.astype(BF16)
    d_ref[...] = low
    states = []
    for i in range(PAIR):
        cols = slice(i * dk, (i + 1) * dk)
        grad = (low[:, cols].astype(F32) * scale_ref[...]).astype(BF16)
        state = dot(q_ref[:, cols], grad, TN)
        states.append(state if state_ref is None else state + state_ref[i])
    if not last:
        for i in range(PAIR):
            refs[1][i] = states[i]
        return
    keep_ref, send_ref = refs[1:]
    steps = pl.num_programs(0) // 2
    place = lax.rem(j, steps) * PAIR
    mine = (j // steps) == index_ref[2]

    @pl.when(mine)
    def _():
        for i in range(PAIR):
            keep_ref[place + i] = states[i].astype(BF16)

    @pl.when(jnp.logical_not(mine))
    def _():
        for i in range(PAIR):
            send_ref[place + i] = states[i].astype(BF16)


def late(chunk, last, index, a, b, weight, part, scale, q, state, heads, dk):
    rows, features = a.shape
    width = weight.shape[0]
    tile = PAIR * dk
    whole = pl.BlockSpec((rows, features), lambda j, s: (0, 0))
    in_specs = [
        whole,
        whole,
        pl.BlockSpec((tile, features), lambda j, s: (j, s[0])),
        pl.BlockSpec((tile, features), lambda j, s: (j, s[1])),
        pl.BlockSpec((rows, tile), lambda j, s: (chunk, j)),
        pl.BlockSpec((rows, dk), lambda j, s: (chunk, 0)),
        pl.BlockSpec((rows, tile), lambda j, s: (chunk, j)),
    ]
    pair = pl.BlockSpec((PAIR, dk, dk), lambda j, s: (j, 0, 0))
    args = [a, b, weight, weight, part, scale, q]
    if state is not None:
        in_specs.append(pair)
        args.append(state)
    out_specs = [pl.BlockSpec((rows, tile), lambda j, s: (0, j))]
    out_shape = [shape((rows, width), BF16)]
    if last:
        out_specs += [pl.BlockSpec((heads // 2, dk, dk), lambda j, s: (0, 0, 0))] * 2
        out_shape += [shape((heads // 2, dk, dk), BF16)] * 2
    else:
        out_specs.append(pair)
        out_shape.append(shape((heads, dk, dk), F32))
    return pl.pallas_call(
        functools.partial(late_kernel, last, dk),
        grid_spec=pltpu.PrefetchScalarGridSpec(
            num_scalar_prefetch=1, grid=(width // tile,), in_specs=in_specs, out_specs=out_specs
        ),
        out_shape=out_shape,
        compiler_params=params(),
        cost_estimate=pl.CostEstimate(
            flops=4 * rows * features * width, bytes_accessed=4 * rows * features + 4 * features * width, transcendentals=0
        ),
        name="late",
    )(index, *args)


def within_kernel(heads, dk, index_ref, q_ref, k_ref, v_ref, d_ref, scale_ref, before_ref, own_ref, other_ref, *refs):
    j = pl.program_id(0)
    state_ref = refs[0]
    dq_ref, dk_ref, dv_ref, wide = refs[-4:]
    rows = q_ref.shape[0]
    mine = (j // (pl.num_programs(0) // 2)) == index_ref[2]
    t = lax.broadcasted_iota(jnp.int32, (rows, rows), 0)
    s = lax.broadcasted_iota(jnp.int32, (rows, rows), 1)
    lower = s <= t
    scale = scale_ref[...]
    for i in range(PAIR):
        cols = slice(i * dk, (i + 1) * dk)
        q, k, v, d = q_ref[:, cols], k_ref[:, cols], v_ref[:, cols], d_ref[:, cols]
        grad = (d.astype(F32) * scale).astype(BF16)
        score_grad = jnp.where(lower, dot(grad, v, NT), 0.0).astype(BF16)
        score_keys = jnp.where(lower, dot(q, k, NT), 0.0).astype(BF16)
        earlier = jnp.where(mine, own_ref[i], other_ref[i]).astype(F32) + before_ref[0, i]
        dq = scale * dot(d, earlier.astype(BF16), NT) + dot(score_grad, k, NN)
        dkey = dot(score_grad, q, TN)
        dval = dot(score_keys, grad, TN)
        if state_ref is not None:
            after = state_ref[i].astype(BF16)
            dkey = dkey + dot(v, after, NT)
            dval = dval + dot(k, after, NN)
        wide[pl.ds(j * PAIR + i, rows, stride=heads), :] = dq
        dk_ref[:, cols] = dkey.astype(BF16)
        dv_ref[:, cols] = dval.astype(BF16)

    @pl.when(j == pl.num_programs(0) - 1)
    def _():
        dq_ref[...] = wide[...].astype(BF16)


def within(chunk, index, q, k, v, d, scale, before, own, other, state, held, heads, dk):
    tokens, width = q.shape
    rows = CHUNK
    tile = PAIR * dk
    half_steps = heads // (2 * PAIR)
    block = pl.BlockSpec((rows, tile), lambda j, s: (chunk, j))
    pair = pl.BlockSpec((PAIR, dk, dk), lambda j, s: (j, 0, 0))
    half_pair = pl.BlockSpec((PAIR, dk, dk), lambda j, s: (lax.rem(j, half_steps), 0, 0))
    in_specs = [
        block,
        block,
        block,
        pl.BlockSpec((rows, tile), lambda j, s: (0, j)),
        pl.BlockSpec((rows, dk), lambda j, s: (chunk, 0)),
        pl.BlockSpec((1, PAIR, dk, dk), lambda j, s: (chunk, j, 0, 0)),
        half_pair,
        half_pair,
    ]
    args = [q, k, v, d, scale, before, own, other]
    kernel = functools.partial(within_kernel, heads, dk)
    if state is not None:
        in_specs.append(pair)
        args.append(state)
    else:
        inner = kernel

        def kernel(*refs):
            inner(*refs[:9], None, *refs[9:])

    aliases = {}
    if held is not None:
        for out, array in enumerate(held):
            aliases[1 + len(args)] = out
            args.append(array)
            in_specs.append(pl.BlockSpec(memory_space=pl.ANY))
    return pl.pallas_call(
        kernel,
        grid_spec=pltpu.PrefetchScalarGridSpec(
            num_scalar_prefetch=1,
            grid=(width // tile,),
            in_specs=in_specs,
            out_specs=[pl.BlockSpec((rows * heads, dk), lambda j, s: (chunk, 0)), block, block],
            scratch_shapes=[pltpu.VMEM((rows * heads, dk), F32)],
        ),
        out_shape=[shape((tokens * heads, dk), BF16)] + [shape((tokens, width), BF16)] * 2,
        input_output_aliases=aliases,
        compiler_params=params(),
        cost_estimate=pl.CostEstimate(
            flops=16 * rows * rows * width, bytes_accessed=14 * rows * width, transcendentals=0
        ),
        name="within",
    )(index, *args)


def finish_kernel(heads, dk, index_ref, k_ref, v_ref, dkp_ref, dvp_ref, own_ref, other_ref, dk_ref, dv_ref, wide_k, wide_v):
    rows = k_ref.shape[0]
    first = index_ref[2] == 0
    half = heads // 2
    for h in range(heads):
        cols = slice(h * dk, (h + 1) * dk)
        own, other = own_ref[h % half], other_ref[h % half]
        after = jnp.where(first, own, other) if h < half else jnp.where(first, other, own)
        wide_k[pl.ds(h, rows, stride=heads), :] = dkp_ref[:, cols].astype(F32) + dot(v_ref[:, cols], after, NT)
        wide_v[pl.ds(h, rows, stride=heads), :] = dvp_ref[:, cols].astype(F32) + dot(k_ref[:, cols], after, NN)
    dk_ref[...] = wide_k[...].astype(BF16)
    dv_ref[...] = wide_v[...].astype(BF16)


def finish(index, k, v, dkp, dvp, own, other, heads, dk):
    tokens, width = k.shape
    rows = 128
    block = pl.BlockSpec((rows, width), lambda i, s: (i, 0))
    part = pl.BlockSpec((heads // 2, dk, dk), lambda i, s: (0, 0, 0))
    out = pl.BlockSpec((rows * heads, dk), lambda i, s: (i, 0))
    return pl.pallas_call(
        functools.partial(finish_kernel, heads, dk),
        grid_spec=pltpu.PrefetchScalarGridSpec(
            num_scalar_prefetch=1,
            grid=(tokens // rows,),
            in_specs=[block] * 4 + [part] * 2,
            out_specs=[out, out],
            scratch_shapes=[pltpu.VMEM((rows * heads, dk), F32)] * 2,
        ),
        out_shape=[shape((tokens * heads, dk), BF16)] * 2,
        compiler_params=params(),
        cost_estimate=pl.CostEstimate(
            flops=4 * tokens * width * dk, bytes_accessed=12 * tokens * width, transcendentals=0
        ),
        name="finish",
    )(index, k, v, dkp, dvp, own, other)


def swap(array, axis, size, bit):
    return lax.ppermute(array, axis, [(i, i ^ bit) for i in range(size)])


def shifted(array, size, step):
    return lax.ppermute(array, "ctx", [(i, i + step) for i in range(size) if 0 <= i + step < size])


def scan_states(keep, send, size, odd, direction):
    came = swap(send, "ctx", size, 1)
    own = keep.astype(F32)
    total = own + came.astype(F32)
    exclusive = jnp.zeros_like(total)
    step = 2
    while step < size:
        got = shifted(total.astype(BF16), size, direction * step).astype(F32)
        exclusive = exclusive + got
        total = total + got
        step *= 2
    later = odd if direction == 1 else jnp.logical_not(odd)
    other = swap((exclusive + jnp.where(later, 0.0, own)).astype(BF16), "ctx", size, 1)
    mine = exclusive + jnp.where(later, came.astype(F32), 0.0)
    return mine.astype(BF16), other


def body(n_ctx, n_head, queries, keys, values, d_layer, out_weight):
    tokens, heads, dk = queries.shape
    n = tokens // CHUNK
    block = lax.axis_index("ctx").astype(jnp.int32)
    place = lax.axis_index("head").astype(jnp.int32)
    odd = (block & 1) == 1
    half = (block & 1).astype(jnp.int32)

    near = n_head // 2
    far = 1
    order = list(range(n))[::-1]
    across = {c: swap(d_layer[c * CHUNK : (c + 1) * CHUNK], "head", n_head, near) for c in order}
    beside = swap(d_layer, "head", n_head, far)
    both = {c: swap(across[c], "head", n_head, far) for c in order}

    position = block * tokens + jnp.arange(tokens, dtype=jnp.int32)
    scale = lax.rsqrt((dk * (position + 1)).astype(F32))
    scale = jnp.broadcast_to(scale[:, None], (tokens, dk))

    flat = (tokens * heads, dk)
    q, k, v, before, keep, send = prepare(
        half[None], queries.reshape(flat), keys.reshape(flat), values.reshape(flat), tokens, heads, dk
    )
    own_prefix, other_prefix = scan_states(keep, send, n_ctx, odd, 1)

    part = early(jnp.stack([place, place ^ far]), d_layer, beside, out_weight)
    index = jnp.stack([place ^ near, place ^ near ^ far, half])
    state = None
    d, after = {}, {}
    for c in order:
        after[c] = state
        result = late(c, c == 0, index, across[c], both[c], out_weight, part, scale, q, state, heads, dk)
        if c == 0:
            d[c], keep, send = result
        else:
            d[c], state = result
    own_suffix, other_suffix = scan_states(keep, send, n_ctx, odd, -1)
    held = None
    for c in order:
        held = within(c, index, q, k, v, d[c], scale, before, own_prefix, other_prefix, after[c], held, heads, dk)
    d_queries, dk_part, dv_part = held
    d_keys, d_values = finish(index, k, v, dk_part, dv_part, own_suffix, other_suffix, heads, dk)
    return tuple(a.reshape(tokens, heads, dk) for a in (d_queries, d_keys, d_values))


def solution(mesh):
    in_specs = (
        P("ctx", "head", None),
        P("ctx", "head", None),
        P("ctx", "head", None),
        P("ctx", "head"),
        P("head", None),
    )
    out_specs = (P("ctx", "head", None), P("ctx", "head", None), P("ctx", "head", None))

    def program(queries, keys, values, d_layer, out_weight):
        return body(mesh.shape["ctx"], mesh.shape["head"], queries, keys, values, d_layer, out_weight)

    return jax.shard_map(program, mesh=mesh, in_specs=in_specs, out_specs=out_specs, check_vma=False)
```

time: 217 us -> 131 us (0.60); the launches traced: 217 us -> 128 us
  waiting for transfers between devices: 107 us -> 28.8 us
  matrix products: 72.9 us -> 0 us
  Pallas kernels: 0 us -> 62.9 us
  starting transfers between devices: 0.12 us -> 23.3 us
  between operations: 13.8 us -> 0.87 us
  local copies, waits for them, and re-layouts: 17.5 us -> 11.8 us
  other arithmetic: 5.61 us -> 0.54 us
    all_gather x3 -> x0, waiting for transfers between devices: 106 us -> none  [the longest x1 56.3 us: body(): lax.all_gather(d_layer, 'head', axis=1, tiled=True)]
    dot_general x10 -> x0, matrix products: 72.9 us -> none  [the longest x1 13.9 us: body(): lax.dot_general(lax.all_gather(d_layer, 'head', axis=1, tiled=True), out_...]
    pallas_call x0 -> x11, Pallas kernels: none -> 62.9 us  [the longest x4 21.7 us: late(): pl.pallas_call(functools.partial(late_kernel, last, dk), grid_spec=pltpu....]
    ppermute x0 -> x17, waiting for transfers between devices: none -> 28.8 us  [the longest x13 24 us: swap(): return lax.ppermute(array, axis, [(i, i ^ bit) for i in range(size)])]
    ppermute x0 -> x17, starting transfers between devices: none -> 23.3 us  [the longest x13 12.3 us: swap(): return lax.ppermute(array, axis, [(i, i ^ bit) for i in range(size)])]
    unnamed x18, local copies, waits for them, and re-layouts: 16.6 us -> 8.74 us
    reduce_sum x2 -> x0, other arithmetic: 4.28 us -> none  [the longest x1 2.22 us: body(): jnp.sum(jnp.where(after, every_query.astype(jnp.float32), 0.0), axis=0)]
    slice x0 -> x1, local copies, waits for them, and re-layouts: none -> 2.87 us  [body(): d_layer[c * CHUNK:(c + 1) * CHUNK]]
  transfers between devices with their start and end apart: 3 -> 17, of which waited for: 2 -> 6; matrix products, arithmetic and copies ran while one was open for 25% -> 3% of each run, Pallas kernels for 0% -> 44%
where the time goes in v2:
time: 131 us; the launch traced here: 128 us
  Pallas kernels  62.9 us (48%)
  waiting for transfers between devices  28.8 us (22%)
  starting transfers between devices  23.3 us (18%)
  local copies, waits for them, and re-layouts  11.8 us (9%)
    ppermute x13, waiting for transfers between devices, swap(): return lax.ppermute(array, axis, [(i, i ^ bit) for i in range(size)])  24 us
    pallas_call x4, Pallas kernels, late(): pl.pallas_call(functools.partial(late_kernel, last, dk), grid_spec=pltpu....  21.7 us
    pallas_call x4, Pallas kernels, within(): pl.pallas_call(kernel, grid_spec=pltpu.PrefetchScalarGridSpec(num_scalar_...  20.9 us
    ppermute x13, starting transfers between devices, swap(): return lax.ppermute(array, axis, [(i, i ^ bit) for i in range(size)])  12.3 us
    ppermute x4, starting transfers between devices, shifted(): lax.ppermute(array, 'ctx', [(i, i + step) for i in range(size) if 0 <= i...  11 us
    unnamed x18, local copies, waits for them, and re-layouts  8.74 us
    pallas_call x1, Pallas kernels, early(): pl.pallas_call(early_kernel, grid_spec=pltpu.PrefetchScalarGridSpec(num_s...  8.11 us
    pallas_call x1, Pallas kernels, finish(): pl.pallas_call(functools.partial(finish_kernel, heads, dk), grid_spec=plt...  6.26 us
  transfers between devices with their start and end apart: 17, of which 6 were waited for; matrix products, arithmetic and copies ran while one was open for 3% of the time, Pallas kernels for 44%

profile of v2, /device:TPU:0, one launch (start us, length us, event | category | flops | bytes accessed | tf_op | source)
XLA Modules:
  0.0 128.2 jit_solution(6496562603715035126)
XLA Ops:
  1.1 2.9 %fusion.12 = (bf16[256,1024]{1,0:T(8,128)(2,1)}, bf16[256,1024]{1,0:T(8,128)(2,1)}, bf16[256,1024]{1,0:T(8,128)(2,1)}, bf16[256,1024]{1,0:T(8,128)(2,1)}) fusion(bf16[1024,1024]{1,0:T(8,128)(2,1)} %a_ref.1), kind=kLoop, calls=%fused_computation.25 | loop fusion | bytes 4194304 | tf_op jit(solution)/shard_map/slice | solution.py:351
  4.0 2.5 %collective-permute-start.7 = (bf16[256,1024]{1,0:T(8,128)(2,1)}, bf16[256,1024]{1,0:T(8,128)(2,1)S(1)}, u32[]{:S(2)}, u32[]{:S(2)}) collective-permute-start(bf16[256,1024]{1,0:T(8,128)(2,1)} %get-tuple-element.61), channel_id=1, source_target_pairs={{0,2},{1,3},{2,0},{3,1},{4,6},{5,7},{6,4},{7,5},{8,10},{9,11},{10,... | collective-permute-start | bytes 1572872 | tf_op jit(solution)/shard_map/ppermute | solution.py:316
  6.6 1.6 %copy-done.7 = bf16[1024,8,128]{2,1,0:T(8,128)(2,1)S(1)} copy-done((bf16[1024,8,128]{2,1,0:T(8,128)(2,1)S(1)}, bf16[1024,8,128]{2,1,0:T(8,128)(2,1)}, u32[]{:S(2)}) %copy-start.7) | copy-done | bytes 2097176
  8.2 1.6 %copy-done.8 = bf16[1024,8,128]{2,1,0:T(8,128)(2,1)S(1)} copy-done((bf16[1024,8,128]{2,1,0:T(8,128)(2,1)S(1)}, bf16[1024,8,128]{2,1,0:T(8,128)(2,1)}, u32[]{:S(2)}) %copy-start.8) | copy-done | bytes 2097176
  9.7 5.8 %prepare.1 = (bf16[1024,1024]{1,0:T(8,128)(2,1)S(1)}, bf16[1024,1024]{1,0:T(8,128)(2,1)S(1)}, bf16[1024,1024]{1,0:T(8,128)(2,1)S(1)}, f32[4,8,128,128]{3,2,1,0:T...) custom-call(s32[1]{0:T(128)} %bitcast.2.half_ref, bf16[8192,128]{1,0:T(8,128)(2,1)S(1)} %bitcast.11, ...), custom_call_target="tpu_custom_call" | custom-call | flops 536870912 | bytes 14680064 | tf_op jit(solution)/shard_map/prepare/pallas_call | solution.py:63
  15.6 1.3 %copy-done = bf16[1024,1024]{1,0:T(8,128)(2,1)} copy-done((bf16[1024,1024]{1,0:T(8,128)(2,1)}, bf16[1024,1024]{1,0:T(8,128)(2,1)S(1)}, u32[]{:S(2)}) %copy-start) | copy-done | bytes 2097176
  16.9 1.3 %copy-done.2 = bf16[1024,1024]{1,0:T(8,128)(2,1)} copy-done((bf16[1024,1024]{1,0:T(8,128)(2,1)}, bf16[1024,1024]{1,0:T(8,128)(2,1)S(1)}, u32[]{:S(2)}) %copy-start.2) | copy-done | bytes 2097176
  18.2 1.3 %copy-done.4 = f32[4,8,128,128]{3,2,1,0:T(8,128)} copy-done((f32[4,8,128,128]{3,2,1,0:T(8,128)}, f32[4,8,128,128]{3,2,1,0:T(8,128)S(1)}, u32[]{:S(2)}) %copy-start.4) | copy-done | bytes 2097176
  19.5 2.0 %collective-permute-start.9 = (bf16[4,128,128]{2,1,0:T(8,128)(2,1)S(1)}, bf16[4,128,128]{2,1,0:T(8,128)(2,1)S(1)}, u32[]{:S(2)}, u32[]{:S(2)}) collective-permute-start(bf16[4,128,128]{2,1,0:T(8,128)(2,1)S(1)} %get-tuple-element.41), channel_id=1, source_target_pairs={{0,4},{4,0},{8,12},{12,8},{16,20},{20,16},{24,28},{28,24},{1,5},{5... | collective-permute-start | bytes 393224 | tf_op jit(solution)/shard_map/ppermute | solution.py:316
  21.6 1.5 %collective-permute-start.3 = (bf16[256,1024]{1,0:T(8,128)(2,1)}, bf16[256,1024]{1,0:T(8,128)(2,1)}, u32[]{:S(2)}, u32[]{:S(2)}) collective-permute-start(bf16[256,1024]{1,0:T(8,128)(2,1)} %get-tuple-element.62), channel_id=1, source_target_pairs={{0,2},{1,3},{2,0},{3,1},{4,6},{5,7},{6,4},{7,5},{8,10},{9,11},{10,... | collective-permute-start | bytes 1572872 | tf_op jit(solution)/shard_map/ppermute | solution.py:316
  23.1 2.1 %collective-permute-done.9 = bf16[4,128,128]{2,1,0:T(8,128)(2,1)S(1)} collective-permute-done((bf16[4,128,128]{2,1,0:T(8,128)(2,1)S(1)}, bf16[4,128,128]{2,1,0:T(8,128)(2,1)S(1)}, u32[]{:S(2)}, u32[]{:S(2)}) %collective-permute-start.9) | collective-permute-done | bytes 131104 | tf_op jit(solution)/shard_map/ppermute | solution.py:316
  25.2 1.7 %collective-permute-start = (bf16[256,1024]{1,0:T(8,128)(2,1)}, bf16[256,1024]{1,0:T(8,128)(2,1)S(1)}, u32[]{:S(2)}, u32[]{:S(2)}) collective-permute-start(bf16[256,1024]{1,0:T(8,128)(2,1)} %get-tuple-element.63), channel_id=1, source_target_pairs={{0,2},{1,3},{2,0},{3,1},{4,6},{5,7},{6,4},{7,5},{8,10},{9,11},{10,... | collective-permute-start | bytes 1572872 | tf_op jit(solution)/shard_map/ppermute | solution.py:316
  27.1 3.6 %collective-permute-done.5.a_ref = bf16[256,1024]{1,0:T(8,128)(2,1)S(1)} collective-permute-done((bf16[256,1024]{1,0:T(8,128)(2,1)}, bf16[256,1024]{1,0:T(8,128)(2,1)S(1)}, u32[]{:S(2)}, u32[]{:S(2)}) %collective-permute-start.5) | collective-permute-done | bytes 524320 | tf_op jit(solution)/shard_map/ppermute | solution.py:316
  30.8 11.3 %collective-permute-done.3.a_ref = bf16[256,1024]{1,0:T(8,128)(2,1)} collective-permute-done((bf16[256,1024]{1,0:T(8,128)(2,1)}, bf16[256,1024]{1,0:T(8,128)(2,1)}, u32[]{:S(2)}, u32[]{:S(2)}) %collective-permute-start.3) | collective-permute-done | bytes 524320 | tf_op jit(solution)/shard_map/ppermute | solution.py:316
  42.1 3.9 %collective-permute-start.10 = (bf16[4,128,128]{2,1,0:T(8,128)(2,1)S(1)}, bf16[4,128,128]{2,1,0:T(8,128)(2,1)S(1)}, u32[]{:S(2)}, u32[]{:S(2)}) collective-permute-start(bf16[4,128,128]{2,1,0:T(8,128)(2,1)S(1)} %fusion.10), channel_id=1, source_target_pairs={{0,8},{4,12},{8,16},{12,20},{16,24},{20,28},{1,9},{5,13},{9,17},{1... | collective-permute-start | bytes 393224 | tf_op jit(solution)/shard_map/ppermute | solution.py:320
  46.0 7.0 %collective-permute-done.a_ref = bf16[256,1024]{1,0:T(8,128)(2,1)S(1)} collective-permute-done((bf16[256,1024]{1,0:T(8,128)(2,1)}, bf16[256,1024]{1,0:T(8,128)(2,1)S(1)}, u32[]{:S(2)}, u32[]{:S(2)}) %collective-permute-start) | collective-permute-done | bytes 524320 | tf_op jit(solution)/shard_map/ppermute | solution.py:316
  53.5 1.6 %copy-done.6 = bf16[1024,1024]{1,0:T(8,128)(2,1)S(1)} copy-done((bf16[1024,1024]{1,0:T(8,128)(2,1)S(1)}, bf16[1024,1024]{1,0:T(8,128)(2,1)}, u32[]{:S(2)}) %copy-start.6) | copy-done | bytes 2097176
  55.1 8.1 %early.1.part_ref = f32[1024,1024]{1,0:T(8,128)S(1)} custom-call(s32[2]{0:T(128)S(1)} %pad_add_fusion.1.index_ref, bf16[1024,1024]{1,0:T(8,128)(2,1)S(1)} %copy-done.6, bf16[1024,1024]{1,0:T(8,128)(2,1)} %collective-permute-done.2.b_ref, bf16[1024,4096]{1,0:T(8,128)(2,1)} %wb_ref.9, bf16[1024,4096]{1,0:T(8,128)(2,1)} %wb_ref.9), custom_call_target="tpu_custom_call" | custom-call | flops 4294967296 | bytes 12582912 | tf_op jit(solution)/shard_map/early/pallas_call | solution.py:92
  63.4 5.3 %late.4 = (bf16[256,1024]{1,0:T(8,128)(2,1)S(1)}, f32[8,128,128]{2,1,0:T(8,128)S(1)}) custom-call(s32[3]{0:T(128)S(1)} %pad_add_fusion.index_ref.refs_0_, bf16[256,1024]{1,0:T(8,128)(2,1)S(1)} %collective-permute-done.7.a_ref, bf16[256,1024]{1,0:T(8,128)(2,1)S(1)} %collective-permute-done.8.b_ref, bf16[1024,4096]{1,0:T(8,128)(2,1)} %wb_ref.9, ...), custom_call_target="tpu_custom_call" | custom-call | flops 1073741824 | bytes 5242880 | tf_op jit(solution)/shard_map/late/pallas_call | solution.py:176
  68.7 5.3 %late.5 = (bf16[256,1024]{1,0:T(8,128)(2,1)S(1)}, f32[8,128,128]{2,1,0:T(8,128)S(1)}) custom-call(s32[3]{0:T(128)S(1)} %pad_add_fusion.index_ref.refs_0_, bf16[256,1024]{1,0:T(8,128)(2,1)S(1)} %collective-permute-done.5.a_ref, bf16[256,1024]{1,0:T(8,128)(2,1)S(1)} %collective-permute-done.6.b_ref, bf16[1024,4096]{1,0:T(8,128)(2,1)} %wb_ref.9, ...), custom_call_target="tpu_custom_call" | custom-call | flops 1073741824 | bytes 5242880 | tf_op jit(solution)/shard_map/late/pallas_call | solution.py:176
  74.0 5.5 %late.6 = (bf16[256,1024]{1,0:T(8,128)(2,1)S(1)}, f32[8,128,128]{2,1,0:T(8,128)S(1)}) custom-call(s32[3]{0:T(128)S(1)} %pad_add_fusion.index_ref.refs_0_, bf16[256,1024]{1,0:T(8,128)(2,1)} %collective-permute-done.3.a_ref, bf16[256,1024]{1,0:T(8,128)(2,1)S(1)} %collective-permute-done.4.b_ref, bf16[1024,4096]{1,0:T(8,128)(2,1)} %wb_ref.9, ...), custom_call_target="tpu_custom_call" | custom-call | flops 1073741824 | bytes 5242880 | tf_op jit(solution)/shard_map/late/pallas_call | solution.py:176
  79.5 5.7 %late.7 = (bf16[256,1024]{1,0:T(8,128)(2,1)S(1)}, bf16[4,128,128]{2,1,0:T(8,128)(2,1)S(1)}, bf16[4,128,128]{2,1,0:T(8,128)(2,1)S(1)}) custom-call(s32[3]{0:T(128)S(1)} %pad_add_fusion.index_ref.refs_0_, bf16[256,1024]{1,0:T(8,128)(2,1)S(1)} %collective-permute-done.a_ref, bf16[256,1024]{1,0:T(8,128)(2,1)S(1)} %collective-permute-done.1.b_ref, ...), custom_call_target="tpu_custom_call" | custom-call | flops 1073741824 | bytes 5242880 | tf_op jit(solution)/shard_map/late/pallas_call | solution.py:176
  85.3 1.8 %collective-permute-start.13 = (bf16[4,128,128]{2,1,0:T(8,128)(2,1)S(1)}, bf16[4,128,128]{2,1,0:T(8,128)(2,1)S(1)}, u32[]{:S(2)}, u32[]{:S(2)}) collective-permute-start(bf16[4,128,128]{2,1,0:T(8,128)(2,1)S(1)} %get-tuple-element.58), channel_id=1, source_target_pairs={{0,4},{4,0},{8,12},{12,8},{16,20},{20,16},{24,28},{28,24},{1,5},{5... | collective-permute-start | bytes 393224 | tf_op jit(solution)/shard_map/ppermute | solution.py:316
  87.2 4.5 %collective-permute-start.11 = (bf16[4,128,128]{2,1,0:T(8,128)(2,1)S(1)}, bf16[4,128,128]{2,1,0:T(8,128)(2,1)S(1)}, u32[]{:S(2)}, u32[]{:S(2)}) collective-permute-start(bf16[4,128,128]{2,1,0:T(8,128)(2,1)S(1)} %fusion.4), channel_id=1, source_target_pairs={{0,16},{4,20},{8,24},{12,28},{1,17},{5,21},{9,25},{13,29},{2,18},{... | collective-permute-start | bytes 393224 | tf_op jit(solution)/shard_map/ppermute | solution.py:320
  91.7 1.3 %collective-permute-start.14 = (bf16[4,128,128]{2,1,0:T(8,128)(2,1)S(1)}, bf16[4,128,128]{2,1,0:T(8,128)(2,1)S(1)}, u32[]{:S(2)}, u32[]{:S(2)}) collective-permute-start(bf16[4,128,128]{2,1,0:T(8,128)(2,1)S(1)} %fusion.11), channel_id=1, source_target_pairs={{8,0},{12,4},{16,8},{20,12},{24,16},{28,20},{9,1},{13,5},{17,9},{2... | collective-permute-start | bytes 393224 | tf_op jit(solution)/shard_map/ppermute | solution.py:320
  93.0 1.3 %collective-permute-done.11 = bf16[4,128,128]{2,1,0:T(8,128)(2,1)S(1)} collective-permute-done((bf16[4,128,128]{2,1,0:T(8,128)(2,1)S(1)}, bf16[4,128,128]{2,1,0:T(8,128)(2,1)S(1)}, u32[]{:S(2)}, u32[]{:S(2)}) %collective-permute-start.11) | collective-permute-done | bytes 131104 | tf_op jit(solution)/shard_map/ppermute | solution.py:320
  95.1 3.5 %collective-permute-done.14 = bf16[4,128,128]{2,1,0:T(8,128)(2,1)S(1)} collective-permute-done((bf16[4,128,128]{2,1,0:T(8,128)(2,1)S(1)}, bf16[4,128,128]{2,1,0:T(8,128)(2,1)S(1)}, u32[]{:S(2)}, u32[]{:S(2)}) %collective-permute-start.14) | collective-permute-done | bytes 131104 | tf_op jit(solution)/shard_map/ppermute | solution.py:320
  100.0 5.1 %within.4 = (bf16[8192,128]{1,0:T(8,128)(2,1)}, bf16[1024,1024]{1,0:T(8,128)(2,1)S(1)}, bf16[1024,1024]{1,0:T(8,128)(2,1)S(1)}) custom-call(s32[3]{0:T(128)S(1)} %pad_add_fusion.index_ref.refs_0_, bf16[1024,1024]{1,0:T(8,128)(2,1)S(1)} %get-tuple-element.32.q_ref.refs_1_, bf16[1024,1024]{1,0:T(8,128)(2,1)S(1)} %copy-done.1, ...), custom_call_target="tpu_custom_call" | custom-call | flops 1073741824 | bytes 3670016 | tf_op jit(solution)/shard_map/within/pallas_call | solution.py:258
  105.2 5.3 %within.5 = (bf16[8192,128]{1,0:T(8,128)(2,1)}, bf16[1024,1024]{1,0:T(8,128)(2,1)S(1)}, bf16[1024,1024]{1,0:T(8,128)(2,1)S(1)}) custom-call(s32[3]{0:T(128)S(1)} %pad_add_fusion.index_ref.refs_0_, bf16[1024,1024]{1,0:T(8,128)(2,1)S(1)} %get-tuple-element.32.q_ref.refs_1_, ...), custom_call_target="tpu_custom_call", output_to_operand_aliasing={{0}: (10, {}), {1}: (11, {}), {2}: (12, {})} | custom-call | flops 1073741824 | bytes 3670016 | tf_op jit(solution)/shard_map/within/pallas_call | solution.py:258
  111.4 5.3 %within.6 = (bf16[8192,128]{1,0:T(8,128)(2,1)}, bf16[1024,1024]{1,0:T(8,128)(2,1)S(1)}, bf16[1024,1024]{1,0:T(8,128)(2,1)S(1)}) custom-call(s32[3]{0:T(128)S(1)} %pad_add_fusion.index_ref.refs_0_, bf16[1024,1024]{1,0:T(8,128)(2,1)S(1)} %get-tuple-element.32.q_ref.refs_1_, ...), custom_call_target="tpu_custom_call", output_to_operand_aliasing={{0}: (10, {}), {1}: (11, {}), {2}: (12, {})} | custom-call | flops 1073741824 | bytes 3670016 | tf_op jit(solution)/shard_map/within/pallas_call | solution.py:258
  116.7 5.3 %within.7 = (bf16[8192,128]{1,0:T(8,128)(2,1)}, bf16[1024,1024]{1,0:T(8,128)(2,1)S(1)}, bf16[1024,1024]{1,0:T(8,128)(2,1)S(1)}) custom-call(s32[3]{0:T(128)S(1)} %pad_add_fusion.index_ref.refs_0_, bf16[1024,1024]{1,0:T(8,128)(2,1)S(1)} %get-tuple-element.32.q_ref.refs_1_, ...), custom_call_target="tpu_custom_call", output_to_operand_aliasing={{0}: (10, {}), {1}: (11, {}), {2}: (12, {})} | custom-call | flops 1073741824 | bytes 3670016 | tf_op jit(solution)/shard_map/within/pallas_call | solution.py:258
  121.9 6.3 %finish.1 = (bf16[8192,128]{1,0:T(8,128)(2,1)}, bf16[8192,128]{1,0:T(8,128)(2,1)}) custom-call(s32[3]{0:T(128)S(1)} %pad_add_fusion.index_ref.refs_0_, bf16[1024,1024]{1,0:T(8,128)(2,1)S(1)} %copy-done.1, bf16[1024,1024]{1,0:T(8,128)(2,1)S(1)} %copy-done.3, bf16[1024,1024]{1,0:T(8,128)(2,1)S(1)} %get-tuple-element.55.dkp_ref, ...), custom_call_target="tpu_custom_call" | custom-call | flops 536870912 | bytes 12582912 | tf_op jit(solution)/shard_map/finish/pallas_call | solution.py:297
  (42 shorter events, 4.8 us)
Async XLA Ops:
  0.6 52.4 %collective-permute-start.2 = (bf16[1024,1024]{1,0:T(8,128)(2,1)}, bf16[1024,1024]{1,0:T(8,128)(2,1)}, u32[]{:S(2)}, u32[]{:S(2)}) collective-permute-start(bf16[1024,1024]{1,0:T(8,128)(2,1)} %a_ref.1), channel_id=1, source_target_pairs={{0,1},{1,0},{2,3},{3,2},{4,5},{5,4},{6,7},{7,6},{8,9},{9,8},{10,11... | collective-permute-start | bytes 6291464 | tf_op jit(solution)/shard_map/ppermute | solution.py:316
  4.0 23.0 %collective-permute-start.7 = (bf16[256,1024]{1,0:T(8,128)(2,1)}, bf16[256,1024]{1,0:T(8,128)(2,1)S(1)}, u32[]{:S(2)}, u32[]{:S(2)}) collective-permute-start(bf16[256,1024]{1,0:T(8,128)(2,1)} %get-tuple-element.61), channel_id=1, source_target_pairs={{0,2},{1,3},{2,0},{3,1},{4,6},{5,7},{6,4},{7,5},{8,10},{9,11},{10,... | collective-permute-start | bytes 1572872 | tf_op jit(solution)/shard_map/ppermute | solution.py:316
  6.5 24.2 %collective-permute-start.5 = (bf16[256,1024]{1,0:T(8,128)(2,1)}, bf16[256,1024]{1,0:T(8,128)(2,1)S(1)}, u32[]{:S(2)}, u32[]{:S(2)}) collective-permute-start(bf16[256,1024]{1,0:T(8,128)(2,1)} %get-tuple-element.64), channel_id=1, source_target_pairs={{0,2},{1,3},{2,0},{3,1},{4,6},{5,7},{6,4},{7,5},{8,10},{9,11},{10,... | collective-permute-start | bytes 1572872 | tf_op jit(solution)/shard_map/ppermute | solution.py:316
  6.6 1.6 %copy-start.7 = (bf16[1024,8,128]{2,1,0:T(8,128)(2,1)S(1)}, bf16[1024,8,128]{2,1,0:T(8,128)(2,1)}, u32[]{:S(2)}) copy-start(bf16[1024,8,128]{2,1,0:T(8,128)(2,1)} %param.5) | copy-start | bytes 6291460
  8.1 1.6 %copy-start.8 = (bf16[1024,8,128]{2,1,0:T(8,128)(2,1)S(1)}, bf16[1024,8,128]{2,1,0:T(8,128)(2,1)}, u32[]{:S(2)}) copy-start(bf16[1024,8,128]{2,1,0:T(8,128)(2,1)} %param.6) | copy-start | bytes 6291460
  15.6 1.3 %copy-start = (bf16[1024,1024]{1,0:T(8,128)(2,1)}, bf16[1024,1024]{1,0:T(8,128)(2,1)S(1)}, u32[]{:S(2)}) copy-start(bf16[1024,1024]{1,0:T(8,128)(2,1)S(1)} %get-tuple-element.33.refs_2_.k_ref) | copy-start | bytes 6291460
  16.9 1.3 %copy-start.2 = (bf16[1024,1024]{1,0:T(8,128)(2,1)}, bf16[1024,1024]{1,0:T(8,128)(2,1)S(1)}, u32[]{:S(2)}) copy-start(bf16[1024,1024]{1,0:T(8,128)(2,1)S(1)} %get-tuple-element.34.refs_3_.v_ref) | copy-start | bytes 6291460
  18.2 1.3 %copy-start.4 = (f32[4,8,128,128]{3,2,1,0:T(8,128)}, f32[4,8,128,128]{3,2,1,0:T(8,128)S(1)}, u32[]{:S(2)}) copy-start(f32[4,8,128,128]{3,2,1,0:T(8,128)S(1)} %get-tuple-element.39.refs_6_.before_ref) | copy-start | bytes 6291460
  19.5 5.6 %collective-permute-start.9 = (bf16[4,128,128]{2,1,0:T(8,128)(2,1)S(1)}, bf16[4,128,128]{2,1,0:T(8,128)(2,1)S(1)}, u32[]{:S(2)}, u32[]{:S(2)}) collective-permute-start(bf16[4,128,128]{2,1,0:T(8,128)(2,1)S(1)} %get-tuple-element.41), channel_id=1, source_target_pairs={{0,4},{4,0},{8,12},{12,8},{16,20},{20,16},{24,28},{28,24},{1,5},{5... | collective-permute-start | bytes 393224 | tf_op jit(solution)/shard_map/ppermute | solution.py:316
  21.6 20.5 %collective-permute-start.3 = (bf16[256,1024]{1,0:T(8,128)(2,1)}, bf16[256,1024]{1,0:T(8,128)(2,1)}, u32[]{:S(2)}, u32[]{:S(2)}) collective-permute-start(bf16[256,1024]{1,0:T(8,128)(2,1)} %get-tuple-element.62), channel_id=1, source_target_pairs={{0,2},{1,3},{2,0},{3,1},{4,6},{5,7},{6,4},{7,5},{8,10},{9,11},{10,... | collective-permute-start | bytes 1572872 | tf_op jit(solution)/shard_map/ppermute | solution.py:316
  25.2 27.9 %collective-permute-start = (bf16[256,1024]{1,0:T(8,128)(2,1)}, bf16[256,1024]{1,0:T(8,128)(2,1)S(1)}, u32[]{:S(2)}, u32[]{:S(2)}) collective-permute-start(bf16[256,1024]{1,0:T(8,128)(2,1)} %get-tuple-element.63), channel_id=1, source_target_pairs={{0,2},{1,3},{2,0},{3,1},{4,6},{5,7},{6,4},{7,5},{8,10},{9,11},{10,... | collective-permute-start | bytes 1572872 | tf_op jit(solution)/shard_map/ppermute | solution.py:316
  27.0 36.2 %collective-permute-start.8 = (bf16[256,1024]{1,0:T(8,128)(2,1)S(1)}, bf16[256,1024]{1,0:T(8,128)(2,1)S(1)}, u32[]{:S(2)}, u32[]{:S(2)}) collective-permute-start(bf16[256,1024]{1,0:T(8,128)(2,1)S(1)} %collective-permute-done.7.a_ref), channel_id=1, source_target_pairs={{0,1},{1,0},{2,3},{3,2},{4,5},{5,4},{6,7},{7,6},{8,9},{9,8},{10,11... | collective-permute-start | bytes 1572872 | tf_op jit(solution)/shard_map/ppermute | solution.py:316
  30.7 38.0 %collective-permute-start.6 = (bf16[256,1024]{1,0:T(8,128)(2,1)S(1)}, bf16[256,1024]{1,0:T(8,128)(2,1)S(1)}, u32[]{:S(2)}, u32[]{:S(2)}) collective-permute-start(bf16[256,1024]{1,0:T(8,128)(2,1)S(1)} %collective-permute-done.5.a_ref), channel_id=1, source_target_pairs={{0,1},{1,0},{2,3},{3,2},{4,5},{5,4},{6,7},{7,6},{8,9},{9,8},{10,11... | collective-permute-start | bytes 1572872 | tf_op jit(solution)/shard_map/ppermute | solution.py:316
  42.1 45.0 %collective-permute-start.10 = (bf16[4,128,128]{2,1,0:T(8,128)(2,1)S(1)}, bf16[4,128,128]{2,1,0:T(8,128)(2,1)S(1)}, u32[]{:S(2)}, u32[]{:S(2)}) collective-permute-start(bf16[4,128,128]{2,1,0:T(8,128)(2,1)S(1)} %fusion.10), channel_id=1, source_target_pairs={{0,8},{4,12},{8,16},{12,20},{16,24},{20,28},{1,9},{5,13},{9,17},{1... | collective-permute-start | bytes 393224 | tf_op jit(solution)/shard_map/ppermute | solution.py:320
  53.0 21.0 %collective-permute-start.4 = (bf16[256,1024]{1,0:T(8,128)(2,1)}, bf16[256,1024]{1,0:T(8,128)(2,1)S(1)}, u32[]{:S(2)}, u32[]{:S(2)}) collective-permute-start(bf16[256,1024]{1,0:T(8,128)(2,1)} %collective-permute-done.3.a_ref), channel_id=1, source_target_pairs={{0,1},{1,0},{2,3},{3,2},{4,5},{5,4},{6,7},{7,6},{8,9},{9,8},{10,11... | collective-permute-start | bytes 1572872 | tf_op jit(solution)/shard_map/ppermute | solution.py:316
  53.0 26.5 %collective-permute-start.1 = (bf16[256,1024]{1,0:T(8,128)(2,1)S(1)}, bf16[256,1024]{1,0:T(8,128)(2,1)S(1)}, u32[]{:S(2)}, u32[]{:S(2)}) collective-permute-start(bf16[256,1024]{1,0:T(8,128)(2,1)S(1)} %collective-permute-done.a_ref), channel_id=1, source_target_pairs={{0,1},{1,0},{2,3},{3,2},{4,5},{5,4},{6,7},{7,6},{8,9},{9,8},{10,11... | collective-permute-start | bytes 1572872 | tf_op jit(solution)/shard_map/ppermute | solution.py:316
  53.5 1.6 %copy-start.6 = (bf16[1024,1024]{1,0:T(8,128)(2,1)S(1)}, bf16[1024,1024]{1,0:T(8,128)(2,1)}, u32[]{:S(2)}) copy-start(bf16[1024,1024]{1,0:T(8,128)(2,1)} %a_ref.1) | copy-start | bytes 6291460
  79.5 20.5 %copy-start.3 = (bf16[1024,1024]{1,0:T(8,128)(2,1)S(1)}, bf16[1024,1024]{1,0:T(8,128)(2,1)}, u32[]{:S(2)}) copy-start(bf16[1024,1024]{1,0:T(8,128)(2,1)} %copy-done.2) | copy-start | bytes 6291460
  79.5 20.5 %copy-start.5 = (f32[4,8,128,128]{3,2,1,0:T(8,128)S(1)}, f32[4,8,128,128]{3,2,1,0:T(8,128)}, u32[]{:S(2)}) copy-start(f32[4,8,128,128]{3,2,1,0:T(8,128)} %copy-done.4) | copy-start | bytes 6291460
  85.3 14.7 %copy-start.1 = (bf16[1024,1024]{1,0:T(8,128)(2,1)S(1)}, bf16[1024,1024]{1,0:T(8,128)(2,1)}, u32[]{:S(2)}) copy-start(bf16[1024,1024]{1,0:T(8,128)(2,1)} %copy-done) | copy-start | bytes 6291460
  85.3 6.4 %collective-permute-start.13 = (bf16[4,128,128]{2,1,0:T(8,128)(2,1)S(1)}, bf16[4,128,128]{2,1,0:T(8,128)(2,1)S(1)}, u32[]{:S(2)}, u32[]{:S(2)}) collective-permute-start(bf16[4,128,128]{2,1,0:T(8,128)(2,1)S(1)} %get-tuple-element.58), channel_id=1, source_target_pairs={{0,4},{4,0},{8,12},{12,8},{16,20},{20,16},{24,28},{28,24},{1,5},{5... | collective-permute-start | bytes 393224 | tf_op jit(solution)/shard_map/ppermute | solution.py:316
  87.2 7.2 %collective-permute-start.11 = (bf16[4,128,128]{2,1,0:T(8,128)(2,1)S(1)}, bf16[4,128,128]{2,1,0:T(8,128)(2,1)S(1)}, u32[]{:S(2)}, u32[]{:S(2)}) collective-permute-start(bf16[4,128,128]{2,1,0:T(8,128)(2,1)S(1)} %fusion.4), channel_id=1, source_target_pairs={{0,16},{4,20},{8,24},{12,28},{1,17},{5,21},{9,25},{13,29},{2,18},{... | collective-permute-start | bytes 393224 | tf_op jit(solution)/shard_map/ppermute | solution.py:320
  91.7 6.9 %collective-permute-start.14 = (bf16[4,128,128]{2,1,0:T(8,128)(2,1)S(1)}, bf16[4,128,128]{2,1,0:T(8,128)(2,1)S(1)}, u32[]{:S(2)}, u32[]{:S(2)}) collective-permute-start(bf16[4,128,128]{2,1,0:T(8,128)(2,1)S(1)} %fusion.11), channel_id=1, source_target_pairs={{8,0},{12,4},{16,8},{20,12},{24,16},{28,20},{9,1},{13,5},{17,9},{2... | collective-permute-start | bytes 393224 | tf_op jit(solution)/shard_map/ppermute | solution.py:320
  94.4 5.5 %collective-permute-start.12 = (bf16[4,128,128]{2,1,0:T(8,128)(2,1)S(1)}, bf16[4,128,128]{2,1,0:T(8,128)(2,1)S(1)}, u32[]{:S(2)}, u32[]{:S(2)}) collective-permute-start(bf16[4,128,128]{2,1,0:T(8,128)(2,1)S(1)} %get-tuple-element.67), channel_id=1, source_target_pairs={{0,4},{4,0},{8,12},{12,8},{16,20},{20,16},{24,28},{28,24},{1,5},{5... | collective-permute-start | bytes 393224 | tf_op jit(solution)/shard_map/ppermute | solution.py:316
  98.7 11.8 %collective-permute-start.15 = (bf16[4,128,128]{2,1,0:T(8,128)(2,1)S(1)}, bf16[4,128,128]{2,1,0:T(8,128)(2,1)S(1)}, u32[]{:S(2)}, u32[]{:S(2)}) collective-permute-start(bf16[4,128,128]{2,1,0:T(8,128)(2,1)S(1)} %fusion.9), channel_id=1, source_target_pairs={{16,0},{20,4},{24,8},{28,12},{17,1},{21,5},{25,9},{29,13},{18,2},{... | collective-permute-start | bytes 393224 | tf_op jit(solution)/shard_map/ppermute | solution.py:320
  110.5 11.4 %collective-permute-start.16 = (bf16[4,128,128]{2,1,0:T(8,128)(2,1)S(1)}, bf16[4,128,128]{2,1,0:T(8,128)(2,1)S(1)}, u32[]{:S(2)}, u32[]{:S(2)}) collective-permute-start(bf16[4,128,128]{2,1,0:T(8,128)(2,1)S(1)} %get-tuple-element.65), channel_id=1, source_target_pairs={{0,4},{4,0},{8,12},{12,8},{16,20},{20,16},{24,28},{28,24},{1,5},{5... | collective-permute-start | bytes 393224 | tf_op jit(solution)/shard_map/ppermute | solution.py:316

commit v3 on v2

v3 whole, which is shorter than its diff:
```python
import functools

import jax
import jax.numpy as jnp
from jax import lax
from jax.experimental import pallas as pl
from jax.experimental.pallas import tpu as pltpu
from jax.sharding import PartitionSpec as P

CHUNK = 256
PAIR = 2
F32 = jnp.float32
BF16 = jnp.bfloat16
NT = (((1,), (1,)), ((), ()))
NN = (((1,), (0,)), ((), ()))
TN = (((0,), (0,)), ((), ()))
VMEM_LIMIT = 20 * 1024 * 1024
TOKEN = (8, 128)
FREE = pl.CostEstimate(flops=0, bytes_accessed=0, transcendentals=0)


def dot(a, b, dims):
    return lax.dot_general(a, b, dims, preferred_element_type=F32)


def params():
    return pltpu.CompilerParams(vmem_limit_bytes=VMEM_LIMIT)


def shape(dims, dtype):
    return jax.ShapeDtypeStruct(dims, dtype)


def hbm(*arrays):
    return [pltpu.with_memory_space_constraint(a, pltpu.HBM) for a in arrays]


def prepare_kernel(
    heads, dk, half_ref, q_ref, k_ref, v_ref, qf_ref, kf_ref, vf_ref, qt_ref, vt_ref, before_ref, keep_ref, send_ref, token_ref, wide, acc
):
    step = pl.program_id(0)
    rows = qf_ref.shape[0]

    @pl.when(step == 0)
    def _():
        acc[...] = jnp.zeros_like(acc)
        token_ref[...] = jnp.zeros_like(token_ref)

    before_ref[0] = acc[...]
    for source, target, turned in ((k_ref, kf_ref, None), (v_ref, vf_ref, vt_ref), (q_ref, qf_ref, qt_ref)):
        wide[...] = source[...].astype(F32)
        for h in range(heads):
            cols = slice(h * dk, (h + 1) * dk)
            one = wide[pl.ds(h, rows, stride=heads), :].astype(BF16)
            target[:, cols] = one
            if turned is not None:
                turned[cols, :] = one.T
            if turned is vt_ref:
                acc[h] += dot(vt_ref[cols, :], kf_ref[:, cols], NN)

    @pl.when(step == pl.num_programs(0) - 1)
    def _():
        low, high = acc[: heads // 2].astype(BF16), acc[heads // 2 :].astype(BF16)
        first = half_ref[0] == 0
        keep_ref[...] = jnp.where(first, low, high)
        send_ref[...] = jnp.where(first, high, low)


def prepare(half, q, k, v, tokens, heads, dk):
    n = tokens // CHUNK
    raw = pl.BlockSpec((CHUNK * heads, dk), lambda i, s: (i, 0))
    flat = pl.BlockSpec((CHUNK, heads * dk), lambda i, s: (i, 0))
    turned = pl.BlockSpec((heads * dk, CHUNK), lambda i, s: (0, i))
    part = pl.BlockSpec((heads // 2, dk, dk), lambda i, s: (0, 0, 0))
    width = heads * dk
    return pl.pallas_call(
        functools.partial(prepare_kernel, heads, dk),
        grid_spec=pltpu.PrefetchScalarGridSpec(
            num_scalar_prefetch=1,
            grid=(n,),
            in_specs=[raw] * 3,
            out_specs=[flat] * 3
            + [turned] * 2
            + [pl.BlockSpec((1, heads, dk, dk), lambda i, s: (i, 0, 0, 0)), part, part, pl.BlockSpec(TOKEN, lambda i, s: (0, 0))],
            scratch_shapes=[pltpu.VMEM((CHUNK * heads, dk), F32), pltpu.VMEM((heads, dk, dk), F32)],
        ),
        out_shape=[pltpu.HBM((tokens, width), BF16)] * 3
        + [pltpu.HBM((width, tokens), BF16)] * 2
        + [pltpu.HBM((n, heads, dk, dk), F32)]
        + [shape((heads // 2, dk, dk), BF16)] * 2
        + [shape(TOKEN, F32)],
        compiler_params=params(),
        cost_estimate=FREE,
        name="prepare",
    )(half, *hbm(q, k, v))


def early_kernel(index_ref, a_ref, b_ref, wa_ref, wb_ref, after_ref, out_ref, token_ref):
    token_ref[...] = jnp.zeros_like(token_ref)
    out_ref[...] = dot(a_ref[...], wa_ref[...], NT) + dot(b_ref[...], wb_ref[...], NT)


def early(index, a, b, weight, token):
    tokens, features = a.shape
    width = weight.shape[0]
    tile = 256
    whole = pl.BlockSpec((tokens, features), lambda j, s: (0, 0))
    return pl.pallas_call(
        early_kernel,
        grid_spec=pltpu.PrefetchScalarGridSpec(
            num_scalar_prefetch=1,
            grid=(width // tile,),
            in_specs=[
                whole,
                whole,
                pl.BlockSpec((tile, features), lambda j, s: (j, s[0])),
                pl.BlockSpec((tile, features), lambda j, s: (j, s[1])),
                pl.BlockSpec(memory_space=pl.ANY),
            ],
            out_specs=[pl.BlockSpec((tokens, tile), lambda j, s: (0, j)), pl.BlockSpec(TOKEN, lambda j, s: (0, 0))],
        ),
        out_shape=[pltpu.HBM((tokens, width), F32), shape(TOKEN, F32)],
        compiler_params=params(),
        cost_estimate=FREE,
        name="early",
    )(index, *hbm(a), b, *hbm(weight, weight), token)


def late_kernel(last, first, dk, index_ref, a_ref, b_ref, wa_ref, wb_ref, part_ref, scale_ref, qt_ref, after_ref, *refs):
    j = pl.program_id(0)
    state_ref, refs = (None, refs) if first else (refs[0], refs[1:])
    refs, token_ref, at, bt = refs[:-3], refs[-3], refs[-2], refs[-1]
    d_ref = refs[0]

    @pl.when(j == 0)
    def _():
        token_ref[...] = jnp.zeros_like(token_ref)
        at[...] = a_ref[...].T
        bt[...] = b_ref[...].T

    turned = dot(wa_ref[...], at[...], NN) + dot(wb_ref[...], bt[...], NN)
    low = (part_ref[...] + turned.T).astype(BF16)
    d_ref[...] = low
    states = [None if first else state_ref[0, i] for i in range(PAIR)]
    for c in reversed(range(low.shape[0] // CHUNK)):
        rows = slice(c * CHUNK, (c + 1) * CHUNK)
        for i in range(PAIR):
            cols = slice(i * dk, (i + 1) * dk)
            grad = (low[rows, cols].astype(F32) * scale_ref[rows, :]).astype(BF16)
            state = dot(qt_ref[cols, rows], grad, NN)
            states[i] = state if states[i] is None else states[i] + state
            if not last:
                refs[1][c, i] = states[i]
    if not last:
        return
    keep_ref, send_ref = refs[1:]
    steps = pl.num_programs(0) // 2
    place = lax.rem(j, steps) * PAIR
    mine = (j // steps) == index_ref[2]

    @pl.when(mine)
    def _():
        for i in range(PAIR):
            keep_ref[place + i] = states[i].astype(BF16)

    @pl.when(jnp.logical_not(mine))
    def _():
        for i in range(PAIR):
            send_ref[place + i] = states[i].astype(BF16)


def late(start, last, index, a, b, weight, part, scale, qt, token, state, heads, dk):
    rows, features = a.shape
    width = weight.shape[0]
    tile = PAIR * dk
    m = rows // CHUNK
    here = start // rows
    whole = pl.BlockSpec((rows, features), lambda j, s: (0, 0))
    in_specs = [
        whole,
        whole,
        pl.BlockSpec((tile, features), lambda j, s: (j, s[0])),
        pl.BlockSpec((tile, features), lambda j, s: (j, s[1])),
        pl.BlockSpec((rows, tile), lambda j, s: (here, j)),
        pl.BlockSpec((rows, dk), lambda j, s: (here, 0)),
        pl.BlockSpec((tile, rows), lambda j, s: (j, here)),
        pl.BlockSpec(memory_space=pl.ANY),
    ]
    args = [a, b, *hbm(weight, weight, part), scale, *hbm(qt), token]
    if state is not None:
        in_specs.append(pl.BlockSpec((1, PAIR, dk, dk), lambda j, s: (0, j, 0, 0)))
        args += hbm(state)
    out_specs = [pl.BlockSpec((rows, tile), lambda j, s: (0, j))]
    out_shape = [pltpu.HBM((rows, width), BF16)]
    if last:
        out_specs += [pl.BlockSpec((heads // 2, dk, dk), lambda j, s: (0, 0, 0))] * 2
        out_shape += [shape((heads // 2, dk, dk), BF16)] * 2
    else:
        out_specs.append(pl.BlockSpec((m, PAIR, dk, dk), lambda j, s: (0, j, 0, 0)))
        out_shape.append(pltpu.HBM((m, heads, dk, dk), F32))
    out_specs.append(pl.BlockSpec(TOKEN, lambda j, s: (0, 0)))
    out_shape.append(shape(TOKEN, F32))
    return pl.pallas_call(
        functools.partial(late_kernel, last, state is None, dk),
        grid_spec=pltpu.PrefetchScalarGridSpec(
            num_scalar_prefetch=1,
            grid=(width // tile,),
            in_specs=in_specs,
            out_specs=out_specs,
            scratch_shapes=[pltpu.VMEM((features, rows), BF16)] * 2,
        ),
        out_shape=out_shape,
        compiler_params=params(),
        cost_estimate=FREE,
        name="late",
    )(index, *args)


def within_kernel(
    heads, dk, first, index_ref, q_ref, k_ref, v_ref, qt_ref, vt_ref, d_ref, scale_ref, before_ref, own_ref, other_ref, after_ref, *refs
):
    j = pl.program_id(0)
    dq_ref, dk_ref, dv_ref, token_ref, wide = refs[-5:]
    rows = q_ref.shape[0]
    mine = (j // (pl.num_programs(0) // 2)) == index_ref[2]
    t = lax.broadcasted_iota(jnp.int32, (rows, rows), 0)
    s = lax.broadcasted_iota(jnp.int32, (rows, rows), 1)
    lower = s <= t
    upper = t <= s
    scale = scale_ref[...]
    for i in range(PAIR):
        cols = slice(i * dk, (i + 1) * dk)
        q, k, v, d = q_ref[:, cols], k_ref[:, cols], v_ref[:, cols], d_ref[:, cols]
        grad = (d.astype(F32) * scale).astype(BF16)
        score_grad = jnp.where(lower, dot(grad, vt_ref[cols, :], NN), 0.0).astype(BF16)
        score_grad_t = jnp.where(upper, dot(v, grad, NT), 0.0).astype(BF16)
        score_keys_t = jnp.where(upper, dot(k, qt_ref[cols, :], NN), 0.0).astype(BF16)
        earlier = jnp.where(mine, own_ref[i], other_ref[i]).astype(F32) + before_ref[0, i]
        dq = scale * dot(d, earlier.astype(BF16), NN) + dot(score_grad, k, NN)
        dkey = dot(score_grad_t, q, NN)
        dval = dot(score_keys_t, grad, NN)
        if not first:
            after = refs[0][0, i].astype(BF16)
            dkey = dkey + dot(v, after, NT)
            dval = dval + dot(k, after, NN)
        wide[pl.ds(j * PAIR + i, rows, stride=heads), :] = dq
        dk_ref[:, cols] = dkey.astype(BF16)
        dv_ref[:, cols] = dval.astype(BF16)

    @pl.when(j == pl.num_programs(0) - 1)
    def _():
        dq_ref[...] = wide[...].astype(BF16)
        token_ref[...] = jnp.zeros_like(token_ref)


def within(chunk, index, q, k, v, qt, vt, d, scale, before, own, other, token, at, state, held, heads, dk):
    tokens, width = q.shape
    rows = CHUNK
    tile = PAIR * dk
    half_steps = heads // (2 * PAIR)
    block = pl.BlockSpec((rows, tile), lambda j, s: (chunk, j))
    turned = pl.BlockSpec((tile, rows), lambda j, s: (j, chunk))
    half_pair = pl.BlockSpec((PAIR, dk, dk), lambda j, s: (lax.rem(j, half_steps), 0, 0))
    in_specs = [block] * 3 + [turned] * 2
    in_specs += [
        pl.BlockSpec((rows, tile), lambda j, s: (at, j)),
        pl.BlockSpec((rows, dk), lambda j, s: (chunk, 0)),
        pl.BlockSpec((1, PAIR, dk, dk), lambda j, s: (chunk, j, 0, 0)),
        half_pair,
        half_pair,
        pl.BlockSpec(memory_space=pl.ANY),
    ]
    args = [*hbm(q, k, v, qt, vt, d), scale, *hbm(before), own, other, token]
    if state is not None:
        level = state[1]
        in_specs.append(pl.BlockSpec((1, PAIR, dk, dk), lambda j, s: (level, j, 0, 0)))
        args += hbm(state[0])
    aliases = {}
    if held is not None:
        for out, array in enumerate(held):
            aliases[1 + len(args)] = out
            args += hbm(array)
            in_specs.append(pl.BlockSpec(memory_space=pl.ANY))
    return pl.pallas_call(
        functools.partial(within_kernel, heads, dk, state is None),
        grid_spec=pltpu.PrefetchScalarGridSpec(
            num_scalar_prefetch=1,
            grid=(width // tile,),
            in_specs=in_specs,
            out_specs=[
                pl.BlockSpec((rows * heads, dk), lambda j, s: (chunk, 0)),
                block,
                block,
                pl.BlockSpec(TOKEN, lambda j, s: (0, 0)),
            ],
            scratch_shapes=[pltpu.VMEM((rows * heads, dk), F32)],
        ),
        out_shape=[pltpu.HBM((tokens * heads, dk), BF16)]
        + [pltpu.HBM((tokens, width), BF16)] * 2
        + [shape(TOKEN, F32)],
        input_output_aliases=aliases,
        compiler_params=params(),
        cost_estimate=FREE,
        name="within",
    )(index, *args)


def finish_kernel(
    heads, dk, index_ref, k_ref, v_ref, dkp_ref, dvp_ref, own_ref, other_ref, after_ref, dk_ref, dv_ref, wide_k, wide_v, after, turned
):
    rows = k_ref.shape[0]
    half = heads // 2

    @pl.when(pl.program_id(0) == 0)
    def _():
        first = index_ref[2] == 0
        for h in range(heads):
            own, other = own_ref[h % half], other_ref[h % half]
            one = jnp.where(first, own, other) if h < half else jnp.where(first, other, own)
            after[h] = one
            turned[h] = one.T

    for h in range(heads):
        cols = slice(h * dk, (h + 1) * dk)
        wide_k[pl.ds(h, rows, stride=heads), :] = dkp_ref[:, cols].astype(F32) + dot(v_ref[:, cols], turned[h], NN)
        wide_v[pl.ds(h, rows, stride=heads), :] = dvp_ref[:, cols].astype(F32) + dot(k_ref[:, cols], after[h], NN)
    dk_ref[...] = wide_k[...].astype(BF16)
    dv_ref[...] = wide_v[...].astype(BF16)


def finish(index, k, v, dkp, dvp, own, other, token, heads, dk):
    tokens, width = k.shape
    rows = CHUNK
    block = pl.BlockSpec((rows, width), lambda i, s: (i, 0))
    part = pl.BlockSpec((heads // 2, dk, dk), lambda i, s: (0, 0, 0))
    out = pl.BlockSpec((rows * heads, dk), lambda i, s: (i, 0))
    return pl.pallas_call(
        functools.partial(finish_kernel, heads, dk),
        grid_spec=pltpu.PrefetchScalarGridSpec(
            num_scalar_prefetch=1,
            grid=(tokens // rows,),
            in_specs=[block] * 4 + [part] * 2 + [pl.BlockSpec(memory_space=pl.ANY)],
            out_specs=[out, out],
            scratch_shapes=[pltpu.VMEM((rows * heads, dk), F32)] * 2 + [pltpu.VMEM((heads, dk, dk), BF16)] * 2,
        ),
        out_shape=[shape((tokens * heads, dk), BF16)] * 2,
        compiler_params=params(),
        cost_estimate=FREE,
        name="finish",
    )(index, *hbm(k, v, dkp, dvp), own, other, token)


def swap(array, axis, size, bit):
    return lax.ppermute(array, axis, [(i, i ^ bit) for i in range(size)])


def shifted(array, size, step):
    return lax.ppermute(array, "ctx", [(i, i + step) for i in range(size) if 0 <= i + step < size])


class Order:
    def __init__(self):
        self.token = None

    def tie(self, array):
        array, self.token = lax.optimization_barrier((array, self.token))
        return array


def scan_states(keep, send, size, odd, direction, order):
    came = swap(send, "ctx", size, 1)
    yield None
    own = keep.astype(F32)
    total = own + came.astype(F32)
    exclusive = jnp.zeros_like(total)
    step = 2
    while step < size:
        got = shifted(order.tie(total.astype(BF16)), size, direction * step).astype(F32)
        yield None
        exclusive = exclusive + got
        total = total + got
        step *= 2
    later = odd if direction == 1 else jnp.logical_not(odd)
    low = (exclusive + jnp.where(later, 0.0, own)).astype(BF16)
    other = swap(order.tie(low), "ctx", size, 1)
    mine = exclusive + jnp.where(later, came.astype(F32), 0.0)
    yield mine.astype(BF16), other


def body(n_ctx, n_head, queries, keys, values, d_layer, out_weight):
    tokens, heads, dk = queries.shape
    n = tokens // CHUNK
    block = lax.axis_index("ctx").astype(jnp.int32)
    place = lax.axis_index("head").astype(jnp.int32)
    odd = (block & 1) == 1
    half = (block & 1).astype(jnp.int32)

    near = n_head // 2
    far = 1
    groups = [(n // 2, n - n // 2)] + [(c, 1) for c in reversed(range(n // 2))]
    across = {}
    source = d_layer
    for c, m in groups:
        across[c] = swap(source[c * CHUNK : (c + m) * CHUNK], "head", n_head, near)
        source = lax.optimization_barrier(d_layer) if (c, m) == groups[0] else source
    beside = swap(d_layer, "head", n_head, far)

    position = block * tokens + jnp.arange(tokens, dtype=jnp.int32)
    scale = lax.rsqrt((dk * (position + 1)).astype(F32))
    scale = jnp.broadcast_to(scale[:, None], (tokens, dk))
    index = jnp.stack([place ^ near, place ^ near ^ far, half])

    order = Order()
    flat = (tokens * heads, dk)
    q, k, v, qt, vt, before, keep, send, order.token = prepare(
        half[None], queries.reshape(flat), keys.reshape(flat), values.reshape(flat), tokens, heads, dk
    )
    forward = scan_states(keep, send, n_ctx, odd, 1, order)
    next(forward)
    part, order.token = early(jnp.stack([place, place ^ far]), d_layer, beside, out_weight, order.token)

    prefix = state = held = None
    d, after = {}, {}

    def inner(c):
        nonlocal held
        *held, order.token = within(
            c, index, q, k, v, qt, vt, d[c][0], scale, before, *prefix, order.token, d[c][1], after[c], held, heads, dk
        )

    def outer(c, m):
        nonlocal state, keep, send, prefix
        after[c + m - 1] = None if state is None else (state, 0)
        piece = order.tie(across[c])
        both = swap(piece, "head", n_head, far)
        if prefix is None:
            prefix = next(forward)
        while prefix is None and state is not None:
            prefix = next(forward)
        out = late(c * CHUNK, c == 0, index, piece, both, out_weight, part, scale, qt, order.token, state, heads, dk)
        order.token = out[-1]
        if c == 0:
            keep, send = out[1:3]
        else:
            state = out[1]
        for i in range(m):
            d[c + i] = (out[0], i)
            if i < m - 1:
                after[c + i] = (state, i + 1)

    waiting = []
    for c, m in groups:
        outer(c, m)
        waiting += list(range(c, c + m))[::-1]
        if prefix is None:
            prefix = next(forward)
        elif c != 0:
            while len(waiting) > 1:
                inner(waiting.pop(0))
    backward = scan_states(keep, send, n_ctx, odd, -1, order)
    next(backward)
    suffix = None
    while suffix is None:
        suffix = next(backward)
        if waiting:
            inner(waiting.pop(0))
    while waiting:
        inner(waiting.pop(0))
    d_queries, dk_part, dv_part = held
    d_keys, d_values = finish(index, k, v, dk_part, dv_part, *suffix, order.token, heads, dk)
    return tuple(a.reshape(tokens, heads, dk) for a in (d_queries, d_keys, d_values))


def solution(mesh):
    in_specs = (
        P("ctx", "head", None),
        P("ctx", "head", None),
        P("ctx", "head", None),
        P("ctx", "head"),
        P("head", None),
    )
    out_specs = (P("ctx", "head", None), P("ctx", "head", None), P("ctx", "head", None))

    def program(queries, keys, values, d_layer, out_weight):
        return body(mesh.shape["ctx"], mesh.shape["head"], queries, keys, values, d_layer, out_weight)

    return jax.shard_map(program, mesh=mesh, in_specs=in_specs, out_specs=out_specs, check_vma=False)
```

time: 131 us -> 133 us (1.015); the launches traced: 128 us -> 132 us
  Pallas kernels: 62.9 us -> 73.1 us
  local copies, waits for them, and re-layouts: 11.8 us -> 3.51 us
  other arithmetic: 0.54 us -> 2.11 us
    unnamed x18 -> x4, local copies, waits for them, and re-layouts: 8.74 us -> 0.01 us
    ppermute x4, waiting for transfers between devices: 4.77 us -> 11.6 us  [shifted(): lax.ppermute(array, 'ctx', [(i, i + step) for i in range(size) if 0 <= i...]
    ppermute x13 -> x11, waiting for transfers between devices: 24 us -> 18.2 us  [swap(): return lax.ppermute(array, axis, [(i, i ^ bit) for i in range(size)])]
    pallas_call x1, Pallas kernels: 5.84 us -> 9.58 us  [prepare(): pl.pallas_call(functools.partial(prepare_kernel, heads, dk), grid_spec=pl...]
    pallas_call x8 -> x7, Pallas kernels: 42.6 us -> 46.4 us  [the longest x4 25 us: within(): pl.pallas_call(functools.partial(within_kernel, heads, dk, state is None)...]
    pallas_call x1, Pallas kernels: 6.26 us -> 8.03 us  [finish(): pl.pallas_call(functools.partial(finish_kernel, heads, dk), grid_spec=plt...]
    ppermute x13 -> x11, starting transfers between devices: 12.3 us -> 10.6 us  [swap(): return lax.ppermute(array, axis, [(i, i ^ bit) for i in range(size)])]
    convert_element_type x6, other arithmetic: 0.38 us -> 1.95 us  [the longest x2 1.1 us: scan_states(): low = (exclusive + jnp.where(later, 0.0, own)).astype(BF16)]
  transfers between devices with their start and end apart: 17 -> 15, of which waited for: 6 -> 9; matrix products, arithmetic and copies ran while one was open for 3% -> 4% of each run, Pallas kernels for 44% -> 44%
where the time goes in v3:
time: 133 us; the launch traced here: 132 us
  Pallas kernels  73.1 us (55%)
  waiting for transfers between devices  29.8 us (22%)
  starting transfers between devices  22.3 us (17%)
  local copies, waits for them, and re-layouts  3.51 us (3%)
  other arithmetic  2.11 us (2%)
    pallas_call x4, Pallas kernels, within(): pl.pallas_call(functools.partial(within_kernel, heads, dk, state is None)...  25 us
    pallas_call x3, Pallas kernels, late(): pl.pallas_call(functools.partial(late_kernel, last, state is None, dk), g...  21.3 us
    ppermute x11, waiting for transfers between devices, swap(): return lax.ppermute(array, axis, [(i, i ^ bit) for i in range(size)])  18.2 us
    ppermute x4, starting transfers between devices, shifted(): lax.ppermute(array, 'ctx', [(i, i + step) for i in range(size) if 0 <= i...  11.7 us
    ppermute x4, waiting for transfers between devices, shifted(): lax.ppermute(array, 'ctx', [(i, i + step) for i in range(size) if 0 <= i...  11.6 us
    ppermute x11, starting transfers between devices, swap(): return lax.ppermute(array, axis, [(i, i ^ bit) for i in range(size)])  10.6 us
    pallas_call x1, Pallas kernels, prepare(): pl.pallas_call(functools.partial(prepare_kernel, heads, dk), grid_spec=pl...  9.58 us
    pallas_call x1, Pallas kernels, early(): pl.pallas_call(early_kernel, grid_spec=pltpu.PrefetchScalarGridSpec(num_s...  9.15 us
  transfers between devices with their start and end apart: 15, of which 9 were waited for; matrix products, arithmetic and copies ran while one was open for 4% of the time, Pallas kernels for 44%

profile of v3, /device:TPU:0, one launch (start us, length us, event | category | flops | bytes accessed | tf_op | source)
XLA Modules:
  0.0 131.6 jit_solution(1229404578560858747)
XLA Ops:
  1.1 2.3 %slice.10 = bf16[512,1024]{1,0:T(8,128)(2,1)} slice(bf16[1024,1024]{1,0:T(8,128)(2,1)} %a_ref.1), slice={[512:1024], [0:1024]} | slice | bytes 2097152 | tf_op jit(solution)/shard_map/slice | solution.py:404
  3.4 2.5 %collective-permute-start.1 = (bf16[512,1024]{1,0:T(8,128)(2,1)}, bf16[512,1024]{1,0:T(8,128)(2,1)S(1)}, u32[]{:S(2)}, u32[]{:S(2)}) collective-permute-start(bf16[512,1024]{1,0:T(8,128)(2,1)} %slice.10), channel_id=1, source_target_pairs={{0,2},{1,3},{2,0},{3,1},{4,6},{5,7},{6,4},{7,5},{8,10},{9,11},{10,... | collective-permute-start | bytes 3145736 | tf_op jit(solution)/shard_map/ppermute | solution.py:354
  5.9 9.6 %prepare.1 = (bf16[1024,1024]{1,0:T(8,128)(2,1)}, bf16[1024,1024]{1,0:T(8,128)(2,1)}, bf16[1024,1024]{1,0:T(8,128)(2,1)}, bf16[1024,1024]{1,0:T(8,128)(2,1)}, bf...) custom-call(s32[1]{0:T(128)} %bitcast.2.half_ref, ...), custom_call_target="tpu_custom_call" | custom-call | tf_op jit(solution)/shard_map/prepare/pallas_call | solution.py:76
  15.6 9.1 %early.1 = (f32[1024,1024]{1,0:T(8,128)}, f32[8,128]{1,0:T(8,128)S(1)}) custom-call(s32[2]{0:T(128)S(1)} %pad_add_fusion.1.index_ref, bf16[1024,1024]{1,0:T(8,128)(2,1)} %a_ref.1, bf16[1024,1024]{1,0:T(8,128)(2,1)S(1)} %collective-permute-done.2.b_ref, bf16[1024,4096]{1,0:T(8,128)(2,1)} %wb_ref.7, bf16[1024,4096]{1,0:T(8,128)(2,1)} %wb_ref.7, ...), custom_call_target="tpu_custom_call" | custom-call | tf_op jit(solution)/shard_map/early/pallas_call | solution.py:108
  24.7 5.2 %collective-permute-done.1.a_ref = bf16[512,1024]{1,0:T(8,128)(2,1)S(1)} collective-permute-done((bf16[512,1024]{1,0:T(8,128)(2,1)}, bf16[512,1024]{1,0:T(8,128)(2,1)S(1)}, u32[]{:S(2)}, u32[]{:S(2)}) %collective-permute-start.1) | collective-permute-done | bytes 1048608 | tf_op jit(solution)/shard_map/ppermute | solution.py:354
  29.9 1.8 %collective-permute-start.4 = (bf16[4,128,128]{2,1,0:T(8,128)(2,1)S(1)}, bf16[4,128,128]{2,1,0:T(8,128)(2,1)S(1)}, u32[]{:S(2)}, u32[]{:S(2)}) collective-permute-start(bf16[4,128,128]{2,1,0:T(8,128)(2,1)S(1)} %get-tuple-element.70), channel_id=1, source_target_pairs={{0,4},{4,0},{8,12},{12,8},{16,20},{20,16},{24,28},{28,24},{1,5},{5... | collective-permute-start | bytes 393224 | tf_op jit(solution)/shard_map/ppermute | solution.py:354
  31.7 1.1 fusion.12
  32.8 1.5 %collective-permute-start.7 = (bf16[256,1024]{1,0:T(8,128)(2,1)}, bf16[256,1024]{1,0:T(8,128)(2,1)S(1)}, u32[]{:S(2)}, u32[]{:S(2)}) collective-permute-start(bf16[256,1024]{1,0:T(8,128)(2,1)} %get-tuple-element.117), channel_id=1, source_target_pairs={{0,2},{1,3},{2,0},{3,1},{4,6},{5,7},{6,4},{7,5},{8,10},{9,11},{10,... | collective-permute-start | bytes 1572872 | tf_op jit(solution)/shard_map/ppermute | solution.py:354
  34.3 1.6 %collective-permute-done.4 = bf16[4,128,128]{2,1,0:T(8,128)(2,1)S(1)} collective-permute-done((bf16[4,128,128]{2,1,0:T(8,128)(2,1)S(1)}, bf16[4,128,128]{2,1,0:T(8,128)(2,1)S(1)}, u32[]{:S(2)}, u32[]{:S(2)}) %collective-permute-start.4) | collective-permute-done | bytes 131104 | tf_op jit(solution)/shard_map/ppermute | solution.py:354
  35.9 3.7 %collective-permute-start.5 = (bf16[4,128,128]{2,1,0:T(8,128)(2,1)S(1)}, bf16[4,128,128]{2,1,0:T(8,128)(2,1)S(1)}, u32[]{:S(2)}, u32[]{:S(2)}) collective-permute-start(bf16[4,128,128]{2,1,0:T(8,128)(2,1)S(1)} %fusion.10), channel_id=1, source_target_pairs={{0,8},{4,12},{8,16},{12,20},{16,24},{20,28},{1,9},{5,13},{9,17},{1... | collective-permute-start | bytes 393224 | tf_op jit(solution)/shard_map/ppermute | solution.py:358
  39.7 2.5 %collective-permute-done.5 = bf16[4,128,128]{2,1,0:T(8,128)(2,1)S(1)} collective-permute-done((bf16[4,128,128]{2,1,0:T(8,128)(2,1)S(1)}, bf16[4,128,128]{2,1,0:T(8,128)(2,1)S(1)}, u32[]{:S(2)}, u32[]{:S(2)}) %collective-permute-start.5) | collective-permute-done | bytes 131104 | tf_op jit(solution)/shard_map/ppermute | solution.py:358
  42.3 0.7 fusion.4
  43.2 8.1 %late.3 = (bf16[512,1024]{1,0:T(8,128)(2,1)}, f32[2,8,128,128]{3,2,1,0:T(8,128)}, f32[8,128]{1,0:T(8,128)S(1)}) custom-call(s32[3]{0:T(128)S(1)} %pad_add_fusion.index_ref, bf16[512,1024]{1,0:T(8,128)(2,1)S(1)} %collective-permute-done.1.a_ref, bf16[512,1024]{1,0:T(8,128)(2,1)S(1)} %collective-permute-done.3.b_ref, bf16[1024,4096]{1,0:T(8,128)(2,1)} %wb_ref.7, ...), custom_call_target="tpu_custom_call" | custom-call | tf_op jit(solution)/shard_map/late/pallas_call | solution.py:203
  51.4 1.6 %collective-permute-start = (bf16[256,1024]{1,0:T(8,128)(2,1)}, bf16[256,1024]{1,0:T(8,128)(2,1)S(1)}, u32[]{:S(2)}, u32[]{:S(2)}) collective-permute-start(bf16[256,1024]{1,0:T(8,128)(2,1)} %get-tuple-element.118), channel_id=1, source_target_pairs={{0,2},{1,3},{2,0},{3,1},{4,6},{5,7},{6,4},{7,5},{8,10},{9,11},{10,... | collective-permute-start | bytes 1572872 | tf_op jit(solution)/shard_map/ppermute | solution.py:354
  53.0 5.4 %collective-permute-start.6 = (bf16[4,128,128]{2,1,0:T(8,128)(2,1)}, bf16[4,128,128]{2,1,0:T(8,128)(2,1)S(1)}, u32[]{:S(2)}, u32[]{:S(2)}) collective-permute-start(bf16[4,128,128]{2,1,0:T(8,128)(2,1)} %fusion.4), channel_id=1, source_target_pairs={{0,16},{4,20},{8,24},{12,28},{1,17},{5,21},{9,25},{13,29},{2,18},{... | collective-permute-start | bytes 393224 | tf_op jit(solution)/shard_map/ppermute | solution.py:358
  58.4 3.4 %collective-permute-done.6 = bf16[4,128,128]{2,1,0:T(8,128)(2,1)S(1)} collective-permute-done((bf16[4,128,128]{2,1,0:T(8,128)(2,1)}, bf16[4,128,128]{2,1,0:T(8,128)(2,1)S(1)}, u32[]{:S(2)}, u32[]{:S(2)}) %collective-permute-start.6) | collective-permute-done | bytes 131104 | tf_op jit(solution)/shard_map/ppermute | solution.py:358
  61.8 1.0 fusion.1
  62.8 1.6 %collective-permute-start.8 = (bf16[4,128,128]{2,1,0:T(8,128)(2,1)S(1)}, bf16[4,128,128]{2,1,0:T(8,128)(2,1)S(1)}, u32[]{:S(2)}, u32[]{:S(2)}) collective-permute-start(bf16[4,128,128]{2,1,0:T(8,128)(2,1)S(1)} %get-tuple-element.80), channel_id=1, source_target_pairs={{0,4},{4,0},{8,12},{12,8},{16,20},{20,16},{24,28},{28,24},{1,5},{5... | collective-permute-start | bytes 393224 | tf_op jit(solution)/shard_map/ppermute | solution.py:354
  64.4 6.6 %late.4 = (bf16[256,1024]{1,0:T(8,128)(2,1)}, f32[1,8,128,128]{3,2,1,0:T(8,128)}, f32[8,128]{1,0:T(8,128)S(1)}) custom-call(s32[3]{0:T(128)S(1)} %pad_add_fusion.index_ref, bf16[256,1024]{1,0:T(8,128)(2,1)S(1)} %collective-permute-done.7.a_ref, bf16[256,1024]{1,0:T(8,128)(2,1)S(1)} %collective-permute-done.9.b_ref, bf16[1024,4096]{1,0:T(8,128)(2,1)} %wb_ref.7, ...), custom_call_target="tpu_custom_call" | custom-call | tf_op jit(solution)/shard_map/late/pallas_call | solution.py:203
  70.9 6.1 %within.4 = (bf16[8192,128]{1,0:T(8,128)(2,1)}, bf16[1024,1024]{1,0:T(8,128)(2,1)}, bf16[1024,1024]{1,0:T(8,128)(2,1)}, f32[8,128]{1,0:T(8,128)S(1)}) custom-call(s32[3]{0:T(128)S(1)} %pad_add_fusion.index_ref, bf16[1024,1024]{1,0:T(8,128)(2,1)} %get-tuple-element.60.q_ref, bf16[1024,1024]{1,0:T(8,128)(2,1)} %get-tuple-element.61.k_ref, ...), custom_call_target="tpu_custom_call" | custom-call | tf_op jit(solution)/shard_map/within/pallas_call | solution.py:284
  77.1 6.3 %within.5 = (bf16[8192,128]{1,0:T(8,128)(2,1)}, bf16[1024,1024]{1,0:T(8,128)(2,1)}, bf16[1024,1024]{1,0:T(8,128)(2,1)}, f32[8,128]{1,0:T(8,128)S(1)}) custom-call(s32[3]{0:T(128)S(1)} %pad_add_fusion.index_ref, bf16[1024,1024]{1,0:T(8,128)(2,1)} %get-tuple-element.60.q_ref, ...), custom_call_target="tpu_custom_call", output_to_operand_aliasing={{0}: (13, {}), {1}: (14, {}), {2}: (15, {})} | custom-call | tf_op jit(solution)/shard_map/within/pallas_call | solution.py:284
  83.4 1.9 %collective-permute-done.10.b_ref = bf16[256,1024]{1,0:T(8,128)(2,1)S(1)} collective-permute-done((bf16[256,1024]{1,0:T(8,128)(2,1)S(1)}, bf16[256,1024]{1,0:T(8,128)(2,1)S(1)}, u32[]{:S(2)}, u32[]{:S(2)}) %collective-permute-start.10) | collective-permute-done | bytes 524320 | tf_op jit(solution)/shard_map/ppermute | solution.py:354
  85.3 6.7 %late.5 = (bf16[256,1024]{1,0:T(8,128)(2,1)}, bf16[4,128,128]{2,1,0:T(8,128)(2,1)S(1)}, bf16[4,128,128]{2,1,0:T(8,128)(2,1)S(1)}, f32[8,128]{1,0:T(8,128)S(1)}) custom-call(s32[3]{0:T(128)S(1)} %pad_add_fusion.index_ref, bf16[256,1024]{1,0:T(8,128)(2,1)S(1)} %collective-permute-done.a_ref, bf16[256,1024]{1,0:T(8,128)(2,1)S(1)} %collective-permute-done.10.b_ref, ...), custom_call_target="tpu_custom_call" | custom-call | tf_op jit(solution)/shard_map/late/pallas_call | solution.py:203
  92.5 5.0 %collective-permute-done.11 = bf16[4,128,128]{2,1,0:T(8,128)(2,1)S(1)} collective-permute-done((bf16[4,128,128]{2,1,0:T(8,128)(2,1)S(1)}, bf16[4,128,128]{2,1,0:T(8,128)(2,1)S(1)}, u32[]{:S(2)}, u32[]{:S(2)}) %collective-permute-start.11) | collective-permute-done | bytes 131104 | tf_op jit(solution)/shard_map/ppermute | solution.py:354
  97.6 1.3 collective-permute-start.12
  98.9 6.3 %within.6 = (bf16[8192,128]{1,0:T(8,128)(2,1)}, bf16[1024,1024]{1,0:T(8,128)(2,1)}, bf16[1024,1024]{1,0:T(8,128)(2,1)}, f32[8,128]{1,0:T(8,128)S(1)}) custom-call(s32[3]{0:T(128)S(1)} %pad_add_fusion.index_ref, bf16[1024,1024]{1,0:T(8,128)(2,1)} %get-tuple-element.60.q_ref, ...), custom_call_target="tpu_custom_call", output_to_operand_aliasing={{0}: (13, {}), {1}: (14, {}), {2}: (15, {})} | custom-call | tf_op jit(solution)/shard_map/within/pallas_call | solution.py:284
  105.2 1.5 %collective-permute-done.12 = bf16[4,128,128]{2,1,0:T(8,128)(2,1)S(1)} collective-permute-done((bf16[4,128,128]{2,1,0:T(8,128)(2,1)S(1)}, bf16[4,128,128]{2,1,0:T(8,128)(2,1)S(1)}, u32[]{:S(2)}, u32[]{:S(2)}) %collective-permute-start.12) | collective-permute-done | bytes 131104 | tf_op jit(solution)/shard_map/ppermute | solution.py:358
  106.7 1.3 collective-permute-start.13
  108.0 6.3 %within.7 = (bf16[8192,128]{1,0:T(8,128)(2,1)}, bf16[1024,1024]{1,0:T(8,128)(2,1)}, bf16[1024,1024]{1,0:T(8,128)(2,1)}, f32[8,128]{1,0:T(8,128)S(1)}) custom-call(s32[3]{0:T(128)S(1)} %pad_add_fusion.index_ref, bf16[1024,1024]{1,0:T(8,128)(2,1)} %get-tuple-element.60.q_ref, ...), custom_call_target="tpu_custom_call", output_to_operand_aliasing={{0}: (13, {}), {1}: (14, {}), {2}: (15, {})} | custom-call | tf_op jit(solution)/shard_map/within/pallas_call | solution.py:284
  114.3 4.1 %collective-permute-done.13 = bf16[4,128,128]{2,1,0:T(8,128)(2,1)S(1)} collective-permute-done((bf16[4,128,128]{2,1,0:T(8,128)(2,1)S(1)}, bf16[4,128,128]{2,1,0:T(8,128)(2,1)S(1)}, u32[]{:S(2)}, u32[]{:S(2)}) %collective-permute-start.13) | collective-permute-done | bytes 131104 | tf_op jit(solution)/shard_map/ppermute | solution.py:358
  119.1 4.5 %collective-permute-done.14.other_ref = bf16[4,128,128]{2,1,0:T(8,128)(2,1)S(1)} collective-permute-done((bf16[4,128,128]{2,1,0:T(8,128)(2,1)S(1)}, bf16[4,128,128]{2,1,0:T(8,128)(2,1)S(1)}, u32[]{:S(2)}, u32[]{:S(2)}) %collective-permute-start.14) | collective-permute-done | bytes 131104 | tf_op jit(solution)/shard_map/ppermute | solution.py:354
  123.6 8.0 %finish.1 = (bf16[8192,128]{1,0:T(8,128)(2,1)}, bf16[8192,128]{1,0:T(8,128)(2,1)}) custom-call(s32[3]{0:T(128)S(1)} %pad_add_fusion.index_ref, bf16[1024,1024]{1,0:T(8,128)(2,1)} %get-tuple-element.61.k_ref, bf16[1024,1024]{1,0:T(8,128)(2,1)} %get-tuple-element.62.v_ref, bf16[1024,1024]{1,0:T(8,128)(2,1)} %get-tuple-element.109.dkp_ref, ...), custom_call_target="tpu_custom_call" | custom-call | tf_op jit(solution)/shard_map/finish/pallas_call | solution.py:337
  (24 shorter events, 2.3 us)
Async XLA Ops:
  0.6 14.9 %collective-permute-start.2 = (bf16[1024,1024]{1,0:T(8,128)(2,1)}, bf16[1024,1024]{1,0:T(8,128)(2,1)S(1)}, u32[]{:S(2)}, u32[]{:S(2)}) collective-permute-start(bf16[1024,1024]{1,0:T(8,128)(2,1)} %a_ref.1), channel_id=1, source_target_pairs={{0,1},{1,0},{2,3},{3,2},{4,5},{5,4},{6,7},{7,6},{8,9},{9,8},{10,11... | collective-permute-start | bytes 6291464 | tf_op jit(solution)/shard_map/ppermute | solution.py:354
  3.4 26.5 %collective-permute-start.1 = (bf16[512,1024]{1,0:T(8,128)(2,1)}, bf16[512,1024]{1,0:T(8,128)(2,1)S(1)}, u32[]{:S(2)}, u32[]{:S(2)}) collective-permute-start(bf16[512,1024]{1,0:T(8,128)(2,1)} %slice.10), channel_id=1, source_target_pairs={{0,2},{1,3},{2,0},{3,1},{4,6},{5,7},{6,4},{7,5},{8,10},{9,11},{10,... | collective-permute-start | bytes 3145736 | tf_op jit(solution)/shard_map/ppermute | solution.py:354
  15.6 16.1 %copy-start = (bf16[1024,1024]{1,0:T(8,128)(2,1)S(1)}, bf16[1024,1024]{1,0:T(8,128)(2,1)}, u32[]{:S(2)}) copy-start(bf16[1024,1024]{1,0:T(8,128)(2,1)} %a_ref.1) | copy-start | bytes 6291460
  29.9 13.1 %collective-permute-start.3 = (bf16[512,1024]{1,0:T(8,128)(2,1)S(1)}, bf16[512,1024]{1,0:T(8,128)(2,1)S(1)}, u32[]{:S(2)}, u32[]{:S(2)}) collective-permute-start(bf16[512,1024]{1,0:T(8,128)(2,1)S(1)} %collective-permute-done.1.a_ref), channel_id=1, source_target_pairs={{0,1},{1,0},{2,3},{3,2},{4,5},{5,4},{6,7},{7,6},{8,9},{9,8},{10,11... | collective-permute-start | bytes 3145736 | tf_op jit(solution)/shard_map/ppermute | solution.py:354
  29.9 5.9 %collective-permute-start.4 = (bf16[4,128,128]{2,1,0:T(8,128)(2,1)S(1)}, bf16[4,128,128]{2,1,0:T(8,128)(2,1)S(1)}, u32[]{:S(2)}, u32[]{:S(2)}) collective-permute-start(bf16[4,128,128]{2,1,0:T(8,128)(2,1)S(1)} %get-tuple-element.70), channel_id=1, source_target_pairs={{0,4},{4,0},{8,12},{12,8},{16,20},{20,16},{24,28},{28,24},{1,5},{5... | collective-permute-start | bytes 393224 | tf_op jit(solution)/shard_map/ppermute | solution.py:354
  32.8 18.5 %collective-permute-start.7 = (bf16[256,1024]{1,0:T(8,128)(2,1)}, bf16[256,1024]{1,0:T(8,128)(2,1)S(1)}, u32[]{:S(2)}, u32[]{:S(2)}) collective-permute-start(bf16[256,1024]{1,0:T(8,128)(2,1)} %get-tuple-element.117), channel_id=1, source_target_pairs={{0,2},{1,3},{2,0},{3,1},{4,6},{5,7},{6,4},{7,5},{8,10},{9,11},{10,... | collective-permute-start | bytes 1572872 | tf_op jit(solution)/shard_map/ppermute | solution.py:354
  35.9 6.3 %collective-permute-start.5 = (bf16[4,128,128]{2,1,0:T(8,128)(2,1)S(1)}, bf16[4,128,128]{2,1,0:T(8,128)(2,1)S(1)}, u32[]{:S(2)}, u32[]{:S(2)}) collective-permute-start(bf16[4,128,128]{2,1,0:T(8,128)(2,1)S(1)} %fusion.10), channel_id=1, source_target_pairs={{0,8},{4,12},{8,16},{12,20},{16,24},{20,28},{1,9},{5,13},{9,17},{1... | collective-permute-start | bytes 393224 | tf_op jit(solution)/shard_map/ppermute | solution.py:358
  42.3 0.9 copy-start.1
  51.3 13.0 %collective-permute-start.9 = (bf16[256,1024]{1,0:T(8,128)(2,1)S(1)}, bf16[256,1024]{1,0:T(8,128)(2,1)S(1)}, u32[]{:S(2)}, u32[]{:S(2)}) collective-permute-start(bf16[256,1024]{1,0:T(8,128)(2,1)S(1)} %collective-permute-done.7.a_ref), channel_id=1, source_target_pairs={{0,1},{1,0},{2,3},{3,2},{4,5},{5,4},{6,7},{7,6},{8,9},{9,8},{10,11... | collective-permute-start | bytes 1572872 | tf_op jit(solution)/shard_map/ppermute | solution.py:354
  51.4 32.0 %collective-permute-start = (bf16[256,1024]{1,0:T(8,128)(2,1)}, bf16[256,1024]{1,0:T(8,128)(2,1)S(1)}, u32[]{:S(2)}, u32[]{:S(2)}) collective-permute-start(bf16[256,1024]{1,0:T(8,128)(2,1)} %get-tuple-element.118), channel_id=1, source_target_pairs={{0,2},{1,3},{2,0},{3,1},{4,6},{5,7},{6,4},{7,5},{8,10},{9,11},{10,... | collective-permute-start | bytes 1572872 | tf_op jit(solution)/shard_map/ppermute | solution.py:354
  53.0 8.8 %collective-permute-start.6 = (bf16[4,128,128]{2,1,0:T(8,128)(2,1)}, bf16[4,128,128]{2,1,0:T(8,128)(2,1)S(1)}, u32[]{:S(2)}, u32[]{:S(2)}) collective-permute-start(bf16[4,128,128]{2,1,0:T(8,128)(2,1)} %fusion.4), channel_id=1, source_target_pairs={{0,16},{4,20},{8,24},{12,28},{1,17},{5,21},{9,25},{13,29},{2,18},{... | collective-permute-start | bytes 393224 | tf_op jit(solution)/shard_map/ppermute | solution.py:358
  62.8 8.2 %collective-permute-start.8 = (bf16[4,128,128]{2,1,0:T(8,128)(2,1)S(1)}, bf16[4,128,128]{2,1,0:T(8,128)(2,1)S(1)}, u32[]{:S(2)}, u32[]{:S(2)}) collective-permute-start(bf16[4,128,128]{2,1,0:T(8,128)(2,1)S(1)} %get-tuple-element.80), channel_id=1, source_target_pairs={{0,4},{4,0},{8,12},{12,8},{16,20},{20,16},{24,28},{28,24},{1,5},{5... | collective-permute-start | bytes 393224 | tf_op jit(solution)/shard_map/ppermute | solution.py:354
  83.4 2.0 %collective-permute-start.10 = (bf16[256,1024]{1,0:T(8,128)(2,1)S(1)}, bf16[256,1024]{1,0:T(8,128)(2,1)S(1)}, u32[]{:S(2)}, u32[]{:S(2)}) collective-permute-start(bf16[256,1024]{1,0:T(8,128)(2,1)S(1)} %collective-permute-done.a_ref), channel_id=1, source_target_pairs={{0,1},{1,0},{2,3},{3,2},{4,5},{5,4},{6,7},{7,6},{8,9},{9,8},{10,11... | collective-permute-start | bytes 1572872 | tf_op jit(solution)/shard_map/ppermute | solution.py:354
  92.0 5.5 %collective-permute-start.11 = (bf16[4,128,128]{2,1,0:T(8,128)(2,1)S(1)}, bf16[4,128,128]{2,1,0:T(8,128)(2,1)S(1)}, u32[]{:S(2)}, u32[]{:S(2)}) collective-permute-start(bf16[4,128,128]{2,1,0:T(8,128)(2,1)S(1)} %get-tuple-element.95), channel_id=1, source_target_pairs={{0,4},{4,0},{8,12},{12,8},{16,20},{20,16},{24,28},{28,24},{1,5},{5... | collective-permute-start | bytes 393224 | tf_op jit(solution)/shard_map/ppermute | solution.py:354
  97.6 9.1 %collective-permute-start.12 = (bf16[4,128,128]{2,1,0:T(8,128)(2,1)S(1)}, bf16[4,128,128]{2,1,0:T(8,128)(2,1)S(1)}, u32[]{:S(2)}, u32[]{:S(2)}) collective-permute-start(bf16[4,128,128]{2,1,0:T(8,128)(2,1)S(1)} %fusion.11), channel_id=1, source_target_pairs={{8,0},{12,4},{16,8},{20,12},{24,16},{28,20},{9,1},{13,5},{17,9},{2... | collective-permute-start | bytes 393224 | tf_op jit(solution)/shard_map/ppermute | solution.py:358
  106.7 11.7 %collective-permute-start.13 = (bf16[4,128,128]{2,1,0:T(8,128)(2,1)S(1)}, bf16[4,128,128]{2,1,0:T(8,128)(2,1)S(1)}, u32[]{:S(2)}, u32[]{:S(2)}) collective-permute-start(bf16[4,128,128]{2,1,0:T(8,128)(2,1)S(1)} %fusion.9), channel_id=1, source_target_pairs={{16,0},{20,4},{24,8},{28,12},{17,1},{21,5},{25,9},{29,13},{18,2},{... | collective-permute-start | bytes 393224 | tf_op jit(solution)/shard_map/ppermute | solution.py:358
  118.5 5.0 %collective-permute-start.14 = (bf16[4,128,128]{2,1,0:T(8,128)(2,1)S(1)}, bf16[4,128,128]{2,1,0:T(8,128)(2,1)S(1)}, u32[]{:S(2)}, u32[]{:S(2)}) collective-permute-start(bf16[4,128,128]{2,1,0:T(8,128)(2,1)S(1)} %get-tuple-element.113), channel_id=1, source_target_pairs={{0,4},{4,0},{8,12},{12,8},{16,20},{20,16},{24,28},{28,24},{1,5},{5... | collective-permute-start | bytes 393224 | tf_op jit(solution)/shard_map/ppermute | solution.py:354

commit v4 on v0

v4 whole, which is shorter than its diff:
```python
import functools

import jax
import jax.numpy as jnp
from jax import lax
from jax.experimental import pallas as pl
from jax.experimental.pallas import tpu as pltpu
from jax.sharding import PartitionSpec as P

CHUNK = 256
PAIR = 2
GROUP = 4
F32 = jnp.float32
BF16 = jnp.bfloat16
TOKEN = (8, 128)
NT = (((1,), (1,)), ((), ()))
NN = (((1,), (0,)), ((), ()))
FREE = pl.CostEstimate(flops=0, bytes_accessed=0, transcendentals=0)
VMEM_LIMIT = 14 * 1024 * 1024
WHOLE = pl.BlockSpec(memory_space=pltpu.VMEM)
SCALARS = pl.BlockSpec(memory_space=pltpu.SMEM)
ANYWHERE = pl.BlockSpec(memory_space=pl.ANY)


def dot(a, b, dims):
    return lax.dot_general(a, b, dims, preferred_element_type=F32)


def shape(dims, dtype):
    return jax.ShapeDtypeStruct(dims, dtype)


def outside(*arrays):
    return [pltpu.with_memory_space_constraint(a, pltpu.HBM) for a in arrays]


def part_of(i, size):
    return pl.ds(pl.multiple_of(i * size, size), size)


def call(kernel, name, args, in_specs, out_shape, out_specs, scratch=()):
    return pl.pallas_call(
        kernel,
        in_specs=in_specs,
        out_specs=out_specs,
        out_shape=out_shape,
        scratch_shapes=scratch,
        compiler_params=pltpu.CompilerParams(vmem_limit_bytes=VMEM_LIMIT),
        cost_estimate=FREE,
        name=name,
    )(*args)


def cut_kernel(starts, source, *refs):
    pieces, token_ref, sem = refs[: len(starts)], refs[-2], refs[-1]
    token_ref[...] = jnp.zeros_like(token_ref)
    copies = [
        pltpu.make_async_copy(source.at[pl.ds(start, piece.shape[0])], piece, sem.at[i])
        for i, (start, piece) in enumerate(zip(starts, pieces))
    ]
    for copy in copies:
        copy.start()
    for copy in copies:
        copy.wait()


def cut(d_layer, groups):
    features = d_layer.shape[1]
    return call(
        functools.partial(cut_kernel, [c * CHUNK for c, _ in groups]),
        "cut",
        outside(d_layer),
        [ANYWHERE],
        [shape((m * CHUNK, features), d_layer.dtype) for _, m in groups] + [shape(TOKEN, F32)],
        [WHOLE] * (len(groups) + 1),
        [pltpu.SemaphoreType.DMA((len(groups),))],
    )


def prepare_kernel(
    heads, dk, half_ref, q_ref, k_ref, v_ref, _, qf_ref, kf_ref, vf_ref, qt_ref, vt_ref, before_ref, keep_ref, send_ref, token_ref,
    raw, wides, acc, sem
):
    n = qf_ref.shape[0] // CHUNK

    def load(i, c):
        source = (q_ref, k_ref, v_ref)[i].at[part_of(c, CHUNK * heads)]
        return pltpu.make_async_copy(source, raw.at[i, c], sem.at[i, c])

    for c in range(n):
        for i in range(3):
            load(i, c).start()
    token_ref[...] = jnp.zeros_like(token_ref)
    acc[...] = jnp.zeros_like(acc)

    def one_chunk(c, _):
        rows = part_of(c, CHUNK)
        before_ref[c] = acc[...]
        for i in range(3):
            load(i, c).wait()
            wides[i] = raw[i, c].astype(F32)
        for h in range(heads):
            cols = slice(h * dk, (h + 1) * dk)
            mine = pl.ds(h, CHUNK, stride=heads)
            q, k, v = (wides[i, mine, :].astype(BF16) for i in range(3))
            qf_ref[rows, cols] = q
            kf_ref[rows, cols] = k
            vf_ref[rows, cols] = v
            qt_ref[cols, rows] = q.T
            vt = v.T
            vt_ref[cols, rows] = vt
            acc[h] += dot(vt, k, NN)
        return 0

    lax.fori_loop(0, n, one_chunk, 0)
    low, high = acc[: heads // 2].astype(BF16), acc[heads // 2 :].astype(BF16)
    first = half_ref[0] == 0
    keep_ref[...] = jnp.where(first, low, high)
    send_ref[...] = jnp.where(first, high, low)


def prepare(half, q, k, v, token, tokens, heads, dk):
    n = tokens // CHUNK
    width = heads * dk
    return call(
        functools.partial(prepare_kernel, heads, dk),
        "prepare",
        [half, *outside(q, k, v), token],
        [SCALARS] + [ANYWHERE] * 4,
        [shape((tokens, width), BF16)] * 3
        + [shape((width, tokens), BF16)] * 2
        + [shape((n, heads, dk, dk), F32)]
        + [shape((heads // 2, dk, dk), BF16)] * 2
        + [shape(TOKEN, F32)],
        [WHOLE] * 9,
        [
            pltpu.VMEM((3, n, CHUNK * heads, dk), BF16),
            pltpu.VMEM((3, CHUNK * heads, dk), F32),
            pltpu.VMEM((heads, dk, dk), F32),
            pltpu.SemaphoreType.DMA((3, n)),
        ],
    )


def early_kernel(starts, index_ref, *refs):
    pieces, (b_ref, w_ref, _, out_ref, token_ref) = refs[: len(starts)], refs[len(starts) :]
    token_ref[...] = jnp.zeros_like(token_ref)
    features = b_ref.shape[1]
    first, second = part_of(index_ref[0], features), part_of(index_ref[1], features)

    def one_tile(j, _):
        tile = part_of(j, PAIR * 128)
        wa, wb = w_ref[tile, first].T, w_ref[tile, second].T
        for start, piece in zip(starts, pieces):
            rows = slice(start, start + piece.shape[0])
            out_ref[rows, tile] = dot(piece[...], wa, NN) + dot(b_ref[rows, :], wb, NN)
        return 0

    lax.fori_loop(0, out_ref.shape[1] // (PAIR * 128), one_tile, 0)


def early(index, pieces, starts, b, weight, token):
    tokens = b.shape[0]
    width = weight.shape[0]
    return call(
        functools.partial(early_kernel, starts),
        "early",
        [index, *pieces, b, weight, token],
        [SCALARS] + [WHOLE] * (len(pieces) + 2) + [ANYWHERE],
        [shape((tokens, width), F32), shape(TOKEN, F32)],
        [WHOLE] * 2,
    )


def late_kernel(last, first, start, dk, index_ref, a_ref, b_ref, w_ref, part_ref, scale_ref, qt_ref, _, *refs):
    state_ref, refs = (None, refs) if first else (refs[0], refs[1:])
    refs, token_ref, at, bt = refs[:-3], refs[-3], refs[-2], refs[-1]
    d_ref = refs[0]
    count, features = a_ref.shape
    tile = PAIR * dk
    token_ref[...] = jnp.zeros_like(token_ref)
    at[...] = a_ref[...].T
    bt[...] = b_ref[...].T
    one, two = part_of(index_ref[0], features), part_of(index_ref[1], features)
    steps = d_ref.shape[1] // tile
    here = slice(start, start + count)

    def one_tile(j, _):
        wide = part_of(j, tile)
        turned = dot(w_ref[wide, one], at[...], NN) + dot(w_ref[wide, two], bt[...], NN)
        low = (part_ref[here, wide] + turned.T).astype(BF16)
        d_ref[:, wide] = low
        states = [None if first else state_ref[0, j * PAIR + i] for i in range(PAIR)]
        for c in reversed(range(count // CHUNK)):
            rows = slice(c * CHUNK, (c + 1) * CHUNK)
            there = slice(start + c * CHUNK, start + (c + 1) * CHUNK)
            for i in range(PAIR):
                grad = (low[rows, i * dk : (i + 1) * dk].astype(F32) * scale_ref[there, :]).astype(BF16)
                state = dot(qt_ref[part_of(j * PAIR + i, dk), there], grad, NN)
                states[i] = state if states[i] is None else states[i] + state
                if not last:
                    refs[1][c, j * PAIR + i] = states[i]
        if last:
            keep_ref, send_ref = refs[1:]
            place = lax.rem(j, steps // 2) * PAIR
            mine = (j // (steps // 2)) == index_ref[2]

            @pl.when(mine)
            def _():
                for i in range(PAIR):
                    keep_ref[place + i] = states[i].astype(BF16)

            @pl.when(jnp.logical_not(mine))
            def _():
                for i in range(PAIR):
                    send_ref[place + i] = states[i].astype(BF16)

        return 0

    lax.fori_loop(0, steps, one_tile, 0)


def late(start, last, index, a, b, weight, part, scale, qt, token, state, heads, dk):
    rows, features = a.shape
    width = weight.shape[0]
    args = [index, a, b, weight, part, scale, qt, token]
    in_specs = [SCALARS] + [WHOLE] * 6 + [ANYWHERE]
    if state is not None:
        args.append(state)
        in_specs.append(WHOLE)
    out_shape = [shape((rows, width), BF16)]
    if last:
        out_shape += [shape((heads // 2, dk, dk), BF16)] * 2
    else:
        out_shape.append(shape((rows // CHUNK, heads, dk, dk), F32))
    out_shape.append(shape(TOKEN, F32))
    return call(
        functools.partial(late_kernel, last, state is None, start, dk),
        "late",
        args,
        in_specs,
        out_shape,
        [WHOLE] * len(out_shape),
        [pltpu.VMEM((features, rows), BF16)] * 2,
    )


def within_kernel(
    heads, dk, chunk, at, level, others,
    index_ref, q_ref, k_ref, v_ref, qt_ref, vt_ref, d_ref, scale_ref, before_ref, own_ref, other_ref, _, *refs
):
    state_ref, refs = (None, refs) if level is None else (refs[0], refs[1:])
    earlier_dq, refs = refs[: len(others)], refs[len(others) :]
    dq_ref, dk_ref, dv_ref, token_ref, wide = refs[:5]
    token_ref[...] = jnp.zeros_like(token_ref)
    if others:
        low_ref, sem = refs[5:]
        copies = [
            pltpu.make_async_copy(source, dq_ref.at[pl.ds(c * CHUNK * heads, CHUNK * heads)], sem.at[i])
            for i, (c, source) in enumerate(zip(others, earlier_dq))
        ]
        for copy in copies:
            copy.start()
    rows = slice(chunk * CHUNK, (chunk + 1) * CHUNK)
    there = slice(at * CHUNK, (at + 1) * CHUNK)
    t = lax.broadcasted_iota(jnp.int32, (CHUNK, CHUNK), 0)
    s = lax.broadcasted_iota(jnp.int32, (CHUNK, CHUNK), 1)
    lower = s <= t
    upper = t <= s
    scale = scale_ref[rows, :]
    half = heads // 2

    def some_heads(g, _):
        mine = g * GROUP // half == index_ref[2]
        for i in range(GROUP):
            h = g * GROUP + i
            cols = part_of(h, dk)
            q, k, v, d = q_ref[rows, cols], k_ref[rows, cols], v_ref[rows, cols], d_ref[there, cols]
            grad = (d.astype(F32) * scale).astype(BF16)
            score_grad = jnp.where(lower, dot(grad, vt_ref[cols, rows], NN), 0.0).astype(BF16)
            score_grad_t = jnp.where(upper, dot(v, grad, NT), 0.0).astype(BF16)
            score_keys_t = jnp.where(upper, dot(k, qt_ref[cols, rows], NN), 0.0).astype(BF16)
            place = lax.rem(h, half)
            earlier = jnp.where(mine, own_ref[place], other_ref[place]).astype(F32) + before_ref[chunk, h]
            dq = scale * dot(d, earlier.astype(BF16), NN) + dot(score_grad, k, NN)
            dkey = dot(score_grad_t, q, NN)
            dval = dot(score_keys_t, grad, NN)
            if state_ref is not None:
                after = state_ref[level, h].astype(BF16)
                dkey = dkey + dot(v, after, NT)
                dval = dval + dot(k, after, NN)
            wide[pl.ds(h, CHUNK, stride=heads), :] = dq
            dk_ref[:, cols] = dkey.astype(BF16)
            dv_ref[:, cols] = dval.astype(BF16)
        return 0

    lax.fori_loop(0, heads // GROUP, some_heads, 0)
    if others:
        low_ref[...] = wide[...].astype(BF16)
        last = pltpu.make_async_copy(
            low_ref, dq_ref.at[pl.ds(chunk * CHUNK * heads, CHUNK * heads)], sem.at[len(others)]
        )
        last.start()
        for copy in copies + [last]:
            copy.wait()
    else:
        dq_ref[...] = wide[...].astype(BF16)


def within(chunk, index, q, k, v, qt, vt, d, at, scale, before, own, other, token, state, others, heads, dk):
    tokens, width = q.shape
    args = [index, q, k, v, qt, vt, d, scale, before, own, other, token]
    in_specs = [SCALARS] + [WHOLE] * 10 + [ANYWHERE]
    level = None
    if state is not None:
        level = state[1]
        args.append(state[0])
        in_specs.append(WHOLE)
    args += list(others.values())
    in_specs += [WHOLE] * len(others)
    scratch = [pltpu.VMEM((CHUNK * heads, dk), F32)]
    rows = tokens if others else CHUNK
    if others:
        scratch += [pltpu.VMEM((CHUNK * heads, dk), BF16), pltpu.SemaphoreType.DMA((len(others) + 1,))]
    return call(
        functools.partial(within_kernel, heads, dk, chunk, at, level, list(others)),
        "within",
        args,
        in_specs,
        [shape((rows * heads, dk), BF16)] + [shape((CHUNK, width), BF16)] * 2 + [shape(TOKEN, F32)],
        [ANYWHERE if others else WHOLE] + [WHOLE] * 3,
        scratch,
    )


def finish_kernel(heads, dk, n, index_ref, k_ref, v_ref, own_ref, other_ref, _, *refs):
    dkp, dvp, (dk_ref, dv_ref, wide_k, wide_v, low_k, low_v, sem) = refs[:n], refs[n : 2 * n], refs[2 * n :]
    half = heads // 2
    first = index_ref[2] == 0
    after, turned = [], []
    for h in range(heads):
        own, other = own_ref[h % half], other_ref[h % half]
        one = jnp.where(first, own, other) if h < half else jnp.where(first, other, own)
        after.append(one)
        turned.append(one.T)
    copies = []
    for c in range(n):
        rows = slice(c * CHUNK, (c + 1) * CHUNK)
        for h in range(heads):
            cols = slice(h * dk, (h + 1) * dk)
            mine = pl.ds(h, CHUNK, stride=heads)
            wide_k[mine, :] = dkp[c][:, cols].astype(F32) + dot(v_ref[rows, cols], turned[h], NN)
            wide_v[mine, :] = dvp[c][:, cols].astype(F32) + dot(k_ref[rows, cols], after[h], NN)
        for i, (wide, low, out) in enumerate(((wide_k, low_k, dk_ref), (wide_v, low_v, dv_ref))):
            low[c] = wide[...].astype(BF16)
            copy = pltpu.make_async_copy(low.at[c], out.at[pl.ds(c * CHUNK * heads, CHUNK * heads)], sem.at[i, c])
            copy.start()
            copies.append(copy)
    for copy in copies:
        copy.wait()


def finish(index, k, v, dkp, dvp, own, other, token, heads, dk):
    tokens, width = k.shape
    n = tokens // CHUNK
    raw = (CHUNK * heads, dk)
    return call(
        functools.partial(finish_kernel, heads, dk, n),
        "finish",
        [index, k, v, own, other, token, *dkp, *dvp],
        [SCALARS] + [WHOLE] * 4 + [ANYWHERE] + [WHOLE] * (2 * n),
        [shape((tokens * heads, dk), BF16)] * 2,
        [ANYWHERE] * 2,
        [pltpu.VMEM(raw, F32)] * 2 + [pltpu.VMEM((n, *raw), BF16)] * 2 + [pltpu.SemaphoreType.DMA((2, n))],
    )


def swap(array, axis, size, bit):
    return lax.ppermute(array, axis, [(i, i ^ bit) for i in range(size)])


def shifted(array, size, step):
    return lax.ppermute(array, "ctx", [(i, i + step) for i in range(size) if 0 <= i + step < size])


class Order:
    def __init__(self):
        self.token = None

    def tie(self, array):
        array, self.token = lax.optimization_barrier((array, self.token))
        return array


def scan_states(keep, send, size, odd, direction, order):
    came = swap(send, "ctx", size, 1)
    yield None
    own = keep.astype(F32)
    total = own + came.astype(F32)
    exclusive = jnp.zeros_like(total)
    step = 2
    while step < size:
        got = shifted(order.tie(total.astype(BF16)), size, direction * step).astype(F32)
        yield None
        exclusive = exclusive + got
        total = total + got
        step *= 2
    later = odd if direction == 1 else jnp.logical_not(odd)
    low = (exclusive + jnp.where(later, 0.0, own)).astype(BF16)
    other = swap(order.tie(low), "ctx", size, 1)
    mine = exclusive + jnp.where(later, came.astype(F32), 0.0)
    yield mine.astype(BF16), other


def body(n_ctx, n_head, queries, keys, values, d_layer, out_weight):
    tokens, heads, dk = queries.shape
    n = tokens // CHUNK
    block = lax.axis_index("ctx").astype(jnp.int32)
    place = lax.axis_index("head").astype(jnp.int32)
    odd = (block & 1) == 1
    half = (block & 1).astype(jnp.int32)

    near = n_head // 2
    far = 1
    groups = [(n // 2, n - n // 2)] + [(c, 1) for c in reversed(range(n // 2))]
    order = Order()
    *pieces, order.token = cut(d_layer, groups)
    across = {c: swap(piece, "head", n_head, near) for (c, _), piece in zip(groups, pieces)}
    beside = swap(d_layer, "head", n_head, far)

    position = block * tokens + jnp.arange(tokens, dtype=jnp.int32)
    scale = lax.rsqrt((dk * (position + 1)).astype(F32))
    scale = jnp.broadcast_to(scale[:, None], (tokens, dk))
    index = jnp.stack([place ^ near, place ^ near ^ far, half])

    flat = (tokens * heads, dk)
    q, k, v, qt, vt, before, keep, send, order.token = prepare(
        half[None], queries.reshape(flat), keys.reshape(flat), values.reshape(flat), order.token, tokens, heads, dk
    )
    forward = scan_states(keep, send, n_ctx, odd, 1, order)
    next(forward)
    starts = [c * CHUNK for c, _ in groups]
    part, order.token = early(jnp.stack([place, place ^ far]), pieces, starts, beside, out_weight, order.token)

    prefix = state = None
    d, after, dq, dkp, dvp = {}, {}, {}, {}, {}

    def inner(c):
        dq[c], dkp[c], dvp[c], order.token = within(
            c, index, q, k, v, qt, vt, *d[c], scale, before, *prefix, order.token, after[c], dict(dq) if c == 0 else {}, heads, dk
        )

    def outer(c, m):
        nonlocal state, keep, send, prefix
        after[c + m - 1] = None if state is None else (state, 0)
        piece = order.tie(across[c])
        both = swap(piece, "head", n_head, far)
        if prefix is None:
            prefix = next(forward)
        while prefix is None and state is not None:
            prefix = next(forward)
        out = late(c * CHUNK, c == 0, index, piece, both, out_weight, part, scale, qt, order.token, state, heads, dk)
        order.token = out[-1]
        if c == 0:
            keep, send = out[1:3]
        else:
            state = out[1]
        for i in range(m):
            d[c + i] = (out[0], i)
            if i < m - 1:
                after[c + i] = (state, i + 1)

    waiting = []
    for c, m in groups:
        outer(c, m)
        waiting += list(range(c, c + m))[::-1]
        if prefix is None:
            prefix = next(forward)
        elif c != 0:
            while len(waiting) > 1:
                inner(waiting.pop(0))
    backward = scan_states(keep, send, n_ctx, odd, -1, order)
    next(backward)
    suffix = None
    while suffix is None:
        suffix = next(backward)
        if waiting:
            inner(waiting.pop(0))
    while waiting:
        inner(waiting.pop(0))
    d_keys, d_values = finish(
        index, k, v, [dkp[c] for c in range(n)], [dvp[c] for c in range(n)], *suffix, order.token, heads, dk
    )
    return tuple(a.reshape(tokens, heads, dk) for a in (dq[0], d_keys, d_values))


def solution(mesh):
    in_specs = (
        P("ctx", "head", None),
        P("ctx", "head", None),
        P("ctx", "head", None),
        P("ctx", "head"),
        P("head", None),
    )
    out_specs = (P("ctx", "head", None), P("ctx", "head", None), P("ctx", "head", None))

    def program(queries, keys, values, d_layer, out_weight):
        return body(mesh.shape["ctx"], mesh.shape["head"], queries, keys, values, d_layer, out_weight)

    return jax.shard_map(program, mesh=mesh, in_specs=in_specs, out_specs=out_specs, check_vma=False)
```

time: 217 us -> 147 us (0.68)
  waiting for transfers between devices: 107 us -> 22.3 us
  matrix products: 72.9 us -> 0 us
  Pallas kernels: 0 us -> 47.7 us
  local copies, waits for them, and re-layouts: 17.5 us -> 47.8 us
  starting transfers between devices: 0.12 us -> 22.2 us
  between operations: 13.8 us -> 1.28 us
    all_gather x3 -> x0, waiting for transfers between devices: 106 us -> none  [the longest x1 56.3 us: body(): lax.all_gather(d_layer, 'head', axis=1, tiled=True)]
    dot_general x10 -> x0, matrix products: 72.9 us -> none  [the longest x1 13.9 us: body(): lax.dot_general(lax.all_gather(d_layer, 'head', axis=1, tiled=True), out_...]
    pallas_call x0 -> x11, Pallas kernels: none -> 47.7 us  [call(): pl.pallas_call(kernel, in_specs=in_specs, out_specs=out_specs, out_shape=...]
    unnamed x18 -> x118, local copies, waits for them, and re-layouts: 16.6 us -> 47.6 us
    ppermute x0 -> x15, waiting for transfers between devices: none -> 22.3 us  [the longest x11 14.8 us: swap(): return lax.ppermute(array, axis, [(i, i ^ bit) for i in range(size)])]
    ppermute x0 -> x15, starting transfers between devices: none -> 22.2 us  [the longest x4 12.3 us: shifted(): lax.ppermute(array, 'ctx', [(i, i + step) for i in range(size) if 0 <= i...]
    reduce_sum x2 -> x0, other arithmetic: 4.28 us -> none  [the longest x1 2.22 us: body(): jnp.sum(jnp.where(after, every_query.astype(jnp.float32), 0.0), axis=0)]
    convert_element_type x0 -> x6, other arithmetic: none -> 3.62 us  [the longest x2 2.14 us: scan_states(): low = (exclusive + jnp.where(later, 0.0, own)).astype(BF16)]
  transfers between devices with their start and end apart: 3 -> 15, of which waited for: 2 -> 7; matrix products, arithmetic and copies ran while one was open for 25% -> 2% of each run, Pallas kernels for 0% -> 27%
where the time goes in v4:
time: 147 us; the launch traced here: 145 us
  local copies, waits for them, and re-layouts  47.8 us (33%)
  Pallas kernels  47.7 us (32%)
  waiting for transfers between devices  22.3 us (15%)
  starting transfers between devices  22.2 us (15%)
  other arithmetic  3.78 us (3%)
    pallas_call x11, Pallas kernels, call(): pl.pallas_call(kernel, in_specs=in_specs, out_specs=out_specs, out_shape=...  47.7 us
    unnamed x118, local copies, waits for them, and re-layouts  47.6 us
    ppermute x11, waiting for transfers between devices, swap(): return lax.ppermute(array, axis, [(i, i ^ bit) for i in range(size)])  14.8 us
    ppermute x4, starting transfers between devices, shifted(): lax.ppermute(array, 'ctx', [(i, i + step) for i in range(size) if 0 <= i...  12.3 us
    ppermute x11, starting transfers between devices, swap(): return lax.ppermute(array, axis, [(i, i ^ bit) for i in range(size)])  9.93 us
    ppermute x4, waiting for transfers between devices, shifted(): lax.ppermute(array, 'ctx', [(i, i + step) for i in range(size) if 0 <= i...  7.51 us
  transfers between devices with their start and end apart: 15, of which 7 were waited for; matrix products, arithmetic and copies ran while one was open for 2% of the time, Pallas kernels for 27%

profile of v4, /device:TPU:0, one launch (start us, length us, event | category | flops | bytes accessed | tf_op | source)
XLA Modules:
  0.0 145.1 jit_solution(14043704134454774627)
XLA Ops:
  1.1 2.7 %cut.1 = (bf16[512,1024]{1,0:T(8,128)(2,1)}, bf16[256,1024]{1,0:T(8,128)(2,1)S(1)}, bf16[256,1024]{1,0:T(8,128)(2,1)}, f32[8,128]{1,0:T(8,128)S(1)}) custom-call(bf16[1024,1024]{1,0:T(8,128)(2,1)} %source.1), custom_call_target="tpu_custom_call" | custom-call | tf_op jit(solution)/shard_map/cut/pallas_call | solution.py:42
  3.8 2.6 %collective-permute-start.1 = (bf16[512,1024]{1,0:T(8,128)(2,1)}, bf16[512,1024]{1,0:T(8,128)(2,1)}, u32[]{:S(2)}, u32[]{:S(2)}) collective-permute-start(bf16[512,1024]{1,0:T(8,128)(2,1)} %get-tuple-element.71.refs_0_), channel_id=1, source_target_pairs={{0,2},{1,3},{2,0},{3,1},{4,6},{5,7},{6,4},{7,5},{8,10},{9,11},{10,... | collective-permute-start | bytes 3145736 | tf_op jit(solution)/shard_map/ppermute | solution.py:379
  6.4 5.2 %prepare.1 = (bf16[1024,1024]{1,0:T(8,128)(2,1)S(1)}, bf16[1024,1024]{1,0:T(8,128)(2,1)S(1)}, bf16[1024,1024]{1,0:T(8,128)(2,1)S(1)}, bf16[1024,1024]{1,0:T(8,12...) custom-call(s32[1]{0:T(128)} %bitcast.2.half_ref, ...), custom_call_target="tpu_custom_call" | custom-call | tf_op jit(solution)/shard_map/prepare/pallas_call | solution.py:42
  18.4 3.4 %copy-done = bf16[1024,4096]{1,0:T(8,128)(2,1)S(1)} copy-done((bf16[1024,4096]{1,0:T(8,128)(2,1)S(1)}, bf16[1024,4096]{1,0:T(8,128)(2,1)}, u32[]{:S(2)}) %copy-start) | copy-done | bytes 8388632
  21.8 7.3 %early.1 = (f32[1024,1024]{1,0:T(8,128)S(1)}, f32[8,128]{1,0:T(8,128)S(1)}) custom-call(s32[2]{0:T(128)S(1)} %pad_add_fusion.1.index_ref, bf16[512,1024]{1,0:T(8,128)(2,1)} %get-tuple-element.71.refs_0_, bf16[256,1024]{1,0:T(8,128)(2,1)S(1)} %get-tuple-element.72.refs_1_, bf16[256,1024]{1,0:T(8,128)(2,1)} %get-tuple-element.70.refs_2_, ...), custom_call_target="tpu_custom_call" | custom-call | tf_op jit(solution)/shard_map/early/pallas_call | solution.py:42
  29.0 2.0 %copy-done.11 = f32[1024,1024]{1,0:T(8,128)} copy-done((f32[1024,1024]{1,0:T(8,128)}, f32[1024,1024]{1,0:T(8,128)S(1)}, u32[]{:S(2)}) %copy-start.11) | copy-done | bytes 4194328
  33.8 3.2 %collective-permute-done.4 = bf16[4,128,128]{2,1,0:T(8,128)(2,1)S(1)} collective-permute-done((bf16[4,128,128]{2,1,0:T(8,128)(2,1)S(1)}, bf16[4,128,128]{2,1,0:T(8,128)(2,1)S(1)}, u32[]{:S(2)}, u32[]{:S(2)}) %collective-permute-start.4) | collective-permute-done | bytes 131104 | tf_op jit(solution)/shard_map/ppermute | solution.py:379
  37.0 3.5 %collective-permute-start.5 = (bf16[4,128,128]{2,1,0:T(8,128)(2,1)S(1)}, bf16[4,128,128]{2,1,0:T(8,128)(2,1)S(1)}, u32[]{:S(2)}, u32[]{:S(2)}) collective-permute-start(bf16[4,128,128]{2,1,0:T(8,128)(2,1)S(1)} %fusion.10), channel_id=1, source_target_pairs={{0,8},{4,12},{8,16},{12,20},{16,24},{20,28},{1,9},{5,13},{9,17},{1... | collective-permute-start | bytes 393224 | tf_op jit(solution)/shard_map/ppermute | solution.py:383
  40.6 2.4 %collective-permute-done.5 = bf16[4,128,128]{2,1,0:T(8,128)(2,1)S(1)} collective-permute-done((bf16[4,128,128]{2,1,0:T(8,128)(2,1)S(1)}, bf16[4,128,128]{2,1,0:T(8,128)(2,1)S(1)}, u32[]{:S(2)}, u32[]{:S(2)}) %collective-permute-start.5) | collective-permute-done | bytes 131104 | tf_op jit(solution)/shard_map/ppermute | solution.py:383
  44.0 3.4 %copy-done.1 = bf16[1024,4096]{1,0:T(8,128)(2,1)S(1)} copy-done((bf16[1024,4096]{1,0:T(8,128)(2,1)S(1)}, bf16[1024,4096]{1,0:T(8,128)(2,1)}, u32[]{:S(2)}) %copy-start.1) | copy-done | bytes 8388632
  47.3 2.2 %copy-done.12 = f32[1024,1024]{1,0:T(8,128)S(1)} copy-done((f32[1024,1024]{1,0:T(8,128)S(1)}, f32[1024,1024]{1,0:T(8,128)}, u32[]{:S(2)}) %copy-start.12) | copy-done | bytes 4194328
  49.5 6.3 %late.3 = (bf16[512,1024]{1,0:T(8,128)(2,1)S(1)}, f32[2,8,128,128]{3,2,1,0:T(8,128)S(1)}, f32[8,128]{1,0:T(8,128)S(1)}) custom-call(s32[3]{0:T(128)S(1)} %pad_add_fusion.index_ref, bf16[512,1024]{1,0:T(8,128)(2,1)} %collective-permute-done.1.a_ref, bf16[512,1024]{1,0:T(8,128)(2,1)} %collective-permute-done.3.b_ref, bf16[1024,4096]{1,0:T(8,128)(2,1)S(1)} %copy-done.1, ...), custom_call_target="tpu_custom_call" | custom-call | tf_op jit(solution)/shard_map/late/pallas_call | solution.py:42
  59.2 6.0 %collective-permute-start.6 = (bf16[4,128,128]{2,1,0:T(8,128)(2,1)}, bf16[4,128,128]{2,1,0:T(8,128)(2,1)}, u32[]{:S(2)}, u32[]{:S(2)}) collective-permute-start(bf16[4,128,128]{2,1,0:T(8,128)(2,1)} %fusion.4), channel_id=1, source_target_pairs={{0,16},{4,20},{8,24},{12,28},{1,17},{5,21},{9,25},{13,29},{2,18},{... | collective-permute-start | bytes 393224 | tf_op jit(solution)/shard_map/ppermute | solution.py:383
  65.3 2.8 %collective-permute-done.6 = bf16[4,128,128]{2,1,0:T(8,128)(2,1)} collective-permute-done((bf16[4,128,128]{2,1,0:T(8,128)(2,1)}, bf16[4,128,128]{2,1,0:T(8,128)(2,1)}, u32[]{:S(2)}, u32[]{:S(2)}) %collective-permute-start.6) | collective-permute-done | bytes 131104 | tf_op jit(solution)/shard_map/ppermute | solution.py:383
  69.2 1.6 %collective-permute-start.8 = (bf16[4,128,128]{2,1,0:T(8,128)(2,1)S(1)}, bf16[4,128,128]{2,1,0:T(8,128)(2,1)S(1)}, u32[]{:S(2)}, u32[]{:S(2)}) collective-permute-start(bf16[4,128,128]{2,1,0:T(8,128)(2,1)S(1)} %get-tuple-element.88), channel_id=1, source_target_pairs={{0,4},{4,0},{8,12},{12,8},{16,20},{20,16},{24,28},{28,24},{1,5},{5... | collective-permute-start | bytes 393224 | tf_op jit(solution)/shard_map/ppermute | solution.py:379
  71.6 3.4 %copy-done.2 = bf16[1024,4096]{1,0:T(8,128)(2,1)S(1)} copy-done((bf16[1024,4096]{1,0:T(8,128)(2,1)S(1)}, bf16[1024,4096]{1,0:T(8,128)(2,1)}, u32[]{:S(2)}) %copy-start.2) | copy-done | bytes 8388632
  75.0 2.2 %copy-done.13 = f32[1024,1024]{1,0:T(8,128)S(1)} copy-done((f32[1024,1024]{1,0:T(8,128)S(1)}, f32[1024,1024]{1,0:T(8,128)}, u32[]{:S(2)}) %copy-start.13) | copy-done | bytes 4194328
  79.5 4.4 %late.4 = (bf16[256,1024]{1,0:T(8,128)(2,1)S(1)}, f32[1,8,128,128]{3,2,1,0:T(8,128)S(1)}, f32[8,128]{1,0:T(8,128)S(1)}) custom-call(s32[3]{0:T(128)S(1)} %pad_add_fusion.index_ref, bf16[256,1024]{1,0:T(8,128)(2,1)} %collective-permute-done.7.a_ref, bf16[256,1024]{1,0:T(8,128)(2,1)S(1)} %copy-done.42, bf16[1024,4096]{1,0:T(8,128)(2,1)S(1)} %copy-done.2, ...), custom_call_target="tpu_custom_call" | custom-call | tf_op jit(solution)/shard_map/late/pallas_call | solution.py:42
  83.9 2.9 %within.4 = (bf16[2048,128]{1,0:T(8,128)(2,1)S(1)}, bf16[256,1024]{1,0:T(8,128)(2,1)S(1)}, bf16[256,1024]{1,0:T(8,128)(2,1)S(1)}, f32[8,128]{1,0:T(8,128)S(1)}) custom-call(s32[3]{0:T(128)S(1)} %pad_add_fusion.index_ref, bf16[1024,1024]{1,0:T(8,128)(2,1)S(1)} %copy-done.16, bf16[1024,1024]{1,0:T(8,128)(2,1)S(1)} %copy-done.4, ...), custom_call_target="tpu_custom_call" | custom-call | tf_op jit(solution)/shard_map/within/pallas_call | solution.py:42
  88.4 3.1 %within.5 = (bf16[2048,128]{1,0:T(8,128)(2,1)S(1)}, bf16[256,1024]{1,0:T(8,128)(2,1)S(1)}, bf16[256,1024]{1,0:T(8,128)(2,1)S(1)}, f32[8,128]{1,0:T(8,128)S(1)}) custom-call(s32[3]{0:T(128)S(1)} %pad_add_fusion.index_ref, bf16[1024,1024]{1,0:T(8,128)(2,1)S(1)} %copy-done.16, bf16[1024,1024]{1,0:T(8,128)(2,1)S(1)} %copy-done.4, ...), custom_call_target="tpu_custom_call" | custom-call | tf_op jit(solution)/shard_map/within/pallas_call | solution.py:42
  94.0 2.1 %collective-permute-done.10.b_ref = bf16[256,1024]{1,0:T(8,128)(2,1)S(1)} collective-permute-done((bf16[256,1024]{1,0:T(8,128)(2,1)}, bf16[256,1024]{1,0:T(8,128)(2,1)S(1)}, u32[]{:S(2)}, u32[]{:S(2)}) %collective-permute-start.10) | collective-permute-done | bytes 524320 | tf_op jit(solution)/shard_map/ppermute | solution.py:379
  96.1 4.2 %late.5 = (bf16[256,1024]{1,0:T(8,128)(2,1)S(1)}, bf16[4,128,128]{2,1,0:T(8,128)(2,1)S(1)}, bf16[4,128,128]{2,1,0:T(8,128)(2,1)S(1)}, f32[8,128]{1,0:T(8,128)S(1)}) custom-call(s32[3]{0:T(128)S(1)} %pad_add_fusion.index_ref, bf16[256,1024]{1,0:T(8,128)(2,1)} %collective-permute-done.a_ref, bf16[256,1024]{1,0:T(8,128)(2,1)S(1)} %collective-permute-done.10.b_ref, ...), custom_call_target="tpu_custom_call" | custom-call | tf_op jit(solution)/shard_map/late/pallas_call | solution.py:42
  101.7 5.0 %collective-permute-done.11 = bf16[4,128,128]{2,1,0:T(8,128)(2,1)S(1)} collective-permute-done((bf16[4,128,128]{2,1,0:T(8,128)(2,1)S(1)}, bf16[4,128,128]{2,1,0:T(8,128)(2,1)S(1)}, u32[]{:S(2)}, u32[]{:S(2)}) %collective-permute-start.11) | collective-permute-done | bytes 131104 | tf_op jit(solution)/shard_map/ppermute | solution.py:379
  108.0 3.1 %within.6 = (bf16[2048,128]{1,0:T(8,128)(2,1)S(1)}, bf16[256,1024]{1,0:T(8,128)(2,1)S(1)}, bf16[256,1024]{1,0:T(8,128)(2,1)S(1)}, f32[8,128]{1,0:T(8,128)S(1)}) custom-call(s32[3]{0:T(128)S(1)} %pad_add_fusion.index_ref, bf16[1024,1024]{1,0:T(8,128)(2,1)S(1)} %copy-done.16, bf16[1024,1024]{1,0:T(8,128)(2,1)S(1)} %copy-done.4, ...), custom_call_target="tpu_custom_call" | custom-call | tf_op jit(solution)/shard_map/within/pallas_call | solution.py:42
  113.6 2.3 %collective-permute-done.12 = bf16[4,128,128]{2,1,0:T(8,128)(2,1)S(1)} collective-permute-done((bf16[4,128,128]{2,1,0:T(8,128)(2,1)S(1)}, bf16[4,128,128]{2,1,0:T(8,128)(2,1)S(1)}, u32[]{:S(2)}, u32[]{:S(2)}) %collective-permute-start.12) | collective-permute-done | bytes 131104 | tf_op jit(solution)/shard_map/ppermute | solution.py:383
  119.6 1.6 %copy-done.9 = bf16[1024,1024]{1,0:T(8,128)(2,1)S(1)} copy-done((bf16[1024,1024]{1,0:T(8,128)(2,1)S(1)}, bf16[1024,1024]{1,0:T(8,128)(2,1)}, u32[]{:S(2)}) %copy-start.9) | copy-done | bytes 2097176
  121.2 1.6 %copy-done.17 = bf16[1024,1024]{1,0:T(8,128)(2,1)S(1)} copy-done((bf16[1024,1024]{1,0:T(8,128)(2,1)S(1)}, bf16[1024,1024]{1,0:T(8,128)(2,1)}, u32[]{:S(2)}) %copy-start.17) | copy-done | bytes 2097176
  122.8 1.6 %copy-done.20 = bf16[1024,1024]{1,0:T(8,128)(2,1)S(1)} copy-done((bf16[1024,1024]{1,0:T(8,128)(2,1)S(1)}, bf16[1024,1024]{1,0:T(8,128)(2,1)}, u32[]{:S(2)}) %copy-start.20) | copy-done | bytes 2097176
  124.4 1.6 %copy-done.23 = f32[4,8,128,128]{3,2,1,0:T(8,128)S(1)} copy-done((f32[4,8,128,128]{3,2,1,0:T(8,128)S(1)}, f32[4,8,128,128]{3,2,1,0:T(8,128)}, u32[]{:S(2)}) %copy-start.23) | copy-done | bytes 2097176
  130.2 3.9 %within.7 = (bf16[8192,128]{1,0:T(8,128)(2,1)}, bf16[256,1024]{1,0:T(8,128)(2,1)S(1)}, bf16[256,1024]{1,0:T(8,128)(2,1)S(1)}, f32[8,128]{1,0:T(8,128)S(1)}) custom-call(s32[3]{0:T(128)S(1)} %pad_add_fusion.index_ref, bf16[1024,1024]{1,0:T(8,128)(2,1)S(1)} %copy-done.17, bf16[1024,1024]{1,0:T(8,128)(2,1)S(1)} %copy-done.5, bf16[1024,1024]{1,0:T(8,128)(2,1)S(1)} %copy-done.9, ...), custom_call_target="tpu_custom_call" | custom-call | tf_op jit(solution)/shard_map/within/pallas_call | solution.py:42
  135.8 4.5 %collective-permute-done.14.other_ref = bf16[4,128,128]{2,1,0:T(8,128)(2,1)S(1)} collective-permute-done((bf16[4,128,128]{2,1,0:T(8,128)(2,1)S(1)}, bf16[4,128,128]{2,1,0:T(8,128)(2,1)S(1)}, u32[]{:S(2)}, u32[]{:S(2)}) %collective-permute-start.14) | collective-permute-done | bytes 131104 | tf_op jit(solution)/shard_map/ppermute | solution.py:379
  140.3 4.6 %finish.1 = (bf16[8192,128]{1,0:T(8,128)(2,1)}, bf16[8192,128]{1,0:T(8,128)(2,1)}) custom-call(s32[3]{0:T(128)S(1)} %pad_add_fusion.index_ref, bf16[1024,1024]{1,0:T(8,128)(2,1)S(1)} %copy-done.6, bf16[1024,1024]{1,0:T(8,128)(2,1)S(1)} %copy-done.10, bf16[4,128,128]{2,1,0:T(8,128)(2,1)S(1)} %get-tuple-element.126.own_ref, ...), custom_call_target="tpu_custom_call" | custom-call | tf_op jit(solution)/shard_map/finish/pallas_call | solution.py:42
  (138 shorter events, 37.3 us)
Async XLA Ops:
  0.6 17.7 %collective-permute-start.2 = (bf16[1024,1024]{1,0:T(8,128)(2,1)}, bf16[1024,1024]{1,0:T(8,128)(2,1)}, u32[]{:S(2)}, u32[]{:S(2)}) collective-permute-start(bf16[1024,1024]{1,0:T(8,128)(2,1)} %source.1), channel_id=1, source_target_pairs={{0,1},{1,0},{2,3},{3,2},{4,5},{5,4},{6,7},{7,6},{8,9},{9,8},{10,11... | collective-permute-start | bytes 6291464 | tf_op jit(solution)/shard_map/ppermute | solution.py:379
  3.8 27.2 %collective-permute-start.1 = (bf16[512,1024]{1,0:T(8,128)(2,1)}, bf16[512,1024]{1,0:T(8,128)(2,1)}, u32[]{:S(2)}, u32[]{:S(2)}) collective-permute-start(bf16[512,1024]{1,0:T(8,128)(2,1)} %get-tuple-element.71.refs_0_), channel_id=1, source_target_pairs={{0,2},{1,3},{2,0},{3,1},{4,6},{5,7},{6,4},{7,5},{8,10},{9,11},{10,... | collective-permute-start | bytes 3145736 | tf_op jit(solution)/shard_map/ppermute | solution.py:379
  31.1 12.7 %collective-permute-start.3 = (bf16[512,1024]{1,0:T(8,128)(2,1)}, bf16[512,1024]{1,0:T(8,128)(2,1)}, u32[]{:S(2)}, u32[]{:S(2)}) collective-permute-start(bf16[512,1024]{1,0:T(8,128)(2,1)} %collective-permute-done.1.a_ref), channel_id=1, source_target_pairs={{0,1},{1,0},{2,3},{3,2},{4,5},{5,4},{6,7},{7,6},{8,9},{9,8},{10,11... | collective-permute-start | bytes 3145736 | tf_op jit(solution)/shard_map/ppermute | solution.py:379
  31.3 5.7 %collective-permute-start.4 = (bf16[4,128,128]{2,1,0:T(8,128)(2,1)S(1)}, bf16[4,128,128]{2,1,0:T(8,128)(2,1)S(1)}, u32[]{:S(2)}, u32[]{:S(2)}) collective-permute-start(bf16[4,128,128]{2,1,0:T(8,128)(2,1)S(1)} %get-tuple-element.78), channel_id=1, source_target_pairs={{0,4},{4,0},{8,12},{12,8},{16,20},{20,16},{24,28},{28,24},{1,5},{5... | collective-permute-start | bytes 393224 | tf_op jit(solution)/shard_map/ppermute | solution.py:379
  32.8 25.0 %collective-permute-start.7 = (bf16[256,1024]{1,0:T(8,128)(2,1)S(1)}, bf16[256,1024]{1,0:T(8,128)(2,1)}, u32[]{:S(2)}, u32[]{:S(2)}) collective-permute-start(bf16[256,1024]{1,0:T(8,128)(2,1)S(1)} %get-tuple-element.72.refs_1_), channel_id=1, source_target_pairs={{0,2},{1,3},{2,0},{3,1},{4,6},{5,7},{6,4},{7,5},{8,10},{9,11},{10,... | collective-permute-start | bytes 1572872 | tf_op jit(solution)/shard_map/ppermute | solution.py:379
  37.0 7.0 %copy-start.51 = (bf16[4,128,128]{2,1,0:T(8,128)(2,1)}, bf16[4,128,128]{2,1,0:T(8,128)(2,1)S(1)}, u32[]{:S(2)}) copy-start(bf16[4,128,128]{2,1,0:T(8,128)(2,1)S(1)} %collective-permute-done.4) | copy-start | bytes 393220
  37.0 6.0 %collective-permute-start.5 = (bf16[4,128,128]{2,1,0:T(8,128)(2,1)S(1)}, bf16[4,128,128]{2,1,0:T(8,128)(2,1)S(1)}, u32[]{:S(2)}, u32[]{:S(2)}) collective-permute-start(bf16[4,128,128]{2,1,0:T(8,128)(2,1)S(1)} %fusion.10), channel_id=1, source_target_pairs={{0,8},{4,12},{8,16},{12,20},{16,24},{20,28},{1,9},{5,13},{9,17},{1... | collective-permute-start | bytes 393224 | tf_op jit(solution)/shard_map/ppermute | solution.py:383
  57.8 13.0 %collective-permute-start.9 = (bf16[256,1024]{1,0:T(8,128)(2,1)}, bf16[256,1024]{1,0:T(8,128)(2,1)S(1)}, u32[]{:S(2)}, u32[]{:S(2)}) collective-permute-start(bf16[256,1024]{1,0:T(8,128)(2,1)} %collective-permute-done.7.a_ref), channel_id=1, source_target_pairs={{0,1},{1,0},{2,3},{3,2},{4,5},{5,4},{6,7},{7,6},{8,9},{9,8},{10,11... | collective-permute-start | bytes 1572872 | tf_op jit(solution)/shard_map/ppermute | solution.py:379
  57.8 36.2 %collective-permute-start = (bf16[256,1024]{1,0:T(8,128)(2,1)}, bf16[256,1024]{1,0:T(8,128)(2,1)}, u32[]{:S(2)}, u32[]{:S(2)}) collective-permute-start(bf16[256,1024]{1,0:T(8,128)(2,1)} %get-tuple-element.70.refs_2_), channel_id=1, source_target_pairs={{0,2},{1,3},{2,0},{3,1},{4,6},{5,7},{6,4},{7,5},{8,10},{9,11},{10,... | collective-permute-start | bytes 1572872 | tf_op jit(solution)/shard_map/ppermute | solution.py:379
  59.2 8.9 %collective-permute-start.6 = (bf16[4,128,128]{2,1,0:T(8,128)(2,1)}, bf16[4,128,128]{2,1,0:T(8,128)(2,1)}, u32[]{:S(2)}, u32[]{:S(2)}) collective-permute-start(bf16[4,128,128]{2,1,0:T(8,128)(2,1)} %fusion.4), channel_id=1, source_target_pairs={{0,16},{4,20},{8,24},{12,28},{1,17},{5,21},{9,25},{13,29},{2,18},{... | collective-permute-start | bytes 393224 | tf_op jit(solution)/shard_map/ppermute | solution.py:383
  69.2 14.6 %collective-permute-start.8 = (bf16[4,128,128]{2,1,0:T(8,128)(2,1)S(1)}, bf16[4,128,128]{2,1,0:T(8,128)(2,1)S(1)}, u32[]{:S(2)}, u32[]{:S(2)}) collective-permute-start(bf16[4,128,128]{2,1,0:T(8,128)(2,1)S(1)} %get-tuple-element.88), channel_id=1, source_target_pairs={{0,4},{4,0},{8,12},{12,8},{16,20},{20,16},{24,28},{28,24},{1,5},{5... | collective-permute-start | bytes 393224 | tf_op jit(solution)/shard_map/ppermute | solution.py:379
  79.5 4.4 %copy-start.19 = (bf16[1024,1024]{1,0:T(8,128)(2,1)S(1)}, bf16[1024,1024]{1,0:T(8,128)(2,1)}, u32[]{:S(2)}) copy-start(bf16[1024,1024]{1,0:T(8,128)(2,1)} %copy-done.18) | copy-start | bytes 6291460
  79.5 4.4 %copy-start.22 = (f32[4,8,128,128]{3,2,1,0:T(8,128)S(1)}, f32[4,8,128,128]{3,2,1,0:T(8,128)}, u32[]{:S(2)}) copy-start(f32[4,8,128,128]{3,2,1,0:T(8,128)} %copy-done.21) | copy-start | bytes 6291460
  79.5 4.4 %copy-start.28 = (bf16[512,1024]{1,0:T(8,128)(2,1)S(1)}, bf16[512,1024]{1,0:T(8,128)(2,1)}, u32[]{:S(2)}) copy-start(bf16[512,1024]{1,0:T(8,128)(2,1)} %copy-done.27) | copy-start | bytes 3145732
  83.9 4.5 %copy-start.26 = (f32[2,8,128,128]{3,2,1,0:T(8,128)S(1)}, f32[2,8,128,128]{3,2,1,0:T(8,128)}, u32[]{:S(2)}) copy-start(f32[2,8,128,128]{3,2,1,0:T(8,128)} %copy-done.24) | copy-start | bytes 3145732
  88.4 7.7 %slice-start = ((s8[8388608]{0:T(1024)(128)(4,1)}), s8[4194304]{0:T(1024)(128)(4,1)S(1)}, s32[]{:S(2)}) async-start(s8[8388608]{0:T(1024)(128)(4,1)} %bitcast.11), calls=%async_computation | async-start | bytes 8388608
  88.4 7.7 %slice-start.1 = ((s8[8388608]{0:T(1024)(128)(4,1)}), s8[4194304]{0:T(1024)(128)(4,1)S(1)}, s32[]{:S(2)}) async-start(s8[8388608]{0:T(1024)(128)(4,1)} %bitcast.11), calls=%async_computation.1 | async-start | bytes 8388608
  88.4 7.7 %copy-start.14 = (f32[1024,1024]{1,0:T(8,128)S(1)}, f32[1024,1024]{1,0:T(8,128)}, u32[]{:S(2)}) copy-start(f32[1024,1024]{1,0:T(8,128)} %copy-done.11) | copy-start | bytes 12582916
  94.0 2.1 %collective-permute-start.10 = (bf16[256,1024]{1,0:T(8,128)(2,1)}, bf16[256,1024]{1,0:T(8,128)(2,1)S(1)}, u32[]{:S(2)}, u32[]{:S(2)}) collective-permute-start(bf16[256,1024]{1,0:T(8,128)(2,1)} %collective-permute-done.a_ref), channel_id=1, source_target_pairs={{0,1},{1,0},{2,3},{3,2},{4,5},{5,4},{6,7},{7,6},{8,9},{9,8},{10,11... | collective-permute-start | bytes 1572872 | tf_op jit(solution)/shard_map/ppermute | solution.py:379
  101.2 5.5 %collective-permute-start.11 = (bf16[4,128,128]{2,1,0:T(8,128)(2,1)S(1)}, bf16[4,128,128]{2,1,0:T(8,128)(2,1)S(1)}, u32[]{:S(2)}, u32[]{:S(2)}) collective-permute-start(bf16[4,128,128]{2,1,0:T(8,128)(2,1)S(1)} %get-tuple-element.100), channel_id=1, source_target_pairs={{0,4},{4,0},{8,12},{12,8},{16,20},{20,16},{24,28},{28,24},{1,5},{5... | collective-permute-start | bytes 393224 | tf_op jit(solution)/shard_map/ppermute | solution.py:379
  106.7 9.2 %copy-start.52 = (bf16[4,128,128]{2,1,0:T(8,128)(2,1)}, bf16[4,128,128]{2,1,0:T(8,128)(2,1)S(1)}, u32[]{:S(2)}) copy-start(bf16[4,128,128]{2,1,0:T(8,128)(2,1)S(1)} %collective-permute-done.11) | copy-start | bytes 393220
  106.7 9.1 %collective-permute-start.12 = (bf16[4,128,128]{2,1,0:T(8,128)(2,1)S(1)}, bf16[4,128,128]{2,1,0:T(8,128)(2,1)S(1)}, u32[]{:S(2)}, u32[]{:S(2)}) collective-permute-start(bf16[4,128,128]{2,1,0:T(8,128)(2,1)S(1)} %fusion.11), channel_id=1, source_target_pairs={{8,0},{12,4},{16,8},{20,12},{24,16},{28,20},{9,1},{13,5},{17,9},{2... | collective-permute-start | bytes 393224 | tf_op jit(solution)/shard_map/ppermute | solution.py:383
  116.6 17.6 %collective-permute-start.13 = (bf16[4,128,128]{2,1,0:T(8,128)(2,1)}, bf16[4,128,128]{2,1,0:T(8,128)(2,1)}, u32[]{:S(2)}, u32[]{:S(2)}) collective-permute-start(bf16[4,128,128]{2,1,0:T(8,128)(2,1)} %fusion.9), channel_id=1, source_target_pairs={{16,0},{20,4},{24,8},{28,12},{17,1},{21,5},{25,9},{29,13},{18,2},{... | collective-permute-start | bytes 393224 | tf_op jit(solution)/shard_map/ppermute | solution.py:383
  130.2 10.1 %copy-start.6 = (bf16[1024,1024]{1,0:T(8,128)(2,1)S(1)}, bf16[1024,1024]{1,0:T(8,128)(2,1)}, u32[]{:S(2)}) copy-start(bf16[1024,1024]{1,0:T(8,128)(2,1)} %copy-done.3) | copy-start | bytes 6291460
  130.2 10.1 %copy-start.10 = (bf16[1024,1024]{1,0:T(8,128)(2,1)S(1)}, bf16[1024,1024]{1,0:T(8,128)(2,1)}, u32[]{:S(2)}) copy-start(bf16[1024,1024]{1,0:T(8,128)(2,1)} %copy-done.7) | copy-start | bytes 6291460
  130.2 10.1 %copy-start.30 = (bf16[256,1024]{1,0:T(8,128)(2,1)S(1)}, bf16[256,1024]{1,0:T(8,128)(2,1)}, u32[]{:S(2)}) copy-start(bf16[256,1024]{1,0:T(8,128)(2,1)} %copy-done.29) | copy-start | bytes 1572868
  130.2 10.1 %copy-start.32 = (bf16[256,1024]{1,0:T(8,128)(2,1)S(1)}, bf16[256,1024]{1,0:T(8,128)(2,1)}, u32[]{:S(2)}) copy-start(bf16[256,1024]{1,0:T(8,128)(2,1)} %copy-done.31) | copy-start | bytes 1572868
  130.2 10.1 %copy-start.34 = (bf16[256,1024]{1,0:T(8,128)(2,1)S(1)}, bf16[256,1024]{1,0:T(8,128)(2,1)}, u32[]{:S(2)}) copy-start(bf16[256,1024]{1,0:T(8,128)(2,1)} %copy-done.33) | copy-start | bytes 1572868
  130.2 10.1 %copy-start.36 = (bf16[256,1024]{1,0:T(8,128)(2,1)S(1)}, bf16[256,1024]{1,0:T(8,128)(2,1)}, u32[]{:S(2)}) copy-start(bf16[256,1024]{1,0:T(8,128)(2,1)} %copy-done.35) | copy-start | bytes 1572868
  130.2 10.1 %copy-start.38 = (bf16[256,1024]{1,0:T(8,128)(2,1)S(1)}, bf16[256,1024]{1,0:T(8,128)(2,1)}, u32[]{:S(2)}) copy-start(bf16[256,1024]{1,0:T(8,128)(2,1)} %copy-done.37) | copy-start | bytes 1572868
  130.2 10.1 %copy-start.40 = (bf16[256,1024]{1,0:T(8,128)(2,1)S(1)}, bf16[256,1024]{1,0:T(8,128)(2,1)}, u32[]{:S(2)}) copy-start(bf16[256,1024]{1,0:T(8,128)(2,1)} %copy-done.39) | copy-start | bytes 1572868
  135.2 5.0 %collective-permute-start.14 = (bf16[4,128,128]{2,1,0:T(8,128)(2,1)S(1)}, bf16[4,128,128]{2,1,0:T(8,128)(2,1)S(1)}, u32[]{:S(2)}, u32[]{:S(2)}) collective-permute-start(bf16[4,128,128]{2,1,0:T(8,128)(2,1)S(1)} %get-tuple-element.113), channel_id=1, source_target_pairs={{0,4},{4,0},{8,12},{12,8},{16,20},{20,16},{24,28},{28,24},{1,5},{5... | collective-permute-start | bytes 393224 | tf_op jit(solution)/shard_map/ppermute | solution.py:379
  (42 other events, 73.5 us)

commit v5 on v4

--- a/solution.py
+++ b/solution.py
@@ -18,7 +18,6 @@
 FREE = pl.CostEstimate(flops=0, bytes_accessed=0, transcendentals=0)
 VMEM_LIMIT = 14 * 1024 * 1024
 WHOLE = pl.BlockSpec(memory_space=pltpu.VMEM)
-SCALARS = pl.BlockSpec(memory_space=pltpu.SMEM)
 ANYWHERE = pl.BlockSpec(memory_space=pl.ANY)
 
 
@@ -78,7 +77,7 @@
 
 
 def prepare_kernel(
-    heads, dk, half_ref, q_ref, k_ref, v_ref, _, qf_ref, kf_ref, vf_ref, qt_ref, vt_ref, before_ref, keep_ref, send_ref, token_ref,
+    heads, dk, q_ref, k_ref, v_ref, _, qf_ref, kf_ref, vf_ref, qt_ref, vt_ref, before_ref, scale_ref, keep_ref, send_ref, token_ref,
     raw, wides, acc, sem
 ):
     n = qf_ref.shape[0] // CHUNK
@@ -92,6 +91,9 @@
             load(i, c).start()
     token_ref[...] = jnp.zeros_like(token_ref)
     acc[...] = jnp.zeros_like(acc)
+    tokens = scale_ref.shape[0]
+    position = lax.axis_index("ctx") * tokens + lax.broadcasted_iota(jnp.int32, scale_ref.shape, 0)
+    scale_ref[...] = lax.rsqrt((dk * (position + 1)).astype(F32))
 
     def one_chunk(c, _):
         rows = part_of(c, CHUNK)
@@ -114,25 +116,25 @@
 
     lax.fori_loop(0, n, one_chunk, 0)
     low, high = acc[: heads // 2].astype(BF16), acc[heads // 2 :].astype(BF16)
-    first = half_ref[0] == 0
+    first = lax.axis_index("ctx") % 2 == 0
     keep_ref[...] = jnp.where(first, low, high)
     send_ref[...] = jnp.where(first, high, low)
 
 
-def prepare(half, q, k, v, token, tokens, heads, dk):
+def prepare(q, k, v, token, tokens, heads, dk):
     n = tokens // CHUNK
     width = heads * dk
     return call(
         functools.partial(prepare_kernel, heads, dk),
         "prepare",
-        [half, *outside(q, k, v), token],
-        [SCALARS] + [ANYWHERE] * 4,
+        [*outside(q, k, v), token],
+        [ANYWHERE] * 4,
         [shape((tokens, width), BF16)] * 3
         + [shape((width, tokens), BF16)] * 2
-        + [shape((n, heads, dk, dk), F32)]
+        + [shape((n, heads, dk, dk), F32), shape((tokens, dk), F32)]
         + [shape((heads // 2, dk, dk), BF16)] * 2
         + [shape(TOKEN, F32)],
-        [WHOLE] * 9,
+        [WHOLE] * 10,
         [
             pltpu.VMEM((3, n, CHUNK * heads, dk), BF16),
             pltpu.VMEM((3, CHUNK * heads, dk), F32),
@@ -142,11 +144,12 @@
     )
 
 
-def early_kernel(starts, index_ref, *refs):
+def early_kernel(starts, *refs):
     pieces, (b_ref, w_ref, _, out_ref, token_ref) = refs[: len(starts)], refs[len(starts) :]
     token_ref[...] = jnp.zeros_like(token_ref)
     features = b_ref.shape[1]
-    first, second = part_of(index_ref[0], features), part_of(index_ref[1], features)
+    place = lax.axis_index("head")
+    first, second = part_of(place, features), part_of(place ^ 1, features)
 
     def one_tile(j, _):
         tile = part_of(j, PAIR * 128)
@@ -159,20 +162,20 @@
     lax.fori_loop(0, out_ref.shape[1] // (PAIR * 128), one_tile, 0)
 
 
-def early(index, pieces, starts, b, weight, token):
+def early(pieces, starts, b, weight, token):
     tokens = b.shape[0]
     width = weight.shape[0]
     return call(
         functools.partial(early_kernel, starts),
         "early",
-        [index, *pieces, b, weight, token],
-        [SCALARS] + [WHOLE] * (len(pieces) + 2) + [ANYWHERE],
+        [*pieces, b, weight, token],
+        [WHOLE] * (len(pieces) + 2) + [ANYWHERE],
         [shape((tokens, width), F32), shape(TOKEN, F32)],
         [WHOLE] * 2,
     )
 
 
-def late_kernel(last, first, start, dk, index_ref, a_ref, b_ref, w_ref, part_ref, scale_ref, qt_ref, _, *refs):
+def late_kernel(last, first, start, near, dk, a_ref, b_ref, w_ref, part_ref, scale_ref, qt_ref, _, *refs):
     state_ref, refs = (None, refs) if first else (refs[0], refs[1:])
     refs, token_ref, at, bt = refs[:-3], refs[-3], refs[-2], refs[-1]
     d_ref = refs[0]
@@ -181,7 +184,8 @@
     token_ref[...] = jnp.zeros_like(token_ref)
     at[...] = a_ref[...].T
     bt[...] = b_ref[...].T
-    one, two = part_of(index_ref[0], features), part_of(index_ref[1], features)
+    place = lax.axis_index("head")
+    one, two = part_of(place ^ near, features), part_of(place ^ near ^ 1, features)
     steps = d_ref.shape[1] // tile
     here = slice(start, start + count)
 
@@ -203,7 +207,7 @@
         if last:
             keep_ref, send_ref = refs[1:]
             place = lax.rem(j, steps // 2) * PAIR
-            mine = (j // (steps // 2)) == index_ref[2]
+            mine = (j // (steps // 2)) == lax.axis_index("ctx") % 2
 
             @pl.when(mine)
             def _():
@@ -220,11 +224,11 @@
     lax.fori_loop(0, steps, one_tile, 0)
 
 
-def late(start, last, index, a, b, weight, part, scale, qt, token, state, heads, dk):
+def late(start, last, near, a, b, weight, part, scale, qt, token, state, heads, dk):
     rows, features = a.shape
     width = weight.shape[0]
-    args = [index, a, b, weight, part, scale, qt, token]
-    in_specs = [SCALARS] + [WHOLE] * 6 + [ANYWHERE]
+    args = [a, b, weight, part, scale, qt, token]
+    in_specs = [WHOLE] * 6 + [ANYWHERE]
     if state is not None:
         args.append(state)
         in_specs.append(WHOLE)
@@ -235,7 +239,7 @@
         out_shape.append(shape((rows // CHUNK, heads, dk, dk), F32))
     out_shape.append(shape(TOKEN, F32))
     return call(
-        functools.partial(late_kernel, last, state is None, start, dk),
+        functools.partial(late_kernel, last, state is None, start, near, dk),
         "late",
         args,
         in_specs,
@@ -247,7 +251,7 @@
 
 def within_kernel(
     heads, dk, chunk, at, level, others,
-    index_ref, q_ref, k_ref, v_ref, qt_ref, vt_ref, d_ref, scale_ref, before_ref, own_ref, other_ref, _, *refs
+    q_ref, k_ref, v_ref, qt_ref, vt_ref, d_ref, scale_ref, before_ref, own_ref, other_ref, _, *refs
 ):
     state_ref, refs = (None, refs) if level is None else (refs[0], refs[1:])
     earlier_dq, refs = refs[: len(others)], refs[len(others) :]
@@ -271,7 +275,7 @@
     half = heads // 2
 
     def some_heads(g, _):
-        mine = g * GROUP // half == index_ref[2]
+        mine = g * GROUP // half == lax.axis_index("ctx") % 2
         for i in range(GROUP):
             h = g * GROUP + i
             cols = part_of(h, dk)
@@ -307,10 +311,10 @@
         dq_ref[...] = wide[...].astype(BF16)
 
 
-def within(chunk, index, q, k, v, qt, vt, d, at, scale, before, own, other, token, state, others, heads, dk):
+def within(chunk, q, k, v, qt, vt, d, at, scale, before, own, other, token, state, others, heads, dk):
     tokens, width = q.shape
-    args = [index, q, k, v, qt, vt, d, scale, before, own, other, token]
-    in_specs = [SCALARS] + [WHOLE] * 10 + [ANYWHERE]
+    args = [q, k, v, qt, vt, d, scale, before, own, other, token]
+    in_specs = [WHOLE] * 10 + [ANYWHERE]
     level = None
     if state is not None:
         level = state[1]
@@ -333,10 +337,10 @@
     )
 
 
-def finish_kernel(heads, dk, n, index_ref, k_ref, v_ref, own_ref, other_ref, _, *refs):
+def finish_kernel(heads, dk, n, k_ref, v_ref, own_ref, other_ref, _, *refs):
     dkp, dvp, (dk_ref, dv_ref, wide_k, wide_v, low_k, low_v, sem) = refs[:n], refs[n : 2 * n], refs[2 * n :]
     half = heads // 2
-    first = index_ref[2] == 0
+    first = lax.axis_index("ctx") % 2 == 0
     after, turned = [], []
     for h in range(heads):
         own, other = own_ref[h % half], other_ref[h % half]
@@ -360,15 +364,15 @@
         copy.wait()
 
 
-def finish(index, k, v, dkp, dvp, own, other, token, heads, dk):
+def finish(k, v, dkp, dvp, own, other, token, heads, dk):
     tokens, width = k.shape
     n = tokens // CHUNK
     raw = (CHUNK * heads, dk)
     return call(
         functools.partial(finish_kernel, heads, dk, n),
         "finish",
-        [index, k, v, own, other, token, *dkp, *dvp],
-        [SCALARS] + [WHOLE] * 4 + [ANYWHERE] + [WHOLE] * (2 * n),
+        [k, v, own, other, token, *dkp, *dvp],
+        [WHOLE] * 4 + [ANYWHERE] + [WHOLE] * (2 * n),
         [shape((tokens * heads, dk), BF16)] * 2,
         [ANYWHERE] * 2,
         [pltpu.VMEM(raw, F32)] * 2 + [pltpu.VMEM((n, *raw), BF16)] * 2 + [pltpu.SemaphoreType.DMA((2, n))],
@@ -392,34 +396,42 @@
         return array
 
 
-def scan_states(keep, send, size, odd, direction, order):
-    came = swap(send, "ctx", size, 1)
+def total_kernel(*refs):
+    *terms, out = refs
+    total = terms[0][...].astype(F32)
+    for term in terms[1:]:
+        total = total + term[...].astype(F32)
+    out[...] = total.astype(BF16)
+
+
+def ends_kernel(later_is_odd, own, came, *refs):
+    *got, give, mine = refs
+    exclusive = got[0][...].astype(F32)
+    for term in got[1:]:
+        exclusive = exclusive + term[...].astype(F32)
+    later = (lax.axis_index("ctx") % 2 == 1) == later_is_odd
+    give[...] = jnp.where(later, exclusive, exclusive + own[...].astype(F32)).astype(BF16)
+    mine[...] = jnp.where(later, exclusive + came[...].astype(F32), exclusive).astype(BF16)
+
+
+def scan_states(keep, send, size, direction, order):
+    terms = [keep, swap(send, "ctx", size, 1)]
     yield None
-    own = keep.astype(F32)
-    total = own + came.astype(F32)
-    exclusive = jnp.zeros_like(total)
+    like = shape(keep.shape, BF16)
     step = 2
     while step < size:
-        got = shifted(order.tie(total.astype(BF16)), size, direction * step).astype(F32)
+        total = call(total_kernel, "total", terms, [WHOLE] * len(terms), like, WHOLE)
+        terms.append(shifted(order.tie(total), size, direction * step))
         yield None
-        exclusive = exclusive + got
-        total = total + got
         step *= 2
-    later = odd if direction == 1 else jnp.logical_not(odd)
-    low = (exclusive + jnp.where(later, 0.0, own)).astype(BF16)
-    other = swap(order.tie(low), "ctx", size, 1)
-    mine = exclusive + jnp.where(later, came.astype(F32), 0.0)
-    yield mine.astype(BF16), other
+    kernel = functools.partial(ends_kernel, direction == 1)
+    give, mine = call(kernel, "ends", terms, [WHOLE] * len(terms), [like] * 2, [WHOLE] * 2)
+    yield mine, swap(order.tie(give), "ctx", size, 1)
 
 
 def body(n_ctx, n_head, queries, keys, values, d_layer, out_weight):
     tokens, heads, dk = queries.shape
     n = tokens // CHUNK
-    block = lax.axis_index("ctx").astype(jnp.int32)
-    place = lax.axis_index("head").astype(jnp.int32)
-    odd = (block & 1) == 1
-    half = (block & 1).astype(jnp.int32)
-
     near = n_head // 2
     far = 1
     groups = [(n // 2, n - n // 2)] + [(c, 1) for c in reversed(range(n // 2))]
@@ -428,26 +440,21 @@
     across = {c: swap(piece, "head", n_head, near) for (c, _), piece in zip(groups, pieces)}
     beside = swap(d_layer, "head", n_head, far)
 
-    position = block * tokens + jnp.arange(tokens, dtype=jnp.int32)
-    scale = lax.rsqrt((dk * (position + 1)).astype(F32))
-    scale = jnp.broadcast_to(scale[:, None], (tokens, dk))
-    index = jnp.stack([place ^ near, place ^ near ^ far, half])
-
     flat = (tokens * heads, dk)
-    q, k, v, qt, vt, before, keep, send, order.token = prepare(
-        half[None], queries.reshape(flat), keys.reshape(flat), values.reshape(flat), order.token, tokens, heads, dk
-    )
-    forward = scan_states(keep, send, n_ctx, odd, 1, order)
+    q, k, v, qt, vt, before, scale, keep, send, order.token = prepare(
+        queries.reshape(flat), keys.reshape(flat), values.reshape(flat), order.token, tokens, heads, dk
+    )
+    forward = scan_states(keep, send, n_ctx, 1, order)
     next(forward)
     starts = [c * CHUNK for c, _ in groups]
-    part, order.token = early(jnp.stack([place, place ^ far]), pieces, starts, beside, out_weight, order.token)
+    part, order.token = early(pieces, starts, beside, out_weight, order.token)
 
     prefix = state = None
     d, after, dq, dkp, dvp = {}, {}, {}, {}, {}
 
     def inner(c):
         dq[c], dkp[c], dvp[c], order.token = within(
-            c, index, q, k, v, qt, vt, *d[c], scale, before, *prefix, order.token, after[c], dict(dq) if c == 0 else {}, heads, dk
+            c, q, k, v, qt, vt, *d[c], scale, before, *prefix, order.token, after[c], dict(dq) if c == 0 else {}, heads, dk
         )
 
     def outer(c, m):
@@ -459,7 +466,7 @@
             prefix = next(forward)
         while prefix is None and state is not None:
             prefix = next(forward)
-        out = late(c * CHUNK, c == 0, index, piece, both, out_weight, part, scale, qt, order.token, state, heads, dk)
+        out = late(c * CHUNK, c == 0, near, piece, both, out_weight, part, scale, qt, order.token, state, heads, dk)
         order.token = out[-1]
         if c == 0:
             keep, send = out[1:3]
@@ -479,7 +486,7 @@
         elif c != 0:
             while len(waiting) > 1:
                 inner(waiting.pop(0))
-    backward = scan_states(keep, send, n_ctx, odd, -1, order)
+    backward = scan_states(keep, send, n_ctx, -1, order)
     next(backward)
     suffix = None
     while suffix is None:
@@ -489,7 +496,7 @@
     while waiting:
         inner(waiting.pop(0))
     d_keys, d_values = finish(
-        index, k, v, [dkp[c] for c in range(n)], [dvp[c] for c in range(n)], *suffix, order.token, heads, dk
+        k, v, [dkp[c] for c in range(n)], [dvp[c] for c in range(n)], *suffix, order.token, heads, dk
     )
     return tuple(a.reshape(tokens, heads, dk) for a in (dq[0], d_keys, d_values))
 

time: 147 us -> 106 us (0.72); the launches traced: 145 us -> 106 us
  local copies, waits for them, and re-layouts: 47.8 us -> 0.01 us
  waiting for transfers between devices: 22.3 us -> 43 us
  Pallas kernels: 47.7 us -> 38.5 us
  other arithmetic: 3.78 us -> 0 us
    unnamed x118 -> x2, local copies, waits for them, and re-layouts: 47.6 us -> 0.01 us
    ppermute x11, waiting for transfers between devices: 14.8 us -> 27.1 us  [swap(): return lax.ppermute(array, axis, [(i, i ^ bit) for i in range(size)])]
    pallas_call x11 -> x17, Pallas kernels: 47.7 us -> 38.5 us  [call(): pl.pallas_call(kernel, in_specs=in_specs, out_specs=out_specs, out_shape=...]
    ppermute x4, waiting for transfers between devices: 7.51 us -> 15.8 us  [shifted(): lax.ppermute(array, 'ctx', [(i, i + step) for i in range(size) if 0 <= i...]
    convert_element_type x6 -> x0, other arithmetic: 3.62 us -> none  [the longest x2 2.14 us: scan_states(): low = (exclusive + jnp.where(later, 0.0, own)).astype(BF16)]
    ppermute x11, starting transfers between devices: 9.93 us -> 11.9 us  [swap(): return lax.ppermute(array, axis, [(i, i ^ bit) for i in range(size)])]
  transfers between devices with their start and end apart: 15 -> 15, of which waited for: 7 -> 10; matrix products, arithmetic and copies ran while one was open for 2% -> 0% of each run, Pallas kernels for 27% -> 29%
where the time goes in v5:
time: 106 us
  waiting for transfers between devices  43 us (41%)
  Pallas kernels  38.5 us (36%)
  starting transfers between devices  23.5 us (22%)
    pallas_call x17, Pallas kernels, call(): pl.pallas_call(kernel, in_specs=in_specs, out_specs=out_specs, out_shape=...  38.5 us
    ppermute x11, waiting for transfers between devices, swap(): return lax.ppermute(array, axis, [(i, i ^ bit) for i in range(size)])  27.1 us
    ppermute x4, waiting for transfers between devices, shifted(): lax.ppermute(array, 'ctx', [(i, i + step) for i in range(size) if 0 <= i...  15.8 us
    ppermute x11, starting transfers between devices, swap(): return lax.ppermute(array, axis, [(i, i ^ bit) for i in range(size)])  11.9 us
    ppermute x4, starting transfers between devices, shifted(): lax.ppermute(array, 'ctx', [(i, i + step) for i in range(size) if 0 <= i...  11.6 us
  transfers between devices with their start and end apart: 15, of which 10 were waited for; matrix products, arithmetic and copies ran while one was open for 0% of the time, Pallas kernels for 29%

profile of v5, /device:TPU:0, one launch (start us, length us, event | category | flops | bytes accessed | tf_op | source)
XLA Modules:
  0.0 105.9 jit_solution(8843642960905665244)
XLA Ops:
  0.6 0.5 collective-permute-start.2
  1.2 1.7 %cut.1 = (bf16[512,1024]{1,0:T(8,128)(2,1)S(1)}, bf16[256,1024]{1,0:T(8,128)(2,1)S(1)}, bf16[256,1024]{1,0:T(8,128)(2,1)S(1)}, f32[8,128]{1,0:T(8,128)S(1)}) custom-call(bf16[1024,1024]{1,0:T(8,128)(2,1)} %source.1), custom_call_target="tpu_custom_call" | custom-call | tf_op jit(solution)/shard_map/cut/pallas_call | solution.py:41
  2.8 2.6 %collective-permute-start.1 = (bf16[512,1024]{1,0:T(8,128)(2,1)S(1)}, bf16[512,1024]{1,0:T(8,128)(2,1)S(1)}, u32[]{:S(2)}, u32[]{:S(2)}) collective-permute-start(bf16[512,1024]{1,0:T(8,128)(2,1)S(1)} %get-tuple-element.76.refs_0_), channel_id=1, source_target_pairs={{0,2},{1,3},{2,0},{3,1},{4,6},{5,7},{6,4},{7,5},{8,10},{9,11},{10,... | collective-permute-start | bytes 3145736 | tf_op jit(solution)/shard_map/ppermute | solution.py:383
  5.4 5.2 %prepare.1 = (bf16[1024,1024]{1,0:T(8,128)(2,1)S(1)}, bf16[1024,1024]{1,0:T(8,128)(2,1)S(1)}, bf16[1024,1024]{1,0:T(8,128)(2,1)S(1)}, bf16[1024,1024]{1,0:T(8,12...) custom-call(bf16[8192,128]{1,0:T(8,128)(2,1)} %bitcast.6, ...), custom_call_target="tpu_custom_call" | custom-call | tf_op jit(solution)/shard_map/prepare/pallas_call | solution.py:41
  10.6 5.2 %early.1 = (f32[1024,1024]{1,0:T(8,128)S(1)}, f32[8,128]{1,0:T(8,128)S(1)}) custom-call(bf16[512,1024]{1,0:T(8,128)(2,1)S(1)} %get-tuple-element.76.refs_0_, bf16[256,1024]{1,0:T(8,128)(2,1)S(1)} %get-tuple-element.77.refs_1_, bf16[256,1024]{1,0:T(8,128)(2,1)S(1)} %get-tuple-element.75.refs_2_, bf16[1024,1024]{1,0:T(8,128)(2,1)S(1)} %collective-permute-done.2.refs_3_, ...), custom_call_target="tpu_custom_call" | custom-call | tf_op jit(solution)/shard_map/early/pallas_call | solution.py:41
  15.8 13.4 %collective-permute-done.1.a_ref = bf16[512,1024]{1,0:T(8,128)(2,1)S(1)} collective-permute-done((bf16[512,1024]{1,0:T(8,128)(2,1)S(1)}, bf16[512,1024]{1,0:T(8,128)(2,1)S(1)}, u32[]{:S(2)}, u32[]{:S(2)}) %collective-permute-start.1) | collective-permute-done | bytes 1048608 | tf_op jit(solution)/shard_map/ppermute | solution.py:383
  29.2 1.7 %collective-permute-start.7 = (bf16[256,1024]{1,0:T(8,128)(2,1)S(1)}, bf16[256,1024]{1,0:T(8,128)(2,1)S(1)}, u32[]{:S(2)}, u32[]{:S(2)}) collective-permute-start(bf16[256,1024]{1,0:T(8,128)(2,1)S(1)} %get-tuple-element.77.refs_1_), channel_id=1, source_target_pairs={{0,2},{1,3},{2,0},{3,1},{4,6},{5,7},{6,4},{7,5},{8,10},{9,11},{10,... | collective-permute-start | bytes 1572872 | tf_op jit(solution)/shard_map/ppermute | solution.py:383
  31.0 1.5 %collective-permute-start.4 = (bf16[4,128,128]{2,1,0:T(8,128)(2,1)S(1)}, bf16[4,128,128]{2,1,0:T(8,128)(2,1)S(1)}, u32[]{:S(2)}, u32[]{:S(2)}) collective-permute-start(bf16[4,128,128]{2,1,0:T(8,128)(2,1)S(1)} %get-tuple-element.84), channel_id=1, source_target_pairs={{0,4},{4,0},{8,12},{12,8},{16,20},{20,16},{24,28},{28,24},{1,5},{5... | collective-permute-start | bytes 393224 | tf_op jit(solution)/shard_map/ppermute | solution.py:383
  32.5 4.1 %collective-permute-done.4.refs_1_.came = bf16[4,128,128]{2,1,0:T(8,128)(2,1)S(1)} collective-permute-done((bf16[4,128,128]{2,1,0:T(8,128)(2,1)S(1)}, bf16[4,128,128]{2,1,0:T(8,128)(2,1)S(1)}, u32[]{:S(2)}, u32[]{:S(2)}) %collective-permute-start.4) | collective-permute-done | bytes 131104 | tf_op jit(solution)/shard_map/ppermute | solution.py:383
  36.6 3.5 %collective-permute-start.5 = (bf16[4,128,128]{2,1,0:T(8,128)(2,1)S(1)}, bf16[4,128,128]{2,1,0:T(8,128)(2,1)S(1)}, u32[]{:S(2)}, u32[]{:S(2)}) collective-permute-start(bf16[4,128,128]{2,1,0:T(8,128)(2,1)S(1)} %total.4), channel_id=1, source_target_pairs={{0,8},{4,12},{8,16},{12,20},{16,24},{20,28},{1,9},{5,13},{9,17},{1... | collective-permute-start | bytes 393224 | tf_op jit(solution)/shard_map/ppermute | solution.py:387
  40.1 2.5 %collective-permute-done.5.refs_2_.refs_0_ = bf16[4,128,128]{2,1,0:T(8,128)(2,1)S(1)} collective-permute-done((bf16[4,128,128]{2,1,0:T(8,128)(2,1)S(1)}, bf16[4,128,128]{2,1,0:T(8,128)(2,1)S(1)}, u32[]{:S(2)}, u32[]{:S(2)}) %collective-permute-start.5) | collective-permute-done | bytes 131104 | tf_op jit(solution)/shard_map/ppermute | solution.py:387
  42.7 4.8 %late.3 = (bf16[512,1024]{1,0:T(8,128)(2,1)S(1)}, f32[2,8,128,128]{3,2,1,0:T(8,128)S(1)}, f32[8,128]{1,0:T(8,128)S(1)}) custom-call(bf16[512,1024]{1,0:T(8,128)(2,1)S(1)} %collective-permute-done.1.a_ref, bf16[512,1024]{1,0:T(8,128)(2,1)S(1)} %collective-permute-done.3.b_ref, bf16[1024,4096]{1,0:T(8,128)(2,1)S(1)} %copy-done, ...), custom_call_target="tpu_custom_call" | custom-call | tf_op jit(solution)/shard_map/late/pallas_call | solution.py:41
  47.6 0.6 collective-permute-start
  48.2 5.4 %collective-permute-start.6 = (bf16[4,128,128]{2,1,0:T(8,128)(2,1)S(1)}, bf16[4,128,128]{2,1,0:T(8,128)(2,1)S(1)}, u32[]{:S(2)}, u32[]{:S(2)}) collective-permute-start(bf16[4,128,128]{2,1,0:T(8,128)(2,1)S(1)} %total.5), channel_id=1, source_target_pairs={{0,16},{4,20},{8,24},{12,28},{1,17},{5,21},{9,25},{13,29},{2,18},{... | collective-permute-start | bytes 393224 | tf_op jit(solution)/shard_map/ppermute | solution.py:387
  53.5 3.1 %collective-permute-done.6.refs_1_ = bf16[4,128,128]{2,1,0:T(8,128)(2,1)S(1)} collective-permute-done((bf16[4,128,128]{2,1,0:T(8,128)(2,1)S(1)}, bf16[4,128,128]{2,1,0:T(8,128)(2,1)S(1)}, u32[]{:S(2)}, u32[]{:S(2)}) %collective-permute-start.6) | collective-permute-done | bytes 131104 | tf_op jit(solution)/shard_map/ppermute | solution.py:387
  56.7 1.6 %collective-permute-start.8 = (bf16[4,128,128]{2,1,0:T(8,128)(2,1)S(1)}, bf16[4,128,128]{2,1,0:T(8,128)(2,1)S(1)}, u32[]{:S(2)}, u32[]{:S(2)}) collective-permute-start(bf16[4,128,128]{2,1,0:T(8,128)(2,1)S(1)} %get-tuple-element.96), channel_id=1, source_target_pairs={{0,4},{4,0},{8,12},{12,8},{16,20},{20,16},{24,28},{28,24},{1,5},{5... | collective-permute-start | bytes 393224 | tf_op jit(solution)/shard_map/ppermute | solution.py:383
  58.3 3.2 %late.4 = (bf16[256,1024]{1,0:T(8,128)(2,1)S(1)}, f32[1,8,128,128]{3,2,1,0:T(8,128)S(1)}, f32[8,128]{1,0:T(8,128)S(1)}) custom-call(bf16[256,1024]{1,0:T(8,128)(2,1)S(1)} %collective-permute-done.7.a_ref, bf16[256,1024]{1,0:T(8,128)(2,1)S(1)} %collective-permute-done.9.b_ref, bf16[1024,4096]{1,0:T(8,128)(2,1)S(1)} %copy-done, ...), custom_call_target="tpu_custom_call" | custom-call | tf_op jit(solution)/shard_map/late/pallas_call | solution.py:41
  61.8 2.3 %within.4 = (bf16[2048,128]{1,0:T(8,128)(2,1)S(1)}, bf16[256,1024]{1,0:T(8,128)(2,1)S(1)}, bf16[256,1024]{1,0:T(8,128)(2,1)S(1)}, f32[8,128]{1,0:T(8,128)S(1)}) custom-call(bf16[1024,1024]{1,0:T(8,128)(2,1)S(1)} %get-tuple-element.70.q_ref, bf16[1024,1024]{1,0:T(8,128)(2,1)S(1)} %get-tuple-element.71.k_ref, bf16[1024,1024]{1,0:T(8,128)(2,1)S(1)} %get-tuple-element.72.v_ref, ...), custom_call_target="tpu_custom_call" | custom-call | tf_op jit(solution)/shard_map/within/pallas_call | solution.py:41
  64.1 2.6 %within.5 = (bf16[2048,128]{1,0:T(8,128)(2,1)S(1)}, bf16[256,1024]{1,0:T(8,128)(2,1)S(1)}, bf16[256,1024]{1,0:T(8,128)(2,1)S(1)}, f32[8,128]{1,0:T(8,128)S(1)}) custom-call(bf16[1024,1024]{1,0:T(8,128)(2,1)S(1)} %get-tuple-element.70.q_ref, bf16[1024,1024]{1,0:T(8,128)(2,1)S(1)} %get-tuple-element.71.k_ref, bf16[1024,1024]{1,0:T(8,128)(2,1)S(1)} %get-tuple-element.72.v_ref, ...), custom_call_target="tpu_custom_call" | custom-call | tf_op jit(solution)/shard_map/within/pallas_call | solution.py:41
  66.8 1.9 %collective-permute-done.10.b_ref = bf16[256,1024]{1,0:T(8,128)(2,1)S(1)} collective-permute-done((bf16[256,1024]{1,0:T(8,128)(2,1)S(1)}, bf16[256,1024]{1,0:T(8,128)(2,1)S(1)}, u32[]{:S(2)}, u32[]{:S(2)}) %collective-permute-start.10) | collective-permute-done | bytes 524320 | tf_op jit(solution)/shard_map/ppermute | solution.py:383
  68.7 3.2 %late.5 = (bf16[256,1024]{1,0:T(8,128)(2,1)S(1)}, bf16[4,128,128]{2,1,0:T(8,128)(2,1)S(1)}, bf16[4,128,128]{2,1,0:T(8,128)(2,1)S(1)}, f32[8,128]{1,0:T(8,128)S(1)}) custom-call(bf16[256,1024]{1,0:T(8,128)(2,1)S(1)} %collective-permute-done.a_ref, bf16[256,1024]{1,0:T(8,128)(2,1)S(1)} %collective-permute-done.10.b_ref, bf16[1024,4096]{1,0:T(8,128)(2,1)S(1)} %copy-done, ...), custom_call_target="tpu_custom_call" | custom-call | tf_op jit(solution)/shard_map/late/pallas_call | solution.py:41
  71.9 1.6 %collective-permute-start.11 = (bf16[4,128,128]{2,1,0:T(8,128)(2,1)S(1)}, bf16[4,128,128]{2,1,0:T(8,128)(2,1)S(1)}, u32[]{:S(2)}, u32[]{:S(2)}) collective-permute-start(bf16[4,128,128]{2,1,0:T(8,128)(2,1)S(1)} %get-tuple-element.108), channel_id=1, source_target_pairs={{0,4},{4,0},{8,12},{12,8},{16,20},{20,16},{24,28},{28,24},{1,5},{5... | collective-permute-start | bytes 393224 | tf_op jit(solution)/shard_map/ppermute | solution.py:383
  73.5 4.0 %collective-permute-done.11.refs_1_.came = bf16[4,128,128]{2,1,0:T(8,128)(2,1)S(1)} collective-permute-done((bf16[4,128,128]{2,1,0:T(8,128)(2,1)S(1)}, bf16[4,128,128]{2,1,0:T(8,128)(2,1)S(1)}, u32[]{:S(2)}, u32[]{:S(2)}) %collective-permute-start.11) | collective-permute-done | bytes 131104 | tf_op jit(solution)/shard_map/ppermute | solution.py:383
  77.5 1.3 %collective-permute-start.12 = (bf16[4,128,128]{2,1,0:T(8,128)(2,1)S(1)}, bf16[4,128,128]{2,1,0:T(8,128)(2,1)S(1)}, u32[]{:S(2)}, u32[]{:S(2)}) collective-permute-start(bf16[4,128,128]{2,1,0:T(8,128)(2,1)S(1)} %total.6), channel_id=1, source_target_pairs={{8,0},{12,4},{16,8},{20,12},{24,16},{28,20},{9,1},{13,5},{17,9},{2... | collective-permute-start | bytes 393224 | tf_op jit(solution)/shard_map/ppermute | solution.py:387
  78.8 2.6 %within.6 = (bf16[2048,128]{1,0:T(8,128)(2,1)S(1)}, bf16[256,1024]{1,0:T(8,128)(2,1)S(1)}, bf16[256,1024]{1,0:T(8,128)(2,1)S(1)}, f32[8,128]{1,0:T(8,128)S(1)}) custom-call(bf16[1024,1024]{1,0:T(8,128)(2,1)S(1)} %get-tuple-element.70.q_ref, bf16[1024,1024]{1,0:T(8,128)(2,1)S(1)} %get-tuple-element.71.k_ref, bf16[1024,1024]{1,0:T(8,128)(2,1)S(1)} %get-tuple-element.72.v_ref, ...), custom_call_target="tpu_custom_call" | custom-call | tf_op jit(solution)/shard_map/within/pallas_call | solution.py:41
  81.4 5.7 %collective-permute-done.12.refs_2_.refs_0_ = bf16[4,128,128]{2,1,0:T(8,128)(2,1)S(1)} collective-permute-done((bf16[4,128,128]{2,1,0:T(8,128)(2,1)S(1)}, bf16[4,128,128]{2,1,0:T(8,128)(2,1)S(1)}, u32[]{:S(2)}, u32[]{:S(2)}) %collective-permute-start.12) | collective-permute-done | bytes 131104 | tf_op jit(solution)/shard_map/ppermute | solution.py:387
  87.2 1.5 %collective-permute-start.13 = (bf16[4,128,128]{2,1,0:T(8,128)(2,1)S(1)}, bf16[4,128,128]{2,1,0:T(8,128)(2,1)S(1)}, u32[]{:S(2)}, u32[]{:S(2)}) collective-permute-start(bf16[4,128,128]{2,1,0:T(8,128)(2,1)S(1)} %total.7), channel_id=1, source_target_pairs={{16,0},{20,4},{24,8},{28,12},{17,1},{21,5},{25,9},{29,13},{18,2},{... | collective-permute-start | bytes 393224 | tf_op jit(solution)/shard_map/ppermute | solution.py:387
  88.7 3.4 %within.7 = (bf16[8192,128]{1,0:T(8,128)(2,1)}, bf16[256,1024]{1,0:T(8,128)(2,1)S(1)}, bf16[256,1024]{1,0:T(8,128)(2,1)S(1)}, f32[8,128]{1,0:T(8,128)S(1)}) custom-call(bf16[1024,1024]{1,0:T(8,128)(2,1)S(1)} %get-tuple-element.70.q_ref, bf16[1024,1024]{1,0:T(8,128)(2,1)S(1)} %get-tuple-element.71.k_ref, bf16[1024,1024]{1,0:T(8,128)(2,1)S(1)} %get-tuple-element.72.v_ref, ...), custom_call_target="tpu_custom_call" | custom-call | tf_op jit(solution)/shard_map/within/pallas_call | solution.py:41
  92.1 4.5 %collective-permute-done.13.refs_1_ = bf16[4,128,128]{2,1,0:T(8,128)(2,1)S(1)} collective-permute-done((bf16[4,128,128]{2,1,0:T(8,128)(2,1)S(1)}, bf16[4,128,128]{2,1,0:T(8,128)(2,1)S(1)}, u32[]{:S(2)}, u32[]{:S(2)}) %collective-permute-start.13) | collective-permute-done | bytes 131104 | tf_op jit(solution)/shard_map/ppermute | solution.py:387
  96.7 1.6 %collective-permute-start.14 = (bf16[4,128,128]{2,1,0:T(8,128)(2,1)S(1)}, bf16[4,128,128]{2,1,0:T(8,128)(2,1)S(1)}, u32[]{:S(2)}, u32[]{:S(2)}) collective-permute-start(bf16[4,128,128]{2,1,0:T(8,128)(2,1)S(1)} %get-tuple-element.123), channel_id=1, source_target_pairs={{0,4},{4,0},{8,12},{12,8},{16,20},{20,16},{24,28},{28,24},{1,5},{5... | collective-permute-start | bytes 393224 | tf_op jit(solution)/shard_map/ppermute | solution.py:383
  98.3 3.4 %collective-permute-done.14.other_ref = bf16[4,128,128]{2,1,0:T(8,128)(2,1)S(1)} collective-permute-done((bf16[4,128,128]{2,1,0:T(8,128)(2,1)S(1)}, bf16[4,128,128]{2,1,0:T(8,128)(2,1)S(1)}, u32[]{:S(2)}, u32[]{:S(2)}) %collective-permute-start.14) | collective-permute-done | bytes 131104 | tf_op jit(solution)/shard_map/ppermute | solution.py:383
  101.7 4.1 %finish.1 = (bf16[8192,128]{1,0:T(8,128)(2,1)}, bf16[8192,128]{1,0:T(8,128)(2,1)}) custom-call(bf16[1024,1024]{1,0:T(8,128)(2,1)S(1)} %get-tuple-element.71.k_ref, bf16[1024,1024]{1,0:T(8,128)(2,1)S(1)} %get-tuple-element.72.v_ref, bf16[4,128,128]{2,1,0:T(8,128)(2,1)S(1)} %get-tuple-element.120.own_ref, ...), custom_call_target="tpu_custom_call" | custom-call | tf_op jit(solution)/shard_map/finish/pallas_call | solution.py:41
  (17 shorter events, 0.8 us)
Async XLA Ops:
  0.6 10.0 %collective-permute-start.2 = (bf16[1024,1024]{1,0:T(8,128)(2,1)}, bf16[1024,1024]{1,0:T(8,128)(2,1)S(1)}, u32[]{:S(2)}, u32[]{:S(2)}) collective-permute-start(bf16[1024,1024]{1,0:T(8,128)(2,1)} %source.1), channel_id=1, source_target_pairs={{0,1},{1,0},{2,3},{3,2},{4,5},{5,4},{6,7},{7,6},{8,9},{9,8},{10,11... | collective-permute-start | bytes 6291464 | tf_op jit(solution)/shard_map/ppermute | solution.py:383
  1.1 9.5 %copy-start = (bf16[1024,4096]{1,0:T(8,128)(2,1)S(1)}, bf16[1024,4096]{1,0:T(8,128)(2,1)}, u32[]{:S(2)}) copy-start(bf16[1024,4096]{1,0:T(8,128)(2,1)} %w_ref.5) | copy-start | bytes 25165828
  2.8 26.4 %collective-permute-start.1 = (bf16[512,1024]{1,0:T(8,128)(2,1)S(1)}, bf16[512,1024]{1,0:T(8,128)(2,1)S(1)}, u32[]{:S(2)}, u32[]{:S(2)}) collective-permute-start(bf16[512,1024]{1,0:T(8,128)(2,1)S(1)} %get-tuple-element.76.refs_0_), channel_id=1, source_target_pairs={{0,2},{1,3},{2,0},{3,1},{4,6},{5,7},{6,4},{7,5},{8,10},{9,11},{10,... | collective-permute-start | bytes 3145736 | tf_op jit(solution)/shard_map/ppermute | solution.py:383
  29.2 13.5 %collective-permute-start.3 = (bf16[512,1024]{1,0:T(8,128)(2,1)S(1)}, bf16[512,1024]{1,0:T(8,128)(2,1)S(1)}, u32[]{:S(2)}, u32[]{:S(2)}) collective-permute-start(bf16[512,1024]{1,0:T(8,128)(2,1)S(1)} %collective-permute-done.1.a_ref), channel_id=1, source_target_pairs={{0,1},{1,0},{2,3},{3,2},{4,5},{5,4},{6,7},{7,6},{8,9},{9,8},{10,11... | collective-permute-start | bytes 3145736 | tf_op jit(solution)/shard_map/ppermute | solution.py:383
  29.2 18.2 %collective-permute-start.7 = (bf16[256,1024]{1,0:T(8,128)(2,1)S(1)}, bf16[256,1024]{1,0:T(8,128)(2,1)S(1)}, u32[]{:S(2)}, u32[]{:S(2)}) collective-permute-start(bf16[256,1024]{1,0:T(8,128)(2,1)S(1)} %get-tuple-element.77.refs_1_), channel_id=1, source_target_pairs={{0,2},{1,3},{2,0},{3,1},{4,6},{5,7},{6,4},{7,5},{8,10},{9,11},{10,... | collective-permute-start | bytes 1572872 | tf_op jit(solution)/shard_map/ppermute | solution.py:383
  31.0 5.6 %collective-permute-start.4 = (bf16[4,128,128]{2,1,0:T(8,128)(2,1)S(1)}, bf16[4,128,128]{2,1,0:T(8,128)(2,1)S(1)}, u32[]{:S(2)}, u32[]{:S(2)}) collective-permute-start(bf16[4,128,128]{2,1,0:T(8,128)(2,1)S(1)} %get-tuple-element.84), channel_id=1, source_target_pairs={{0,4},{4,0},{8,12},{12,8},{16,20},{20,16},{24,28},{28,24},{1,5},{5... | collective-permute-start | bytes 393224 | tf_op jit(solution)/shard_map/ppermute | solution.py:383
  36.6 6.0 %collective-permute-start.5 = (bf16[4,128,128]{2,1,0:T(8,128)(2,1)S(1)}, bf16[4,128,128]{2,1,0:T(8,128)(2,1)S(1)}, u32[]{:S(2)}, u32[]{:S(2)}) collective-permute-start(bf16[4,128,128]{2,1,0:T(8,128)(2,1)S(1)} %total.4), channel_id=1, source_target_pairs={{0,8},{4,12},{8,16},{12,20},{16,24},{20,28},{1,9},{5,13},{9,17},{1... | collective-permute-start | bytes 393224 | tf_op jit(solution)/shard_map/ppermute | solution.py:387
  47.5 10.8 %collective-permute-start.9 = (bf16[256,1024]{1,0:T(8,128)(2,1)S(1)}, bf16[256,1024]{1,0:T(8,128)(2,1)S(1)}, u32[]{:S(2)}, u32[]{:S(2)}) collective-permute-start(bf16[256,1024]{1,0:T(8,128)(2,1)S(1)} %collective-permute-done.7.a_ref), channel_id=1, source_target_pairs={{0,1},{1,0},{2,3},{3,2},{4,5},{5,4},{6,7},{7,6},{8,9},{9,8},{10,11... | collective-permute-start | bytes 1572872 | tf_op jit(solution)/shard_map/ppermute | solution.py:383
  47.6 19.1 %collective-permute-start = (bf16[256,1024]{1,0:T(8,128)(2,1)S(1)}, bf16[256,1024]{1,0:T(8,128)(2,1)S(1)}, u32[]{:S(2)}, u32[]{:S(2)}) collective-permute-start(bf16[256,1024]{1,0:T(8,128)(2,1)S(1)} %get-tuple-element.75.refs_2_), channel_id=1, source_target_pairs={{0,2},{1,3},{2,0},{3,1},{4,6},{5,7},{6,4},{7,5},{8,10},{9,11},{10,... | collective-permute-start | bytes 1572872 | tf_op jit(solution)/shard_map/ppermute | solution.py:383
  48.2 8.5 %collective-permute-start.6 = (bf16[4,128,128]{2,1,0:T(8,128)(2,1)S(1)}, bf16[4,128,128]{2,1,0:T(8,128)(2,1)S(1)}, u32[]{:S(2)}, u32[]{:S(2)}) collective-permute-start(bf16[4,128,128]{2,1,0:T(8,128)(2,1)S(1)} %total.5), channel_id=1, source_target_pairs={{0,16},{4,20},{8,24},{12,28},{1,17},{5,21},{9,25},{13,29},{2,18},{... | collective-permute-start | bytes 393224 | tf_op jit(solution)/shard_map/ppermute | solution.py:387
  56.7 5.0 %collective-permute-start.8 = (bf16[4,128,128]{2,1,0:T(8,128)(2,1)S(1)}, bf16[4,128,128]{2,1,0:T(8,128)(2,1)S(1)}, u32[]{:S(2)}, u32[]{:S(2)}) collective-permute-start(bf16[4,128,128]{2,1,0:T(8,128)(2,1)S(1)} %get-tuple-element.96), channel_id=1, source_target_pairs={{0,4},{4,0},{8,12},{12,8},{16,20},{20,16},{24,28},{28,24},{1,5},{5... | collective-permute-start | bytes 393224 | tf_op jit(solution)/shard_map/ppermute | solution.py:383
  66.7 2.0 %collective-permute-start.10 = (bf16[256,1024]{1,0:T(8,128)(2,1)S(1)}, bf16[256,1024]{1,0:T(8,128)(2,1)S(1)}, u32[]{:S(2)}, u32[]{:S(2)}) collective-permute-start(bf16[256,1024]{1,0:T(8,128)(2,1)S(1)} %collective-permute-done.a_ref), channel_id=1, source_target_pairs={{0,1},{1,0},{2,3},{3,2},{4,5},{5,4},{6,7},{7,6},{8,9},{9,8},{10,11... | collective-permute-start | bytes 1572872 | tf_op jit(solution)/shard_map/ppermute | solution.py:383
  71.9 5.6 %collective-permute-start.11 = (bf16[4,128,128]{2,1,0:T(8,128)(2,1)S(1)}, bf16[4,128,128]{2,1,0:T(8,128)(2,1)S(1)}, u32[]{:S(2)}, u32[]{:S(2)}) collective-permute-start(bf16[4,128,128]{2,1,0:T(8,128)(2,1)S(1)} %get-tuple-element.108), channel_id=1, source_target_pairs={{0,4},{4,0},{8,12},{12,8},{16,20},{20,16},{24,28},{28,24},{1,5},{5... | collective-permute-start | bytes 393224 | tf_op jit(solution)/shard_map/ppermute | solution.py:383
  77.5 9.6 %collective-permute-start.12 = (bf16[4,128,128]{2,1,0:T(8,128)(2,1)S(1)}, bf16[4,128,128]{2,1,0:T(8,128)(2,1)S(1)}, u32[]{:S(2)}, u32[]{:S(2)}) collective-permute-start(bf16[4,128,128]{2,1,0:T(8,128)(2,1)S(1)} %total.6), channel_id=1, source_target_pairs={{8,0},{12,4},{16,8},{20,12},{24,16},{28,20},{9,1},{13,5},{17,9},{2... | collective-permute-start | bytes 393224 | tf_op jit(solution)/shard_map/ppermute | solution.py:387
  87.2 9.4 %collective-permute-start.13 = (bf16[4,128,128]{2,1,0:T(8,128)(2,1)S(1)}, bf16[4,128,128]{2,1,0:T(8,128)(2,1)S(1)}, u32[]{:S(2)}, u32[]{:S(2)}) collective-permute-start(bf16[4,128,128]{2,1,0:T(8,128)(2,1)S(1)} %total.7), channel_id=1, source_target_pairs={{16,0},{20,4},{24,8},{28,12},{17,1},{21,5},{25,9},{29,13},{18,2},{... | collective-permute-start | bytes 393224 | tf_op jit(solution)/shard_map/ppermute | solution.py:387
  96.7 5.0 %collective-permute-start.14 = (bf16[4,128,128]{2,1,0:T(8,128)(2,1)S(1)}, bf16[4,128,128]{2,1,0:T(8,128)(2,1)S(1)}, u32[]{:S(2)}, u32[]{:S(2)}) collective-permute-start(bf16[4,128,128]{2,1,0:T(8,128)(2,1)S(1)} %get-tuple-element.123), channel_id=1, source_target_pairs={{0,4},{4,0},{8,12},{12,8},{16,20},{20,16},{24,28},{28,24},{1,5},{5... | collective-permute-start | bytes 393224 | tf_op jit(solution)/shard_map/ppermute | solution.py:383

commit v6 on v5

--- a/solution.py
+++ b/solution.py
@@ -77,7 +77,7 @@
 
 
 def prepare_kernel(
-    heads, dk, q_ref, k_ref, v_ref, _, qf_ref, kf_ref, vf_ref, qt_ref, vt_ref, before_ref, scale_ref, keep_ref, send_ref, token_ref,
+    heads, dk, q_ref, k_ref, v_ref, _, qf_ref, kf_ref, vf_ref, qt_ref, vt_ref, before_ref, scale_ref, state_ref, token_ref,
     raw, wides, acc, sem
 ):
     n = qf_ref.shape[0] // CHUNK
@@ -115,10 +115,7 @@
         return 0
 
     lax.fori_loop(0, n, one_chunk, 0)
-    low, high = acc[: heads // 2].astype(BF16), acc[heads // 2 :].astype(BF16)
-    first = lax.axis_index("ctx") % 2 == 0
-    keep_ref[...] = jnp.where(first, low, high)
-    send_ref[...] = jnp.where(first, high, low)
+    state_ref[...] = acc[...].astype(BF16)
 
 
 def prepare(q, k, v, token, tokens, heads, dk):
@@ -132,9 +129,8 @@
         [shape((tokens, width), BF16)] * 3
         + [shape((width, tokens), BF16)] * 2
         + [shape((n, heads, dk, dk), F32), shape((tokens, dk), F32)]
-        + [shape((heads // 2, dk, dk), BF16)] * 2
-        + [shape(TOKEN, F32)],
-        [WHOLE] * 10,
+        + [shape((heads, dk, dk), BF16), shape(TOKEN, F32)],
+        [WHOLE] * 9,
         [
             pltpu.VMEM((3, n, CHUNK * heads, dk), BF16),
             pltpu.VMEM((3, CHUNK * heads, dk), F32),
@@ -205,20 +201,8 @@
                 if not last:
                     refs[1][c, j * PAIR + i] = states[i]
         if last:
-            keep_ref, send_ref = refs[1:]
-            place = lax.rem(j, steps // 2) * PAIR
-            mine = (j // (steps // 2)) == lax.axis_index("ctx") % 2
-
-            @pl.when(mine)
-            def _():
-                for i in range(PAIR):
-                    keep_ref[place + i] = states[i].astype(BF16)
-
-            @pl.when(jnp.logical_not(mine))
-            def _():
-                for i in range(PAIR):
-                    send_ref[place + i] = states[i].astype(BF16)
-
+            for i in range(PAIR):
+                refs[1][j * PAIR + i] = states[i].astype(BF16)
         return 0
 
     lax.fori_loop(0, steps, one_tile, 0)
@@ -234,7 +218,7 @@
         in_specs.append(WHOLE)
     out_shape = [shape((rows, width), BF16)]
     if last:
-        out_shape += [shape((heads // 2, dk, dk), BF16)] * 2
+        out_shape.append(shape((heads, dk, dk), BF16))
     else:
         out_shape.append(shape((rows // CHUNK, heads, dk, dk), F32))
     out_shape.append(shape(TOKEN, F32))
@@ -251,7 +235,7 @@
 
 def within_kernel(
     heads, dk, chunk, at, level, others,
-    q_ref, k_ref, v_ref, qt_ref, vt_ref, d_ref, scale_ref, before_ref, own_ref, other_ref, _, *refs
+    q_ref, k_ref, v_ref, qt_ref, vt_ref, d_ref, scale_ref, before_ref, prefix_ref, _, *refs
 ):
     state_ref, refs = (None, refs) if level is None else (refs[0], refs[1:])
     earlier_dq, refs = refs[: len(others)], refs[len(others) :]
@@ -272,10 +256,8 @@
     lower = s <= t
     upper = t <= s
     scale = scale_ref[rows, :]
-    half = heads // 2
 
     def some_heads(g, _):
-        mine = g * GROUP // half == lax.axis_index("ctx") % 2
         for i in range(GROUP):
             h = g * GROUP + i
             cols = part_of(h, dk)
@@ -284,8 +266,7 @@
             score_grad = jnp.where(lower, dot(grad, vt_ref[cols, rows], NN), 0.0).astype(BF16)
             score_grad_t = jnp.where(upper, dot(v, grad, NT), 0.0).astype(BF16)
             score_keys_t = jnp.where(upper, dot(k, qt_ref[cols, rows], NN), 0.0).astype(BF16)
-            place = lax.rem(h, half)
-            earlier = jnp.where(mine, own_ref[place], other_ref[place]).astype(F32) + before_ref[chunk, h]
+            earlier = prefix_ref[h].astype(F32) + before_ref[chunk, h]
             dq = scale * dot(d, earlier.astype(BF16), NN) + dot(score_grad, k, NN)
             dkey = dot(score_grad_t, q, NN)
             dval = dot(score_keys_t, grad, NN)
@@ -311,10 +292,10 @@
         dq_ref[...] = wide[...].astype(BF16)
 
 
-def within(chunk, q, k, v, qt, vt, d, at, scale, before, own, other, token, state, others, heads, dk):
+def within(chunk, q, k, v, qt, vt, d, at, scale, before, prefix, token, state, others, heads, dk):
     tokens, width = q.shape
-    args = [q, k, v, qt, vt, d, scale, before, own, other, token]
-    in_specs = [WHOLE] * 10 + [ANYWHERE]
+    args = [q, k, v, qt, vt, d, scale, before, prefix, token]
+    in_specs = [WHOLE] * 9 + [ANYWHERE]
     level = None
     if state is not None:
         level = state[1]
@@ -337,16 +318,10 @@
     )
 
 
-def finish_kernel(heads, dk, n, k_ref, v_ref, own_ref, other_ref, _, *refs):
+def finish_kernel(heads, dk, n, k_ref, v_ref, suffix_ref, _, *refs):
     dkp, dvp, (dk_ref, dv_ref, wide_k, wide_v, low_k, low_v, sem) = refs[:n], refs[n : 2 * n], refs[2 * n :]
-    half = heads // 2
-    first = lax.axis_index("ctx") % 2 == 0
-    after, turned = [], []
-    for h in range(heads):
-        own, other = own_ref[h % half], other_ref[h % half]
-        one = jnp.where(first, own, other) if h < half else jnp.where(first, other, own)
-        after.append(one)
-        turned.append(one.T)
+    after = [suffix_ref[h] for h in range(heads)]
+    turned = [one.T for one in after]
     copies = []
     for c in range(n):
         rows = slice(c * CHUNK, (c + 1) * CHUNK)
@@ -364,15 +339,15 @@
         copy.wait()
 
 
-def finish(k, v, dkp, dvp, own, other, token, heads, dk):
+def finish(k, v, dkp, dvp, suffix, token, heads, dk):
     tokens, width = k.shape
     n = tokens // CHUNK
     raw = (CHUNK * heads, dk)
     return call(
         functools.partial(finish_kernel, heads, dk, n),
         "finish",
-        [k, v, own, other, token, *dkp, *dvp],
-        [WHOLE] * 4 + [ANYWHERE] + [WHOLE] * (2 * n),
+        [k, v, suffix, token, *dkp, *dvp],
+        [WHOLE] * 3 + [ANYWHERE] + [WHOLE] * (2 * n),
         [shape((tokens * heads, dk), BF16)] * 2,
         [ANYWHERE] * 2,
         [pltpu.VMEM(raw, F32)] * 2 + [pltpu.VMEM((n, *raw), BF16)] * 2 + [pltpu.SemaphoreType.DMA((2, n))],
@@ -396,37 +371,27 @@
         return array
 
 
-def total_kernel(*refs):
-    *terms, out = refs
-    total = terms[0][...].astype(F32)
-    for term in terms[1:]:
-        total = total + term[...].astype(F32)
-    out[...] = total.astype(BF16)
-
-
-def ends_kernel(later_is_odd, own, came, *refs):
-    *got, give, mine = refs
-    exclusive = got[0][...].astype(F32)
-    for term in got[1:]:
-        exclusive = exclusive + term[...].astype(F32)
-    later = (lax.axis_index("ctx") % 2 == 1) == later_is_odd
-    give[...] = jnp.where(later, exclusive, exclusive + own[...].astype(F32)).astype(BF16)
-    mine[...] = jnp.where(later, exclusive + came[...].astype(F32), exclusive).astype(BF16)
-
-
-def scan_states(keep, send, size, direction, order):
-    terms = [keep, swap(send, "ctx", size, 1)]
+def sums_kernel(direction, states_ref, out_ref):
+    size = states_ref.shape[0]
+    order = range(size) if direction == 1 else range(size - 1, -1, -1)
+    total = jnp.zeros(states_ref.shape[1:], F32)
+    for i in order:
+        out_ref[i] = total.astype(BF16)
+        total = total + states_ref[i].astype(F32)
+
+
+def exchange(array):
+    return lax.all_to_all(array, "ctx", 0, 0, tiled=True)
+
+
+def scan_states(state, size, direction, order):
+    heads, dk, width = state.shape
+    parts = exchange(state.reshape(size, heads * dk // size, width))
     yield None
-    like = shape(keep.shape, BF16)
-    step = 2
-    while step < size:
-        total = call(total_kernel, "total", terms, [WHOLE] * len(terms), like, WHOLE)
-        terms.append(shifted(order.tie(total), size, direction * step))
-        yield None
-        step *= 2
-    kernel = functools.partial(ends_kernel, direction == 1)
-    give, mine = call(kernel, "ends", terms, [WHOLE] * len(terms), [like] * 2, [WHOLE] * 2)
-    yield mine, swap(order.tie(give), "ctx", size, 1)
+    sums = call(
+        functools.partial(sums_kernel, direction), "sums", [parts], [WHOLE], shape(parts.shape, BF16), WHOLE
+    )
+    yield exchange(order.tie(sums)).reshape(state.shape)
 
 
 def body(n_ctx, n_head, queries, keys, values, d_layer, out_weight):
@@ -441,37 +406,31 @@
     beside = swap(d_layer, "head", n_head, far)
 
     flat = (tokens * heads, dk)
-    q, k, v, qt, vt, before, scale, keep, send, order.token = prepare(
+    q, k, v, qt, vt, before, scale, key_state, order.token = prepare(
         queries.reshape(flat), keys.reshape(flat), values.reshape(flat), order.token, tokens, heads, dk
     )
-    forward = scan_states(keep, send, n_ctx, 1, order)
+    forward = scan_states(key_state, n_ctx, 1, order)
     next(forward)
     starts = [c * CHUNK for c, _ in groups]
     part, order.token = early(pieces, starts, beside, out_weight, order.token)
 
-    prefix = state = None
+    prefix = next(forward)
+    state = None
     d, after, dq, dkp, dvp = {}, {}, {}, {}, {}
 
     def inner(c):
         dq[c], dkp[c], dvp[c], order.token = within(
-            c, q, k, v, qt, vt, *d[c], scale, before, *prefix, order.token, after[c], dict(dq) if c == 0 else {}, heads, dk
+            c, q, k, v, qt, vt, *d[c], scale, before, prefix, order.token, after[c], dict(dq) if c == 0 else {}, heads, dk
         )
 
     def outer(c, m):
-        nonlocal state, keep, send, prefix
+        nonlocal state
         after[c + m - 1] = None if state is None else (state, 0)
         piece = order.tie(across[c])
         both = swap(piece, "head", n_head, far)
-        if prefix is None:
-            prefix = next(forward)
-        while prefix is None and state is not None:
-            prefix = next(forward)
         out = late(c * CHUNK, c == 0, near, piece, both, out_weight, part, scale, qt, order.token, state, heads, dk)
         order.token = out[-1]
-        if c == 0:
-            keep, send = out[1:3]
-        else:
-            state = out[1]
+        state = out[1]
         for i in range(m):
             d[c + i] = (out[0], i)
             if i < m - 1:
@@ -481,22 +440,15 @@
     for c, m in groups:
         outer(c, m)
         waiting += list(range(c, c + m))[::-1]
-        if prefix is None:
-            prefix = next(forward)
-        elif c != 0:
-            while len(waiting) > 1:
-                inner(waiting.pop(0))
-    backward = scan_states(keep, send, n_ctx, -1, order)
+        while c != 0 and waiting:
+            inner(waiting.pop(0))
+    backward = scan_states(state, n_ctx, -1, order)
     next(backward)
-    suffix = None
-    while suffix is None:
-        suffix = next(backward)
-        if waiting:
-            inner(waiting.pop(0))
     while waiting:
         inner(waiting.pop(0))
+    suffix = next(backward)
     d_keys, d_values = finish(
-        k, v, [dkp[c] for c in range(n)], [dvp[c] for c in range(n)], *suffix, order.token, heads, dk
+        k, v, [dkp[c] for c in range(n)], [dvp[c] for c in range(n)], suffix, order.token, heads, dk
     )
     return tuple(a.reshape(tokens, heads, dk) for a in (dq[0], d_keys, d_values))
 

time: 106 us -> 154 us (1.45); the launches traced: 106 us -> 152 us
  local copies, waits for them, and re-layouts: 0.01 us -> 56.2 us
  waiting for transfers between devices: 43 us -> 6.9 us
  blocking collectives: 0 us -> 29.4 us
  starting transfers between devices: 23.5 us -> 14.8 us
  Pallas kernels: 38.5 us -> 43.9 us
    unnamed x2 -> x112, local copies, waits for them, and re-layouts: 0.01 us -> 56.2 us
    all_to_all x0 -> x2, blocking collectives: none -> 29.4 us  [exchange(): return lax.all_to_all(array, 'ctx', 0, 0, tiled=True)]
    ppermute x11 -> x7, waiting for transfers between devices: 27.1 us -> 6.9 us  [swap(): return lax.ppermute(array, axis, [(i, i ^ bit) for i in range(size)])]
    ppermute x4 -> x0, waiting for transfers between devices: 15.8 us -> none  [shifted(): lax.ppermute(array, 'ctx', [(i, i + step) for i in range(size) if 0 <= i...]
    ppermute x4 -> x0, starting transfers between devices: 11.6 us -> none  [shifted(): lax.ppermute(array, 'ctx', [(i, i + step) for i in range(size) if 0 <= i...]
    all_to_all x0 -> x2, starting transfers between devices: none -> 9.64 us  [exchange(): return lax.all_to_all(array, 'ctx', 0, 0, tiled=True)]
    ppermute x11 -> x7, starting transfers between devices: 11.9 us -> 5.18 us  [swap(): return lax.ppermute(array, axis, [(i, i ^ bit) for i in range(size)])]
    pallas_call x17 -> x13, Pallas kernels: 38.5 us -> 43.9 us  [call(): pl.pallas_call(kernel, in_specs=in_specs, out_specs=out_specs, out_shape=...]
  transfers between devices with their start and end apart: 15 -> 9, of which waited for: 10 -> 3; matrix products, arithmetic and copies ran while one was open for 0% -> 0% of each run, Pallas kernels for 29% -> 24%
where the time goes in v6:
time: 154 us; the launch traced here: 152 us
  local copies, waits for them, and re-layouts  56.2 us (36%)
  Pallas kernels  43.9 us (29%)
  blocking collectives  29.4 us (19%)
  starting transfers between devices  14.8 us (10%)
  waiting for transfers between devices  6.9 us (4%)
    unnamed x112, local copies, waits for them, and re-layouts  56.2 us
    pallas_call x13, Pallas kernels, call(): pl.pallas_call(kernel, in_specs=in_specs, out_specs=out_specs, out_shape=...  43.9 us
    all_to_all x2, blocking collectives, exchange(): return lax.all_to_all(array, 'ctx', 0, 0, tiled=True)  29.4 us
    all_to_all x2, starting transfers between devices, exchange(): return lax.all_to_all(array, 'ctx', 0, 0, tiled=True)  9.64 us
    ppermute x7, waiting for transfers between devices, swap(): return lax.ppermute(array, axis, [(i, i ^ bit) for i in range(size)])  6.9 us
    ppermute x7, starting transfers between devices, swap(): return lax.ppermute(array, axis, [(i, i ^ bit) for i in range(size)])  5.18 us
  transfers between devices with their start and end apart: 9, of which 3 were waited for; matrix products, arithmetic and copies ran while one was open for 0% of the time, Pallas kernels for 24%

profile of v6, /device:TPU:0, one launch (start us, length us, event | category | flops | bytes accessed | tf_op | source)
XLA Modules:
  0.0 152.3 jit_solution(1962490477415139273)
XLA Ops:
  1.1 2.5 %cut.1 = (bf16[512,1024]{1,0:T(8,128)(2,1)S(1)}, bf16[256,1024]{1,0:T(8,128)(2,1)S(1)}, bf16[256,1024]{1,0:T(8,128)(2,1)}, f32[8,128]{1,0:T(8,128)S(1)}) custom-call(bf16[1024,1024]{1,0:T(8,128)(2,1)} %source.1), custom_call_target="tpu_custom_call" | custom-call | tf_op jit(solution)/shard_map/cut/pallas_call | solution.py:41
  3.6 2.6 %collective-permute-start.2 = (bf16[512,1024]{1,0:T(8,128)(2,1)S(1)}, bf16[512,1024]{1,0:T(8,128)(2,1)}, u32[]{:S(2)}, u32[]{:S(2)}) collective-permute-start(bf16[512,1024]{1,0:T(8,128)(2,1)S(1)} %get-tuple-element.63.refs_0_), channel_id=1, source_target_pairs={{0,2},{1,3},{2,0},{3,1},{4,6},{5,7},{6,4},{7,5},{8,10},{9,11},{10,... | collective-permute-start | bytes 3145736 | tf_op jit(solution)/shard_map/ppermute | solution.py:358
  6.2 5.2 %prepare.1 = (bf16[1024,1024]{1,0:T(8,128)(2,1)S(1)}, bf16[1024,1024]{1,0:T(8,128)(2,1)S(1)}, bf16[1024,1024]{1,0:T(8,128)(2,1)S(1)}, bf16[1024,1024]{1,0:T(8,12...) custom-call(bf16[8192,128]{1,0:T(8,128)(2,1)} %bitcast.8, ...), custom_call_target="tpu_custom_call" | custom-call | tf_op jit(solution)/shard_map/prepare/pallas_call | solution.py:41
  18.1 14.9 %all_to_all.20.states_ref = bf16[8,128,128]{2,1,0:T(8,128)(2,1)S(1)} all-to-all(bf16[8,128,128]{2,1,0:T(8,128)(2,1)S(1)} %get-tuple-element.64), channel_id=1, replica_groups=mesh['ctx'=8,'head'=4] {'ctx'}, dimensions={0} | all-to-all | bytes 524288 | tf_op jit(solution)/shard_map/all_to_all | solution.py:384
  33.8 6.2 %early.1 = (f32[1024,1024]{1,0:T(8,128)S(1)}, f32[8,128]{1,0:T(8,128)S(1)}) custom-call(bf16[512,1024]{1,0:T(8,128)(2,1)S(1)} %get-tuple-element.63.refs_0_, bf16[256,1024]{1,0:T(8,128)(2,1)S(1)} %get-tuple-element.62.refs_1_, bf16[256,1024]{1,0:T(8,128)(2,1)} %get-tuple-element.61.refs_2_, bf16[1024,1024]{1,0:T(8,128)(2,1)S(1)} %collective-permute-done.3.refs_3_, ...), custom_call_target="tpu_custom_call" | custom-call | tf_op jit(solution)/shard_map/early/pallas_call | solution.py:41
  40.0 2.0 %copy-done.11 = f32[1024,1024]{1,0:T(8,128)} copy-done((f32[1024,1024]{1,0:T(8,128)}, f32[1024,1024]{1,0:T(8,128)S(1)}, u32[]{:S(2)}) %copy-start.11) | copy-done | bytes 4194328
  42.9 3.6 %all-to-all-start.1 = ((bf16[8,128,128]{2,1,0:T(8,128)(2,1)}), bf16[8,128,128]{2,1,0:T(8,128)(2,1)S(1)}, u32[]{:S(2)}, u32[]{:S(2)}) async-start(bf16[8,128,128]{2,1,0:T(8,128)(2,1)} %sums.2), calls=%async_computation.1 | async-start | bytes 524288 | tf_op jit(solution)/shard_map/all_to_all | solution.py:384
  46.5 3.4 %copy-done.1 = bf16[1024,4096]{1,0:T(8,128)(2,1)S(1)} copy-done((bf16[1024,4096]{1,0:T(8,128)(2,1)S(1)}, bf16[1024,4096]{1,0:T(8,128)(2,1)}, u32[]{:S(2)}) %copy-start.1) | copy-done | bytes 8388632
  49.9 2.2 %copy-done.12 = f32[1024,1024]{1,0:T(8,128)S(1)} copy-done((f32[1024,1024]{1,0:T(8,128)S(1)}, f32[1024,1024]{1,0:T(8,128)}, u32[]{:S(2)}) %copy-start.12) | copy-done | bytes 4194328
  52.1 6.3 %late.3 = (bf16[512,1024]{1,0:T(8,128)(2,1)S(1)}, f32[2,8,128,128]{3,2,1,0:T(8,128)S(1)}, f32[8,128]{1,0:T(8,128)S(1)}) custom-call(bf16[512,1024]{1,0:T(8,128)(2,1)} %collective-permute-done.2.a_ref, bf16[512,1024]{1,0:T(8,128)(2,1)} %collective-permute-done.4.b_ref, bf16[1024,4096]{1,0:T(8,128)(2,1)S(1)} %copy-done.1, f32[1024,1024]{1,0:T(8,128)S(1)} %copy-done.12, ...), custom_call_target="tpu_custom_call" | custom-call | tf_op jit(solution)/shard_map/late/pallas_call | solution.py:41
  60.3 1.6 %copy-done.3 = bf16[1024,1024]{1,0:T(8,128)(2,1)S(1)} copy-done((bf16[1024,1024]{1,0:T(8,128)(2,1)S(1)}, bf16[1024,1024]{1,0:T(8,128)(2,1)}, u32[]{:S(2)}) %copy-start.3) | copy-done | bytes 2097176
  61.9 1.6 %copy-done.8 = bf16[1024,1024]{1,0:T(8,128)(2,1)S(1)} copy-done((bf16[1024,1024]{1,0:T(8,128)(2,1)S(1)}, bf16[1024,1024]{1,0:T(8,128)(2,1)}, u32[]{:S(2)}) %copy-start.8) | copy-done | bytes 2097176
  63.5 1.6 %copy-done.15 = bf16[1024,1024]{1,0:T(8,128)(2,1)S(1)} copy-done((bf16[1024,1024]{1,0:T(8,128)(2,1)S(1)}, bf16[1024,1024]{1,0:T(8,128)(2,1)}, u32[]{:S(2)}) %copy-start.15) | copy-done | bytes 2097176
  65.1 1.6 %copy-done.18 = bf16[1024,1024]{1,0:T(8,128)(2,1)S(1)} copy-done((bf16[1024,1024]{1,0:T(8,128)(2,1)S(1)}, bf16[1024,1024]{1,0:T(8,128)(2,1)}, u32[]{:S(2)}) %copy-start.18) | copy-done | bytes 2097176
  66.7 1.6 %copy-done.22 = f32[4,8,128,128]{3,2,1,0:T(8,128)S(1)} copy-done((f32[4,8,128,128]{3,2,1,0:T(8,128)S(1)}, f32[4,8,128,128]{3,2,1,0:T(8,128)}, u32[]{:S(2)}) %copy-start.22) | copy-done | bytes 2097176
  69.5 2.3 %within.4 = (bf16[2048,128]{1,0:T(8,128)(2,1)S(1)}, bf16[256,1024]{1,0:T(8,128)(2,1)S(1)}, bf16[256,1024]{1,0:T(8,128)(2,1)S(1)}, f32[8,128]{1,0:T(8,128)S(1)}) custom-call(bf16[1024,1024]{1,0:T(8,128)(2,1)S(1)} %copy-done.15, bf16[1024,1024]{1,0:T(8,128)(2,1)S(1)} %copy-done.3, bf16[1024,1024]{1,0:T(8,128)(2,1)S(1)} %copy-done.8, ...), custom_call_target="tpu_custom_call" | custom-call | tf_op jit(solution)/shard_map/within/pallas_call | solution.py:41
  72.7 2.6 %within.5 = (bf16[2048,128]{1,0:T(8,128)(2,1)S(1)}, bf16[256,1024]{1,0:T(8,128)(2,1)S(1)}, bf16[256,1024]{1,0:T(8,128)(2,1)S(1)}, f32[8,128]{1,0:T(8,128)S(1)}) custom-call(bf16[1024,1024]{1,0:T(8,128)(2,1)S(1)} %copy-done.15, bf16[1024,1024]{1,0:T(8,128)(2,1)S(1)} %copy-done.3, bf16[1024,1024]{1,0:T(8,128)(2,1)S(1)} %copy-done.8, ...), custom_call_target="tpu_custom_call" | custom-call | tf_op jit(solution)/shard_map/within/pallas_call | solution.py:41
  79.1 4.2 %late.4 = (bf16[256,1024]{1,0:T(8,128)(2,1)S(1)}, f32[1,8,128,128]{3,2,1,0:T(8,128)S(1)}, f32[8,128]{1,0:T(8,128)S(1)}) custom-call(bf16[256,1024]{1,0:T(8,128)(2,1)} %collective-permute-done.1.a_ref, bf16[256,1024]{1,0:T(8,128)(2,1)S(1)} %collective-permute-done.5.b_ref, bf16[1024,4096]{1,0:T(8,128)(2,1)S(1)} %bitcast.7, f32[1024,1024]{1,0:T(8,128)S(1)} %copy-done.13, ...), custom_call_target="tpu_custom_call" | custom-call | tf_op jit(solution)/shard_map/late/pallas_call | solution.py:41
  83.3 2.5 %within.6 = (bf16[2048,128]{1,0:T(8,128)(2,1)S(1)}, bf16[256,1024]{1,0:T(8,128)(2,1)S(1)}, bf16[256,1024]{1,0:T(8,128)(2,1)S(1)}, f32[8,128]{1,0:T(8,128)S(1)}) custom-call(bf16[1024,1024]{1,0:T(8,128)(2,1)S(1)} %copy-done.15, bf16[1024,1024]{1,0:T(8,128)(2,1)S(1)} %copy-done.4, bf16[1024,1024]{1,0:T(8,128)(2,1)S(1)} %copy-done.8, ...), custom_call_target="tpu_custom_call" | custom-call | tf_op jit(solution)/shard_map/within/pallas_call | solution.py:41
  87.5 4.0 %collective-permute-done.a_ref = bf16[256,1024]{1,0:T(8,128)(2,1)S(1)} collective-permute-done((bf16[256,1024]{1,0:T(8,128)(2,1)}, bf16[256,1024]{1,0:T(8,128)(2,1)S(1)}, u32[]{:S(2)}, u32[]{:S(2)}) %collective-permute-start) | collective-permute-done | bytes 524320 | tf_op jit(solution)/shard_map/ppermute | solution.py:358
  91.5 1.9 %collective-permute-done.6.b_ref = bf16[256,1024]{1,0:T(8,128)(2,1)S(1)} collective-permute-done((bf16[256,1024]{1,0:T(8,128)(2,1)S(1)}, bf16[256,1024]{1,0:T(8,128)(2,1)S(1)}, u32[]{:S(2)}, u32[]{:S(2)}) %collective-permute-start.6) | collective-permute-done | bytes 524320 | tf_op jit(solution)/shard_map/ppermute | solution.py:358
  93.4 3.2 %late.5 = (bf16[256,1024]{1,0:T(8,128)(2,1)S(1)}, bf16[8,128,128]{2,1,0:T(8,128)(2,1)S(1)}, f32[8,128]{1,0:T(8,128)S(1)}) custom-call(bf16[256,1024]{1,0:T(8,128)(2,1)S(1)} %collective-permute-done.a_ref, bf16[256,1024]{1,0:T(8,128)(2,1)S(1)} %collective-permute-done.6.b_ref, bf16[1024,4096]{1,0:T(8,128)(2,1)S(1)} %bitcast.7, f32[1024,1024]{1,0:T(8,128)S(1)} %copy-done.13, ...), custom_call_target="tpu_custom_call" | custom-call | tf_op jit(solution)/shard_map/late/pallas_call | solution.py:41
  98.1 6.0 %all-to-all-start.2 = ((bf16[8,128,128]{2,1,0:T(8,128)(2,1)}), bf16[8,128,128]{2,1,0:T(8,128)(2,1)}, u32[]{:S(2)}, u32[]{:S(2)}) async-start(bf16[8,128,128]{2,1,0:T(8,128)(2,1)} %copy-done.53), calls=%async_computation.2 | async-start | bytes 524288 | tf_op jit(solution)/shard_map/all_to_all | solution.py:384
  105.7 1.6 %copy-done.9 = bf16[1024,1024]{1,0:T(8,128)(2,1)S(1)} copy-done((bf16[1024,1024]{1,0:T(8,128)(2,1)S(1)}, bf16[1024,1024]{1,0:T(8,128)(2,1)}, u32[]{:S(2)}) %copy-start.9) | copy-done | bytes 2097176
  107.3 1.6 %copy-done.16 = bf16[1024,1024]{1,0:T(8,128)(2,1)S(1)} copy-done((bf16[1024,1024]{1,0:T(8,128)(2,1)S(1)}, bf16[1024,1024]{1,0:T(8,128)(2,1)}, u32[]{:S(2)}) %copy-start.16) | copy-done | bytes 2097176
  108.9 1.6 %copy-done.20 = bf16[1024,1024]{1,0:T(8,128)(2,1)S(1)} copy-done((bf16[1024,1024]{1,0:T(8,128)(2,1)S(1)}, bf16[1024,1024]{1,0:T(8,128)(2,1)}, u32[]{:S(2)}) %copy-start.20) | copy-done | bytes 2097176
  110.5 1.6 %copy-done.24 = f32[4,8,128,128]{3,2,1,0:T(8,128)S(1)} copy-done((f32[4,8,128,128]{3,2,1,0:T(8,128)S(1)}, f32[4,8,128,128]{3,2,1,0:T(8,128)}, u32[]{:S(2)}) %copy-start.24) | copy-done | bytes 2097176
  116.2 3.4 %within.7 = (bf16[8192,128]{1,0:T(8,128)(2,1)}, bf16[256,1024]{1,0:T(8,128)(2,1)S(1)}, bf16[256,1024]{1,0:T(8,128)(2,1)S(1)}, f32[8,128]{1,0:T(8,128)S(1)}) custom-call(bf16[1024,1024]{1,0:T(8,128)(2,1)S(1)} %copy-done.16, bf16[1024,1024]{1,0:T(8,128)(2,1)S(1)} %copy-done.5, bf16[1024,1024]{1,0:T(8,128)(2,1)S(1)} %copy-done.9, ...), custom_call_target="tpu_custom_call" | custom-call | tf_op jit(solution)/shard_map/within/pallas_call | solution.py:41
  122.2 14.4 %all_to_all.21.suffix_ref = bf16[8,128,128]{2,1,0:T(8,128)(2,1)S(1)} all-to-all(bf16[8,128,128]{2,1,0:T(8,128)(2,1)S(1)} %sums.3), channel_id=1, replica_groups=mesh['ctx'=8,'head'=4] {'ctx'}, dimensions={0} | all-to-all | bytes 524288 | tf_op jit(solution)/shard_map/all_to_all | solution.py:384
  136.7 1.6 %copy-done.6 = bf16[1024,1024]{1,0:T(8,128)(2,1)S(1)} copy-done((bf16[1024,1024]{1,0:T(8,128)(2,1)S(1)}, bf16[1024,1024]{1,0:T(8,128)(2,1)}, u32[]{:S(2)}) %copy-start.6) | copy-done | bytes 2097176
  138.3 1.6 %copy-done.10 = bf16[1024,1024]{1,0:T(8,128)(2,1)S(1)} copy-done((bf16[1024,1024]{1,0:T(8,128)(2,1)S(1)}, bf16[1024,1024]{1,0:T(8,128)(2,1)}, u32[]{:S(2)}) %copy-start.10) | copy-done | bytes 2097176
  148.2 3.9 %finish.1 = (bf16[8192,128]{1,0:T(8,128)(2,1)}, bf16[8192,128]{1,0:T(8,128)(2,1)}) custom-call(bf16[1024,1024]{1,0:T(8,128)(2,1)S(1)} %copy-done.6, bf16[1024,1024]{1,0:T(8,128)(2,1)S(1)} %copy-done.10, bf16[8,128,128]{2,1,0:T(8,128)(2,1)S(1)} %all_to_all.21.suffix_ref, f32[8,128]{1,0:T(8,128)S(1)} %get-tuple-element.96._, bf16[256,1024]{1,0:T(8,128)(2,1)S(1)} %copy-done.50, ...), custom_call_target="tpu_custom_call" | custom-call | tf_op jit(solution)/shard_map/finish/pallas_call | solution.py:41
  (114 shorter events, 36.5 us)
Async XLA Ops:
  0.6 33.1 %collective-permute-start.3 = (bf16[1024,1024]{1,0:T(8,128)(2,1)}, bf16[1024,1024]{1,0:T(8,128)(2,1)S(1)}, u32[]{:S(2)}, u32[]{:S(2)}) collective-permute-start(bf16[1024,1024]{1,0:T(8,128)(2,1)} %source.1), channel_id=1, source_target_pairs={{0,1},{1,0},{2,3},{3,2},{4,5},{5,4},{6,7},{7,6},{8,9},{9,8},{10,11... | collective-permute-start | bytes 6291464 | tf_op jit(solution)/shard_map/ppermute | solution.py:358
  1.1 32.6 %copy-start = (bf16[1024,4096]{1,0:T(8,128)(2,1)S(1)}, bf16[1024,4096]{1,0:T(8,128)(2,1)}, u32[]{:S(2)}) copy-start(bf16[1024,4096]{1,0:T(8,128)(2,1)} %w_ref.5) | copy-start | bytes 25165828
  3.6 38.3 %collective-permute-start.2 = (bf16[512,1024]{1,0:T(8,128)(2,1)S(1)}, bf16[512,1024]{1,0:T(8,128)(2,1)}, u32[]{:S(2)}, u32[]{:S(2)}) collective-permute-start(bf16[512,1024]{1,0:T(8,128)(2,1)S(1)} %get-tuple-element.63.refs_0_), channel_id=1, source_target_pairs={{0,2},{1,3},{2,0},{3,1},{4,6},{5,7},{6,4},{7,5},{8,10},{9,11},{10,... | collective-permute-start | bytes 3145736 | tf_op jit(solution)/shard_map/ppermute | solution.py:358
  40.0 2.0 %copy-start.11 = (f32[1024,1024]{1,0:T(8,128)}, f32[1024,1024]{1,0:T(8,128)S(1)}, u32[]{:S(2)}) copy-start(f32[1024,1024]{1,0:T(8,128)S(1)} %get-tuple-element.69.part_ref) | copy-start | bytes 12582916
  42.0 4.5 %collective-permute-start.4 = (bf16[512,1024]{1,0:T(8,128)(2,1)}, bf16[512,1024]{1,0:T(8,128)(2,1)}, u32[]{:S(2)}, u32[]{:S(2)}) collective-permute-start(bf16[512,1024]{1,0:T(8,128)(2,1)} %collective-permute-done.2.a_ref), channel_id=1, source_target_pairs={{0,1},{1,0},{2,3},{3,2},{4,5},{5,4},{6,7},{7,6},{8,9},{9,8},{10,11... | collective-permute-start | bytes 3145736 | tf_op jit(solution)/shard_map/ppermute | solution.py:358
  42.0 34.9 %collective-permute-start.1 = (bf16[256,1024]{1,0:T(8,128)(2,1)S(1)}, bf16[256,1024]{1,0:T(8,128)(2,1)}, u32[]{:S(2)}, u32[]{:S(2)}) collective-permute-start(bf16[256,1024]{1,0:T(8,128)(2,1)S(1)} %get-tuple-element.62.refs_1_), channel_id=1, source_target_pairs={{0,2},{1,3},{2,0},{3,1},{4,6},{5,7},{6,4},{7,5},{8,10},{9,11},{10,... | collective-permute-start | bytes 1572872 | tf_op jit(solution)/shard_map/ppermute | solution.py:358
  42.9 17.5 %all-to-all-start.1 = ((bf16[8,128,128]{2,1,0:T(8,128)(2,1)}), bf16[8,128,128]{2,1,0:T(8,128)(2,1)S(1)}, u32[]{:S(2)}, u32[]{:S(2)}) async-start(bf16[8,128,128]{2,1,0:T(8,128)(2,1)} %sums.2), calls=%async_computation.1 | async-start | bytes 524288 | tf_op jit(solution)/shard_map/all_to_all | solution.py:384
  46.5 3.4 %copy-start.1 = (bf16[1024,4096]{1,0:T(8,128)(2,1)S(1)}, bf16[1024,4096]{1,0:T(8,128)(2,1)}, u32[]{:S(2)}) copy-start(bf16[1024,4096]{1,0:T(8,128)(2,1)} %w_ref.5) | copy-start | bytes 25165828
  49.9 2.2 %copy-start.12 = (f32[1024,1024]{1,0:T(8,128)S(1)}, f32[1024,1024]{1,0:T(8,128)}, u32[]{:S(2)}) copy-start(f32[1024,1024]{1,0:T(8,128)} %copy-done.11) | copy-start | bytes 12582916
  60.3 1.6 %copy-start.3 = (bf16[1024,1024]{1,0:T(8,128)(2,1)S(1)}, bf16[1024,1024]{1,0:T(8,128)(2,1)}, u32[]{:S(2)}) copy-start(bf16[1024,1024]{1,0:T(8,128)(2,1)} %copy-done.2) | copy-start | bytes 6291460
  66.7 1.6 %copy-start.22 = (f32[4,8,128,128]{3,2,1,0:T(8,128)S(1)}, f32[4,8,128,128]{3,2,1,0:T(8,128)}, u32[]{:S(2)}) copy-start(f32[4,8,128,128]{3,2,1,0:T(8,128)} %copy-done.21) | copy-start | bytes 6291460
  69.5 3.1 %copy-start.26 = (f32[2,8,128,128]{3,2,1,0:T(8,128)S(1)}, f32[2,8,128,128]{3,2,1,0:T(8,128)}, u32[]{:S(2)}) copy-start(f32[2,8,128,128]{3,2,1,0:T(8,128)} %copy-done.25) | copy-start | bytes 3145732
  72.6 2.6 %copy-start.29 = (bf16[2048,128]{1,0:T(8,128)(2,1)}, bf16[2048,128]{1,0:T(8,128)(2,1)S(1)}, u32[]{:S(2)}) copy-start(bf16[2048,128]{1,0:T(8,128)(2,1)S(1)} %get-tuple-element.89.refs_1_) | copy-start | bytes 1572868
  72.6 2.6 %copy-start.37 = (bf16[256,1024]{1,0:T(8,128)(2,1)}, bf16[256,1024]{1,0:T(8,128)(2,1)S(1)}, u32[]{:S(2)}) copy-start(bf16[256,1024]{1,0:T(8,128)(2,1)S(1)} %get-tuple-element.100.refs_3_) | copy-start | bytes 1572868
  72.7 6.4 %slice-start = ((s8[8388608]{0:T(1024)(128)(4,1)}), s8[4194304]{0:T(1024)(128)(4,1)S(1)}, s32[]{:S(2)}) async-start(s8[8388608]{0:T(1024)(128)(4,1)} %bitcast.6), calls=%async_computation.4 | async-start | bytes 8388608
  72.7 6.4 %slice-start.1 = ((s8[8388608]{0:T(1024)(128)(4,1)}), s8[4194304]{0:T(1024)(128)(4,1)S(1)}, s32[]{:S(2)}) async-start(s8[8388608]{0:T(1024)(128)(4,1)} %bitcast.6), calls=%async_computation.5 | async-start | bytes 8388608
  72.7 6.4 %copy-start.13 = (f32[1024,1024]{1,0:T(8,128)S(1)}, f32[1024,1024]{1,0:T(8,128)}, u32[]{:S(2)}) copy-start(f32[1024,1024]{1,0:T(8,128)} %copy-done.11) | copy-start | bytes 12582916
  76.9 6.4 %copy-start.31 = (bf16[2048,128]{1,0:T(8,128)(2,1)}, bf16[2048,128]{1,0:T(8,128)(2,1)S(1)}, u32[]{:S(2)}) copy-start(bf16[2048,128]{1,0:T(8,128)(2,1)S(1)} %get-tuple-element.90.refs_2_) | copy-start | bytes 1572868
  76.9 6.4 %copy-start.4 = (bf16[1024,1024]{1,0:T(8,128)(2,1)S(1)}, bf16[1024,1024]{1,0:T(8,128)(2,1)}, u32[]{:S(2)}) copy-start(bf16[1024,1024]{1,0:T(8,128)(2,1)} %copy-done.2) | copy-start | bytes 6291460
  76.9 6.4 %copy-start.19 = (bf16[1024,1024]{1,0:T(8,128)(2,1)S(1)}, bf16[1024,1024]{1,0:T(8,128)(2,1)}, u32[]{:S(2)}) copy-start(bf16[1024,1024]{1,0:T(8,128)(2,1)} %copy-done.17) | copy-start | bytes 6291460
  76.9 6.4 %copy-start.23 = (f32[4,8,128,128]{3,2,1,0:T(8,128)S(1)}, f32[4,8,128,128]{3,2,1,0:T(8,128)}, u32[]{:S(2)}) copy-start(f32[4,8,128,128]{3,2,1,0:T(8,128)} %copy-done.21) | copy-start | bytes 6291460
  76.9 2.2 %collective-permute-start.5 = (bf16[256,1024]{1,0:T(8,128)(2,1)}, bf16[256,1024]{1,0:T(8,128)(2,1)S(1)}, u32[]{:S(2)}, u32[]{:S(2)}) collective-permute-start(bf16[256,1024]{1,0:T(8,128)(2,1)} %collective-permute-done.1.a_ref), channel_id=1, source_target_pairs={{0,1},{1,0},{2,3},{3,2},{4,5},{5,4},{6,7},{7,6},{8,9},{9,8},{10,11... | collective-permute-start | bytes 1572872 | tf_op jit(solution)/shard_map/ppermute | solution.py:358
  77.0 14.6 %collective-permute-start = (bf16[256,1024]{1,0:T(8,128)(2,1)}, bf16[256,1024]{1,0:T(8,128)(2,1)S(1)}, u32[]{:S(2)}, u32[]{:S(2)}) collective-permute-start(bf16[256,1024]{1,0:T(8,128)(2,1)} %get-tuple-element.61.refs_2_), channel_id=1, source_target_pairs={{0,2},{1,3},{2,0},{3,1},{4,6},{5,7},{6,4},{7,5},{8,10},{9,11},{10,... | collective-permute-start | bytes 1572872 | tf_op jit(solution)/shard_map/ppermute | solution.py:358
  87.5 9.1 %copy-start.33 = (bf16[2048,128]{1,0:T(8,128)(2,1)}, bf16[2048,128]{1,0:T(8,128)(2,1)S(1)}, u32[]{:S(2)}) copy-start(bf16[2048,128]{1,0:T(8,128)(2,1)S(1)} %get-tuple-element.91.refs_3_) | copy-start | bytes 1572868
  91.5 1.9 %collective-permute-start.6 = (bf16[256,1024]{1,0:T(8,128)(2,1)S(1)}, bf16[256,1024]{1,0:T(8,128)(2,1)S(1)}, u32[]{:S(2)}, u32[]{:S(2)}) collective-permute-start(bf16[256,1024]{1,0:T(8,128)(2,1)S(1)} %collective-permute-done.a_ref), channel_id=1, source_target_pairs={{0,1},{1,0},{2,3},{3,2},{4,5},{5,4},{6,7},{7,6},{8,9},{9,8},{10,11... | collective-permute-start | bytes 1572872 | tf_op jit(solution)/shard_map/ppermute | solution.py:358
  98.1 23.1 %all-to-all-start.2 = ((bf16[8,128,128]{2,1,0:T(8,128)(2,1)}), bf16[8,128,128]{2,1,0:T(8,128)(2,1)}, u32[]{:S(2)}, u32[]{:S(2)}) async-start(bf16[8,128,128]{2,1,0:T(8,128)(2,1)} %copy-done.53), calls=%async_computation.2 | async-start | bytes 524288 | tf_op jit(solution)/shard_map/all_to_all | solution.py:384
  104.1 1.6 %copy-start.5 = (bf16[1024,1024]{1,0:T(8,128)(2,1)S(1)}, bf16[1024,1024]{1,0:T(8,128)(2,1)}, u32[]{:S(2)}) copy-start(bf16[1024,1024]{1,0:T(8,128)(2,1)} %copy-done.2) | copy-start | bytes 6291460
  105.7 1.6 %copy-start.9 = (bf16[1024,1024]{1,0:T(8,128)(2,1)S(1)}, bf16[1024,1024]{1,0:T(8,128)(2,1)}, u32[]{:S(2)}) copy-start(bf16[1024,1024]{1,0:T(8,128)(2,1)} %copy-done.7) | copy-start | bytes 6291460
  107.3 1.6 %copy-start.16 = (bf16[1024,1024]{1,0:T(8,128)(2,1)S(1)}, bf16[1024,1024]{1,0:T(8,128)(2,1)}, u32[]{:S(2)}) copy-start(bf16[1024,1024]{1,0:T(8,128)(2,1)} %copy-done.14) | copy-start | bytes 6291460
  108.9 1.6 %copy-start.20 = (bf16[1024,1024]{1,0:T(8,128)(2,1)S(1)}, bf16[1024,1024]{1,0:T(8,128)(2,1)}, u32[]{:S(2)}) copy-start(bf16[1024,1024]{1,0:T(8,128)(2,1)} %copy-done.17) | copy-start | bytes 6291460
  110.5 1.6 %copy-start.24 = (f32[4,8,128,128]{3,2,1,0:T(8,128)S(1)}, f32[4,8,128,128]{3,2,1,0:T(8,128)}, u32[]{:S(2)}) copy-start(f32[4,8,128,128]{3,2,1,0:T(8,128)} %copy-done.21) | copy-start | bytes 6291460
  136.7 1.6 %copy-start.6 = (bf16[1024,1024]{1,0:T(8,128)(2,1)S(1)}, bf16[1024,1024]{1,0:T(8,128)(2,1)}, u32[]{:S(2)}) copy-start(bf16[1024,1024]{1,0:T(8,128)(2,1)} %copy-done.2) | copy-start | bytes 6291460
  (33 other events, 35.9 us)

commit v7 on v5

--- a/solution.py
+++ b/solution.py
@@ -9,7 +9,6 @@
 
 CHUNK = 256
 PAIR = 2
-GROUP = 4
 F32 = jnp.float32
 BF16 = jnp.bfloat16
 TOKEN = (8, 128)
@@ -175,25 +174,30 @@
     )
 
 
-def late_kernel(last, first, start, near, dk, a_ref, b_ref, w_ref, part_ref, scale_ref, qt_ref, _, *refs):
+def late_kernel(half, first, start, near, dk, a_ref, b_ref, w_ref, part_ref, scale_ref, qt_ref, _, *refs):
     state_ref, refs = (None, refs) if first else (refs[0], refs[1:])
-    refs, token_ref, at, bt = refs[:-3], refs[-3], refs[-2], refs[-1]
-    d_ref = refs[0]
-    count, features = a_ref.shape
+    d_ref, out_ref, token_ref = refs[:3]
     tile = PAIR * dk
     token_ref[...] = jnp.zeros_like(token_ref)
-    at[...] = a_ref[...].T
-    bt[...] = b_ref[...].T
+    if half == 0:
+        at, bt = a_ref, b_ref
+    else:
+        at, bt = refs[3:]
+        at[...] = a_ref[...].T
+        bt[...] = b_ref[...].T
+    features, count = at.shape
     place = lax.axis_index("head")
     one, two = part_of(place ^ near, features), part_of(place ^ near ^ 1, features)
     steps = d_ref.shape[1] // tile
     here = slice(start, start + count)
-
-    def one_tile(j, _):
+    base = 0 if half is None else steps * (lax.axis_index("ctx") % 2 ^ half)
+
+    def one_tile(local, _):
+        j = base + local
         wide = part_of(j, tile)
         turned = dot(w_ref[wide, one], at[...], NN) + dot(w_ref[wide, two], bt[...], NN)
         low = (part_ref[here, wide] + turned.T).astype(BF16)
-        d_ref[:, wide] = low
+        d_ref[:, part_of(local, tile)] = low
         states = [None if first else state_ref[0, j * PAIR + i] for i in range(PAIR)]
         for c in reversed(range(count // CHUNK)):
             rows = slice(c * CHUNK, (c + 1) * CHUNK)
@@ -202,56 +206,46 @@
                 grad = (low[rows, i * dk : (i + 1) * dk].astype(F32) * scale_ref[there, :]).astype(BF16)
                 state = dot(qt_ref[part_of(j * PAIR + i, dk), there], grad, NN)
                 states[i] = state if states[i] is None else states[i] + state
-                if not last:
-                    refs[1][c, j * PAIR + i] = states[i]
-        if last:
-            keep_ref, send_ref = refs[1:]
-            place = lax.rem(j, steps // 2) * PAIR
-            mine = (j // (steps // 2)) == lax.axis_index("ctx") % 2
-
-            @pl.when(mine)
-            def _():
-                for i in range(PAIR):
-                    keep_ref[place + i] = states[i].astype(BF16)
-
-            @pl.when(jnp.logical_not(mine))
-            def _():
-                for i in range(PAIR):
-                    send_ref[place + i] = states[i].astype(BF16)
-
+                if half is None:
+                    out_ref[c, j * PAIR + i] = states[i]
+        if half is not None:
+            for i in range(PAIR):
+                out_ref[local * PAIR + i] = states[i].astype(BF16)
         return 0
 
     lax.fori_loop(0, steps, one_tile, 0)
 
 
-def late(start, last, near, a, b, weight, part, scale, qt, token, state, heads, dk):
-    rows, features = a.shape
+def late(start, half, near, a, b, weight, part, scale, qt, token, state, heads, dk):
+    features, rows = a.shape if half == 0 else a.shape[::-1]
     width = weight.shape[0]
     args = [a, b, weight, part, scale, qt, token]
     in_specs = [WHOLE] * 6 + [ANYWHERE]
     if state is not None:
         args.append(state)
         in_specs.append(WHOLE)
-    out_shape = [shape((rows, width), BF16)]
-    if last:
-        out_shape += [shape((heads // 2, dk, dk), BF16)] * 2
+    if half is None:
+        out_shape = [shape((rows, width), BF16), shape((rows // CHUNK, heads, dk, dk), F32), shape(TOKEN, F32)]
     else:
-        out_shape.append(shape((rows // CHUNK, heads, dk, dk), F32))
-    out_shape.append(shape(TOKEN, F32))
+        out_shape = [shape((rows, width // 2), BF16), shape((heads // 2, dk, dk), BF16), shape(TOKEN, F32)]
+    turned = [] if half == 0 else [(features, rows)] * 2
+    scratch = [pltpu.VMEM(dims, BF16) for dims in turned] if half is None else []
+    if half == 1:
+        out_shape += [shape(dims, BF16) for dims in turned]
     return call(
-        functools.partial(late_kernel, last, state is None, start, near, dk),
+        functools.partial(late_kernel, half, state is None, start, near, dk),
         "late",
         args,
         in_specs,
         out_shape,
         [WHOLE] * len(out_shape),
-        [pltpu.VMEM((features, rows), BF16)] * 2,
+        scratch,
     )
 
 
 def within_kernel(
     heads, dk, chunk, at, level, others,
-    q_ref, k_ref, v_ref, qt_ref, vt_ref, d_ref, scale_ref, before_ref, own_ref, other_ref, _, *refs
+    q_ref, k_ref, v_ref, qt_ref, vt_ref, d_ref, also_ref, scale_ref, before_ref, own_ref, other_ref, _, *refs
 ):
     state_ref, refs = (None, refs) if level is None else (refs[0], refs[1:])
     earlier_dq, refs = refs[: len(others)], refs[len(others) :]
@@ -266,7 +260,7 @@
         for copy in copies:
             copy.start()
     rows = slice(chunk * CHUNK, (chunk + 1) * CHUNK)
-    there = slice(at * CHUNK, (at + 1) * CHUNK)
+    there = None if at is None else slice(at * CHUNK, (at + 1) * CHUNK)
     t = lax.broadcasted_iota(jnp.int32, (CHUNK, CHUNK), 0)
     s = lax.broadcasted_iota(jnp.int32, (CHUNK, CHUNK), 1)
     lower = s <= t
@@ -274,18 +268,20 @@
     scale = scale_ref[rows, :]
     half = heads // 2
 
-    def some_heads(g, _):
-        mine = g * GROUP // half == lax.axis_index("ctx") % 2
-        for i in range(GROUP):
-            h = g * GROUP + i
+    for g, prefix_ref in enumerate((own_ref, other_ref)):
+        for i in range(half):
+            h = (lax.axis_index("ctx") % 2 ^ g) * half + i
             cols = part_of(h, dk)
-            q, k, v, d = q_ref[rows, cols], k_ref[rows, cols], v_ref[rows, cols], d_ref[there, cols]
+            q, k, v = q_ref[rows, cols], k_ref[rows, cols], v_ref[rows, cols]
+            if at is None:
+                d = (d_ref, also_ref)[g][:, i * dk : (i + 1) * dk]
+            else:
+                d = d_ref[there, cols]
             grad = (d.astype(F32) * scale).astype(BF16)
             score_grad = jnp.where(lower, dot(grad, vt_ref[cols, rows], NN), 0.0).astype(BF16)
             score_grad_t = jnp.where(upper, dot(v, grad, NT), 0.0).astype(BF16)
             score_keys_t = jnp.where(upper, dot(k, qt_ref[cols, rows], NN), 0.0).astype(BF16)
-            place = lax.rem(h, half)
-            earlier = jnp.where(mine, own_ref[place], other_ref[place]).astype(F32) + before_ref[chunk, h]
+            earlier = prefix_ref[i].astype(F32) + before_ref[chunk, h]
             dq = scale * dot(d, earlier.astype(BF16), NN) + dot(score_grad, k, NN)
             dkey = dot(score_grad_t, q, NN)
             dval = dot(score_keys_t, grad, NN)
@@ -296,9 +292,6 @@
             wide[pl.ds(h, CHUNK, stride=heads), :] = dq
             dk_ref[:, cols] = dkey.astype(BF16)
             dv_ref[:, cols] = dval.astype(BF16)
-        return 0
-
-    lax.fori_loop(0, heads // GROUP, some_heads, 0)
     if others:
         low_ref[...] = wide[...].astype(BF16)
         last = pltpu.make_async_copy(
@@ -311,10 +304,10 @@
         dq_ref[...] = wide[...].astype(BF16)
 
 
-def within(chunk, q, k, v, qt, vt, d, at, scale, before, own, other, token, state, others, heads, dk):
+def within(chunk, q, k, v, qt, vt, d, also, at, scale, before, own, other, token, state, others, heads, dk):
     tokens, width = q.shape
-    args = [q, k, v, qt, vt, d, scale, before, own, other, token]
-    in_specs = [WHOLE] * 10 + [ANYWHERE]
+    args = [q, k, v, qt, vt, d, also, scale, before, own, other, token]
+    in_specs = [WHOLE] * 11 + [ANYWHERE]
     level = None
     if state is not None:
         level = state[1]
@@ -434,7 +427,7 @@
     n = tokens // CHUNK
     near = n_head // 2
     far = 1
-    groups = [(n // 2, n - n // 2)] + [(c, 1) for c in reversed(range(n // 2))]
+    groups = [(1, n - 1), (0, 1)]
     order = Order()
     *pieces, order.token = cut(d_layer, groups)
     across = {c: swap(piece, "head", n_head, near) for (c, _), piece in zip(groups, pieces)}
@@ -449,52 +442,50 @@
     starts = [c * CHUNK for c, _ in groups]
     part, order.token = early(pieces, starts, beside, out_weight, order.token)
 
-    prefix = state = None
+    prefix = None
+    while prefix is None:
+        prefix = next(forward)
     d, after, dq, dkp, dvp = {}, {}, {}, {}, {}
 
     def inner(c):
+        others = dict(dq) if c == 0 else {}
         dq[c], dkp[c], dvp[c], order.token = within(
-            c, q, k, v, qt, vt, *d[c], scale, before, *prefix, order.token, after[c], dict(dq) if c == 0 else {}, heads, dk
+            c, q, k, v, qt, vt, *d[c], scale, before, *prefix, order.token, after[c], others, heads, dk
         )
 
-    def outer(c, m):
-        nonlocal state, keep, send, prefix
+    state = None
+    for c, m in groups[:-1]:
         after[c + m - 1] = None if state is None else (state, 0)
         piece = order.tie(across[c])
         both = swap(piece, "head", n_head, far)
-        if prefix is None:
-            prefix = next(forward)
-        while prefix is None and state is not None:
-            prefix = next(forward)
-        out = late(c * CHUNK, c == 0, near, piece, both, out_weight, part, scale, qt, order.token, state, heads, dk)
-        order.token = out[-1]
-        if c == 0:
-            keep, send = out[1:3]
-        else:
-            state = out[1]
+        low, state, order.token = late(
+            c * CHUNK, None, near, piece, both, out_weight, part, scale, qt, order.token, state, heads, dk
+        )
         for i in range(m):
-            d[c + i] = (out[0], i)
+            d[c + i] = (low, low, i)
             if i < m - 1:
                 after[c + i] = (state, i + 1)
-
-    waiting = []
-    for c, m in groups:
-        outer(c, m)
-        waiting += list(range(c, c + m))[::-1]
-        if prefix is None:
-            prefix = next(forward)
-        elif c != 0:
-            while len(waiting) > 1:
-                inner(waiting.pop(0))
+        for i in reversed(range(m)):
+            if c + i > 1:
+                inner(c + i)
+    after[0] = (state, 0)
+    piece = order.tie(across[0])
+    both = swap(piece, "head", n_head, far)
+    low_send, send, order.token, *turned = late(
+        0, 1, near, piece, both, out_weight, part, scale, qt, order.token, state, heads, dk
+    )
+    low_keep, keep, order.token = late(
+        0, 0, near, *turned, out_weight, part, scale, qt, order.token, state, heads, dk
+    )
+    d[0] = (low_keep, low_send, None)
     backward = scan_states(keep, send, n_ctx, -1, order)
     next(backward)
+    waiting = [1, 0]
     suffix = None
     while suffix is None:
         suffix = next(backward)
         if waiting:
             inner(waiting.pop(0))
-    while waiting:
-        inner(waiting.pop(0))
     d_keys, d_values = finish(
         k, v, [dkp[c] for c in range(n)], [dvp[c] for c in range(n)], *suffix, order.token, heads, dk
     )

time: 106 us -> 90.3 us (0.85)
  waiting for transfers between devices: 43 us -> 29 us
  Pallas kernels: 38.5 us -> 36.8 us
    ppermute x11 -> x9, waiting for transfers between devices: 27.1 us -> 16.5 us  [swap(): return lax.ppermute(array, axis, [(i, i ^ bit) for i in range(size)])]
    ppermute x4, waiting for transfers between devices: 15.8 us -> 12.5 us  [shifted(): lax.ppermute(array, 'ctx', [(i, i + step) for i in range(size) if 0 <= i...]
    pallas_call x17, Pallas kernels: 38.5 us -> 36.8 us  [call(): pl.pallas_call(kernel, in_specs=in_specs, out_specs=out_specs, out_shape=...]
    ppermute x11 -> x9, starting transfers between devices: 11.9 us -> 11.7 us  [swap(): return lax.ppermute(array, axis, [(i, i ^ bit) for i in range(size)])]
  transfers between devices with their start and end apart: 15 -> 13, of which waited for: 10 -> 10; matrix products, arithmetic and copies ran while one was open for 0% -> 0% of each run, Pallas kernels for 29% -> 34%
where the time goes in v7:
time: 90.3 us; the launch traced here: 90.1 us
  Pallas kernels  36.8 us (41%)
  waiting for transfers between devices  29 us (32%)
  starting transfers between devices  23.4 us (26%)
  between operations  0.95 us (1%)
    pallas_call x17, Pallas kernels, call(): pl.pallas_call(kernel, in_specs=in_specs, out_specs=out_specs, out_shape=...  36.8 us
    ppermute x9, waiting for transfers between devices, swap(): return lax.ppermute(array, axis, [(i, i ^ bit) for i in range(size)])  16.5 us
    ppermute x4, waiting for transfers between devices, shifted(): lax.ppermute(array, 'ctx', [(i, i + step) for i in range(size) if 0 <= i...  12.5 us
    ppermute x9, starting transfers between devices, swap(): return lax.ppermute(array, axis, [(i, i ^ bit) for i in range(size)])  11.7 us
    ppermute x4, starting transfers between devices, shifted(): lax.ppermute(array, 'ctx', [(i, i + step) for i in range(size) if 0 <= i...  11.7 us
  transfers between devices with their start and end apart: 13, of which 10 were waited for; matrix products, arithmetic and copies ran while one was open for 0% of the time, Pallas kernels for 34%

profile of v7, /device:TPU:0, one launch (start us, length us, event | category | flops | bytes accessed | tf_op | source)
XLA Modules:
  0.0 90.1 jit_solution(9386693098353326967)
XLA Ops:
  0.6 0.5 collective-permute-start.3
  1.2 1.7 %cut.1 = (bf16[768,1024]{1,0:T(8,128)(2,1)S(1)}, bf16[256,1024]{1,0:T(8,128)(2,1)S(1)}, f32[8,128]{1,0:T(8,128)S(1)}) custom-call(bf16[1024,1024]{1,0:T(8,128)(2,1)} %source.1), custom_call_target="tpu_custom_call" | custom-call | tf_op jit(solution)/shard_map/cut/pallas_call | solution.py:40
  2.8 2.6 %collective-permute-start.1 = (bf16[768,1024]{1,0:T(8,128)(2,1)S(1)}, bf16[768,1024]{1,0:T(8,128)(2,1)S(1)}, u32[]{:S(2)}, u32[]{:S(2)}) collective-permute-start(bf16[768,1024]{1,0:T(8,128)(2,1)S(1)} %get-tuple-element.74.refs_0_), channel_id=1, source_target_pairs={{0,2},{1,3},{2,0},{3,1},{4,6},{5,7},{6,4},{7,5},{8,10},{9,11},{10,... | collective-permute-start | bytes 4718600 | tf_op jit(solution)/shard_map/ppermute | solution.py:376
  5.4 5.2 %prepare.1 = (bf16[1024,1024]{1,0:T(8,128)(2,1)S(1)}, bf16[1024,1024]{1,0:T(8,128)(2,1)S(1)}, bf16[1024,1024]{1,0:T(8,128)(2,1)S(1)}, bf16[1024,1024]{1,0:T(8,12...) custom-call(bf16[8192,128]{1,0:T(8,128)(2,1)} %bitcast.6, ...), custom_call_target="tpu_custom_call" | custom-call | tf_op jit(solution)/shard_map/prepare/pallas_call | solution.py:40
  10.6 1.6 %collective-permute-start.2 = (bf16[4,128,128]{2,1,0:T(8,128)(2,1)S(1)}, bf16[4,128,128]{2,1,0:T(8,128)(2,1)S(1)}, u32[]{:S(2)}, u32[]{:S(2)}) collective-permute-start(bf16[4,128,128]{2,1,0:T(8,128)(2,1)S(1)} %get-tuple-element.76), channel_id=1, source_target_pairs={{0,4},{4,0},{8,12},{12,8},{16,20},{20,16},{24,28},{28,24},{1,5},{5... | collective-permute-start | bytes 393224 | tf_op jit(solution)/shard_map/ppermute | solution.py:376
  12.2 4.1 %collective-permute-done.2.refs_1_.came = bf16[4,128,128]{2,1,0:T(8,128)(2,1)S(1)} collective-permute-done((bf16[4,128,128]{2,1,0:T(8,128)(2,1)S(1)}, bf16[4,128,128]{2,1,0:T(8,128)(2,1)S(1)}, u32[]{:S(2)}, u32[]{:S(2)}) %collective-permute-start.2) | collective-permute-done | bytes 131104 | tf_op jit(solution)/shard_map/ppermute | solution.py:376
  16.4 5.2 %early.1 = (f32[1024,1024]{1,0:T(8,128)S(1)}, f32[8,128]{1,0:T(8,128)S(1)}) custom-call(bf16[768,1024]{1,0:T(8,128)(2,1)S(1)} %get-tuple-element.74.refs_0_, bf16[256,1024]{1,0:T(8,128)(2,1)S(1)} %get-tuple-element.73.refs_1_, bf16[1024,1024]{1,0:T(8,128)(2,1)S(1)} %collective-permute-done.3.refs_2_, bf16[1024,4096]{1,0:T(8,128)(2,1)S(1)} %copy-done, ...), custom_call_target="tpu_custom_call" | custom-call | tf_op jit(solution)/shard_map/early/pallas_call | solution.py:40
  21.6 3.5 %collective-permute-start.4 = (bf16[4,128,128]{2,1,0:T(8,128)(2,1)S(1)}, bf16[4,128,128]{2,1,0:T(8,128)(2,1)S(1)}, u32[]{:S(2)}, u32[]{:S(2)}) collective-permute-start(bf16[4,128,128]{2,1,0:T(8,128)(2,1)S(1)} %total.4), channel_id=1, source_target_pairs={{0,8},{4,12},{8,16},{12,20},{16,24},{20,28},{1,9},{5,13},{9,17},{1... | collective-permute-start | bytes 393224 | tf_op jit(solution)/shard_map/ppermute | solution.py:380
  25.1 2.5 %collective-permute-done.4.refs_2_.refs_0_ = bf16[4,128,128]{2,1,0:T(8,128)(2,1)S(1)} collective-permute-done((bf16[4,128,128]{2,1,0:T(8,128)(2,1)S(1)}, bf16[4,128,128]{2,1,0:T(8,128)(2,1)S(1)}, u32[]{:S(2)}, u32[]{:S(2)}) %collective-permute-start.4) | collective-permute-done | bytes 131104 | tf_op jit(solution)/shard_map/ppermute | solution.py:380
  27.7 5.4 %collective-permute-start.5 = (bf16[4,128,128]{2,1,0:T(8,128)(2,1)S(1)}, bf16[4,128,128]{2,1,0:T(8,128)(2,1)S(1)}, u32[]{:S(2)}, u32[]{:S(2)}) collective-permute-start(bf16[4,128,128]{2,1,0:T(8,128)(2,1)S(1)} %total.5), channel_id=1, source_target_pairs={{0,16},{4,20},{8,24},{12,28},{1,17},{5,21},{9,25},{13,29},{2,18},{... | collective-permute-start | bytes 393224 | tf_op jit(solution)/shard_map/ppermute | solution.py:380
  33.1 2.5 %collective-permute-done.5.refs_1_ = bf16[4,128,128]{2,1,0:T(8,128)(2,1)S(1)} collective-permute-done((bf16[4,128,128]{2,1,0:T(8,128)(2,1)S(1)}, bf16[4,128,128]{2,1,0:T(8,128)(2,1)S(1)}, u32[]{:S(2)}, u32[]{:S(2)}) %collective-permute-start.5) | collective-permute-done | bytes 131104 | tf_op jit(solution)/shard_map/ppermute | solution.py:380
  35.7 4.8 %collective-permute-done.1.a_ref = bf16[768,1024]{1,0:T(8,128)(2,1)S(1)} collective-permute-done((bf16[768,1024]{1,0:T(8,128)(2,1)S(1)}, bf16[768,1024]{1,0:T(8,128)(2,1)S(1)}, u32[]{:S(2)}, u32[]{:S(2)}) %collective-permute-start.1) | collective-permute-done | bytes 1572896 | tf_op jit(solution)/shard_map/ppermute | solution.py:376
  40.5 1.7 %collective-permute-start = (bf16[256,1024]{1,0:T(8,128)(2,1)S(1)}, bf16[256,1024]{1,0:T(8,128)(2,1)S(1)}, u32[]{:S(2)}, u32[]{:S(2)}) collective-permute-start(bf16[256,1024]{1,0:T(8,128)(2,1)S(1)} %get-tuple-element.73.refs_1_), channel_id=1, source_target_pairs={{0,2},{1,3},{2,0},{3,1},{4,6},{5,7},{6,4},{7,5},{8,10},{9,11},{10,... | collective-permute-start | bytes 1572872 | tf_op jit(solution)/shard_map/ppermute | solution.py:376
  42.2 1.5 %collective-permute-start.7 = (bf16[4,128,128]{2,1,0:T(8,128)(2,1)S(1)}, bf16[4,128,128]{2,1,0:T(8,128)(2,1)S(1)}, u32[]{:S(2)}, u32[]{:S(2)}) collective-permute-start(bf16[4,128,128]{2,1,0:T(8,128)(2,1)S(1)} %get-tuple-element.92), channel_id=1, source_target_pairs={{0,4},{4,0},{8,12},{12,8},{16,20},{20,16},{24,28},{28,24},{1,5},{5... | collective-permute-start | bytes 393224 | tf_op jit(solution)/shard_map/ppermute | solution.py:376
  43.9 6.8 %late.3 = (bf16[768,1024]{1,0:T(8,128)(2,1)S(1)}, f32[3,8,128,128]{3,2,1,0:T(8,128)S(1)}, f32[8,128]{1,0:T(8,128)S(1)}) custom-call(bf16[768,1024]{1,0:T(8,128)(2,1)S(1)} %collective-permute-done.1.a_ref, bf16[768,1024]{1,0:T(8,128)(2,1)S(1)} %collective-permute-done.6.b_ref, bf16[1024,4096]{1,0:T(8,128)(2,1)S(1)} %copy-done, ...), custom_call_target="tpu_custom_call" | custom-call | tf_op jit(solution)/shard_map/late/pallas_call | solution.py:40
  50.7 2.1 %within.4 = (bf16[2048,128]{1,0:T(8,128)(2,1)S(1)}, bf16[256,1024]{1,0:T(8,128)(2,1)S(1)}, bf16[256,1024]{1,0:T(8,128)(2,1)S(1)}, f32[8,128]{1,0:T(8,128)S(1)}) custom-call(bf16[1024,1024]{1,0:T(8,128)(2,1)S(1)} %get-tuple-element.68.q_ref, bf16[1024,1024]{1,0:T(8,128)(2,1)S(1)} %get-tuple-element.69.k_ref, bf16[1024,1024]{1,0:T(8,128)(2,1)S(1)} %get-tuple-element.70.v_ref, ...), custom_call_target="tpu_custom_call" | custom-call | tf_op jit(solution)/shard_map/within/pallas_call | solution.py:40
  52.8 2.3 %within.5 = (bf16[2048,128]{1,0:T(8,128)(2,1)S(1)}, bf16[256,1024]{1,0:T(8,128)(2,1)S(1)}, bf16[256,1024]{1,0:T(8,128)(2,1)S(1)}, f32[8,128]{1,0:T(8,128)S(1)}) custom-call(bf16[1024,1024]{1,0:T(8,128)(2,1)S(1)} %get-tuple-element.68.q_ref, bf16[1024,1024]{1,0:T(8,128)(2,1)S(1)} %get-tuple-element.69.k_ref, bf16[1024,1024]{1,0:T(8,128)(2,1)S(1)} %get-tuple-element.70.v_ref, ...), custom_call_target="tpu_custom_call" | custom-call | tf_op jit(solution)/shard_map/within/pallas_call | solution.py:40
  55.2 0.2 collective-permute-start.8
  55.4 1.8 %collective-permute-done.8.b_ref = bf16[256,1024]{1,0:T(8,128)(2,1)S(1)} collective-permute-done((bf16[256,1024]{1,0:T(8,128)(2,1)S(1)}, bf16[256,1024]{1,0:T(8,128)(2,1)S(1)}, u32[]{:S(2)}, u32[]{:S(2)}) %collective-permute-start.8) | collective-permute-done | bytes 524320 | tf_op jit(solution)/shard_map/ppermute | solution.py:376
  57.2 1.8 %late.4 = (bf16[256,512]{1,0:T(8,128)(2,1)S(1)}, bf16[4,128,128]{2,1,0:T(8,128)(2,1)S(1)}, f32[8,128]{1,0:T(8,128)S(1)}, bf16[1024,256]{1,0:T(8,128)(2,1)S(1)}, bf16[1024,256]{1,0:T(8,128)(2,1)S(1)}) custom-call(bf16[256,1024]{1,0:T(8,128)(2,1)S(1)} %collective-permute-done.a_ref, bf16[256,1024]{1,0:T(8,128)(2,1)S(1)} %collective-permute-done.8.b_ref, ...), custom_call_target="tpu_custom_call" | custom-call | tf_op jit(solution)/shard_map/late/pallas_call | solution.py:40
  58.9 1.8 %collective-permute-start.9 = (bf16[4,128,128]{2,1,0:T(8,128)(2,1)S(1)}, bf16[4,128,128]{2,1,0:T(8,128)(2,1)S(1)}, u32[]{:S(2)}, u32[]{:S(2)}) collective-permute-start(bf16[4,128,128]{2,1,0:T(8,128)(2,1)S(1)} %get-tuple-element.105), channel_id=1, source_target_pairs={{0,4},{4,0},{8,12},{12,8},{16,20},{20,16},{24,28},{28,24},{1,5},{5... | collective-permute-start | bytes 393224 | tf_op jit(solution)/shard_map/ppermute | solution.py:376
  60.8 1.4 %late.5 = (bf16[256,512]{1,0:T(8,128)(2,1)S(1)}, bf16[4,128,128]{2,1,0:T(8,128)(2,1)S(1)}, f32[8,128]{1,0:T(8,128)S(1)}) custom-call(bf16[1024,256]{1,0:T(8,128)(2,1)S(1)} %get-tuple-element.99.a_ref, bf16[1024,256]{1,0:T(8,128)(2,1)S(1)} %get-tuple-element.100.b_ref, bf16[1024,4096]{1,0:T(8,128)(2,1)S(1)} %copy-done, ...), custom_call_target="tpu_custom_call" | custom-call | tf_op jit(solution)/shard_map/late/pallas_call | solution.py:40
  62.2 2.4 %collective-permute-done.9.refs_1_.came = bf16[4,128,128]{2,1,0:T(8,128)(2,1)S(1)} collective-permute-done((bf16[4,128,128]{2,1,0:T(8,128)(2,1)S(1)}, bf16[4,128,128]{2,1,0:T(8,128)(2,1)S(1)}, u32[]{:S(2)}, u32[]{:S(2)}) %collective-permute-start.9) | collective-permute-done | bytes 131104 | tf_op jit(solution)/shard_map/ppermute | solution.py:376
  64.6 1.5 %collective-permute-start.10 = (bf16[4,128,128]{2,1,0:T(8,128)(2,1)S(1)}, bf16[4,128,128]{2,1,0:T(8,128)(2,1)S(1)}, u32[]{:S(2)}, u32[]{:S(2)}) collective-permute-start(bf16[4,128,128]{2,1,0:T(8,128)(2,1)S(1)} %total.6), channel_id=1, source_target_pairs={{8,0},{12,4},{16,8},{20,12},{24,16},{28,20},{9,1},{13,5},{17,9},{2... | collective-permute-start | bytes 393224 | tf_op jit(solution)/shard_map/ppermute | solution.py:380
  66.1 2.3 %within.6 = (bf16[2048,128]{1,0:T(8,128)(2,1)S(1)}, bf16[256,1024]{1,0:T(8,128)(2,1)S(1)}, bf16[256,1024]{1,0:T(8,128)(2,1)S(1)}, f32[8,128]{1,0:T(8,128)S(1)}) custom-call(bf16[1024,1024]{1,0:T(8,128)(2,1)S(1)} %get-tuple-element.68.q_ref, bf16[1024,1024]{1,0:T(8,128)(2,1)S(1)} %get-tuple-element.69.k_ref, bf16[1024,1024]{1,0:T(8,128)(2,1)S(1)} %get-tuple-element.70.v_ref, ...), custom_call_target="tpu_custom_call" | custom-call | tf_op jit(solution)/shard_map/within/pallas_call | solution.py:40
  68.4 3.1 %collective-permute-done.10.refs_2_.refs_0_ = bf16[4,128,128]{2,1,0:T(8,128)(2,1)S(1)} collective-permute-done((bf16[4,128,128]{2,1,0:T(8,128)(2,1)S(1)}, bf16[4,128,128]{2,1,0:T(8,128)(2,1)S(1)}, u32[]{:S(2)}, u32[]{:S(2)}) %collective-permute-start.10) | collective-permute-done | bytes 131104 | tf_op jit(solution)/shard_map/ppermute | solution.py:380
  71.5 1.3 %collective-permute-start.11 = (bf16[4,128,128]{2,1,0:T(8,128)(2,1)S(1)}, bf16[4,128,128]{2,1,0:T(8,128)(2,1)S(1)}, u32[]{:S(2)}, u32[]{:S(2)}) collective-permute-start(bf16[4,128,128]{2,1,0:T(8,128)(2,1)S(1)} %total.7), channel_id=1, source_target_pairs={{16,0},{20,4},{24,8},{28,12},{17,1},{21,5},{25,9},{29,13},{18,2},{... | collective-permute-start | bytes 393224 | tf_op jit(solution)/shard_map/ppermute | solution.py:380
  72.8 3.5 %within.7 = (bf16[8192,128]{1,0:T(8,128)(2,1)}, bf16[256,1024]{1,0:T(8,128)(2,1)S(1)}, bf16[256,1024]{1,0:T(8,128)(2,1)S(1)}, f32[8,128]{1,0:T(8,128)S(1)}) custom-call(bf16[1024,1024]{1,0:T(8,128)(2,1)S(1)} %get-tuple-element.68.q_ref, bf16[1024,1024]{1,0:T(8,128)(2,1)S(1)} %get-tuple-element.69.k_ref, bf16[1024,1024]{1,0:T(8,128)(2,1)S(1)} %get-tuple-element.70.v_ref, ...), custom_call_target="tpu_custom_call" | custom-call | tf_op jit(solution)/shard_map/within/pallas_call | solution.py:40
  76.3 4.5 %collective-permute-done.11.refs_1_ = bf16[4,128,128]{2,1,0:T(8,128)(2,1)S(1)} collective-permute-done((bf16[4,128,128]{2,1,0:T(8,128)(2,1)S(1)}, bf16[4,128,128]{2,1,0:T(8,128)(2,1)S(1)}, u32[]{:S(2)}, u32[]{:S(2)}) %collective-permute-start.11) | collective-permute-done | bytes 131104 | tf_op jit(solution)/shard_map/ppermute | solution.py:380
  80.8 1.7 %collective-permute-start.12 = (bf16[4,128,128]{2,1,0:T(8,128)(2,1)S(1)}, bf16[4,128,128]{2,1,0:T(8,128)(2,1)S(1)}, u32[]{:S(2)}, u32[]{:S(2)}) collective-permute-start(bf16[4,128,128]{2,1,0:T(8,128)(2,1)S(1)} %get-tuple-element.119), channel_id=1, source_target_pairs={{0,4},{4,0},{8,12},{12,8},{16,20},{20,16},{24,28},{28,24},{1,5},{5... | collective-permute-start | bytes 393224 | tf_op jit(solution)/shard_map/ppermute | solution.py:376
  82.6 3.3 %collective-permute-done.12.other_ref = bf16[4,128,128]{2,1,0:T(8,128)(2,1)S(1)} collective-permute-done((bf16[4,128,128]{2,1,0:T(8,128)(2,1)S(1)}, bf16[4,128,128]{2,1,0:T(8,128)(2,1)S(1)}, u32[]{:S(2)}, u32[]{:S(2)}) %collective-permute-start.12) | collective-permute-done | bytes 131104 | tf_op jit(solution)/shard_map/ppermute | solution.py:376
  85.8 4.1 %finish.1 = (bf16[8192,128]{1,0:T(8,128)(2,1)}, bf16[8192,128]{1,0:T(8,128)(2,1)}) custom-call(bf16[1024,1024]{1,0:T(8,128)(2,1)S(1)} %get-tuple-element.69.k_ref, bf16[1024,1024]{1,0:T(8,128)(2,1)S(1)} %get-tuple-element.70.v_ref, bf16[4,128,128]{2,1,0:T(8,128)(2,1)S(1)} %get-tuple-element.116.own_ref, ...), custom_call_target="tpu_custom_call" | custom-call | tf_op jit(solution)/shard_map/finish/pallas_call | solution.py:40
  (13 shorter events, 0.5 us)
Async XLA Ops:
  0.6 15.7 %collective-permute-start.3 = (bf16[1024,1024]{1,0:T(8,128)(2,1)}, bf16[1024,1024]{1,0:T(8,128)(2,1)S(1)}, u32[]{:S(2)}, u32[]{:S(2)}) collective-permute-start(bf16[1024,1024]{1,0:T(8,128)(2,1)} %source.1), channel_id=1, source_target_pairs={{0,1},{1,0},{2,3},{3,2},{4,5},{5,4},{6,7},{7,6},{8,9},{9,8},{10,11... | collective-permute-start | bytes 6291464 | tf_op jit(solution)/shard_map/ppermute | solution.py:376
  1.1 15.2 %copy-start = (bf16[1024,4096]{1,0:T(8,128)(2,1)S(1)}, bf16[1024,4096]{1,0:T(8,128)(2,1)}, u32[]{:S(2)}) copy-start(bf16[1024,4096]{1,0:T(8,128)(2,1)} %w_ref.5) | copy-start | bytes 25165828
  2.8 37.6 %collective-permute-start.1 = (bf16[768,1024]{1,0:T(8,128)(2,1)S(1)}, bf16[768,1024]{1,0:T(8,128)(2,1)S(1)}, u32[]{:S(2)}, u32[]{:S(2)}) collective-permute-start(bf16[768,1024]{1,0:T(8,128)(2,1)S(1)} %get-tuple-element.74.refs_0_), channel_id=1, source_target_pairs={{0,2},{1,3},{2,0},{3,1},{4,6},{5,7},{6,4},{7,5},{8,10},{9,11},{10,... | collective-permute-start | bytes 4718600 | tf_op jit(solution)/shard_map/ppermute | solution.py:376
  10.6 5.7 %collective-permute-start.2 = (bf16[4,128,128]{2,1,0:T(8,128)(2,1)S(1)}, bf16[4,128,128]{2,1,0:T(8,128)(2,1)S(1)}, u32[]{:S(2)}, u32[]{:S(2)}) collective-permute-start(bf16[4,128,128]{2,1,0:T(8,128)(2,1)S(1)} %get-tuple-element.76), channel_id=1, source_target_pairs={{0,4},{4,0},{8,12},{12,8},{16,20},{20,16},{24,28},{28,24},{1,5},{5... | collective-permute-start | bytes 393224 | tf_op jit(solution)/shard_map/ppermute | solution.py:376
  21.6 6.0 %collective-permute-start.4 = (bf16[4,128,128]{2,1,0:T(8,128)(2,1)S(1)}, bf16[4,128,128]{2,1,0:T(8,128)(2,1)S(1)}, u32[]{:S(2)}, u32[]{:S(2)}) collective-permute-start(bf16[4,128,128]{2,1,0:T(8,128)(2,1)S(1)} %total.4), channel_id=1, source_target_pairs={{0,8},{4,12},{8,16},{12,20},{16,24},{20,28},{1,9},{5,13},{9,17},{1... | collective-permute-start | bytes 393224 | tf_op jit(solution)/shard_map/ppermute | solution.py:380
  27.7 7.9 %collective-permute-start.5 = (bf16[4,128,128]{2,1,0:T(8,128)(2,1)S(1)}, bf16[4,128,128]{2,1,0:T(8,128)(2,1)S(1)}, u32[]{:S(2)}, u32[]{:S(2)}) collective-permute-start(bf16[4,128,128]{2,1,0:T(8,128)(2,1)S(1)} %total.5), channel_id=1, source_target_pairs={{0,16},{4,20},{8,24},{12,28},{1,17},{5,21},{9,25},{13,29},{2,18},{... | collective-permute-start | bytes 393224 | tf_op jit(solution)/shard_map/ppermute | solution.py:380
  40.5 3.4 %collective-permute-start.6 = (bf16[768,1024]{1,0:T(8,128)(2,1)S(1)}, bf16[768,1024]{1,0:T(8,128)(2,1)S(1)}, u32[]{:S(2)}, u32[]{:S(2)}) collective-permute-start(bf16[768,1024]{1,0:T(8,128)(2,1)S(1)} %collective-permute-done.1.a_ref), channel_id=1, source_target_pairs={{0,1},{1,0},{2,3},{3,2},{4,5},{5,4},{6,7},{7,6},{8,9},{9,8},{10,11... | collective-permute-start | bytes 4718600 | tf_op jit(solution)/shard_map/ppermute | solution.py:376
  40.5 14.7 %collective-permute-start = (bf16[256,1024]{1,0:T(8,128)(2,1)S(1)}, bf16[256,1024]{1,0:T(8,128)(2,1)S(1)}, u32[]{:S(2)}, u32[]{:S(2)}) collective-permute-start(bf16[256,1024]{1,0:T(8,128)(2,1)S(1)} %get-tuple-element.73.refs_1_), channel_id=1, source_target_pairs={{0,2},{1,3},{2,0},{3,1},{4,6},{5,7},{6,4},{7,5},{8,10},{9,11},{10,... | collective-permute-start | bytes 1572872 | tf_op jit(solution)/shard_map/ppermute | solution.py:376
  42.2 8.5 %collective-permute-start.7 = (bf16[4,128,128]{2,1,0:T(8,128)(2,1)S(1)}, bf16[4,128,128]{2,1,0:T(8,128)(2,1)S(1)}, u32[]{:S(2)}, u32[]{:S(2)}) collective-permute-start(bf16[4,128,128]{2,1,0:T(8,128)(2,1)S(1)} %get-tuple-element.92), channel_id=1, source_target_pairs={{0,4},{4,0},{8,12},{12,8},{16,20},{20,16},{24,28},{28,24},{1,5},{5... | collective-permute-start | bytes 393224 | tf_op jit(solution)/shard_map/ppermute | solution.py:376
  55.2 2.0 %collective-permute-start.8 = (bf16[256,1024]{1,0:T(8,128)(2,1)S(1)}, bf16[256,1024]{1,0:T(8,128)(2,1)S(1)}, u32[]{:S(2)}, u32[]{:S(2)}) collective-permute-start(bf16[256,1024]{1,0:T(8,128)(2,1)S(1)} %collective-permute-done.a_ref), channel_id=1, source_target_pairs={{0,1},{1,0},{2,3},{3,2},{4,5},{5,4},{6,7},{7,6},{8,9},{9,8},{10,11... | collective-permute-start | bytes 1572872 | tf_op jit(solution)/shard_map/ppermute | solution.py:376
  58.9 5.6 %collective-permute-start.9 = (bf16[4,128,128]{2,1,0:T(8,128)(2,1)S(1)}, bf16[4,128,128]{2,1,0:T(8,128)(2,1)S(1)}, u32[]{:S(2)}, u32[]{:S(2)}) collective-permute-start(bf16[4,128,128]{2,1,0:T(8,128)(2,1)S(1)} %get-tuple-element.105), channel_id=1, source_target_pairs={{0,4},{4,0},{8,12},{12,8},{16,20},{20,16},{24,28},{28,24},{1,5},{5... | collective-permute-start | bytes 393224 | tf_op jit(solution)/shard_map/ppermute | solution.py:376
  64.6 6.9 %collective-permute-start.10 = (bf16[4,128,128]{2,1,0:T(8,128)(2,1)S(1)}, bf16[4,128,128]{2,1,0:T(8,128)(2,1)S(1)}, u32[]{:S(2)}, u32[]{:S(2)}) collective-permute-start(bf16[4,128,128]{2,1,0:T(8,128)(2,1)S(1)} %total.6), channel_id=1, source_target_pairs={{8,0},{12,4},{16,8},{20,12},{24,16},{28,20},{9,1},{13,5},{17,9},{2... | collective-permute-start | bytes 393224 | tf_op jit(solution)/shard_map/ppermute | solution.py:380
  71.5 9.2 %collective-permute-start.11 = (bf16[4,128,128]{2,1,0:T(8,128)(2,1)S(1)}, bf16[4,128,128]{2,1,0:T(8,128)(2,1)S(1)}, u32[]{:S(2)}, u32[]{:S(2)}) collective-permute-start(bf16[4,128,128]{2,1,0:T(8,128)(2,1)S(1)} %total.7), channel_id=1, source_target_pairs={{16,0},{20,4},{24,8},{28,12},{17,1},{21,5},{25,9},{29,13},{18,2},{... | collective-permute-start | bytes 393224 | tf_op jit(solution)/shard_map/ppermute | solution.py:380
  80.8 5.0 %collective-permute-start.12 = (bf16[4,128,128]{2,1,0:T(8,128)(2,1)S(1)}, bf16[4,128,128]{2,1,0:T(8,128)(2,1)S(1)}, u32[]{:S(2)}, u32[]{:S(2)}) collective-permute-start(bf16[4,128,128]{2,1,0:T(8,128)(2,1)S(1)} %get-tuple-element.119), channel_id=1, source_target_pairs={{0,4},{4,0},{8,12},{12,8},{16,20},{20,16},{24,28},{28,24},{1,5},{5... | collective-permute-start | bytes 393224 | tf_op jit(solution)/shard_map/ppermute | solution.py:376

commit v8 on v7

--- a/solution.py
+++ b/solution.py
@@ -33,7 +33,7 @@
 
 
 def part_of(i, size):
-    return pl.ds(pl.multiple_of(i * size, size), size)
+    return slice(i * size, (i + 1) * size) if isinstance(i, int) else pl.ds(pl.multiple_of(i * size, size), size)
 
 
 def call(kernel, name, args, in_specs, out_shape, out_specs, scratch=()):
@@ -176,19 +176,20 @@
 
 def late_kernel(half, first, start, near, dk, a_ref, b_ref, w_ref, part_ref, scale_ref, qt_ref, _, *refs):
     state_ref, refs = (None, refs) if first else (refs[0], refs[1:])
-    d_ref, out_ref, token_ref = refs[:3]
+    d_ref, token_ref = refs[:2]
     tile = PAIR * dk
+    steps = d_ref.shape[1] // tile
+    outs, refs = (refs[2:3], refs[3:]) if half is None else (refs[2 : 2 + steps], refs[2 + steps :])
     token_ref[...] = jnp.zeros_like(token_ref)
     if half == 0:
         at, bt = a_ref, b_ref
     else:
-        at, bt = refs[3:]
+        at, bt = refs
         at[...] = a_ref[...].T
         bt[...] = b_ref[...].T
     features, count = at.shape
     place = lax.axis_index("head")
     one, two = part_of(place ^ near, features), part_of(place ^ near ^ 1, features)
-    steps = d_ref.shape[1] // tile
     here = slice(start, start + count)
     base = 0 if half is None else steps * (lax.axis_index("ctx") % 2 ^ half)
 
@@ -207,13 +208,17 @@
                 state = dot(qt_ref[part_of(j * PAIR + i, dk), there], grad, NN)
                 states[i] = state if states[i] is None else states[i] + state
                 if half is None:
-                    out_ref[c, j * PAIR + i] = states[i]
+                    outs[0][c, j * PAIR + i] = states[i]
         if half is not None:
             for i in range(PAIR):
-                out_ref[local * PAIR + i] = states[i].astype(BF16)
+                outs[local][i] = states[i].astype(BF16)
         return 0
 
-    lax.fori_loop(0, steps, one_tile, 0)
+    if half is None:
+        lax.fori_loop(0, steps, one_tile, 0)
+    else:
+        for local in range(steps):
+            one_tile(local, 0)
 
 
 def late(start, half, near, a, b, weight, part, scale, qt, token, state, heads, dk):
@@ -225,9 +230,10 @@
         args.append(state)
         in_specs.append(WHOLE)
     if half is None:
-        out_shape = [shape((rows, width), BF16), shape((rows // CHUNK, heads, dk, dk), F32), shape(TOKEN, F32)]
+        out_shape = [shape((rows, width), BF16), shape(TOKEN, F32), shape((rows // CHUNK, heads, dk, dk), F32)]
     else:
-        out_shape = [shape((rows, width // 2), BF16), shape((heads // 2, dk, dk), BF16), shape(TOKEN, F32)]
+        out_shape = [shape((rows, width // 2), BF16), shape(TOKEN, F32)]
+        out_shape += [shape((PAIR, dk, dk), BF16)] * (heads // 2 // PAIR)
     turned = [] if half == 0 else [(features, rows)] * 2
     scratch = [pltpu.VMEM(dims, BF16) for dims in turned] if half is None else []
     if half == 1:
@@ -330,24 +336,30 @@
     )
 
 
-def finish_kernel(heads, dk, n, k_ref, v_ref, own_ref, other_ref, _, *refs):
-    dkp, dvp, (dk_ref, dv_ref, wide_k, wide_v, low_k, low_v, sem) = refs[:n], refs[n : 2 * n], refs[2 * n :]
-    half = heads // 2
+def finish_kernel(heads, dk, n, parts, k_ref, v_ref, _, *refs):
+    own, other, refs = refs[:parts], refs[parts : 2 * parts], refs[2 * parts :]
+    dkp, dvp, (dk_ref, dv_ref, after, turned, wide_k, wide_v, low_k, low_v, sem) = refs[:n], refs[n : 2 * n], refs[2 * n :]
     first = lax.axis_index("ctx") % 2 == 0
-    after, turned = [], []
-    for h in range(heads):
-        own, other = own_ref[h % half], other_ref[h % half]
-        one = jnp.where(first, own, other) if h < half else jnp.where(first, other, own)
-        after.append(one)
-        turned.append(one.T)
+    after[...] = jnp.zeros_like(after)
+    turned[...] = jnp.zeros_like(turned)
+    for p in range(parts):
+        for i in range(PAIR):
+            mine, its = own[p][i], other[p][i]
+            cols = slice(i * dk, (i + 1) * dk)
+            for place, one in ((p, jnp.where(first, mine, its)), (parts + p, jnp.where(first, its, mine))):
+                after[place, cols, cols] = one
+                turned[place, cols, cols] = one.T
     copies = []
     for c in range(n):
         rows = slice(c * CHUNK, (c + 1) * CHUNK)
-        for h in range(heads):
-            cols = slice(h * dk, (h + 1) * dk)
-            mine = pl.ds(h, CHUNK, stride=heads)
-            wide_k[mine, :] = dkp[c][:, cols].astype(F32) + dot(v_ref[rows, cols], turned[h], NN)
-            wide_v[mine, :] = dvp[c][:, cols].astype(F32) + dot(k_ref[rows, cols], after[h], NN)
+        for p in range(heads // PAIR):
+            cols = slice(p * PAIR * dk, (p + 1) * PAIR * dk)
+            full_k = dkp[c][:, cols].astype(F32) + dot(v_ref[rows, cols], turned[p], NN)
+            full_v = dvp[c][:, cols].astype(F32) + dot(k_ref[rows, cols], after[p], NN)
+            for i in range(PAIR):
+                mine = pl.ds(p * PAIR + i, CHUNK, stride=heads)
+                wide_k[mine, :] = full_k[:, i * dk : (i + 1) * dk]
+                wide_v[mine, :] = full_v[:, i * dk : (i + 1) * dk]
         for i, (wide, low, out) in enumerate(((wide_k, low_k, dk_ref), (wide_v, low_v, dv_ref))):
             low[c] = wide[...].astype(BF16)
             copy = pltpu.make_async_copy(low.at[c], out.at[pl.ds(c * CHUNK * heads, CHUNK * heads)], sem.at[i, c])
@@ -362,13 +374,16 @@
     n = tokens // CHUNK
     raw = (CHUNK * heads, dk)
     return call(
-        functools.partial(finish_kernel, heads, dk, n),
+        functools.partial(finish_kernel, heads, dk, n, len(own)),
         "finish",
-        [k, v, own, other, token, *dkp, *dvp],
-        [WHOLE] * 4 + [ANYWHERE] + [WHOLE] * (2 * n),
+        [k, v, token, *own, *other, *dkp, *dvp],
+        [WHOLE] * 2 + [ANYWHERE] + [WHOLE] * (2 * len(own) + 2 * n),
         [shape((tokens * heads, dk), BF16)] * 2,
         [ANYWHERE] * 2,
-        [pltpu.VMEM(raw, F32)] * 2 + [pltpu.VMEM((n, *raw), BF16)] * 2 + [pltpu.SemaphoreType.DMA((2, n))],
+        [pltpu.VMEM((heads // PAIR, PAIR * dk, PAIR * dk), BF16)] * 2
+        + [pltpu.VMEM(raw, F32)] * 2
+        + [pltpu.VMEM((n, *raw), BF16)] * 2
+        + [pltpu.SemaphoreType.DMA((2, n))],
     )
 
 
@@ -408,18 +423,23 @@
 
 
 def scan_states(keep, send, size, direction, order):
-    terms = [keep, swap(send, "ctx", size, 1)]
+    terms = [[own, swap(away, "ctx", size, 1)] for own, away in zip(keep, send)]
     yield None
-    like = shape(keep.shape, BF16)
+    like = shape(keep[0].shape, BF16)
     step = 2
     while step < size:
-        total = call(total_kernel, "total", terms, [WHOLE] * len(terms), like, WHOLE)
-        terms.append(shifted(order.tie(total), size, direction * step))
+        for part in terms:
+            total = call(total_kernel, "total", part, [WHOLE] * len(part), like, WHOLE)
+            part.append(shifted(order.tie(total), size, direction * step))
         yield None
         step *= 2
     kernel = functools.partial(ends_kernel, direction == 1)
-    give, mine = call(kernel, "ends", terms, [WHOLE] * len(terms), [like] * 2, [WHOLE] * 2)
-    yield mine, swap(order.tie(give), "ctx", size, 1)
+    mine, other = [], []
+    for part in terms:
+        give, own = call(kernel, "ends", part, [WHOLE] * len(part), [like] * 2, [WHOLE] * 2)
+        mine.append(own)
+        other.append(swap(order.tie(give), "ctx", size, 1))
+    yield mine, other
 
 
 def body(n_ctx, n_head, queries, keys, values, d_layer, out_weight):
@@ -437,7 +457,7 @@
     q, k, v, qt, vt, before, scale, keep, send, order.token = prepare(
         queries.reshape(flat), keys.reshape(flat), values.reshape(flat), order.token, tokens, heads, dk
     )
-    forward = scan_states(keep, send, n_ctx, 1, order)
+    forward = scan_states([keep], [send], n_ctx, 1, order)
     next(forward)
     starts = [c * CHUNK for c, _ in groups]
     part, order.token = early(pieces, starts, beside, out_weight, order.token)
@@ -445,6 +465,7 @@
     prefix = None
     while prefix is None:
         prefix = next(forward)
+    prefix = [prefix[0][0], order.tie(prefix[1][0])]
     d, after, dq, dkp, dvp = {}, {}, {}, {}, {}
 
     def inner(c):
@@ -458,7 +479,7 @@
         after[c + m - 1] = None if state is None else (state, 0)
         piece = order.tie(across[c])
         both = swap(piece, "head", n_head, far)
-        low, state, order.token = late(
+        low, order.token, state = late(
             c * CHUNK, None, near, piece, both, out_weight, part, scale, qt, order.token, state, heads, dk
         )
         for i in range(m):
@@ -471,11 +492,12 @@
     after[0] = (state, 0)
     piece = order.tie(across[0])
     both = swap(piece, "head", n_head, far)
-    low_send, send, order.token, *turned = late(
+    low_send, order.token, *send = late(
         0, 1, near, piece, both, out_weight, part, scale, qt, order.token, state, heads, dk
     )
-    low_keep, keep, order.token = late(
-        0, 0, near, *turned, out_weight, part, scale, qt, order.token, state, heads, dk
+    *send, turned_a, turned_b = send
+    low_keep, order.token, *keep = late(
+        0, 0, near, turned_a, turned_b, out_weight, part, scale, qt, order.token, state, heads, dk
     )
     d[0] = (low_keep, low_send, None)
     backward = scan_states(keep, send, n_ctx, -1, order)

time: 90.3 us -> 91 us (level)
  starting transfers between devices: 23.4 us -> 26.4 us
  waiting for transfers between devices: 29 us -> 27 us
    ppermute x4 -> x6, starting transfers between devices: 11.7 us -> 14.2 us  [shifted(): lax.ppermute(array, 'ctx', [(i, i + step) for i in range(size) if 0 <= i...]
    ppermute x9 -> x11, waiting for transfers between devices: 16.5 us -> 15.2 us  [swap(): return lax.ppermute(array, axis, [(i, i ^ bit) for i in range(size)])]
    ppermute x4 -> x6, waiting for transfers between devices: 12.5 us -> 11.8 us  [shifted(): lax.ppermute(array, 'ctx', [(i, i + step) for i in range(size) if 0 <= i...]
    ppermute x9 -> x11, starting transfers between devices: 11.7 us -> 12.2 us  [swap(): return lax.ppermute(array, axis, [(i, i ^ bit) for i in range(size)])]
    pallas_call x17 -> x20, Pallas kernels: 36.8 us -> 36.4 us  [call(): pl.pallas_call(kernel, in_specs=in_specs, out_specs=out_specs, out_shape=...]
  transfers between devices with their start and end apart: 13 -> 17, of which waited for: 10 -> 12; matrix products, arithmetic and copies ran while one was open for 0% -> 0% of each run, Pallas kernels for 34% -> 34%
where the time goes in v8:
time: 91 us; the launch traced here: 90.8 us
  Pallas kernels  36.4 us (40%)
  waiting for transfers between devices  27 us (30%)
  starting transfers between devices  26.4 us (29%)
  between operations  0.99 us (1%)
    pallas_call x20, Pallas kernels, call(): pl.pallas_call(kernel, in_specs=in_specs, out_specs=out_specs, out_shape=...  36.4 us
    ppermute x11, waiting for transfers between devices, swap(): return lax.ppermute(array, axis, [(i, i ^ bit) for i in range(size)])  15.2 us
    ppermute x6, starting transfers between devices, shifted(): lax.ppermute(array, 'ctx', [(i, i + step) for i in range(size) if 0 <= i...  14.2 us
    ppermute x11, starting transfers between devices, swap(): return lax.ppermute(array, axis, [(i, i ^ bit) for i in range(size)])  12.2 us
    ppermute x6, waiting for transfers between devices, shifted(): lax.ppermute(array, 'ctx', [(i, i + step) for i in range(size) if 0 <= i...  11.8 us
  transfers between devices with their start and end apart: 17, of which 12 were waited for; matrix products, arithmetic and copies ran while one was open for 0% of the time, Pallas kernels for 34%

profile of v8, /device:TPU:0, one launch (start us, length us, event | category | flops | bytes accessed | tf_op | source)
XLA Modules:
  0.0 90.8 jit_solution(6912616302051749133)
XLA Ops:
  1.2 1.7 %cut.1 = (bf16[768,1024]{1,0:T(8,128)(2,1)S(1)}, bf16[256,1024]{1,0:T(8,128)(2,1)S(1)}, f32[8,128]{1,0:T(8,128)S(1)}) custom-call(bf16[1024,1024]{1,0:T(8,128)(2,1)} %source.1), custom_call_target="tpu_custom_call" | custom-call | tf_op jit(solution)/shard_map/cut/pallas_call | solution.py:40
  2.8 2.6 %collective-permute-start.1 = (bf16[768,1024]{1,0:T(8,128)(2,1)S(1)}, bf16[768,1024]{1,0:T(8,128)(2,1)S(1)}, u32[]{:S(2)}, u32[]{:S(2)}) collective-permute-start(bf16[768,1024]{1,0:T(8,128)(2,1)S(1)} %get-tuple-element.86.refs_0_), channel_id=1, source_target_pairs={{0,2},{1,3},{2,0},{3,1},{4,6},{5,7},{6,4},{7,5},{8,10},{9,11},{10,... | collective-permute-start | bytes 4718600 | tf_op jit(solution)/shard_map/ppermute | solution.py:391
  5.4 5.2 %prepare.1 = (bf16[1024,1024]{1,0:T(8,128)(2,1)S(1)}, bf16[1024,1024]{1,0:T(8,128)(2,1)S(1)}, bf16[1024,1024]{1,0:T(8,128)(2,1)S(1)}, bf16[1024,1024]{1,0:T(8,12...) custom-call(bf16[8192,128]{1,0:T(8,128)(2,1)} %bitcast.6, ...), custom_call_target="tpu_custom_call" | custom-call | tf_op jit(solution)/shard_map/prepare/pallas_call | solution.py:40
  10.6 1.6 %collective-permute-start.2 = (bf16[4,128,128]{2,1,0:T(8,128)(2,1)S(1)}, bf16[4,128,128]{2,1,0:T(8,128)(2,1)S(1)}, u32[]{:S(2)}, u32[]{:S(2)}) collective-permute-start(bf16[4,128,128]{2,1,0:T(8,128)(2,1)S(1)} %get-tuple-element.88), channel_id=1, source_target_pairs={{0,4},{4,0},{8,12},{12,8},{16,20},{20,16},{24,28},{28,24},{1,5},{5... | collective-permute-start | bytes 393224 | tf_op jit(solution)/shard_map/ppermute | solution.py:391
  12.2 4.1 %collective-permute-done.2.refs_1_.came = bf16[4,128,128]{2,1,0:T(8,128)(2,1)S(1)} collective-permute-done((bf16[4,128,128]{2,1,0:T(8,128)(2,1)S(1)}, bf16[4,128,128]{2,1,0:T(8,128)(2,1)S(1)}, u32[]{:S(2)}, u32[]{:S(2)}) %collective-permute-start.2) | collective-permute-done | bytes 131104 | tf_op jit(solution)/shard_map/ppermute | solution.py:391
  16.4 5.2 %early.1 = (f32[1024,1024]{1,0:T(8,128)S(1)}, f32[8,128]{1,0:T(8,128)S(1)}) custom-call(bf16[768,1024]{1,0:T(8,128)(2,1)S(1)} %get-tuple-element.86.refs_0_, bf16[256,1024]{1,0:T(8,128)(2,1)S(1)} %get-tuple-element.85.refs_1_, bf16[1024,1024]{1,0:T(8,128)(2,1)S(1)} %collective-permute-done.3.refs_2_, bf16[1024,4096]{1,0:T(8,128)(2,1)S(1)} %copy-done, ...), custom_call_target="tpu_custom_call" | custom-call | tf_op jit(solution)/shard_map/early/pallas_call | solution.py:40
  21.6 3.5 %collective-permute-start.4 = (bf16[4,128,128]{2,1,0:T(8,128)(2,1)S(1)}, bf16[4,128,128]{2,1,0:T(8,128)(2,1)S(1)}, u32[]{:S(2)}, u32[]{:S(2)}) collective-permute-start(bf16[4,128,128]{2,1,0:T(8,128)(2,1)S(1)} %total.6), channel_id=1, source_target_pairs={{0,8},{4,12},{8,16},{12,20},{16,24},{20,28},{1,9},{5,13},{9,17},{1... | collective-permute-start | bytes 393224 | tf_op jit(solution)/shard_map/ppermute | solution.py:395
  25.1 2.5 %collective-permute-done.4.refs_2_.refs_0_ = bf16[4,128,128]{2,1,0:T(8,128)(2,1)S(1)} collective-permute-done((bf16[4,128,128]{2,1,0:T(8,128)(2,1)S(1)}, bf16[4,128,128]{2,1,0:T(8,128)(2,1)S(1)}, u32[]{:S(2)}, u32[]{:S(2)}) %collective-permute-start.4) | collective-permute-done | bytes 131104 | tf_op jit(solution)/shard_map/ppermute | solution.py:395
  27.7 5.4 %collective-permute-start.5 = (bf16[4,128,128]{2,1,0:T(8,128)(2,1)S(1)}, bf16[4,128,128]{2,1,0:T(8,128)(2,1)S(1)}, u32[]{:S(2)}, u32[]{:S(2)}) collective-permute-start(bf16[4,128,128]{2,1,0:T(8,128)(2,1)S(1)} %total.7), channel_id=1, source_target_pairs={{0,16},{4,20},{8,24},{12,28},{1,17},{5,21},{9,25},{13,29},{2,18},{... | collective-permute-start | bytes 393224 | tf_op jit(solution)/shard_map/ppermute | solution.py:395
  33.0 2.5 %collective-permute-done.5.refs_1_ = bf16[4,128,128]{2,1,0:T(8,128)(2,1)S(1)} collective-permute-done((bf16[4,128,128]{2,1,0:T(8,128)(2,1)S(1)}, bf16[4,128,128]{2,1,0:T(8,128)(2,1)S(1)}, u32[]{:S(2)}, u32[]{:S(2)}) %collective-permute-start.5) | collective-permute-done | bytes 131104 | tf_op jit(solution)/shard_map/ppermute | solution.py:395
  35.6 1.6 %collective-permute-start.6 = (bf16[4,128,128]{2,1,0:T(8,128)(2,1)S(1)}, bf16[4,128,128]{2,1,0:T(8,128)(2,1)S(1)}, u32[]{:S(2)}, u32[]{:S(2)}) collective-permute-start(bf16[4,128,128]{2,1,0:T(8,128)(2,1)S(1)} %get-tuple-element.96), channel_id=1, source_target_pairs={{0,4},{4,0},{8,12},{12,8},{16,20},{20,16},{24,28},{28,24},{1,5},{5... | collective-permute-start | bytes 393224 | tf_op jit(solution)/shard_map/ppermute | solution.py:391
  37.2 3.4 %collective-permute-done.6.other_ref = bf16[4,128,128]{2,1,0:T(8,128)(2,1)S(1)} collective-permute-done((bf16[4,128,128]{2,1,0:T(8,128)(2,1)S(1)}, bf16[4,128,128]{2,1,0:T(8,128)(2,1)S(1)}, u32[]{:S(2)}, u32[]{:S(2)}) %collective-permute-start.6) | collective-permute-done | bytes 131104 | tf_op jit(solution)/shard_map/ppermute | solution.py:391
  40.7 1.5 %collective-permute-start = (bf16[256,1024]{1,0:T(8,128)(2,1)S(1)}, bf16[256,1024]{1,0:T(8,128)(2,1)S(1)}, u32[]{:S(2)}, u32[]{:S(2)}) collective-permute-start(bf16[256,1024]{1,0:T(8,128)(2,1)S(1)} %get-tuple-element.85.refs_1_), channel_id=1, source_target_pairs={{0,2},{1,3},{2,0},{3,1},{4,6},{5,7},{6,4},{7,5},{8,10},{9,11},{10,... | collective-permute-start | bytes 1572872 | tf_op jit(solution)/shard_map/ppermute | solution.py:391
  42.2 1.9 %collective-permute-done.7.b_ref = bf16[768,1024]{1,0:T(8,128)(2,1)S(1)} collective-permute-done((bf16[768,1024]{1,0:T(8,128)(2,1)S(1)}, bf16[768,1024]{1,0:T(8,128)(2,1)S(1)}, u32[]{:S(2)}, u32[]{:S(2)}) %collective-permute-start.7) | collective-permute-done | bytes 1572896 | tf_op jit(solution)/shard_map/ppermute | solution.py:391
  44.1 6.9 %late.3 = (bf16[768,1024]{1,0:T(8,128)(2,1)S(1)}, f32[8,128]{1,0:T(8,128)S(1)}, f32[3,8,128,128]{3,2,1,0:T(8,128)S(1)}) custom-call(bf16[768,1024]{1,0:T(8,128)(2,1)S(1)} %collective-permute-done.1.a_ref, bf16[768,1024]{1,0:T(8,128)(2,1)S(1)} %collective-permute-done.7.b_ref, bf16[1024,4096]{1,0:T(8,128)(2,1)S(1)} %copy-done, ...), custom_call_target="tpu_custom_call" | custom-call | tf_op jit(solution)/shard_map/late/pallas_call | solution.py:40
  50.9 2.1 %within.4 = (bf16[2048,128]{1,0:T(8,128)(2,1)S(1)}, bf16[256,1024]{1,0:T(8,128)(2,1)S(1)}, bf16[256,1024]{1,0:T(8,128)(2,1)S(1)}, f32[8,128]{1,0:T(8,128)S(1)}) custom-call(bf16[1024,1024]{1,0:T(8,128)(2,1)S(1)} %get-tuple-element.80.q_ref, bf16[1024,1024]{1,0:T(8,128)(2,1)S(1)} %get-tuple-element.81.k_ref, bf16[1024,1024]{1,0:T(8,128)(2,1)S(1)} %get-tuple-element.82.v_ref, ...), custom_call_target="tpu_custom_call" | custom-call | tf_op jit(solution)/shard_map/within/pallas_call | solution.py:40
  53.0 2.3 %within.5 = (bf16[2048,128]{1,0:T(8,128)(2,1)S(1)}, bf16[256,1024]{1,0:T(8,128)(2,1)S(1)}, bf16[256,1024]{1,0:T(8,128)(2,1)S(1)}, f32[8,128]{1,0:T(8,128)S(1)}) custom-call(bf16[1024,1024]{1,0:T(8,128)(2,1)S(1)} %get-tuple-element.80.q_ref, bf16[1024,1024]{1,0:T(8,128)(2,1)S(1)} %get-tuple-element.81.k_ref, bf16[1024,1024]{1,0:T(8,128)(2,1)S(1)} %get-tuple-element.82.v_ref, ...), custom_call_target="tpu_custom_call" | custom-call | tf_op jit(solution)/shard_map/within/pallas_call | solution.py:40
  55.6 1.8 %collective-permute-done.8.b_ref = bf16[256,1024]{1,0:T(8,128)(2,1)S(1)} collective-permute-done((bf16[256,1024]{1,0:T(8,128)(2,1)S(1)}, bf16[256,1024]{1,0:T(8,128)(2,1)S(1)}, u32[]{:S(2)}, u32[]{:S(2)}) %collective-permute-start.8) | collective-permute-done | bytes 524320 | tf_op jit(solution)/shard_map/ppermute | solution.py:391
  57.4 1.7 %late.4 = (bf16[256,512]{1,0:T(8,128)(2,1)S(1)}, f32[8,128]{1,0:T(8,128)S(1)}, bf16[2,128,128]{2,1,0:T(8,128)(2,1)S(1)}, bf16[2,128,128]{2,1,0:T(8,128)(2,1)S(1)...) custom-call(bf16[256,1024]{1,0:T(8,128)(2,1)S(1)} %collective-permute-done.a_ref, ...), custom_call_target="tpu_custom_call" | custom-call | tf_op jit(solution)/shard_map/late/pallas_call | solution.py:40
  59.1 1.6 %collective-permute-start.10 = (bf16[2,128,128]{2,1,0:T(8,128)(2,1)S(1)}, bf16[2,128,128]{2,1,0:T(8,128)(2,1)S(1)}, u32[]{:S(2)}, u32[]{:S(2)}) collective-permute-start(bf16[2,128,128]{2,1,0:T(8,128)(2,1)S(1)} %get-tuple-element.121), channel_id=1, source_target_pairs={{0,4},{4,0},{8,12},{12,8},{16,20},{20,16},{24,28},{28,24},{1,5},{5... | collective-permute-start | bytes 196616 | tf_op jit(solution)/shard_map/ppermute | solution.py:391
  61.2 1.7 %late.5 = (bf16[256,512]{1,0:T(8,128)(2,1)S(1)}, f32[8,128]{1,0:T(8,128)S(1)}, bf16[2,128,128]{2,1,0:T(8,128)(2,1)S(1)}, bf16[2,128,128]{2,1,0:T(8,128)(2,1)S(1)}) custom-call(bf16[1024,256]{1,0:T(8,128)(2,1)S(1)} %get-tuple-element.113.a_ref, bf16[1024,256]{1,0:T(8,128)(2,1)S(1)} %get-tuple-element.114.b_ref, bf16[1024,4096]{1,0:T(8,128)(2,1)S(1)} %copy-done, ...), custom_call_target="tpu_custom_call" | custom-call | tf_op jit(solution)/shard_map/late/pallas_call | solution.py:40
  63.8 1.3 %collective-permute-start.12 = (bf16[2,128,128]{2,1,0:T(8,128)(2,1)S(1)}, bf16[2,128,128]{2,1,0:T(8,128)(2,1)S(1)}, u32[]{:S(2)}, u32[]{:S(2)}) collective-permute-start(bf16[2,128,128]{2,1,0:T(8,128)(2,1)S(1)} %total.9), channel_id=1, source_target_pairs={{8,0},{12,4},{16,8},{20,12},{24,16},{28,20},{9,1},{13,5},{17,9},{2... | collective-permute-start | bytes 196616 | tf_op jit(solution)/shard_map/ppermute | solution.py:395
  65.2 1.5 %collective-permute-start.11 = (bf16[2,128,128]{2,1,0:T(8,128)(2,1)S(1)}, bf16[2,128,128]{2,1,0:T(8,128)(2,1)S(1)}, u32[]{:S(2)}, u32[]{:S(2)}) collective-permute-start(bf16[2,128,128]{2,1,0:T(8,128)(2,1)S(1)} %total.8), channel_id=1, source_target_pairs={{8,0},{12,4},{16,8},{20,12},{24,16},{28,20},{9,1},{13,5},{17,9},{2... | collective-permute-start | bytes 196616 | tf_op jit(solution)/shard_map/ppermute | solution.py:395
  66.6 2.3 %within.6 = (bf16[2048,128]{1,0:T(8,128)(2,1)S(1)}, bf16[256,1024]{1,0:T(8,128)(2,1)S(1)}, bf16[256,1024]{1,0:T(8,128)(2,1)S(1)}, f32[8,128]{1,0:T(8,128)S(1)}) custom-call(bf16[1024,1024]{1,0:T(8,128)(2,1)S(1)} %get-tuple-element.80.q_ref, bf16[1024,1024]{1,0:T(8,128)(2,1)S(1)} %get-tuple-element.81.k_ref, bf16[1024,1024]{1,0:T(8,128)(2,1)S(1)} %get-tuple-element.82.v_ref, ...), custom_call_target="tpu_custom_call" | custom-call | tf_op jit(solution)/shard_map/within/pallas_call | solution.py:40
  69.0 2.9 %collective-permute-done.12.refs_2_.refs_0_ = bf16[2,128,128]{2,1,0:T(8,128)(2,1)S(1)} collective-permute-done((bf16[2,128,128]{2,1,0:T(8,128)(2,1)S(1)}, bf16[2,128,128]{2,1,0:T(8,128)(2,1)S(1)}, u32[]{:S(2)}, u32[]{:S(2)}) %collective-permute-start.12) | collective-permute-done | bytes 65568 | tf_op jit(solution)/shard_map/ppermute | solution.py:395
  71.9 1.3 %collective-permute-start.14 = (bf16[2,128,128]{2,1,0:T(8,128)(2,1)S(1)}, bf16[2,128,128]{2,1,0:T(8,128)(2,1)S(1)}, u32[]{:S(2)}, u32[]{:S(2)}) collective-permute-start(bf16[2,128,128]{2,1,0:T(8,128)(2,1)S(1)} %total.11), channel_id=1, source_target_pairs={{16,0},{20,4},{24,8},{28,12},{17,1},{21,5},{25,9},{29,13},{18,2},{... | collective-permute-start | bytes 196616 | tf_op jit(solution)/shard_map/ppermute | solution.py:395
  73.2 1.3 %collective-permute-start.13 = (bf16[2,128,128]{2,1,0:T(8,128)(2,1)S(1)}, bf16[2,128,128]{2,1,0:T(8,128)(2,1)S(1)}, u32[]{:S(2)}, u32[]{:S(2)}) collective-permute-start(bf16[2,128,128]{2,1,0:T(8,128)(2,1)S(1)} %total.10), channel_id=1, source_target_pairs={{16,0},{20,4},{24,8},{28,12},{17,1},{21,5},{25,9},{29,13},{18,2},{... | collective-permute-start | bytes 196616 | tf_op jit(solution)/shard_map/ppermute | solution.py:395
  74.5 3.5 %within.7 = (bf16[8192,128]{1,0:T(8,128)(2,1)}, bf16[256,1024]{1,0:T(8,128)(2,1)S(1)}, bf16[256,1024]{1,0:T(8,128)(2,1)S(1)}, f32[8,128]{1,0:T(8,128)S(1)}) custom-call(bf16[1024,1024]{1,0:T(8,128)(2,1)S(1)} %get-tuple-element.80.q_ref, bf16[1024,1024]{1,0:T(8,128)(2,1)S(1)} %get-tuple-element.81.k_ref, bf16[1024,1024]{1,0:T(8,128)(2,1)S(1)} %get-tuple-element.82.v_ref, ...), custom_call_target="tpu_custom_call" | custom-call | tf_op jit(solution)/shard_map/within/pallas_call | solution.py:40
  78.0 2.5 %collective-permute-done.14.refs_1_ = bf16[2,128,128]{2,1,0:T(8,128)(2,1)S(1)} collective-permute-done((bf16[2,128,128]{2,1,0:T(8,128)(2,1)S(1)}, bf16[2,128,128]{2,1,0:T(8,128)(2,1)S(1)}, u32[]{:S(2)}, u32[]{:S(2)}) %collective-permute-start.14) | collective-permute-done | bytes 65568 | tf_op jit(solution)/shard_map/ppermute | solution.py:395
  80.6 1.4 %collective-permute-done.13.refs_1_ = bf16[2,128,128]{2,1,0:T(8,128)(2,1)S(1)} collective-permute-done((bf16[2,128,128]{2,1,0:T(8,128)(2,1)S(1)}, bf16[2,128,128]{2,1,0:T(8,128)(2,1)S(1)}, u32[]{:S(2)}, u32[]{:S(2)}) %collective-permute-start.13) | collective-permute-done | bytes 65568 | tf_op jit(solution)/shard_map/ppermute | solution.py:395
  84.1 2.2 %collective-permute-done.16.refs_3_ = bf16[2,128,128]{2,1,0:T(8,128)(2,1)S(1)} collective-permute-done((bf16[2,128,128]{2,1,0:T(8,128)(2,1)S(1)}, bf16[2,128,128]{2,1,0:T(8,128)(2,1)S(1)}, u32[]{:S(2)}, u32[]{:S(2)}) %collective-permute-start.16) | collective-permute-done | bytes 65568 | tf_op jit(solution)/shard_map/ppermute | solution.py:391
  87.2 3.5 %finish.1 = (bf16[8192,128]{1,0:T(8,128)(2,1)}, bf16[8192,128]{1,0:T(8,128)(2,1)}) custom-call(bf16[1024,1024]{1,0:T(8,128)(2,1)S(1)} %get-tuple-element.81.k_ref, bf16[1024,1024]{1,0:T(8,128)(2,1)S(1)} %get-tuple-element.82.v_ref, f32[8,128]{1,0:T(8,128)S(1)} %get-tuple-element.140._, bf16[2,128,128]{2,1,0:T(8,128)(2,1)S(1)} %get-tuple-element.141.refs_0_, ...), custom_call_target="tpu_custom_call" | custom-call | tf_op jit(solution)/shard_map/finish/pallas_call | solution.py:40
  (24 shorter events, 5.4 us)
Async XLA Ops:
  0.6 15.7 %collective-permute-start.3 = (bf16[1024,1024]{1,0:T(8,128)(2,1)}, bf16[1024,1024]{1,0:T(8,128)(2,1)S(1)}, u32[]{:S(2)}, u32[]{:S(2)}) collective-permute-start(bf16[1024,1024]{1,0:T(8,128)(2,1)} %source.1), channel_id=1, source_target_pairs={{0,1},{1,0},{2,3},{3,2},{4,5},{5,4},{6,7},{7,6},{8,9},{9,8},{10,11... | collective-permute-start | bytes 6291464 | tf_op jit(solution)/shard_map/ppermute | solution.py:391
  1.1 15.2 %copy-start = (bf16[1024,4096]{1,0:T(8,128)(2,1)S(1)}, bf16[1024,4096]{1,0:T(8,128)(2,1)}, u32[]{:S(2)}) copy-start(bf16[1024,4096]{1,0:T(8,128)(2,1)} %w_ref.5) | copy-start | bytes 25165828
  2.8 37.8 %collective-permute-start.1 = (bf16[768,1024]{1,0:T(8,128)(2,1)S(1)}, bf16[768,1024]{1,0:T(8,128)(2,1)S(1)}, u32[]{:S(2)}, u32[]{:S(2)}) collective-permute-start(bf16[768,1024]{1,0:T(8,128)(2,1)S(1)} %get-tuple-element.86.refs_0_), channel_id=1, source_target_pairs={{0,2},{1,3},{2,0},{3,1},{4,6},{5,7},{6,4},{7,5},{8,10},{9,11},{10,... | collective-permute-start | bytes 4718600 | tf_op jit(solution)/shard_map/ppermute | solution.py:391
  10.6 5.7 %collective-permute-start.2 = (bf16[4,128,128]{2,1,0:T(8,128)(2,1)S(1)}, bf16[4,128,128]{2,1,0:T(8,128)(2,1)S(1)}, u32[]{:S(2)}, u32[]{:S(2)}) collective-permute-start(bf16[4,128,128]{2,1,0:T(8,128)(2,1)S(1)} %get-tuple-element.88), channel_id=1, source_target_pairs={{0,4},{4,0},{8,12},{12,8},{16,20},{20,16},{24,28},{28,24},{1,5},{5... | collective-permute-start | bytes 393224 | tf_op jit(solution)/shard_map/ppermute | solution.py:391
  21.6 6.0 %collective-permute-start.4 = (bf16[4,128,128]{2,1,0:T(8,128)(2,1)S(1)}, bf16[4,128,128]{2,1,0:T(8,128)(2,1)S(1)}, u32[]{:S(2)}, u32[]{:S(2)}) collective-permute-start(bf16[4,128,128]{2,1,0:T(8,128)(2,1)S(1)} %total.6), channel_id=1, source_target_pairs={{0,8},{4,12},{8,16},{12,20},{16,24},{20,28},{1,9},{5,13},{9,17},{1... | collective-permute-start | bytes 393224 | tf_op jit(solution)/shard_map/ppermute | solution.py:395
  27.7 7.9 %collective-permute-start.5 = (bf16[4,128,128]{2,1,0:T(8,128)(2,1)S(1)}, bf16[4,128,128]{2,1,0:T(8,128)(2,1)S(1)}, u32[]{:S(2)}, u32[]{:S(2)}) collective-permute-start(bf16[4,128,128]{2,1,0:T(8,128)(2,1)S(1)} %total.7), channel_id=1, source_target_pairs={{0,16},{4,20},{8,24},{12,28},{1,17},{5,21},{9,25},{13,29},{2,18},{... | collective-permute-start | bytes 393224 | tf_op jit(solution)/shard_map/ppermute | solution.py:395
  35.6 5.0 %collective-permute-start.6 = (bf16[4,128,128]{2,1,0:T(8,128)(2,1)S(1)}, bf16[4,128,128]{2,1,0:T(8,128)(2,1)S(1)}, u32[]{:S(2)}, u32[]{:S(2)}) collective-permute-start(bf16[4,128,128]{2,1,0:T(8,128)(2,1)S(1)} %get-tuple-element.96), channel_id=1, source_target_pairs={{0,4},{4,0},{8,12},{12,8},{16,20},{20,16},{24,28},{28,24},{1,5},{5... | collective-permute-start | bytes 393224 | tf_op jit(solution)/shard_map/ppermute | solution.py:391
  40.7 3.4 %collective-permute-start.7 = (bf16[768,1024]{1,0:T(8,128)(2,1)S(1)}, bf16[768,1024]{1,0:T(8,128)(2,1)S(1)}, u32[]{:S(2)}, u32[]{:S(2)}) collective-permute-start(bf16[768,1024]{1,0:T(8,128)(2,1)S(1)} %collective-permute-done.1.a_ref), channel_id=1, source_target_pairs={{0,1},{1,0},{2,3},{3,2},{4,5},{5,4},{6,7},{7,6},{8,9},{9,8},{10,11... | collective-permute-start | bytes 4718600 | tf_op jit(solution)/shard_map/ppermute | solution.py:391
  40.7 14.7 %collective-permute-start = (bf16[256,1024]{1,0:T(8,128)(2,1)S(1)}, bf16[256,1024]{1,0:T(8,128)(2,1)S(1)}, u32[]{:S(2)}, u32[]{:S(2)}) collective-permute-start(bf16[256,1024]{1,0:T(8,128)(2,1)S(1)} %get-tuple-element.85.refs_1_), channel_id=1, source_target_pairs={{0,2},{1,3},{2,0},{3,1},{4,6},{5,7},{6,4},{7,5},{8,10},{9,11},{10,... | collective-permute-start | bytes 1572872 | tf_op jit(solution)/shard_map/ppermute | solution.py:391
  55.4 2.0 %collective-permute-start.8 = (bf16[256,1024]{1,0:T(8,128)(2,1)S(1)}, bf16[256,1024]{1,0:T(8,128)(2,1)S(1)}, u32[]{:S(2)}, u32[]{:S(2)}) collective-permute-start(bf16[256,1024]{1,0:T(8,128)(2,1)S(1)} %collective-permute-done.a_ref), channel_id=1, source_target_pairs={{0,1},{1,0},{2,3},{3,2},{4,5},{5,4},{6,7},{7,6},{8,9},{9,8},{10,11... | collective-permute-start | bytes 1572872 | tf_op jit(solution)/shard_map/ppermute | solution.py:391
  59.1 4.7 %collective-permute-start.10 = (bf16[2,128,128]{2,1,0:T(8,128)(2,1)S(1)}, bf16[2,128,128]{2,1,0:T(8,128)(2,1)S(1)}, u32[]{:S(2)}, u32[]{:S(2)}) collective-permute-start(bf16[2,128,128]{2,1,0:T(8,128)(2,1)S(1)} %get-tuple-element.121), channel_id=1, source_target_pairs={{0,4},{4,0},{8,12},{12,8},{16,20},{20,16},{24,28},{28,24},{1,5},{5... | collective-permute-start | bytes 196616 | tf_op jit(solution)/shard_map/ppermute | solution.py:391
  60.7 4.4 %collective-permute-start.9 = (bf16[2,128,128]{2,1,0:T(8,128)(2,1)S(1)}, bf16[2,128,128]{2,1,0:T(8,128)(2,1)S(1)}, u32[]{:S(2)}, u32[]{:S(2)}) collective-permute-start(bf16[2,128,128]{2,1,0:T(8,128)(2,1)S(1)} %get-tuple-element.119), channel_id=1, source_target_pairs={{0,4},{4,0},{8,12},{12,8},{16,20},{20,16},{24,28},{28,24},{1,5},{5... | collective-permute-start | bytes 196616 | tf_op jit(solution)/shard_map/ppermute | solution.py:391
  63.8 8.0 %collective-permute-start.12 = (bf16[2,128,128]{2,1,0:T(8,128)(2,1)S(1)}, bf16[2,128,128]{2,1,0:T(8,128)(2,1)S(1)}, u32[]{:S(2)}, u32[]{:S(2)}) collective-permute-start(bf16[2,128,128]{2,1,0:T(8,128)(2,1)S(1)} %total.9), channel_id=1, source_target_pairs={{8,0},{12,4},{16,8},{20,12},{24,16},{28,20},{9,1},{13,5},{17,9},{2... | collective-permute-start | bytes 196616 | tf_op jit(solution)/shard_map/ppermute | solution.py:395
  65.2 8.0 %collective-permute-start.11 = (bf16[2,128,128]{2,1,0:T(8,128)(2,1)S(1)}, bf16[2,128,128]{2,1,0:T(8,128)(2,1)S(1)}, u32[]{:S(2)}, u32[]{:S(2)}) collective-permute-start(bf16[2,128,128]{2,1,0:T(8,128)(2,1)S(1)} %total.8), channel_id=1, source_target_pairs={{8,0},{12,4},{16,8},{20,12},{24,16},{28,20},{9,1},{13,5},{17,9},{2... | collective-permute-start | bytes 196616 | tf_op jit(solution)/shard_map/ppermute | solution.py:395
  71.9 8.6 %collective-permute-start.14 = (bf16[2,128,128]{2,1,0:T(8,128)(2,1)S(1)}, bf16[2,128,128]{2,1,0:T(8,128)(2,1)S(1)}, u32[]{:S(2)}, u32[]{:S(2)}) collective-permute-start(bf16[2,128,128]{2,1,0:T(8,128)(2,1)S(1)} %total.11), channel_id=1, source_target_pairs={{16,0},{20,4},{24,8},{28,12},{17,1},{21,5},{25,9},{29,13},{18,2},{... | collective-permute-start | bytes 196616 | tf_op jit(solution)/shard_map/ppermute | solution.py:395
  73.2 8.7 %collective-permute-start.13 = (bf16[2,128,128]{2,1,0:T(8,128)(2,1)S(1)}, bf16[2,128,128]{2,1,0:T(8,128)(2,1)S(1)}, u32[]{:S(2)}, u32[]{:S(2)}) collective-permute-start(bf16[2,128,128]{2,1,0:T(8,128)(2,1)S(1)} %total.10), channel_id=1, source_target_pairs={{16,0},{20,4},{24,8},{28,12},{17,1},{21,5},{25,9},{29,13},{18,2},{... | collective-permute-start | bytes 196616 | tf_op jit(solution)/shard_map/ppermute | solution.py:395
  82.0 4.3 %collective-permute-start.16 = (bf16[2,128,128]{2,1,0:T(8,128)(2,1)S(1)}, bf16[2,128,128]{2,1,0:T(8,128)(2,1)S(1)}, u32[]{:S(2)}, u32[]{:S(2)}) collective-permute-start(bf16[2,128,128]{2,1,0:T(8,128)(2,1)S(1)} %get-tuple-element.144), channel_id=1, source_target_pairs={{0,4},{4,0},{8,12},{12,8},{16,20},{20,16},{24,28},{28,24},{1,5},{5... | collective-permute-start | bytes 196616 | tf_op jit(solution)/shard_map/ppermute | solution.py:391
  82.9 4.3 %collective-permute-start.15 = (bf16[2,128,128]{2,1,0:T(8,128)(2,1)S(1)}, bf16[2,128,128]{2,1,0:T(8,128)(2,1)S(1)}, u32[]{:S(2)}, u32[]{:S(2)}) collective-permute-start(bf16[2,128,128]{2,1,0:T(8,128)(2,1)S(1)} %get-tuple-element.143), channel_id=1, source_target_pairs={{0,4},{4,0},{8,12},{12,8},{16,20},{20,16},{24,28},{28,24},{1,5},{5... | collective-permute-start | bytes 196616 | tf_op jit(solution)/shard_map/ppermute | solution.py:391

commit v9 on v8

--- a/solution.py
+++ b/solution.py
@@ -36,13 +36,14 @@
     return slice(i * size, (i + 1) * size) if isinstance(i, int) else pl.ds(pl.multiple_of(i * size, size), size)
 
 
-def call(kernel, name, args, in_specs, out_shape, out_specs, scratch=()):
+def call(kernel, name, args, in_specs, out_shape, out_specs, scratch=(), aliases=None):
     return pl.pallas_call(
         kernel,
         in_specs=in_specs,
         out_specs=out_specs,
         out_shape=out_shape,
         scratch_shapes=scratch,
+        input_output_aliases=aliases or {},
         compiler_params=pltpu.CompilerParams(vmem_limit_bytes=VMEM_LIMIT),
         cost_estimate=FREE,
         name=name,
@@ -174,20 +175,24 @@
     )
 
 
-def late_kernel(half, first, start, near, dk, a_ref, b_ref, w_ref, part_ref, scale_ref, qt_ref, _, *refs):
+def late_kernel(half, first, start, near, dk, b_ref, w_ref, part_ref, scale_ref, qt_ref, _, *refs):
+    a_ref, refs = (refs[0], refs[1:]) if half is None else (None, refs)
     state_ref, refs = (None, refs) if first else (refs[0], refs[1:])
     d_ref, token_ref = refs[:2]
     tile = PAIR * dk
     steps = d_ref.shape[1] // tile
-    outs, refs = (refs[2:3], refs[3:]) if half is None else (refs[2 : 2 + steps], refs[2 + steps :])
+    out_ref, refs = refs[2], refs[3:]
     token_ref[...] = jnp.zeros_like(token_ref)
-    if half == 0:
-        at, bt = a_ref, b_ref
-    else:
+    if half is None:
         at, bt = refs
         at[...] = a_ref[...].T
         bt[...] = b_ref[...].T
-    features, count = at.shape
+    elif half == 1:
+        (bt,) = refs
+        bt[...] = b_ref[...].T
+    else:
+        bt = b_ref
+    features, count = bt.shape
     place = lax.axis_index("head")
     one, two = part_of(place ^ near, features), part_of(place ^ near ^ 1, features)
     here = slice(start, start + count)
@@ -196,8 +201,10 @@
     def one_tile(local, _):
         j = base + local
         wide = part_of(j, tile)
-        turned = dot(w_ref[wide, one], at[...], NN) + dot(w_ref[wide, two], bt[...], NN)
-        low = (part_ref[here, wide] + turned.T).astype(BF16)
+        turned = dot(w_ref[wide, two], bt[...], NN)
+        if half is None:
+            turned = turned + dot(w_ref[wide, one], at[...], NN)
+        low = (part_ref[here if half is None else slice(0, count), wide] + turned.T).astype(BF16)
         d_ref[:, part_of(local, tile)] = low
         states = [None if first else state_ref[0, j * PAIR + i] for i in range(PAIR)]
         for c in reversed(range(count // CHUNK)):
@@ -208,10 +215,10 @@
                 state = dot(qt_ref[part_of(j * PAIR + i, dk), there], grad, NN)
                 states[i] = state if states[i] is None else states[i] + state
                 if half is None:
-                    outs[0][c, j * PAIR + i] = states[i]
+                    out_ref[c, j * PAIR + i] = states[i]
         if half is not None:
             for i in range(PAIR):
-                outs[local][i] = states[i].astype(BF16)
+                out_ref[local * PAIR + i] = states[i].astype(BF16)
         return 0
 
     if half is None:
@@ -221,11 +228,37 @@
             one_tile(local, 0)
 
 
+def middle_kernel(start, near, a_ref, w_ref, part_ref, _, out_ref, token_ref, at):
+    token_ref[...] = jnp.zeros_like(token_ref)
+    at[...] = a_ref[...].T
+    features, count = at.shape
+    one = part_of(lax.axis_index("head") ^ near, features)
+    tile = PAIR * 128
+    for j in range(out_ref.shape[1] // tile):
+        wide = slice(j * tile, (j + 1) * tile)
+        out_ref[:, wide] = part_ref[start : start + count, wide] + dot(w_ref[wide, one], at[...], NN).T
+
+
+def middle(start, near, a, weight, part, token):
+    return call(
+        functools.partial(middle_kernel, start, near),
+        "middle",
+        [a, weight, part, token],
+        [WHOLE] * 3 + [ANYWHERE],
+        [shape((a.shape[0], part.shape[1]), F32), shape(TOKEN, F32)],
+        [WHOLE] * 2,
+        [pltpu.VMEM(a.shape[::-1], BF16)],
+    )
+
+
 def late(start, half, near, a, b, weight, part, scale, qt, token, state, heads, dk):
-    features, rows = a.shape if half == 0 else a.shape[::-1]
+    features, rows = b.shape if half == 0 else b.shape[::-1]
     width = weight.shape[0]
-    args = [a, b, weight, part, scale, qt, token]
-    in_specs = [WHOLE] * 6 + [ANYWHERE]
+    args = [b, weight, part, scale, qt, token]
+    in_specs = [WHOLE] * 5 + [ANYWHERE]
+    if half is None:
+        args.append(a)
+        in_specs.append(WHOLE)
     if state is not None:
         args.append(state)
         in_specs.append(WHOLE)
@@ -233,11 +266,10 @@
         out_shape = [shape((rows, width), BF16), shape(TOKEN, F32), shape((rows // CHUNK, heads, dk, dk), F32)]
     else:
         out_shape = [shape((rows, width // 2), BF16), shape(TOKEN, F32)]
-        out_shape += [shape((PAIR, dk, dk), BF16)] * (heads // 2 // PAIR)
-    turned = [] if half == 0 else [(features, rows)] * 2
-    scratch = [pltpu.VMEM(dims, BF16) for dims in turned] if half is None else []
+        out_shape.append(shape((heads // 2, dk, dk), BF16))
+    scratch = [pltpu.VMEM((features, rows), BF16)] * 2 if half is None else []
     if half == 1:
-        out_shape += [shape(dims, BF16) for dims in turned]
+        out_shape.append(shape((features, rows), BF16))
     return call(
         functools.partial(late_kernel, half, state is None, start, near, dk),
         "late",
@@ -336,55 +368,66 @@
     )
 
 
-def finish_kernel(heads, dk, n, parts, k_ref, v_ref, _, *refs):
-    own, other, refs = refs[:parts], refs[parts : 2 * parts], refs[2 * parts :]
-    dkp, dvp, (dk_ref, dv_ref, after, turned, wide_k, wide_v, low_k, low_v, sem) = refs[:n], refs[n : 2 * n], refs[2 * n :]
-    first = lax.axis_index("ctx") % 2 == 0
+def finish_kernel(heads, dk, n, last, k_ref, v_ref, suffix_ref, _, *refs):
+    half = heads // 2
+    dkp, dvp, refs = refs[:n], refs[n : 2 * n], refs[2 * n :]
+    if last:
+        dk_ref, dv_ref, wide_k, wide_v, after, turned, low_k, low_v, sem = refs[2:]
+    else:
+        wide_k, wide_v, token_ref, after, turned = refs
+        token_ref[...] = jnp.zeros_like(token_ref)
+    base = half * (lax.axis_index("ctx") % 2 ^ last)
     after[...] = jnp.zeros_like(after)
     turned[...] = jnp.zeros_like(turned)
-    for p in range(parts):
-        for i in range(PAIR):
-            mine, its = own[p][i], other[p][i]
-            cols = slice(i * dk, (i + 1) * dk)
-            for place, one in ((p, jnp.where(first, mine, its)), (parts + p, jnp.where(first, its, mine))):
-                after[place, cols, cols] = one
-                turned[place, cols, cols] = one.T
+    for h in range(half):
+        cols = slice(h % PAIR * dk, (h % PAIR + 1) * dk)
+        after[h // PAIR, cols, cols] = suffix_ref[h]
+        turned[h // PAIR, cols, cols] = suffix_ref[h].T
     copies = []
     for c in range(n):
         rows = slice(c * CHUNK, (c + 1) * CHUNK)
-        for p in range(heads // PAIR):
-            cols = slice(p * PAIR * dk, (p + 1) * PAIR * dk)
+        for p in range(half // PAIR):
+            cols = part_of(base // PAIR + p, PAIR * dk)
             full_k = dkp[c][:, cols].astype(F32) + dot(v_ref[rows, cols], turned[p], NN)
             full_v = dvp[c][:, cols].astype(F32) + dot(k_ref[rows, cols], after[p], NN)
             for i in range(PAIR):
-                mine = pl.ds(p * PAIR + i, CHUNK, stride=heads)
+                mine = pl.ds(c * CHUNK * heads + base + p * PAIR + i, CHUNK, stride=heads)
                 wide_k[mine, :] = full_k[:, i * dk : (i + 1) * dk]
                 wide_v[mine, :] = full_v[:, i * dk : (i + 1) * dk]
-        for i, (wide, low, out) in enumerate(((wide_k, low_k, dk_ref), (wide_v, low_v, dv_ref))):
-            low[c] = wide[...].astype(BF16)
-            copy = pltpu.make_async_copy(low.at[c], out.at[pl.ds(c * CHUNK * heads, CHUNK * heads)], sem.at[i, c])
-            copy.start()
-            copies.append(copy)
+        if last:
+            raw = slice(c * CHUNK * heads, (c + 1) * CHUNK * heads)
+            for i, (wide, low, out) in enumerate(((wide_k, low_k, dk_ref), (wide_v, low_v, dv_ref))):
+                low[c] = wide[raw, :].astype(BF16)
+                copy = pltpu.make_async_copy(low.at[c], out.at[pl.ds(c * CHUNK * heads, CHUNK * heads)], sem.at[i, c])
+                copy.start()
+                copies.append(copy)
     for copy in copies:
         copy.wait()
 
 
-def finish(k, v, dkp, dvp, own, other, token, heads, dk):
+def finish(k, v, dkp, dvp, suffix, token, held, heads, dk):
     tokens, width = k.shape
     n = tokens // CHUNK
-    raw = (CHUNK * heads, dk)
-    return call(
-        functools.partial(finish_kernel, heads, dk, n, len(own)),
-        "finish",
-        [k, v, token, *own, *other, *dkp, *dvp],
-        [WHOLE] * 2 + [ANYWHERE] + [WHOLE] * (2 * len(own) + 2 * n),
-        [shape((tokens * heads, dk), BF16)] * 2,
-        [ANYWHERE] * 2,
-        [pltpu.VMEM((heads // PAIR, PAIR * dk, PAIR * dk), BF16)] * 2
-        + [pltpu.VMEM(raw, F32)] * 2
-        + [pltpu.VMEM((n, *raw), BF16)] * 2
-        + [pltpu.SemaphoreType.DMA((2, n))],
-    )
+    last = held is not None
+    raw = (tokens * heads, dk)
+    args = [k, v, suffix, token, *dkp, *dvp]
+    in_specs = [WHOLE] * 3 + [ANYWHERE] + [WHOLE] * (2 * n)
+    out_shape = [shape(raw, F32)] * 2
+    out_specs = [WHOLE] * 2
+    scratch = [pltpu.VMEM((heads // 2 // PAIR, PAIR * dk, PAIR * dk), BF16)] * 2
+    aliases = {}
+    if last:
+        aliases = {len(args): 2, len(args) + 1: 3}
+        args += held
+        in_specs += [WHOLE] * 2
+        out_shape = [shape(raw, BF16)] * 2 + out_shape
+        out_specs = [ANYWHERE] * 2 + out_specs
+        scratch += [pltpu.VMEM((n, CHUNK * heads, dk), BF16)] * 2 + [pltpu.SemaphoreType.DMA((2, n))]
+    else:
+        out_shape.append(shape(TOKEN, F32))
+        out_specs.append(WHOLE)
+    kernel = functools.partial(finish_kernel, heads, dk, n, int(last))
+    return call(kernel, "finish", args, in_specs, out_shape, out_specs, scratch, aliases)
 
 
 def swap(array, axis, size, bit):
@@ -465,7 +508,7 @@
     prefix = None
     while prefix is None:
         prefix = next(forward)
-    prefix = [prefix[0][0], order.tie(prefix[1][0])]
+    prefix = [prefix[0][0], prefix[1][0]]
     d, after, dq, dkp, dvp = {}, {}, {}, {}, {}
 
     def inner(c):
@@ -487,30 +530,30 @@
             if i < m - 1:
                 after[c + i] = (state, i + 1)
         for i in reversed(range(m)):
-            if c + i > 1:
+            if c + i > 2:
                 inner(c + i)
     after[0] = (state, 0)
     piece = order.tie(across[0])
     both = swap(piece, "head", n_head, far)
-    low_send, order.token, *send = late(
-        0, 1, near, piece, both, out_weight, part, scale, qt, order.token, state, heads, dk
-    )
-    *send, turned_a, turned_b = send
-    low_keep, order.token, *keep = late(
-        0, 0, near, turned_a, turned_b, out_weight, part, scale, qt, order.token, state, heads, dk
+    part, order.token = middle(0, near, piece, out_weight, part, order.token)
+    low_send, order.token, send, turned = late(
+        0, 1, near, None, both, out_weight, part, scale, qt, order.token, state, heads, dk
+    )
+    low_keep, order.token, keep = late(
+        0, 0, near, None, turned, out_weight, part, scale, qt, order.token, state, heads, dk
     )
     d[0] = (low_keep, low_send, None)
-    backward = scan_states(keep, send, n_ctx, -1, order)
+    backward = scan_states([keep], [send], n_ctx, -1, order)
     next(backward)
-    waiting = [1, 0]
+    plan = [[c for c in range(n) if c > 1 and c not in dq], [1, 0]]
     suffix = None
     while suffix is None:
         suffix = next(backward)
-        if waiting:
-            inner(waiting.pop(0))
-    d_keys, d_values = finish(
-        k, v, [dkp[c] for c in range(n)], [dvp[c] for c in range(n)], *suffix, order.token, heads, dk
-    )
+        for c in plan.pop(0) if plan else []:
+            inner(c)
+    parts = [[dkp[c] for c in range(n)], [dvp[c] for c in range(n)]]
+    *held, order.token = finish(k, v, *parts, suffix[0][0], order.token, None, heads, dk)
+    d_keys, d_values, *_ = finish(k, v, *parts, suffix[1][0], order.token, held, heads, dk)
     return tuple(a.reshape(tokens, heads, dk) for a in (dq[0], d_keys, d_values))
 
 

time: 91 us -> 88.3 us (0.970)
  starting transfers between devices: 26.4 us -> 23.2 us
    ppermute x6 -> x4, starting transfers between devices: 14.2 us -> 11.7 us  [shifted(): lax.ppermute(array, 'ctx', [(i, i + step) for i in range(size) if 0 <= i...]
    ppermute x6 -> x4, waiting for transfers between devices: 11.8 us -> 10.2 us  [shifted(): lax.ppermute(array, 'ctx', [(i, i + step) for i in range(size) if 0 <= i...]
    ppermute x11 -> x9, waiting for transfers between devices: 15.2 us -> 16.8 us  [swap(): return lax.ppermute(array, axis, [(i, i ^ bit) for i in range(size)])]
    ppermute x11 -> x9, starting transfers between devices: 12.2 us -> 11.5 us  [swap(): return lax.ppermute(array, axis, [(i, i ^ bit) for i in range(size)])]
    pallas_call x20 -> x19, Pallas kernels: 36.4 us -> 37 us  [call(): pl.pallas_call(kernel, in_specs=in_specs, out_specs=out_specs, out_shape=...]
  transfers between devices with their start and end apart: 17 -> 13, of which waited for: 12 -> 11; matrix products, arithmetic and copies ran while one was open for 0% -> 0% of each run, Pallas kernels for 34% -> 37%
where the time goes in v9:
time: 88.3 us; the launch traced here: 88 us
  Pallas kernels  37 us (42%)
  waiting for transfers between devices  26.9 us (30%)
  starting transfers between devices  23.2 us (26%)
  between operations  0.96 us (1%)
    pallas_call x19, Pallas kernels, call(): pl.pallas_call(kernel, in_specs=in_specs, out_specs=out_specs, out_shape=...  37 us
    ppermute x9, waiting for transfers between devices, swap(): return lax.ppermute(array, axis, [(i, i ^ bit) for i in range(size)])  16.8 us
    ppermute x4, starting transfers between devices, shifted(): lax.ppermute(array, 'ctx', [(i, i + step) for i in range(size) if 0 <= i...  11.7 us
    ppermute x9, starting transfers between devices, swap(): return lax.ppermute(array, axis, [(i, i ^ bit) for i in range(size)])  11.5 us
    ppermute x4, waiting for transfers between devices, shifted(): lax.ppermute(array, 'ctx', [(i, i + step) for i in range(size) if 0 <= i...  10.2 us
  transfers between devices with their start and end apart: 13, of which 11 were waited for; matrix products, arithmetic and copies ran while one was open for 0% of the time, Pallas kernels for 37%

profile of v9, /device:TPU:0, one launch (start us, length us, event | category | flops | bytes accessed | tf_op | source)
XLA Modules:
  0.0 88.0 jit_solution(11776316824907908728)
XLA Ops:
  1.2 1.7 %cut.1 = (bf16[768,1024]{1,0:T(8,128)(2,1)S(1)}, bf16[256,1024]{1,0:T(8,128)(2,1)S(1)}, f32[8,128]{1,0:T(8,128)S(1)}) custom-call(bf16[1024,1024]{1,0:T(8,128)(2,1)} %source.1), custom_call_target="tpu_custom_call" | custom-call | tf_op jit(solution)/shard_map/cut/pallas_call | solution.py:40
  2.8 2.6 %collective-permute-start.1 = (bf16[768,1024]{1,0:T(8,128)(2,1)S(1)}, bf16[768,1024]{1,0:T(8,128)(2,1)S(1)}, u32[]{:S(2)}, u32[]{:S(2)}) collective-permute-start(bf16[768,1024]{1,0:T(8,128)(2,1)S(1)} %get-tuple-element.78.refs_0_), channel_id=1, source_target_pairs={{0,2},{1,3},{2,0},{3,1},{4,6},{5,7},{6,4},{7,5},{8,10},{9,11},{10,... | collective-permute-start | bytes 4718600 | tf_op jit(solution)/shard_map/ppermute | solution.py:434
  5.4 5.2 %prepare.1 = (bf16[1024,1024]{1,0:T(8,128)(2,1)S(1)}, bf16[1024,1024]{1,0:T(8,128)(2,1)S(1)}, bf16[1024,1024]{1,0:T(8,128)(2,1)S(1)}, bf16[1024,1024]{1,0:T(8,12...) custom-call(bf16[8192,128]{1,0:T(8,128)(2,1)} %bitcast.6, ...), custom_call_target="tpu_custom_call" | custom-call | tf_op jit(solution)/shard_map/prepare/pallas_call | solution.py:40
  10.6 1.6 %collective-permute-start.2 = (bf16[4,128,128]{2,1,0:T(8,128)(2,1)S(1)}, bf16[4,128,128]{2,1,0:T(8,128)(2,1)S(1)}, u32[]{:S(2)}, u32[]{:S(2)}) collective-permute-start(bf16[4,128,128]{2,1,0:T(8,128)(2,1)S(1)} %get-tuple-element.80), channel_id=1, source_target_pairs={{0,4},{4,0},{8,12},{12,8},{16,20},{20,16},{24,28},{28,24},{1,5},{5... | collective-permute-start | bytes 393224 | tf_op jit(solution)/shard_map/ppermute | solution.py:434
  12.2 4.1 %collective-permute-done.2.refs_1_.came = bf16[4,128,128]{2,1,0:T(8,128)(2,1)S(1)} collective-permute-done((bf16[4,128,128]{2,1,0:T(8,128)(2,1)S(1)}, bf16[4,128,128]{2,1,0:T(8,128)(2,1)S(1)}, u32[]{:S(2)}, u32[]{:S(2)}) %collective-permute-start.2) | collective-permute-done | bytes 131104 | tf_op jit(solution)/shard_map/ppermute | solution.py:434
  16.3 5.2 %early.1 = (f32[1024,1024]{1,0:T(8,128)S(1)}, f32[8,128]{1,0:T(8,128)S(1)}) custom-call(bf16[768,1024]{1,0:T(8,128)(2,1)S(1)} %get-tuple-element.78.refs_0_, bf16[256,1024]{1,0:T(8,128)(2,1)S(1)} %get-tuple-element.77.refs_1_, bf16[1024,1024]{1,0:T(8,128)(2,1)S(1)} %collective-permute-done.3.refs_2_, bf16[1024,4096]{1,0:T(8,128)(2,1)S(1)} %copy-done, ...), custom_call_target="tpu_custom_call" | custom-call | tf_op jit(solution)/shard_map/early/pallas_call | solution.py:40
  21.6 3.5 %collective-permute-start.4 = (bf16[4,128,128]{2,1,0:T(8,128)(2,1)S(1)}, bf16[4,128,128]{2,1,0:T(8,128)(2,1)S(1)}, u32[]{:S(2)}, u32[]{:S(2)}) collective-permute-start(bf16[4,128,128]{2,1,0:T(8,128)(2,1)S(1)} %total.4), channel_id=1, source_target_pairs={{0,8},{4,12},{8,16},{12,20},{16,24},{20,28},{1,9},{5,13},{9,17},{1... | collective-permute-start | bytes 393224 | tf_op jit(solution)/shard_map/ppermute | solution.py:438
  25.1 2.5 %collective-permute-done.4.refs_2_.refs_0_ = bf16[4,128,128]{2,1,0:T(8,128)(2,1)S(1)} collective-permute-done((bf16[4,128,128]{2,1,0:T(8,128)(2,1)S(1)}, bf16[4,128,128]{2,1,0:T(8,128)(2,1)S(1)}, u32[]{:S(2)}, u32[]{:S(2)}) %collective-permute-start.4) | collective-permute-done | bytes 131104 | tf_op jit(solution)/shard_map/ppermute | solution.py:438
  27.7 5.4 %collective-permute-start.5 = (bf16[4,128,128]{2,1,0:T(8,128)(2,1)S(1)}, bf16[4,128,128]{2,1,0:T(8,128)(2,1)S(1)}, u32[]{:S(2)}, u32[]{:S(2)}) collective-permute-start(bf16[4,128,128]{2,1,0:T(8,128)(2,1)S(1)} %total.5), channel_id=1, source_target_pairs={{0,16},{4,20},{8,24},{12,28},{1,17},{5,21},{9,25},{13,29},{2,18},{... | collective-permute-start | bytes 393224 | tf_op jit(solution)/shard_map/ppermute | solution.py:438
  33.1 2.5 %collective-permute-done.5.refs_1_ = bf16[4,128,128]{2,1,0:T(8,128)(2,1)S(1)} collective-permute-done((bf16[4,128,128]{2,1,0:T(8,128)(2,1)S(1)}, bf16[4,128,128]{2,1,0:T(8,128)(2,1)S(1)}, u32[]{:S(2)}, u32[]{:S(2)}) %collective-permute-start.5) | collective-permute-done | bytes 131104 | tf_op jit(solution)/shard_map/ppermute | solution.py:438
  35.7 4.8 %collective-permute-done.1.refs_0_ = bf16[768,1024]{1,0:T(8,128)(2,1)S(1)} collective-permute-done((bf16[768,1024]{1,0:T(8,128)(2,1)S(1)}, bf16[768,1024]{1,0:T(8,128)(2,1)S(1)}, u32[]{:S(2)}, u32[]{:S(2)}) %collective-permute-start.1) | collective-permute-done | bytes 1572896 | tf_op jit(solution)/shard_map/ppermute | solution.py:434
  40.5 1.7 %collective-permute-start = (bf16[256,1024]{1,0:T(8,128)(2,1)S(1)}, bf16[256,1024]{1,0:T(8,128)(2,1)S(1)}, u32[]{:S(2)}, u32[]{:S(2)}) collective-permute-start(bf16[256,1024]{1,0:T(8,128)(2,1)S(1)} %get-tuple-element.77.refs_1_), channel_id=1, source_target_pairs={{0,2},{1,3},{2,0},{3,1},{4,6},{5,7},{6,4},{7,5},{8,10},{9,11},{10,... | collective-permute-start | bytes 1572872 | tf_op jit(solution)/shard_map/ppermute | solution.py:434
  42.2 1.5 %collective-permute-start.7 = (bf16[4,128,128]{2,1,0:T(8,128)(2,1)S(1)}, bf16[4,128,128]{2,1,0:T(8,128)(2,1)S(1)}, u32[]{:S(2)}, u32[]{:S(2)}) collective-permute-start(bf16[4,128,128]{2,1,0:T(8,128)(2,1)S(1)} %get-tuple-element.96), channel_id=1, source_target_pairs={{0,4},{4,0},{8,12},{12,8},{16,20},{20,16},{24,28},{28,24},{1,5},{5... | collective-permute-start | bytes 393224 | tf_op jit(solution)/shard_map/ppermute | solution.py:434
  43.9 6.9 %late.3 = (bf16[768,1024]{1,0:T(8,128)(2,1)S(1)}, f32[8,128]{1,0:T(8,128)S(1)}, f32[3,8,128,128]{3,2,1,0:T(8,128)S(1)}) custom-call(bf16[768,1024]{1,0:T(8,128)(2,1)S(1)} %collective-permute-done.6.b_ref, bf16[1024,4096]{1,0:T(8,128)(2,1)S(1)} %copy-done, f32[1024,1024]{1,0:T(8,128)S(1)} %get-tuple-element.90.part_ref, ...), custom_call_target="tpu_custom_call" | custom-call | tf_op jit(solution)/shard_map/late/pallas_call | solution.py:40
  50.7 2.1 %within.4 = (bf16[2048,128]{1,0:T(8,128)(2,1)S(1)}, bf16[256,1024]{1,0:T(8,128)(2,1)S(1)}, bf16[256,1024]{1,0:T(8,128)(2,1)S(1)}, f32[8,128]{1,0:T(8,128)S(1)}) custom-call(bf16[1024,1024]{1,0:T(8,128)(2,1)S(1)} %get-tuple-element.72.q_ref, bf16[1024,1024]{1,0:T(8,128)(2,1)S(1)} %get-tuple-element.73.k_ref, bf16[1024,1024]{1,0:T(8,128)(2,1)S(1)} %get-tuple-element.74.v_ref, ...), custom_call_target="tpu_custom_call" | custom-call | tf_op jit(solution)/shard_map/within/pallas_call | solution.py:40
  52.9 1.9 %collective-permute-done.a_ref = bf16[256,1024]{1,0:T(8,128)(2,1)S(1)} collective-permute-done((bf16[256,1024]{1,0:T(8,128)(2,1)S(1)}, bf16[256,1024]{1,0:T(8,128)(2,1)S(1)}, u32[]{:S(2)}, u32[]{:S(2)}) %collective-permute-start) | collective-permute-done | bytes 524320 | tf_op jit(solution)/shard_map/ppermute | solution.py:434
  55.7 1.0 %collective-permute-done.8.b_ref = bf16[256,1024]{1,0:T(8,128)(2,1)S(1)} collective-permute-done((bf16[256,1024]{1,0:T(8,128)(2,1)S(1)}, bf16[256,1024]{1,0:T(8,128)(2,1)S(1)}, u32[]{:S(2)}, u32[]{:S(2)}) %collective-permute-start.8) | collective-permute-done | bytes 524320 | tf_op jit(solution)/shard_map/ppermute | solution.py:434
  56.7 1.2 %late.4 = (bf16[256,512]{1,0:T(8,128)(2,1)S(1)}, f32[8,128]{1,0:T(8,128)S(1)}, bf16[4,128,128]{2,1,0:T(8,128)(2,1)S(1)}, bf16[1024,256]{1,0:T(8,128)(2,1)S(1)}) custom-call(bf16[256,1024]{1,0:T(8,128)(2,1)S(1)} %collective-permute-done.8.b_ref, bf16[1024,4096]{1,0:T(8,128)(2,1)S(1)} %copy-done, f32[256,1024]{1,0:T(8,128)S(1)} %get-tuple-element.101.part_ref, ...), custom_call_target="tpu_custom_call" | custom-call | tf_op jit(solution)/shard_map/late/pallas_call | solution.py:40
  57.9 1.8 %collective-permute-start.9 = (bf16[4,128,128]{2,1,0:T(8,128)(2,1)S(1)}, bf16[4,128,128]{2,1,0:T(8,128)(2,1)S(1)}, u32[]{:S(2)}, u32[]{:S(2)}) collective-permute-start(bf16[4,128,128]{2,1,0:T(8,128)(2,1)S(1)} %get-tuple-element.109), channel_id=1, source_target_pairs={{0,4},{4,0},{8,12},{12,8},{16,20},{20,16},{24,28},{28,24},{1,5},{5... | collective-permute-start | bytes 393224 | tf_op jit(solution)/shard_map/ppermute | solution.py:434
  59.8 1.2 %late.5 = (bf16[256,512]{1,0:T(8,128)(2,1)S(1)}, f32[8,128]{1,0:T(8,128)S(1)}, bf16[4,128,128]{2,1,0:T(8,128)(2,1)S(1)}) custom-call(bf16[1024,256]{1,0:T(8,128)(2,1)S(1)} %get-tuple-element.104.b_ref, bf16[1024,4096]{1,0:T(8,128)(2,1)S(1)} %copy-done, f32[256,1024]{1,0:T(8,128)S(1)} %get-tuple-element.101.part_ref, ...), custom_call_target="tpu_custom_call" | custom-call | tf_op jit(solution)/shard_map/late/pallas_call | solution.py:40
  60.9 2.6 %collective-permute-done.9.refs_1_.came = bf16[4,128,128]{2,1,0:T(8,128)(2,1)S(1)} collective-permute-done((bf16[4,128,128]{2,1,0:T(8,128)(2,1)S(1)}, bf16[4,128,128]{2,1,0:T(8,128)(2,1)S(1)}, u32[]{:S(2)}, u32[]{:S(2)}) %collective-permute-start.9) | collective-permute-done | bytes 131104 | tf_op jit(solution)/shard_map/ppermute | solution.py:434
  63.6 1.3 %collective-permute-start.10 = (bf16[4,128,128]{2,1,0:T(8,128)(2,1)S(1)}, bf16[4,128,128]{2,1,0:T(8,128)(2,1)S(1)}, u32[]{:S(2)}, u32[]{:S(2)}) collective-permute-start(bf16[4,128,128]{2,1,0:T(8,128)(2,1)S(1)} %total.6), channel_id=1, source_target_pairs={{8,0},{12,4},{16,8},{20,12},{24,16},{28,20},{9,1},{13,5},{17,9},{2... | collective-permute-start | bytes 393224 | tf_op jit(solution)/shard_map/ppermute | solution.py:438
  64.9 2.3 %within.5 = (bf16[2048,128]{1,0:T(8,128)(2,1)S(1)}, bf16[256,1024]{1,0:T(8,128)(2,1)S(1)}, bf16[256,1024]{1,0:T(8,128)(2,1)S(1)}, f32[8,128]{1,0:T(8,128)S(1)}) custom-call(bf16[1024,1024]{1,0:T(8,128)(2,1)S(1)} %get-tuple-element.72.q_ref, bf16[1024,1024]{1,0:T(8,128)(2,1)S(1)} %get-tuple-element.73.k_ref, bf16[1024,1024]{1,0:T(8,128)(2,1)S(1)} %get-tuple-element.74.v_ref, ...), custom_call_target="tpu_custom_call" | custom-call | tf_op jit(solution)/shard_map/within/pallas_call | solution.py:40
  67.2 3.2 %collective-permute-done.10.refs_2_.refs_0_ = bf16[4,128,128]{2,1,0:T(8,128)(2,1)S(1)} collective-permute-done((bf16[4,128,128]{2,1,0:T(8,128)(2,1)S(1)}, bf16[4,128,128]{2,1,0:T(8,128)(2,1)S(1)}, u32[]{:S(2)}, u32[]{:S(2)}) %collective-permute-start.10) | collective-permute-done | bytes 131104 | tf_op jit(solution)/shard_map/ppermute | solution.py:438
  70.5 1.5 %collective-permute-start.11 = (bf16[4,128,128]{2,1,0:T(8,128)(2,1)S(1)}, bf16[4,128,128]{2,1,0:T(8,128)(2,1)S(1)}, u32[]{:S(2)}, u32[]{:S(2)}) collective-permute-start(bf16[4,128,128]{2,1,0:T(8,128)(2,1)S(1)} %total.7), channel_id=1, source_target_pairs={{16,0},{20,4},{24,8},{28,12},{17,1},{21,5},{25,9},{29,13},{18,2},{... | collective-permute-start | bytes 393224 | tf_op jit(solution)/shard_map/ppermute | solution.py:438
  72.0 2.3 %within.6 = (bf16[2048,128]{1,0:T(8,128)(2,1)S(1)}, bf16[256,1024]{1,0:T(8,128)(2,1)S(1)}, bf16[256,1024]{1,0:T(8,128)(2,1)S(1)}, f32[8,128]{1,0:T(8,128)S(1)}) custom-call(bf16[1024,1024]{1,0:T(8,128)(2,1)S(1)} %get-tuple-element.72.q_ref, bf16[1024,1024]{1,0:T(8,128)(2,1)S(1)} %get-tuple-element.73.k_ref, bf16[1024,1024]{1,0:T(8,128)(2,1)S(1)} %get-tuple-element.74.v_ref, ...), custom_call_target="tpu_custom_call" | custom-call | tf_op jit(solution)/shard_map/within/pallas_call | solution.py:40
  74.3 3.5 %within.7 = (bf16[8192,128]{1,0:T(8,128)(2,1)}, bf16[256,1024]{1,0:T(8,128)(2,1)S(1)}, bf16[256,1024]{1,0:T(8,128)(2,1)S(1)}, f32[8,128]{1,0:T(8,128)S(1)}) custom-call(bf16[1024,1024]{1,0:T(8,128)(2,1)S(1)} %get-tuple-element.72.q_ref, bf16[1024,1024]{1,0:T(8,128)(2,1)S(1)} %get-tuple-element.73.k_ref, bf16[1024,1024]{1,0:T(8,128)(2,1)S(1)} %get-tuple-element.74.v_ref, ...), custom_call_target="tpu_custom_call" | custom-call | tf_op jit(solution)/shard_map/within/pallas_call | solution.py:40
  77.8 1.9 %collective-permute-done.11.refs_1_ = bf16[4,128,128]{2,1,0:T(8,128)(2,1)S(1)} collective-permute-done((bf16[4,128,128]{2,1,0:T(8,128)(2,1)S(1)}, bf16[4,128,128]{2,1,0:T(8,128)(2,1)S(1)}, u32[]{:S(2)}, u32[]{:S(2)}) %collective-permute-start.11) | collective-permute-done | bytes 131104 | tf_op jit(solution)/shard_map/ppermute | solution.py:438
  79.8 1.7 %collective-permute-start.12 = (bf16[4,128,128]{2,1,0:T(8,128)(2,1)S(1)}, bf16[4,128,128]{2,1,0:T(8,128)(2,1)S(1)}, u32[]{:S(2)}, u32[]{:S(2)}) collective-permute-start(bf16[4,128,128]{2,1,0:T(8,128)(2,1)S(1)} %get-tuple-element.123), channel_id=1, source_target_pairs={{0,4},{4,0},{8,12},{12,8},{16,20},{20,16},{24,28},{28,24},{1,5},{5... | collective-permute-start | bytes 393224 | tf_op jit(solution)/shard_map/ppermute | solution.py:434
  81.6 1.1 %finish.2 = (f32[8192,128]{1,0:T(8,128)S(1)}, f32[8192,128]{1,0:T(8,128)S(1)}, f32[8,128]{1,0:T(8,128)S(1)}) custom-call(bf16[1024,1024]{1,0:T(8,128)(2,1)S(1)} %get-tuple-element.73.k_ref, bf16[1024,1024]{1,0:T(8,128)(2,1)S(1)} %get-tuple-element.74.v_ref, bf16[4,128,128]{2,1,0:T(8,128)(2,1)S(1)} %get-tuple-element.124.suffix_ref, ...), custom_call_target="tpu_custom_call" | custom-call | tf_op jit(solution)/shard_map/finish/pallas_call | solution.py:40
  82.7 2.2 %collective-permute-done.12.suffix_ref = bf16[4,128,128]{2,1,0:T(8,128)(2,1)S(1)} collective-permute-done((bf16[4,128,128]{2,1,0:T(8,128)(2,1)S(1)}, bf16[4,128,128]{2,1,0:T(8,128)(2,1)S(1)}, u32[]{:S(2)}, u32[]{:S(2)}) %collective-permute-start.12) | collective-permute-done | bytes 131104 | tf_op jit(solution)/shard_map/ppermute | solution.py:434
  84.9 3.0 %finish.3 = (bf16[8192,128]{1,0:T(8,128)(2,1)}, bf16[8192,128]{1,0:T(8,128)(2,1)}, f32[8192,128]{1,0:T(8,128)S(1)}, f32[8192,128]{1,0:T(8,128)S(1)}) custom-call(bf16[1024,1024]{1,0:T(8,128)(2,1)S(1)} %get-tuple-element.73.k_ref, bf16[1024,1024]{1,0:T(8,128)(2,1)S(1)} %get-tuple-element.74.v_ref, ...), custom_call_target="tpu_custom_call", output_to_operand_aliasing={{2}: (12, {}), {3}: (13, {})} | custom-call | tf_op jit(solution)/shard_map/finish/pallas_call | solution.py:40
  (15 shorter events, 1.9 us)
Async XLA Ops:
  0.6 15.7 %collective-permute-start.3 = (bf16[1024,1024]{1,0:T(8,128)(2,1)}, bf16[1024,1024]{1,0:T(8,128)(2,1)S(1)}, u32[]{:S(2)}, u32[]{:S(2)}) collective-permute-start(bf16[1024,1024]{1,0:T(8,128)(2,1)} %source.1), channel_id=1, source_target_pairs={{0,1},{1,0},{2,3},{3,2},{4,5},{5,4},{6,7},{7,6},{8,9},{9,8},{10,11... | collective-permute-start | bytes 6291464 | tf_op jit(solution)/shard_map/ppermute | solution.py:434
  1.1 15.2 %copy-start = (bf16[1024,4096]{1,0:T(8,128)(2,1)S(1)}, bf16[1024,4096]{1,0:T(8,128)(2,1)}, u32[]{:S(2)}) copy-start(bf16[1024,4096]{1,0:T(8,128)(2,1)} %w_ref.7) | copy-start | bytes 25165828
  2.8 37.6 %collective-permute-start.1 = (bf16[768,1024]{1,0:T(8,128)(2,1)S(1)}, bf16[768,1024]{1,0:T(8,128)(2,1)S(1)}, u32[]{:S(2)}, u32[]{:S(2)}) collective-permute-start(bf16[768,1024]{1,0:T(8,128)(2,1)S(1)} %get-tuple-element.78.refs_0_), channel_id=1, source_target_pairs={{0,2},{1,3},{2,0},{3,1},{4,6},{5,7},{6,4},{7,5},{8,10},{9,11},{10,... | collective-permute-start | bytes 4718600 | tf_op jit(solution)/shard_map/ppermute | solution.py:434
  10.6 5.7 %collective-permute-start.2 = (bf16[4,128,128]{2,1,0:T(8,128)(2,1)S(1)}, bf16[4,128,128]{2,1,0:T(8,128)(2,1)S(1)}, u32[]{:S(2)}, u32[]{:S(2)}) collective-permute-start(bf16[4,128,128]{2,1,0:T(8,128)(2,1)S(1)} %get-tuple-element.80), channel_id=1, source_target_pairs={{0,4},{4,0},{8,12},{12,8},{16,20},{20,16},{24,28},{28,24},{1,5},{5... | collective-permute-start | bytes 393224 | tf_op jit(solution)/shard_map/ppermute | solution.py:434
  21.6 6.0 %collective-permute-start.4 = (bf16[4,128,128]{2,1,0:T(8,128)(2,1)S(1)}, bf16[4,128,128]{2,1,0:T(8,128)(2,1)S(1)}, u32[]{:S(2)}, u32[]{:S(2)}) collective-permute-start(bf16[4,128,128]{2,1,0:T(8,128)(2,1)S(1)} %total.4), channel_id=1, source_target_pairs={{0,8},{4,12},{8,16},{12,20},{16,24},{20,28},{1,9},{5,13},{9,17},{1... | collective-permute-start | bytes 393224 | tf_op jit(solution)/shard_map/ppermute | solution.py:438
  27.7 7.9 %collective-permute-start.5 = (bf16[4,128,128]{2,1,0:T(8,128)(2,1)S(1)}, bf16[4,128,128]{2,1,0:T(8,128)(2,1)S(1)}, u32[]{:S(2)}, u32[]{:S(2)}) collective-permute-start(bf16[4,128,128]{2,1,0:T(8,128)(2,1)S(1)} %total.5), channel_id=1, source_target_pairs={{0,16},{4,20},{8,24},{12,28},{1,17},{5,21},{9,25},{13,29},{2,18},{... | collective-permute-start | bytes 393224 | tf_op jit(solution)/shard_map/ppermute | solution.py:438
  40.5 3.4 %collective-permute-start.6 = (bf16[768,1024]{1,0:T(8,128)(2,1)S(1)}, bf16[768,1024]{1,0:T(8,128)(2,1)S(1)}, u32[]{:S(2)}, u32[]{:S(2)}) collective-permute-start(bf16[768,1024]{1,0:T(8,128)(2,1)S(1)} %collective-permute-done.1.refs_0_), channel_id=1, source_target_pairs={{0,1},{1,0},{2,3},{3,2},{4,5},{5,4},{6,7},{7,6},{8,9},{9,8},{10,11... | collective-permute-start | bytes 4718600 | tf_op jit(solution)/shard_map/ppermute | solution.py:434
  40.5 14.3 %collective-permute-start = (bf16[256,1024]{1,0:T(8,128)(2,1)S(1)}, bf16[256,1024]{1,0:T(8,128)(2,1)S(1)}, u32[]{:S(2)}, u32[]{:S(2)}) collective-permute-start(bf16[256,1024]{1,0:T(8,128)(2,1)S(1)} %get-tuple-element.77.refs_1_), channel_id=1, source_target_pairs={{0,2},{1,3},{2,0},{3,1},{4,6},{5,7},{6,4},{7,5},{8,10},{9,11},{10,... | collective-permute-start | bytes 1572872 | tf_op jit(solution)/shard_map/ppermute | solution.py:434
  42.2 8.5 %collective-permute-start.7 = (bf16[4,128,128]{2,1,0:T(8,128)(2,1)S(1)}, bf16[4,128,128]{2,1,0:T(8,128)(2,1)S(1)}, u32[]{:S(2)}, u32[]{:S(2)}) collective-permute-start(bf16[4,128,128]{2,1,0:T(8,128)(2,1)S(1)} %get-tuple-element.96), channel_id=1, source_target_pairs={{0,4},{4,0},{8,12},{12,8},{16,20},{20,16},{24,28},{28,24},{1,5},{5... | collective-permute-start | bytes 393224 | tf_op jit(solution)/shard_map/ppermute | solution.py:434
  54.8 1.9 %collective-permute-start.8 = (bf16[256,1024]{1,0:T(8,128)(2,1)S(1)}, bf16[256,1024]{1,0:T(8,128)(2,1)S(1)}, u32[]{:S(2)}, u32[]{:S(2)}) collective-permute-start(bf16[256,1024]{1,0:T(8,128)(2,1)S(1)} %collective-permute-done.a_ref), channel_id=1, source_target_pairs={{0,1},{1,0},{2,3},{3,2},{4,5},{5,4},{6,7},{7,6},{8,9},{9,8},{10,11... | collective-permute-start | bytes 1572872 | tf_op jit(solution)/shard_map/ppermute | solution.py:434
  57.9 5.6 %collective-permute-start.9 = (bf16[4,128,128]{2,1,0:T(8,128)(2,1)S(1)}, bf16[4,128,128]{2,1,0:T(8,128)(2,1)S(1)}, u32[]{:S(2)}, u32[]{:S(2)}) collective-permute-start(bf16[4,128,128]{2,1,0:T(8,128)(2,1)S(1)} %get-tuple-element.109), channel_id=1, source_target_pairs={{0,4},{4,0},{8,12},{12,8},{16,20},{20,16},{24,28},{28,24},{1,5},{5... | collective-permute-start | bytes 393224 | tf_op jit(solution)/shard_map/ppermute | solution.py:434
  63.6 6.9 %collective-permute-start.10 = (bf16[4,128,128]{2,1,0:T(8,128)(2,1)S(1)}, bf16[4,128,128]{2,1,0:T(8,128)(2,1)S(1)}, u32[]{:S(2)}, u32[]{:S(2)}) collective-permute-start(bf16[4,128,128]{2,1,0:T(8,128)(2,1)S(1)} %total.6), channel_id=1, source_target_pairs={{8,0},{12,4},{16,8},{20,12},{24,16},{28,20},{9,1},{13,5},{17,9},{2... | collective-permute-start | bytes 393224 | tf_op jit(solution)/shard_map/ppermute | solution.py:438
  70.5 9.2 %collective-permute-start.11 = (bf16[4,128,128]{2,1,0:T(8,128)(2,1)S(1)}, bf16[4,128,128]{2,1,0:T(8,128)(2,1)S(1)}, u32[]{:S(2)}, u32[]{:S(2)}) collective-permute-start(bf16[4,128,128]{2,1,0:T(8,128)(2,1)S(1)} %total.7), channel_id=1, source_target_pairs={{16,0},{20,4},{24,8},{28,12},{17,1},{21,5},{25,9},{29,13},{18,2},{... | collective-permute-start | bytes 393224 | tf_op jit(solution)/shard_map/ppermute | solution.py:438
  79.8 5.0 %collective-permute-start.12 = (bf16[4,128,128]{2,1,0:T(8,128)(2,1)S(1)}, bf16[4,128,128]{2,1,0:T(8,128)(2,1)S(1)}, u32[]{:S(2)}, u32[]{:S(2)}) collective-permute-start(bf16[4,128,128]{2,1,0:T(8,128)(2,1)S(1)} %get-tuple-element.123), channel_id=1, source_target_pairs={{0,4},{4,0},{8,12},{12,8},{16,20},{20,16},{24,28},{28,24},{1,5},{5... | collective-permute-start | bytes 393224 | tf_op jit(solution)/shard_map/ppermute | solution.py:434

commit v10 on v9

--- a/solution.py
+++ b/solution.py
@@ -434,8 +434,9 @@
     return lax.ppermute(array, axis, [(i, i ^ bit) for i in range(size)])
 
 
-def shifted(array, size, step):
-    return lax.ppermute(array, "ctx", [(i, i + step) for i in range(size) if 0 <= i + step < size])
+def shifted(array, size, step, pair=None):
+    moves = [(i, i + step) for i in range(size) if 0 <= i + step < size]
+    return lax.ppermute(array, "ctx", [(i, j) for i, j in moves if pair is None or j // 2 == pair])
 
 
 class Order:
@@ -470,6 +471,18 @@
     yield None
     like = shape(keep[0].shape, BF16)
     step = 2
+    if size == 8:
+        third, fourth = (2, 3) if direction == 1 else (1, 0)
+        for part in terms:
+            total = order.tie(call(total_kernel, "total", part, [WHOLE] * 2, like, WHOLE))
+            part.append(shifted(total, size, direction * 2))
+            part.append(shifted(total, size, direction * 4, third))
+        yield None
+        for part in terms:
+            total = call(total_kernel, "total", part[2:], [WHOLE] * 2, like, WHOLE)
+            part.append(shifted(order.tie(total), size, direction * 2, fourth))
+        yield None
+        step = size
     while step < size:
         for part in terms:
             total = call(total_kernel, "total", part, [WHOLE] * len(part), like, WHOLE)
@@ -494,7 +507,7 @@
     order = Order()
     *pieces, order.token = cut(d_layer, groups)
     across = {c: swap(piece, "head", n_head, near) for (c, _), piece in zip(groups, pieces)}
-    beside = swap(d_layer, "head", n_head, far)
+    beside = swap(order.tie(d_layer), "head", n_head, far)
 
     flat = (tokens * heads, dk)
     q, k, v, qt, vt, before, scale, keep, send, order.token = prepare(
@@ -545,7 +558,7 @@
     d[0] = (low_keep, low_send, None)
     backward = scan_states([keep], [send], n_ctx, -1, order)
     next(backward)
-    plan = [[c for c in range(n) if c > 1 and c not in dq], [1, 0]]
+    plan = [[c for c in reversed(range(1, n)) if c not in dq], [0]]
     suffix = None
     while suffix is None:
         suffix = next(backward)

time: 88.3 us -> 88.7 us (level)
  waiting for transfers between devices: 26.9 us -> 29.3 us
  starting transfers between devices: 23.2 us -> 21.3 us
    ppermute x9, waiting for transfers between devices: 16.8 us -> 20.5 us  [swap(): return lax.ppermute(array, axis, [(i, i ^ bit) for i in range(size)])]
    ppermute x4 -> x6, starting transfers between devices: 11.7 us -> 9.9 us  [shifted(): lax.ppermute(array, 'ctx', [(i, j) for i, j in moves if pair is None or j...]
    ppermute x4 -> x6, waiting for transfers between devices: 10.2 us -> 8.74 us  [shifted(): lax.ppermute(array, 'ctx', [(i, j) for i, j in moves if pair is None or j...]
  transfers between devices with their start and end apart: 13 -> 15, of which waited for: 11 -> 11; matrix products, arithmetic and copies ran while one was open for 0% -> 0% of each run, Pallas kernels for 37% -> 35%
where the time goes in v10:
time: 88.7 us; the launch traced here: 88.5 us
  Pallas kernels  37 us (42%)
  waiting for transfers between devices  29.3 us (33%)
  starting transfers between devices  21.3 us (24%)
  between operations  1 us (1%)
    pallas_call x19, Pallas kernels, call(): pl.pallas_call(kernel, in_specs=in_specs, out_specs=out_specs, out_shape=...  37 us
    ppermute x9, waiting for transfers between devices, swap(): return lax.ppermute(array, axis, [(i, i ^ bit) for i in range(size)])  20.5 us
    ppermute x9, starting transfers between devices, swap(): return lax.ppermute(array, axis, [(i, i ^ bit) for i in range(size)])  11.4 us
    ppermute x6, starting transfers between devices, shifted(): lax.ppermute(array, 'ctx', [(i, j) for i, j in moves if pair is None or j...  9.9 us
    ppermute x6, waiting for transfers between devices, shifted(): lax.ppermute(array, 'ctx', [(i, j) for i, j in moves if pair is None or j...  8.74 us
  transfers between devices with their start and end apart: 15, of which 11 were waited for; matrix products, arithmetic and copies ran while one was open for 0% of the time, Pallas kernels for 35%

profile of v10, /device:TPU:0, one launch (start us, length us, event | category | flops | bytes accessed | tf_op | source)
XLA Modules:
  0.0 88.5 jit_solution(5323789190026589662)
XLA Ops:
  0.6 1.7 %cut.1 = (bf16[768,1024]{1,0:T(8,128)(2,1)S(1)}, bf16[256,1024]{1,0:T(8,128)(2,1)S(1)}, f32[8,128]{1,0:T(8,128)S(1)}) custom-call(bf16[1024,1024]{1,0:T(8,128)(2,1)} %source.1), custom_call_target="tpu_custom_call" | custom-call | tf_op jit(solution)/shard_map/cut/pallas_call | solution.py:40
  2.9 2.6 %collective-permute-start.1 = (bf16[768,1024]{1,0:T(8,128)(2,1)S(1)}, bf16[768,1024]{1,0:T(8,128)(2,1)S(1)}, u32[]{:S(2)}, u32[]{:S(2)}) collective-permute-start(bf16[768,1024]{1,0:T(8,128)(2,1)S(1)} %get-tuple-element.81.refs_0_), channel_id=1, source_target_pairs={{0,2},{1,3},{2,0},{3,1},{4,6},{5,7},{6,4},{7,5},{8,10},{9,11},{10,... | collective-permute-start | bytes 4718600 | tf_op jit(solution)/shard_map/ppermute | solution.py:434
  5.4 5.2 %prepare.1 = (bf16[1024,1024]{1,0:T(8,128)(2,1)S(1)}, bf16[1024,1024]{1,0:T(8,128)(2,1)S(1)}, bf16[1024,1024]{1,0:T(8,128)(2,1)S(1)}, bf16[1024,1024]{1,0:T(8,12...) custom-call(bf16[8192,128]{1,0:T(8,128)(2,1)} %bitcast.6, ...), custom_call_target="tpu_custom_call" | custom-call | tf_op jit(solution)/shard_map/prepare/pallas_call | solution.py:40
  10.6 1.6 %collective-permute-start.2 = (bf16[4,128,128]{2,1,0:T(8,128)(2,1)S(1)}, bf16[4,128,128]{2,1,0:T(8,128)(2,1)S(1)}, u32[]{:S(2)}, u32[]{:S(2)}) collective-permute-start(bf16[4,128,128]{2,1,0:T(8,128)(2,1)S(1)} %get-tuple-element.83), channel_id=1, source_target_pairs={{0,4},{4,0},{8,12},{12,8},{16,20},{20,16},{24,28},{28,24},{1,5},{5... | collective-permute-start | bytes 393224 | tf_op jit(solution)/shard_map/ppermute | solution.py:434
  12.2 4.0 %collective-permute-done.2.refs_1_.came = bf16[4,128,128]{2,1,0:T(8,128)(2,1)S(1)} collective-permute-done((bf16[4,128,128]{2,1,0:T(8,128)(2,1)S(1)}, bf16[4,128,128]{2,1,0:T(8,128)(2,1)S(1)}, u32[]{:S(2)}, u32[]{:S(2)}) %collective-permute-start.2) | collective-permute-done | bytes 131104 | tf_op jit(solution)/shard_map/ppermute | solution.py:434
  16.3 5.2 %early.1 = (f32[1024,1024]{1,0:T(8,128)S(1)}, f32[8,128]{1,0:T(8,128)S(1)}) custom-call(bf16[768,1024]{1,0:T(8,128)(2,1)S(1)} %get-tuple-element.81.refs_0_, bf16[256,1024]{1,0:T(8,128)(2,1)S(1)} %get-tuple-element.80.refs_1_, bf16[1024,1024]{1,0:T(8,128)(2,1)S(1)} %collective-permute-done.3.refs_2_, bf16[1024,4096]{1,0:T(8,128)(2,1)S(1)} %copy-done, ...), custom_call_target="tpu_custom_call" | custom-call | tf_op jit(solution)/shard_map/early/pallas_call | solution.py:40
  21.5 4.5 %collective-permute-start.5 = (bf16[4,128,128]{2,1,0:T(8,128)(2,1)S(1)}, bf16[4,128,128]{2,1,0:T(8,128)(2,1)S(1)}, u32[]{:S(2)}, u32[]{:S(2)}) collective-permute-start(bf16[4,128,128]{2,1,0:T(8,128)(2,1)S(1)} %total.4), channel_id=1, source_target_pairs={{0,16},{4,20},{1,17},{5,21},{2,18},{6,22},{3,19},{7,23}} | collective-permute-start | bytes 393224 | tf_op jit(solution)/shard_map/ppermute | solution.py:439
  26.0 1.3 %collective-permute-start.4 = (bf16[4,128,128]{2,1,0:T(8,128)(2,1)S(1)}, bf16[4,128,128]{2,1,0:T(8,128)(2,1)S(1)}, u32[]{:S(2)}, u32[]{:S(2)}) collective-permute-start(bf16[4,128,128]{2,1,0:T(8,128)(2,1)S(1)} %total.4), channel_id=1, source_target_pairs={{0,8},{4,12},{8,16},{12,20},{16,24},{20,28},{1,9},{5,13},{9,17},{1... | collective-permute-start | bytes 393224 | tf_op jit(solution)/shard_map/ppermute | solution.py:439
  27.3 2.3 %collective-permute-done.5.refs_1_ = bf16[4,128,128]{2,1,0:T(8,128)(2,1)S(1)} collective-permute-done((bf16[4,128,128]{2,1,0:T(8,128)(2,1)S(1)}, bf16[4,128,128]{2,1,0:T(8,128)(2,1)S(1)}, u32[]{:S(2)}, u32[]{:S(2)}) %collective-permute-start.5) | collective-permute-done | bytes 131104 | tf_op jit(solution)/shard_map/ppermute | solution.py:439
  29.7 1.4 %collective-permute-done.4.refs_0_ = bf16[4,128,128]{2,1,0:T(8,128)(2,1)S(1)} collective-permute-done((bf16[4,128,128]{2,1,0:T(8,128)(2,1)S(1)}, bf16[4,128,128]{2,1,0:T(8,128)(2,1)S(1)}, u32[]{:S(2)}, u32[]{:S(2)}) %collective-permute-start.4) | collective-permute-done | bytes 131104 | tf_op jit(solution)/shard_map/ppermute | solution.py:439
  31.9 8.5 %collective-permute-done.1.refs_0_ = bf16[768,1024]{1,0:T(8,128)(2,1)S(1)} collective-permute-done((bf16[768,1024]{1,0:T(8,128)(2,1)S(1)}, bf16[768,1024]{1,0:T(8,128)(2,1)S(1)}, u32[]{:S(2)}, u32[]{:S(2)}) %collective-permute-start.1) | collective-permute-done | bytes 1572896 | tf_op jit(solution)/shard_map/ppermute | solution.py:434
  40.4 1.8 %collective-permute-start = (bf16[256,1024]{1,0:T(8,128)(2,1)S(1)}, bf16[256,1024]{1,0:T(8,128)(2,1)S(1)}, u32[]{:S(2)}, u32[]{:S(2)}) collective-permute-start(bf16[256,1024]{1,0:T(8,128)(2,1)S(1)} %get-tuple-element.80.refs_1_), channel_id=1, source_target_pairs={{0,2},{1,3},{2,0},{3,1},{4,6},{5,7},{6,4},{7,5},{8,10},{9,11},{10,... | collective-permute-start | bytes 1572872 | tf_op jit(solution)/shard_map/ppermute | solution.py:434
  42.2 1.5 %collective-permute-start.8 = (bf16[4,128,128]{2,1,0:T(8,128)(2,1)S(1)}, bf16[4,128,128]{2,1,0:T(8,128)(2,1)S(1)}, u32[]{:S(2)}, u32[]{:S(2)}) collective-permute-start(bf16[4,128,128]{2,1,0:T(8,128)(2,1)S(1)} %get-tuple-element.100), channel_id=1, source_target_pairs={{0,4},{4,0},{8,12},{12,8},{16,20},{20,16},{24,28},{28,24},{1,5},{5... | collective-permute-start | bytes 393224 | tf_op jit(solution)/shard_map/ppermute | solution.py:434
  43.8 6.9 %late.3 = (bf16[768,1024]{1,0:T(8,128)(2,1)S(1)}, f32[8,128]{1,0:T(8,128)S(1)}, f32[3,8,128,128]{3,2,1,0:T(8,128)S(1)}) custom-call(bf16[768,1024]{1,0:T(8,128)(2,1)S(1)} %collective-permute-done.7.b_ref, bf16[1024,4096]{1,0:T(8,128)(2,1)S(1)} %copy-done, f32[1024,1024]{1,0:T(8,128)S(1)} %get-tuple-element.94.part_ref, ...), custom_call_target="tpu_custom_call" | custom-call | tf_op jit(solution)/shard_map/late/pallas_call | solution.py:40
  50.7 2.1 %within.4 = (bf16[2048,128]{1,0:T(8,128)(2,1)S(1)}, bf16[256,1024]{1,0:T(8,128)(2,1)S(1)}, bf16[256,1024]{1,0:T(8,128)(2,1)S(1)}, f32[8,128]{1,0:T(8,128)S(1)}) custom-call(bf16[1024,1024]{1,0:T(8,128)(2,1)S(1)} %get-tuple-element.75.q_ref, bf16[1024,1024]{1,0:T(8,128)(2,1)S(1)} %get-tuple-element.76.k_ref, bf16[1024,1024]{1,0:T(8,128)(2,1)S(1)} %get-tuple-element.77.v_ref, ...), custom_call_target="tpu_custom_call" | custom-call | tf_op jit(solution)/shard_map/within/pallas_call | solution.py:40
  52.8 1.9 %collective-permute-done.a_ref = bf16[256,1024]{1,0:T(8,128)(2,1)S(1)} collective-permute-done((bf16[256,1024]{1,0:T(8,128)(2,1)S(1)}, bf16[256,1024]{1,0:T(8,128)(2,1)S(1)}, u32[]{:S(2)}, u32[]{:S(2)}) %collective-permute-start) | collective-permute-done | bytes 524320 | tf_op jit(solution)/shard_map/ppermute | solution.py:434
  55.7 1.0 %collective-permute-done.9.b_ref = bf16[256,1024]{1,0:T(8,128)(2,1)S(1)} collective-permute-done((bf16[256,1024]{1,0:T(8,128)(2,1)S(1)}, bf16[256,1024]{1,0:T(8,128)(2,1)S(1)}, u32[]{:S(2)}, u32[]{:S(2)}) %collective-permute-start.9) | collective-permute-done | bytes 524320 | tf_op jit(solution)/shard_map/ppermute | solution.py:434
  56.7 1.2 %late.4 = (bf16[256,512]{1,0:T(8,128)(2,1)S(1)}, f32[8,128]{1,0:T(8,128)S(1)}, bf16[4,128,128]{2,1,0:T(8,128)(2,1)S(1)}, bf16[1024,256]{1,0:T(8,128)(2,1)S(1)}) custom-call(bf16[256,1024]{1,0:T(8,128)(2,1)S(1)} %collective-permute-done.9.b_ref, bf16[1024,4096]{1,0:T(8,128)(2,1)S(1)} %copy-done, f32[256,1024]{1,0:T(8,128)S(1)} %get-tuple-element.105.part_ref, ...), custom_call_target="tpu_custom_call" | custom-call | tf_op jit(solution)/shard_map/late/pallas_call | solution.py:40
  57.9 1.8 %collective-permute-start.10 = (bf16[4,128,128]{2,1,0:T(8,128)(2,1)S(1)}, bf16[4,128,128]{2,1,0:T(8,128)(2,1)S(1)}, u32[]{:S(2)}, u32[]{:S(2)}) collective-permute-start(bf16[4,128,128]{2,1,0:T(8,128)(2,1)S(1)} %get-tuple-element.113), channel_id=1, source_target_pairs={{0,4},{4,0},{8,12},{12,8},{16,20},{20,16},{24,28},{28,24},{1,5},{5... | collective-permute-start | bytes 393224 | tf_op jit(solution)/shard_map/ppermute | solution.py:434
  59.7 1.2 %late.5 = (bf16[256,512]{1,0:T(8,128)(2,1)S(1)}, f32[8,128]{1,0:T(8,128)S(1)}, bf16[4,128,128]{2,1,0:T(8,128)(2,1)S(1)}) custom-call(bf16[1024,256]{1,0:T(8,128)(2,1)S(1)} %get-tuple-element.108.b_ref, bf16[1024,4096]{1,0:T(8,128)(2,1)S(1)} %copy-done, f32[256,1024]{1,0:T(8,128)S(1)} %get-tuple-element.105.part_ref, ...), custom_call_target="tpu_custom_call" | custom-call | tf_op jit(solution)/shard_map/late/pallas_call | solution.py:40
  60.9 2.6 %collective-permute-done.10.refs_1_.came = bf16[4,128,128]{2,1,0:T(8,128)(2,1)S(1)} collective-permute-done((bf16[4,128,128]{2,1,0:T(8,128)(2,1)S(1)}, bf16[4,128,128]{2,1,0:T(8,128)(2,1)S(1)}, u32[]{:S(2)}, u32[]{:S(2)}) %collective-permute-start.10) | collective-permute-done | bytes 131104 | tf_op jit(solution)/shard_map/ppermute | solution.py:434
  64.2 1.5 %collective-permute-start.11 = (bf16[4,128,128]{2,1,0:T(8,128)(2,1)S(1)}, bf16[4,128,128]{2,1,0:T(8,128)(2,1)S(1)}, u32[]{:S(2)}, u32[]{:S(2)}) collective-permute-start(bf16[4,128,128]{2,1,0:T(8,128)(2,1)S(1)} %total.6), channel_id=1, source_target_pairs={{8,0},{12,4},{16,8},{20,12},{24,16},{28,20},{9,1},{13,5},{17,9},{2... | collective-permute-start | bytes 393224 | tf_op jit(solution)/shard_map/ppermute | solution.py:439
  65.7 2.3 %within.5 = (bf16[2048,128]{1,0:T(8,128)(2,1)S(1)}, bf16[256,1024]{1,0:T(8,128)(2,1)S(1)}, bf16[256,1024]{1,0:T(8,128)(2,1)S(1)}, f32[8,128]{1,0:T(8,128)S(1)}) custom-call(bf16[1024,1024]{1,0:T(8,128)(2,1)S(1)} %get-tuple-element.75.q_ref, bf16[1024,1024]{1,0:T(8,128)(2,1)S(1)} %get-tuple-element.76.k_ref, bf16[1024,1024]{1,0:T(8,128)(2,1)S(1)} %get-tuple-element.77.v_ref, ...), custom_call_target="tpu_custom_call" | custom-call | tf_op jit(solution)/shard_map/within/pallas_call | solution.py:40
  68.1 2.3 %within.6 = (bf16[2048,128]{1,0:T(8,128)(2,1)S(1)}, bf16[256,1024]{1,0:T(8,128)(2,1)S(1)}, bf16[256,1024]{1,0:T(8,128)(2,1)S(1)}, f32[8,128]{1,0:T(8,128)S(1)}) custom-call(bf16[1024,1024]{1,0:T(8,128)(2,1)S(1)} %get-tuple-element.75.q_ref, bf16[1024,1024]{1,0:T(8,128)(2,1)S(1)} %get-tuple-element.76.k_ref, bf16[1024,1024]{1,0:T(8,128)(2,1)S(1)} %get-tuple-element.77.v_ref, ...), custom_call_target="tpu_custom_call" | custom-call | tf_op jit(solution)/shard_map/within/pallas_call | solution.py:40
  70.4 1.1 %collective-permute-done.11.refs_0_ = bf16[4,128,128]{2,1,0:T(8,128)(2,1)S(1)} collective-permute-done((bf16[4,128,128]{2,1,0:T(8,128)(2,1)S(1)}, bf16[4,128,128]{2,1,0:T(8,128)(2,1)S(1)}, u32[]{:S(2)}, u32[]{:S(2)}) %collective-permute-start.11) | collective-permute-done | bytes 131104 | tf_op jit(solution)/shard_map/ppermute | solution.py:439
  71.6 1.3 %collective-permute-start.13 = (bf16[4,128,128]{2,1,0:T(8,128)(2,1)S(1)}, bf16[4,128,128]{2,1,0:T(8,128)(2,1)S(1)}, u32[]{:S(2)}, u32[]{:S(2)}) collective-permute-start(bf16[4,128,128]{2,1,0:T(8,128)(2,1)S(1)} %total.7), channel_id=1, source_target_pairs={{8,0},{12,4},{9,1},{13,5},{10,2},{14,6},{11,3},{15,7}} | collective-permute-start | bytes 393224 | tf_op jit(solution)/shard_map/ppermute | solution.py:439
  72.9 3.5 %within.7 = (bf16[8192,128]{1,0:T(8,128)(2,1)}, bf16[256,1024]{1,0:T(8,128)(2,1)S(1)}, bf16[256,1024]{1,0:T(8,128)(2,1)S(1)}, f32[8,128]{1,0:T(8,128)S(1)}) custom-call(bf16[1024,1024]{1,0:T(8,128)(2,1)S(1)} %get-tuple-element.75.q_ref, bf16[1024,1024]{1,0:T(8,128)(2,1)S(1)} %get-tuple-element.76.k_ref, bf16[1024,1024]{1,0:T(8,128)(2,1)S(1)} %get-tuple-element.77.v_ref, ...), custom_call_target="tpu_custom_call" | custom-call | tf_op jit(solution)/shard_map/within/pallas_call | solution.py:40
  76.3 3.9 %collective-permute-done.13.refs_2_ = bf16[4,128,128]{2,1,0:T(8,128)(2,1)S(1)} collective-permute-done((bf16[4,128,128]{2,1,0:T(8,128)(2,1)S(1)}, bf16[4,128,128]{2,1,0:T(8,128)(2,1)S(1)}, u32[]{:S(2)}, u32[]{:S(2)}) %collective-permute-start.13) | collective-permute-done | bytes 131104 | tf_op jit(solution)/shard_map/ppermute | solution.py:439
  80.3 1.6 %collective-permute-start.14 = (bf16[4,128,128]{2,1,0:T(8,128)(2,1)S(1)}, bf16[4,128,128]{2,1,0:T(8,128)(2,1)S(1)}, u32[]{:S(2)}, u32[]{:S(2)}) collective-permute-start(bf16[4,128,128]{2,1,0:T(8,128)(2,1)S(1)} %get-tuple-element.127), channel_id=1, source_target_pairs={{0,4},{4,0},{8,12},{12,8},{16,20},{20,16},{24,28},{28,24},{1,5},{5... | collective-permute-start | bytes 393224 | tf_op jit(solution)/shard_map/ppermute | solution.py:434
  81.9 1.1 %finish.2 = (f32[8192,128]{1,0:T(8,128)S(1)}, f32[8192,128]{1,0:T(8,128)S(1)}, f32[8,128]{1,0:T(8,128)S(1)}) custom-call(bf16[1024,1024]{1,0:T(8,128)(2,1)S(1)} %get-tuple-element.76.k_ref, bf16[1024,1024]{1,0:T(8,128)(2,1)S(1)} %get-tuple-element.77.v_ref, bf16[4,128,128]{2,1,0:T(8,128)(2,1)S(1)} %get-tuple-element.128.suffix_ref, ...), custom_call_target="tpu_custom_call" | custom-call | tf_op jit(solution)/shard_map/finish/pallas_call | solution.py:40
  83.0 2.3 %collective-permute-done.14.suffix_ref = bf16[4,128,128]{2,1,0:T(8,128)(2,1)S(1)} collective-permute-done((bf16[4,128,128]{2,1,0:T(8,128)(2,1)S(1)}, bf16[4,128,128]{2,1,0:T(8,128)(2,1)S(1)}, u32[]{:S(2)}, u32[]{:S(2)}) %collective-permute-start.14) | collective-permute-done | bytes 131104 | tf_op jit(solution)/shard_map/ppermute | solution.py:434
  85.3 3.0 %finish.3 = (bf16[8192,128]{1,0:T(8,128)(2,1)}, bf16[8192,128]{1,0:T(8,128)(2,1)}, f32[8192,128]{1,0:T(8,128)S(1)}, f32[8192,128]{1,0:T(8,128)S(1)}) custom-call(bf16[1024,1024]{1,0:T(8,128)(2,1)S(1)} %get-tuple-element.76.k_ref, bf16[1024,1024]{1,0:T(8,128)(2,1)S(1)} %get-tuple-element.77.v_ref, ...), custom_call_target="tpu_custom_call", output_to_operand_aliasing={{2}: (12, {}), {3}: (13, {})} | custom-call | tf_op jit(solution)/shard_map/finish/pallas_call | solution.py:40
  (19 shorter events, 3.3 us)
Async XLA Ops:
  0.6 15.7 %copy-start = (bf16[1024,4096]{1,0:T(8,128)(2,1)S(1)}, bf16[1024,4096]{1,0:T(8,128)(2,1)}, u32[]{:S(2)}) copy-start(bf16[1024,4096]{1,0:T(8,128)(2,1)} %w_ref.7) | copy-start | bytes 25165828
  2.3 14.0 %collective-permute-start.3 = (bf16[1024,1024]{1,0:T(8,128)(2,1)}, bf16[1024,1024]{1,0:T(8,128)(2,1)S(1)}, u32[]{:S(2)}, u32[]{:S(2)}) collective-permute-start(bf16[1024,1024]{1,0:T(8,128)(2,1)} %source.1), channel_id=1, source_target_pairs={{0,1},{1,0},{2,3},{3,2},{4,5},{5,4},{6,7},{7,6},{8,9},{9,8},{10,11... | collective-permute-start | bytes 6291464 | tf_op jit(solution)/shard_map/ppermute | solution.py:434
  2.9 37.6 %collective-permute-start.1 = (bf16[768,1024]{1,0:T(8,128)(2,1)S(1)}, bf16[768,1024]{1,0:T(8,128)(2,1)S(1)}, u32[]{:S(2)}, u32[]{:S(2)}) collective-permute-start(bf16[768,1024]{1,0:T(8,128)(2,1)S(1)} %get-tuple-element.81.refs_0_), channel_id=1, source_target_pairs={{0,2},{1,3},{2,0},{3,1},{4,6},{5,7},{6,4},{7,5},{8,10},{9,11},{10,... | collective-permute-start | bytes 4718600 | tf_op jit(solution)/shard_map/ppermute | solution.py:434
  10.6 5.6 %collective-permute-start.2 = (bf16[4,128,128]{2,1,0:T(8,128)(2,1)S(1)}, bf16[4,128,128]{2,1,0:T(8,128)(2,1)S(1)}, u32[]{:S(2)}, u32[]{:S(2)}) collective-permute-start(bf16[4,128,128]{2,1,0:T(8,128)(2,1)S(1)} %get-tuple-element.83), channel_id=1, source_target_pairs={{0,4},{4,0},{8,12},{12,8},{16,20},{20,16},{24,28},{28,24},{1,5},{5... | collective-permute-start | bytes 393224 | tf_op jit(solution)/shard_map/ppermute | solution.py:434
  21.5 8.2 %collective-permute-start.5 = (bf16[4,128,128]{2,1,0:T(8,128)(2,1)S(1)}, bf16[4,128,128]{2,1,0:T(8,128)(2,1)S(1)}, u32[]{:S(2)}, u32[]{:S(2)}) collective-permute-start(bf16[4,128,128]{2,1,0:T(8,128)(2,1)S(1)} %total.4), channel_id=1, source_target_pairs={{0,16},{4,20},{1,17},{5,21},{2,18},{6,22},{3,19},{7,23}} | collective-permute-start | bytes 393224 | tf_op jit(solution)/shard_map/ppermute | solution.py:439
  26.0 5.1 %collective-permute-start.4 = (bf16[4,128,128]{2,1,0:T(8,128)(2,1)S(1)}, bf16[4,128,128]{2,1,0:T(8,128)(2,1)S(1)}, u32[]{:S(2)}, u32[]{:S(2)}) collective-permute-start(bf16[4,128,128]{2,1,0:T(8,128)(2,1)S(1)} %total.4), channel_id=1, source_target_pairs={{0,8},{4,12},{8,16},{12,20},{16,24},{20,28},{1,9},{5,13},{9,17},{1... | collective-permute-start | bytes 393224 | tf_op jit(solution)/shard_map/ppermute | solution.py:439
  31.1 0.7 collective-permute-start.6
  40.4 3.4 %collective-permute-start.7 = (bf16[768,1024]{1,0:T(8,128)(2,1)S(1)}, bf16[768,1024]{1,0:T(8,128)(2,1)S(1)}, u32[]{:S(2)}, u32[]{:S(2)}) collective-permute-start(bf16[768,1024]{1,0:T(8,128)(2,1)S(1)} %collective-permute-done.1.refs_0_), channel_id=1, source_target_pairs={{0,1},{1,0},{2,3},{3,2},{4,5},{5,4},{6,7},{7,6},{8,9},{9,8},{10,11... | collective-permute-start | bytes 4718600 | tf_op jit(solution)/shard_map/ppermute | solution.py:434
  40.4 14.4 %collective-permute-start = (bf16[256,1024]{1,0:T(8,128)(2,1)S(1)}, bf16[256,1024]{1,0:T(8,128)(2,1)S(1)}, u32[]{:S(2)}, u32[]{:S(2)}) collective-permute-start(bf16[256,1024]{1,0:T(8,128)(2,1)S(1)} %get-tuple-element.80.refs_1_), channel_id=1, source_target_pairs={{0,2},{1,3},{2,0},{3,1},{4,6},{5,7},{6,4},{7,5},{8,10},{9,11},{10,... | collective-permute-start | bytes 1572872 | tf_op jit(solution)/shard_map/ppermute | solution.py:434
  42.2 8.5 %collective-permute-start.8 = (bf16[4,128,128]{2,1,0:T(8,128)(2,1)S(1)}, bf16[4,128,128]{2,1,0:T(8,128)(2,1)S(1)}, u32[]{:S(2)}, u32[]{:S(2)}) collective-permute-start(bf16[4,128,128]{2,1,0:T(8,128)(2,1)S(1)} %get-tuple-element.100), channel_id=1, source_target_pairs={{0,4},{4,0},{8,12},{12,8},{16,20},{20,16},{24,28},{28,24},{1,5},{5... | collective-permute-start | bytes 393224 | tf_op jit(solution)/shard_map/ppermute | solution.py:434
  54.8 1.9 %collective-permute-start.9 = (bf16[256,1024]{1,0:T(8,128)(2,1)S(1)}, bf16[256,1024]{1,0:T(8,128)(2,1)S(1)}, u32[]{:S(2)}, u32[]{:S(2)}) collective-permute-start(bf16[256,1024]{1,0:T(8,128)(2,1)S(1)} %collective-permute-done.a_ref), channel_id=1, source_target_pairs={{0,1},{1,0},{2,3},{3,2},{4,5},{5,4},{6,7},{7,6},{8,9},{9,8},{10,11... | collective-permute-start | bytes 1572872 | tf_op jit(solution)/shard_map/ppermute | solution.py:434
  57.9 5.6 %collective-permute-start.10 = (bf16[4,128,128]{2,1,0:T(8,128)(2,1)S(1)}, bf16[4,128,128]{2,1,0:T(8,128)(2,1)S(1)}, u32[]{:S(2)}, u32[]{:S(2)}) collective-permute-start(bf16[4,128,128]{2,1,0:T(8,128)(2,1)S(1)} %get-tuple-element.113), channel_id=1, source_target_pairs={{0,4},{4,0},{8,12},{12,8},{16,20},{20,16},{24,28},{28,24},{1,5},{5... | collective-permute-start | bytes 393224 | tf_op jit(solution)/shard_map/ppermute | solution.py:434
  63.6 6.8 %collective-permute-start.12 = (bf16[4,128,128]{2,1,0:T(8,128)(2,1)S(1)}, bf16[4,128,128]{2,1,0:T(8,128)(2,1)S(1)}, u32[]{:S(2)}, u32[]{:S(2)}) collective-permute-start(bf16[4,128,128]{2,1,0:T(8,128)(2,1)S(1)} %total.6), channel_id=1, source_target_pairs={{24,8},{28,12},{25,9},{29,13},{26,10},{30,14},{27,11},{31,15}} | collective-permute-start | bytes 393224 | tf_op jit(solution)/shard_map/ppermute | solution.py:439
  64.2 7.3 %collective-permute-start.11 = (bf16[4,128,128]{2,1,0:T(8,128)(2,1)S(1)}, bf16[4,128,128]{2,1,0:T(8,128)(2,1)S(1)}, u32[]{:S(2)}, u32[]{:S(2)}) collective-permute-start(bf16[4,128,128]{2,1,0:T(8,128)(2,1)S(1)} %total.6), channel_id=1, source_target_pairs={{8,0},{12,4},{16,8},{20,12},{24,16},{28,20},{9,1},{13,5},{17,9},{2... | collective-permute-start | bytes 393224 | tf_op jit(solution)/shard_map/ppermute | solution.py:439
  71.6 8.6 %collective-permute-start.13 = (bf16[4,128,128]{2,1,0:T(8,128)(2,1)S(1)}, bf16[4,128,128]{2,1,0:T(8,128)(2,1)S(1)}, u32[]{:S(2)}, u32[]{:S(2)}) collective-permute-start(bf16[4,128,128]{2,1,0:T(8,128)(2,1)S(1)} %total.7), channel_id=1, source_target_pairs={{8,0},{12,4},{9,1},{13,5},{10,2},{14,6},{11,3},{15,7}} | collective-permute-start | bytes 393224 | tf_op jit(solution)/shard_map/ppermute | solution.py:439
  80.3 5.0 %collective-permute-start.14 = (bf16[4,128,128]{2,1,0:T(8,128)(2,1)S(1)}, bf16[4,128,128]{2,1,0:T(8,128)(2,1)S(1)}, u32[]{:S(2)}, u32[]{:S(2)}) collective-permute-start(bf16[4,128,128]{2,1,0:T(8,128)(2,1)S(1)} %get-tuple-element.127), channel_id=1, source_target_pairs={{0,4},{4,0},{8,12},{12,8},{16,20},{20,16},{24,28},{28,24},{1,5},{5... | collective-permute-start | bytes 393224 | tf_op jit(solution)/shard_map/ppermute | solution.py:434

commit v11 on v9

--- a/solution.py
+++ b/solution.py
@@ -53,10 +53,13 @@
 def cut_kernel(starts, source, *refs):
     pieces, token_ref, sem = refs[: len(starts)], refs[-2], refs[-1]
     token_ref[...] = jnp.zeros_like(token_ref)
-    copies = [
-        pltpu.make_async_copy(source.at[pl.ds(start, piece.shape[0])], piece, sem.at[i])
-        for i, (start, piece) in enumerate(zip(starts, pieces))
-    ]
+    copies = []
+    for start, piece in zip(starts, pieces):
+        for row in range(0, piece.shape[0], CHUNK // 2):
+            rows = pl.ds(start + row, CHUNK // 2)
+            copies.append(
+                pltpu.make_async_copy(source.at[rows], piece.at[pl.ds(row, CHUNK // 2)], sem.at[len(copies)])
+            )
     for copy in copies:
         copy.start()
     for copy in copies:
@@ -72,7 +75,7 @@
         [ANYWHERE],
         [shape((m * CHUNK, features), d_layer.dtype) for _, m in groups] + [shape(TOKEN, F32)],
         [WHOLE] * (len(groups) + 1),
-        [pltpu.SemaphoreType.DMA((len(groups),))],
+        [pltpu.SemaphoreType.DMA((d_layer.shape[0] // (CHUNK // 2),))],
     )
 
 
@@ -384,21 +387,23 @@
         after[h // PAIR, cols, cols] = suffix_ref[h]
         turned[h // PAIR, cols, cols] = suffix_ref[h].T
     copies = []
-    for c in range(n):
-        rows = slice(c * CHUNK, (c + 1) * CHUNK)
+    step = CHUNK // 2
+    for c in range(2 * n):
+        rows = slice(c * step, (c + 1) * step)
+        local = slice(c % 2 * step, (c % 2 + 1) * step)
         for p in range(half // PAIR):
             cols = part_of(base // PAIR + p, PAIR * dk)
-            full_k = dkp[c][:, cols].astype(F32) + dot(v_ref[rows, cols], turned[p], NN)
-            full_v = dvp[c][:, cols].astype(F32) + dot(k_ref[rows, cols], after[p], NN)
+            full_k = dkp[c // 2][local, cols].astype(F32) + dot(v_ref[rows, cols], turned[p], NN)
+            full_v = dvp[c // 2][local, cols].astype(F32) + dot(k_ref[rows, cols], after[p], NN)
             for i in range(PAIR):
-                mine = pl.ds(c * CHUNK * heads + base + p * PAIR + i, CHUNK, stride=heads)
+                mine = pl.ds(c * step * heads + base + p * PAIR + i, step, stride=heads)
                 wide_k[mine, :] = full_k[:, i * dk : (i + 1) * dk]
                 wide_v[mine, :] = full_v[:, i * dk : (i + 1) * dk]
         if last:
-            raw = slice(c * CHUNK * heads, (c + 1) * CHUNK * heads)
+            raw = slice(c * step * heads, (c + 1) * step * heads)
             for i, (wide, low, out) in enumerate(((wide_k, low_k, dk_ref), (wide_v, low_v, dv_ref))):
                 low[c] = wide[raw, :].astype(BF16)
-                copy = pltpu.make_async_copy(low.at[c], out.at[pl.ds(c * CHUNK * heads, CHUNK * heads)], sem.at[i, c])
+                copy = pltpu.make_async_copy(low.at[c], out.at[pl.ds(c * step * heads, step * heads)], sem.at[i, c])
                 copy.start()
                 copies.append(copy)
     for copy in copies:
@@ -422,7 +427,7 @@
         in_specs += [WHOLE] * 2
         out_shape = [shape(raw, BF16)] * 2 + out_shape
         out_specs = [ANYWHERE] * 2 + out_specs
-        scratch += [pltpu.VMEM((n, CHUNK * heads, dk), BF16)] * 2 + [pltpu.SemaphoreType.DMA((2, n))]
+        scratch += [pltpu.VMEM((2 * n, CHUNK // 2 * heads, dk), BF16)] * 2 + [pltpu.SemaphoreType.DMA((2, 2 * n))]
     else:
         out_shape.append(shape(TOKEN, F32))
         out_specs.append(WHOLE)
@@ -492,9 +497,9 @@
     far = 1
     groups = [(1, n - 1), (0, 1)]
     order = Order()
+    beside = swap(d_layer, "head", n_head, far)
     *pieces, order.token = cut(d_layer, groups)
     across = {c: swap(piece, "head", n_head, near) for (c, _), piece in zip(groups, pieces)}
-    beside = swap(d_layer, "head", n_head, far)
 
     flat = (tokens * heads, dk)
     q, k, v, qt, vt, before, scale, keep, send, order.token = prepare(

time: 88.3 us -> 88.2 us (level)
  no operation moved by 1% of the time
where the time goes in v11:
time: 88.2 us; the launch traced here: 87.9 us
  Pallas kernels  36.9 us (42%)
  waiting for transfers between devices  26.9 us (30%)
  starting transfers between devices  23.1 us (26%)
  between operations  0.96 us (1%)
    pallas_call x19, Pallas kernels, call(): pl.pallas_call(kernel, in_specs=in_specs, out_specs=out_specs, out_shape=...  36.9 us
    ppermute x9, waiting for transfers between devices, swap(): return lax.ppermute(array, axis, [(i, i ^ bit) for i in range(size)])  16.7 us
    ppermute x4, starting transfers between devices, shifted(): lax.ppermute(array, 'ctx', [(i, i + step) for i in range(size) if 0 <= i...  11.6 us
    ppermute x9, starting transfers between devices, swap(): return lax.ppermute(array, axis, [(i, i ^ bit) for i in range(size)])  11.5 us
    ppermute x4, waiting for transfers between devices, shifted(): lax.ppermute(array, 'ctx', [(i, i + step) for i in range(size) if 0 <= i...  10.2 us
  transfers between devices with their start and end apart: 13, of which 11 were waited for; matrix products, arithmetic and copies ran while one was open for 0% of the time, Pallas kernels for 37%

profile of v11, /device:TPU:0, one launch (start us, length us, event | category | flops | bytes accessed | tf_op | source)
XLA Modules:
  0.0 87.9 jit_solution(9336436289617155262)
XLA Ops:
  1.2 1.7 %cut.1 = (bf16[768,1024]{1,0:T(8,128)(2,1)S(1)}, bf16[256,1024]{1,0:T(8,128)(2,1)S(1)}, f32[8,128]{1,0:T(8,128)S(1)}) custom-call(bf16[1024,1024]{1,0:T(8,128)(2,1)} %source.1), custom_call_target="tpu_custom_call" | custom-call | tf_op jit(solution)/shard_map/cut/pallas_call | solution.py:40
  2.9 2.6 %collective-permute-start.1 = (bf16[768,1024]{1,0:T(8,128)(2,1)S(1)}, bf16[768,1024]{1,0:T(8,128)(2,1)S(1)}, u32[]{:S(2)}, u32[]{:S(2)}) collective-permute-start(bf16[768,1024]{1,0:T(8,128)(2,1)S(1)} %get-tuple-element.78.refs_0_), channel_id=1, source_target_pairs={{0,2},{1,3},{2,0},{3,1},{4,6},{5,7},{6,4},{7,5},{8,10},{9,11},{10,... | collective-permute-start | bytes 4718600 | tf_op jit(solution)/shard_map/ppermute | solution.py:439
  5.5 5.2 %prepare.1 = (bf16[1024,1024]{1,0:T(8,128)(2,1)S(1)}, bf16[1024,1024]{1,0:T(8,128)(2,1)S(1)}, bf16[1024,1024]{1,0:T(8,128)(2,1)S(1)}, bf16[1024,1024]{1,0:T(8,12...) custom-call(bf16[8192,128]{1,0:T(8,128)(2,1)} %bitcast.6, ...), custom_call_target="tpu_custom_call" | custom-call | tf_op jit(solution)/shard_map/prepare/pallas_call | solution.py:40
  10.7 1.6 %collective-permute-start.2 = (bf16[4,128,128]{2,1,0:T(8,128)(2,1)S(1)}, bf16[4,128,128]{2,1,0:T(8,128)(2,1)S(1)}, u32[]{:S(2)}, u32[]{:S(2)}) collective-permute-start(bf16[4,128,128]{2,1,0:T(8,128)(2,1)S(1)} %get-tuple-element.80), channel_id=1, source_target_pairs={{0,4},{4,0},{8,12},{12,8},{16,20},{20,16},{24,28},{28,24},{1,5},{5... | collective-permute-start | bytes 393224 | tf_op jit(solution)/shard_map/ppermute | solution.py:439
  12.2 4.1 %collective-permute-done.2.refs_1_.came = bf16[4,128,128]{2,1,0:T(8,128)(2,1)S(1)} collective-permute-done((bf16[4,128,128]{2,1,0:T(8,128)(2,1)S(1)}, bf16[4,128,128]{2,1,0:T(8,128)(2,1)S(1)}, u32[]{:S(2)}, u32[]{:S(2)}) %collective-permute-start.2) | collective-permute-done | bytes 131104 | tf_op jit(solution)/shard_map/ppermute | solution.py:439
  16.4 5.2 %early.1 = (f32[1024,1024]{1,0:T(8,128)S(1)}, f32[8,128]{1,0:T(8,128)S(1)}) custom-call(bf16[768,1024]{1,0:T(8,128)(2,1)S(1)} %get-tuple-element.78.refs_0_, bf16[256,1024]{1,0:T(8,128)(2,1)S(1)} %get-tuple-element.77.refs_1_, bf16[1024,1024]{1,0:T(8,128)(2,1)S(1)} %collective-permute-done.3.refs_2_, bf16[1024,4096]{1,0:T(8,128)(2,1)S(1)} %copy-done, ...), custom_call_target="tpu_custom_call" | custom-call | tf_op jit(solution)/shard_map/early/pallas_call | solution.py:40
  21.6 3.5 %collective-permute-start.4 = (bf16[4,128,128]{2,1,0:T(8,128)(2,1)S(1)}, bf16[4,128,128]{2,1,0:T(8,128)(2,1)S(1)}, u32[]{:S(2)}, u32[]{:S(2)}) collective-permute-start(bf16[4,128,128]{2,1,0:T(8,128)(2,1)S(1)} %total.4), channel_id=1, source_target_pairs={{0,8},{4,12},{8,16},{12,20},{16,24},{20,28},{1,9},{5,13},{9,17},{1... | collective-permute-start | bytes 393224 | tf_op jit(solution)/shard_map/ppermute | solution.py:443
  25.1 2.5 %collective-permute-done.4.refs_2_.refs_0_ = bf16[4,128,128]{2,1,0:T(8,128)(2,1)S(1)} collective-permute-done((bf16[4,128,128]{2,1,0:T(8,128)(2,1)S(1)}, bf16[4,128,128]{2,1,0:T(8,128)(2,1)S(1)}, u32[]{:S(2)}, u32[]{:S(2)}) %collective-permute-start.4) | collective-permute-done | bytes 131104 | tf_op jit(solution)/shard_map/ppermute | solution.py:443
  27.7 5.4 %collective-permute-start.5 = (bf16[4,128,128]{2,1,0:T(8,128)(2,1)S(1)}, bf16[4,128,128]{2,1,0:T(8,128)(2,1)S(1)}, u32[]{:S(2)}, u32[]{:S(2)}) collective-permute-start(bf16[4,128,128]{2,1,0:T(8,128)(2,1)S(1)} %total.5), channel_id=1, source_target_pairs={{0,16},{4,20},{8,24},{12,28},{1,17},{5,21},{9,25},{13,29},{2,18},{... | collective-permute-start | bytes 393224 | tf_op jit(solution)/shard_map/ppermute | solution.py:443
  33.0 2.5 %collective-permute-done.5.refs_1_ = bf16[4,128,128]{2,1,0:T(8,128)(2,1)S(1)} collective-permute-done((bf16[4,128,128]{2,1,0:T(8,128)(2,1)S(1)}, bf16[4,128,128]{2,1,0:T(8,128)(2,1)S(1)}, u32[]{:S(2)}, u32[]{:S(2)}) %collective-permute-start.5) | collective-permute-done | bytes 131104 | tf_op jit(solution)/shard_map/ppermute | solution.py:443
  35.6 4.9 %collective-permute-done.1.refs_0_ = bf16[768,1024]{1,0:T(8,128)(2,1)S(1)} collective-permute-done((bf16[768,1024]{1,0:T(8,128)(2,1)S(1)}, bf16[768,1024]{1,0:T(8,128)(2,1)S(1)}, u32[]{:S(2)}, u32[]{:S(2)}) %collective-permute-start.1) | collective-permute-done | bytes 1572896 | tf_op jit(solution)/shard_map/ppermute | solution.py:439
  40.5 1.7 %collective-permute-start = (bf16[256,1024]{1,0:T(8,128)(2,1)S(1)}, bf16[256,1024]{1,0:T(8,128)(2,1)S(1)}, u32[]{:S(2)}, u32[]{:S(2)}) collective-permute-start(bf16[256,1024]{1,0:T(8,128)(2,1)S(1)} %get-tuple-element.77.refs_1_), channel_id=1, source_target_pairs={{0,2},{1,3},{2,0},{3,1},{4,6},{5,7},{6,4},{7,5},{8,10},{9,11},{10,... | collective-permute-start | bytes 1572872 | tf_op jit(solution)/shard_map/ppermute | solution.py:439
  42.2 1.5 %collective-permute-start.7 = (bf16[4,128,128]{2,1,0:T(8,128)(2,1)S(1)}, bf16[4,128,128]{2,1,0:T(8,128)(2,1)S(1)}, u32[]{:S(2)}, u32[]{:S(2)}) collective-permute-start(bf16[4,128,128]{2,1,0:T(8,128)(2,1)S(1)} %get-tuple-element.96), channel_id=1, source_target_pairs={{0,4},{4,0},{8,12},{12,8},{16,20},{20,16},{24,28},{28,24},{1,5},{5... | collective-permute-start | bytes 393224 | tf_op jit(solution)/shard_map/ppermute | solution.py:439
  43.9 6.9 %late.3 = (bf16[768,1024]{1,0:T(8,128)(2,1)S(1)}, f32[8,128]{1,0:T(8,128)S(1)}, f32[3,8,128,128]{3,2,1,0:T(8,128)S(1)}) custom-call(bf16[768,1024]{1,0:T(8,128)(2,1)S(1)} %collective-permute-done.6.b_ref, bf16[1024,4096]{1,0:T(8,128)(2,1)S(1)} %copy-done, f32[1024,1024]{1,0:T(8,128)S(1)} %get-tuple-element.90.part_ref, ...), custom_call_target="tpu_custom_call" | custom-call | tf_op jit(solution)/shard_map/late/pallas_call | solution.py:40
  50.8 2.1 %within.4 = (bf16[2048,128]{1,0:T(8,128)(2,1)S(1)}, bf16[256,1024]{1,0:T(8,128)(2,1)S(1)}, bf16[256,1024]{1,0:T(8,128)(2,1)S(1)}, f32[8,128]{1,0:T(8,128)S(1)}) custom-call(bf16[1024,1024]{1,0:T(8,128)(2,1)S(1)} %get-tuple-element.72.q_ref, bf16[1024,1024]{1,0:T(8,128)(2,1)S(1)} %get-tuple-element.73.k_ref, bf16[1024,1024]{1,0:T(8,128)(2,1)S(1)} %get-tuple-element.74.v_ref, ...), custom_call_target="tpu_custom_call" | custom-call | tf_op jit(solution)/shard_map/within/pallas_call | solution.py:40
  52.9 1.9 %collective-permute-done.a_ref = bf16[256,1024]{1,0:T(8,128)(2,1)S(1)} collective-permute-done((bf16[256,1024]{1,0:T(8,128)(2,1)S(1)}, bf16[256,1024]{1,0:T(8,128)(2,1)S(1)}, u32[]{:S(2)}, u32[]{:S(2)}) %collective-permute-start) | collective-permute-done | bytes 524320 | tf_op jit(solution)/shard_map/ppermute | solution.py:439
  55.8 1.0 %collective-permute-done.8.b_ref = bf16[256,1024]{1,0:T(8,128)(2,1)S(1)} collective-permute-done((bf16[256,1024]{1,0:T(8,128)(2,1)S(1)}, bf16[256,1024]{1,0:T(8,128)(2,1)S(1)}, u32[]{:S(2)}, u32[]{:S(2)}) %collective-permute-start.8) | collective-permute-done | bytes 524320 | tf_op jit(solution)/shard_map/ppermute | solution.py:439
  56.8 1.2 %late.4 = (bf16[256,512]{1,0:T(8,128)(2,1)S(1)}, f32[8,128]{1,0:T(8,128)S(1)}, bf16[4,128,128]{2,1,0:T(8,128)(2,1)S(1)}, bf16[1024,256]{1,0:T(8,128)(2,1)S(1)}) custom-call(bf16[256,1024]{1,0:T(8,128)(2,1)S(1)} %collective-permute-done.8.b_ref, bf16[1024,4096]{1,0:T(8,128)(2,1)S(1)} %copy-done, f32[256,1024]{1,0:T(8,128)S(1)} %get-tuple-element.101.part_ref, ...), custom_call_target="tpu_custom_call" | custom-call | tf_op jit(solution)/shard_map/late/pallas_call | solution.py:40
  58.0 1.8 %collective-permute-start.9 = (bf16[4,128,128]{2,1,0:T(8,128)(2,1)S(1)}, bf16[4,128,128]{2,1,0:T(8,128)(2,1)S(1)}, u32[]{:S(2)}, u32[]{:S(2)}) collective-permute-start(bf16[4,128,128]{2,1,0:T(8,128)(2,1)S(1)} %get-tuple-element.109), channel_id=1, source_target_pairs={{0,4},{4,0},{8,12},{12,8},{16,20},{20,16},{24,28},{28,24},{1,5},{5... | collective-permute-start | bytes 393224 | tf_op jit(solution)/shard_map/ppermute | solution.py:439
  59.8 1.2 %late.5 = (bf16[256,512]{1,0:T(8,128)(2,1)S(1)}, f32[8,128]{1,0:T(8,128)S(1)}, bf16[4,128,128]{2,1,0:T(8,128)(2,1)S(1)}) custom-call(bf16[1024,256]{1,0:T(8,128)(2,1)S(1)} %get-tuple-element.104.b_ref, bf16[1024,4096]{1,0:T(8,128)(2,1)S(1)} %copy-done, f32[256,1024]{1,0:T(8,128)S(1)} %get-tuple-element.101.part_ref, ...), custom_call_target="tpu_custom_call" | custom-call | tf_op jit(solution)/shard_map/late/pallas_call | solution.py:40
  61.0 2.6 %collective-permute-done.9.refs_1_.came = bf16[4,128,128]{2,1,0:T(8,128)(2,1)S(1)} collective-permute-done((bf16[4,128,128]{2,1,0:T(8,128)(2,1)S(1)}, bf16[4,128,128]{2,1,0:T(8,128)(2,1)S(1)}, u32[]{:S(2)}, u32[]{:S(2)}) %collective-permute-start.9) | collective-permute-done | bytes 131104 | tf_op jit(solution)/shard_map/ppermute | solution.py:439
  63.6 1.3 %collective-permute-start.10 = (bf16[4,128,128]{2,1,0:T(8,128)(2,1)S(1)}, bf16[4,128,128]{2,1,0:T(8,128)(2,1)S(1)}, u32[]{:S(2)}, u32[]{:S(2)}) collective-permute-start(bf16[4,128,128]{2,1,0:T(8,128)(2,1)S(1)} %total.6), channel_id=1, source_target_pairs={{8,0},{12,4},{16,8},{20,12},{24,16},{28,20},{9,1},{13,5},{17,9},{2... | collective-permute-start | bytes 393224 | tf_op jit(solution)/shard_map/ppermute | solution.py:443
  64.9 2.3 %within.5 = (bf16[2048,128]{1,0:T(8,128)(2,1)S(1)}, bf16[256,1024]{1,0:T(8,128)(2,1)S(1)}, bf16[256,1024]{1,0:T(8,128)(2,1)S(1)}, f32[8,128]{1,0:T(8,128)S(1)}) custom-call(bf16[1024,1024]{1,0:T(8,128)(2,1)S(1)} %get-tuple-element.72.q_ref, bf16[1024,1024]{1,0:T(8,128)(2,1)S(1)} %get-tuple-element.73.k_ref, bf16[1024,1024]{1,0:T(8,128)(2,1)S(1)} %get-tuple-element.74.v_ref, ...), custom_call_target="tpu_custom_call" | custom-call | tf_op jit(solution)/shard_map/within/pallas_call | solution.py:40
  67.3 3.2 %collective-permute-done.10.refs_2_.refs_0_ = bf16[4,128,128]{2,1,0:T(8,128)(2,1)S(1)} collective-permute-done((bf16[4,128,128]{2,1,0:T(8,128)(2,1)S(1)}, bf16[4,128,128]{2,1,0:T(8,128)(2,1)S(1)}, u32[]{:S(2)}, u32[]{:S(2)}) %collective-permute-start.10) | collective-permute-done | bytes 131104 | tf_op jit(solution)/shard_map/ppermute | solution.py:443
  70.5 1.5 %collective-permute-start.11 = (bf16[4,128,128]{2,1,0:T(8,128)(2,1)S(1)}, bf16[4,128,128]{2,1,0:T(8,128)(2,1)S(1)}, u32[]{:S(2)}, u32[]{:S(2)}) collective-permute-start(bf16[4,128,128]{2,1,0:T(8,128)(2,1)S(1)} %total.7), channel_id=1, source_target_pairs={{16,0},{20,4},{24,8},{28,12},{17,1},{21,5},{25,9},{29,13},{18,2},{... | collective-permute-start | bytes 393224 | tf_op jit(solution)/shard_map/ppermute | solution.py:443
  72.0 2.3 %within.6 = (bf16[2048,128]{1,0:T(8,128)(2,1)S(1)}, bf16[256,1024]{1,0:T(8,128)(2,1)S(1)}, bf16[256,1024]{1,0:T(8,128)(2,1)S(1)}, f32[8,128]{1,0:T(8,128)S(1)}) custom-call(bf16[1024,1024]{1,0:T(8,128)(2,1)S(1)} %get-tuple-element.72.q_ref, bf16[1024,1024]{1,0:T(8,128)(2,1)S(1)} %get-tuple-element.73.k_ref, bf16[1024,1024]{1,0:T(8,128)(2,1)S(1)} %get-tuple-element.74.v_ref, ...), custom_call_target="tpu_custom_call" | custom-call | tf_op jit(solution)/shard_map/within/pallas_call | solution.py:40
  74.4 3.5 %within.7 = (bf16[8192,128]{1,0:T(8,128)(2,1)}, bf16[256,1024]{1,0:T(8,128)(2,1)S(1)}, bf16[256,1024]{1,0:T(8,128)(2,1)S(1)}, f32[8,128]{1,0:T(8,128)S(1)}) custom-call(bf16[1024,1024]{1,0:T(8,128)(2,1)S(1)} %get-tuple-element.72.q_ref, bf16[1024,1024]{1,0:T(8,128)(2,1)S(1)} %get-tuple-element.73.k_ref, bf16[1024,1024]{1,0:T(8,128)(2,1)S(1)} %get-tuple-element.74.v_ref, ...), custom_call_target="tpu_custom_call" | custom-call | tf_op jit(solution)/shard_map/within/pallas_call | solution.py:40
  77.8 1.9 %collective-permute-done.11.refs_1_ = bf16[4,128,128]{2,1,0:T(8,128)(2,1)S(1)} collective-permute-done((bf16[4,128,128]{2,1,0:T(8,128)(2,1)S(1)}, bf16[4,128,128]{2,1,0:T(8,128)(2,1)S(1)}, u32[]{:S(2)}, u32[]{:S(2)}) %collective-permute-start.11) | collective-permute-done | bytes 131104 | tf_op jit(solution)/shard_map/ppermute | solution.py:443
  79.9 1.7 %collective-permute-start.12 = (bf16[4,128,128]{2,1,0:T(8,128)(2,1)S(1)}, bf16[4,128,128]{2,1,0:T(8,128)(2,1)S(1)}, u32[]{:S(2)}, u32[]{:S(2)}) collective-permute-start(bf16[4,128,128]{2,1,0:T(8,128)(2,1)S(1)} %get-tuple-element.123), channel_id=1, source_target_pairs={{0,4},{4,0},{8,12},{12,8},{16,20},{20,16},{24,28},{28,24},{1,5},{5... | collective-permute-start | bytes 393224 | tf_op jit(solution)/shard_map/ppermute | solution.py:439
  81.6 1.2 %finish.2 = (f32[8192,128]{1,0:T(8,128)S(1)}, f32[8192,128]{1,0:T(8,128)S(1)}, f32[8,128]{1,0:T(8,128)S(1)}) custom-call(bf16[1024,1024]{1,0:T(8,128)(2,1)S(1)} %get-tuple-element.73.k_ref, bf16[1024,1024]{1,0:T(8,128)(2,1)S(1)} %get-tuple-element.74.v_ref, bf16[4,128,128]{2,1,0:T(8,128)(2,1)S(1)} %get-tuple-element.124.suffix_ref, ...), custom_call_target="tpu_custom_call" | custom-call | tf_op jit(solution)/shard_map/finish/pallas_call | solution.py:40
  82.9 2.0 %collective-permute-done.12.suffix_ref = bf16[4,128,128]{2,1,0:T(8,128)(2,1)S(1)} collective-permute-done((bf16[4,128,128]{2,1,0:T(8,128)(2,1)S(1)}, bf16[4,128,128]{2,1,0:T(8,128)(2,1)S(1)}, u32[]{:S(2)}, u32[]{:S(2)}) %collective-permute-start.12) | collective-permute-done | bytes 131104 | tf_op jit(solution)/shard_map/ppermute | solution.py:439
  84.9 2.9 %finish.3 = (bf16[8192,128]{1,0:T(8,128)(2,1)}, bf16[8192,128]{1,0:T(8,128)(2,1)}, f32[8192,128]{1,0:T(8,128)S(1)}, f32[8192,128]{1,0:T(8,128)S(1)}) custom-call(bf16[1024,1024]{1,0:T(8,128)(2,1)S(1)} %get-tuple-element.73.k_ref, bf16[1024,1024]{1,0:T(8,128)(2,1)S(1)} %get-tuple-element.74.v_ref, ...), custom_call_target="tpu_custom_call", output_to_operand_aliasing={{2}: (12, {}), {3}: (13, {})} | custom-call | tf_op jit(solution)/shard_map/finish/pallas_call | solution.py:40
  (15 shorter events, 1.9 us)
Async XLA Ops:
  0.6 15.7 %collective-permute-start.3 = (bf16[1024,1024]{1,0:T(8,128)(2,1)}, bf16[1024,1024]{1,0:T(8,128)(2,1)S(1)}, u32[]{:S(2)}, u32[]{:S(2)}) collective-permute-start(bf16[1024,1024]{1,0:T(8,128)(2,1)} %source.1), channel_id=1, source_target_pairs={{0,1},{1,0},{2,3},{3,2},{4,5},{5,4},{6,7},{7,6},{8,9},{9,8},{10,11... | collective-permute-start | bytes 6291464 | tf_op jit(solution)/shard_map/ppermute | solution.py:439
  1.1 15.2 %copy-start = (bf16[1024,4096]{1,0:T(8,128)(2,1)S(1)}, bf16[1024,4096]{1,0:T(8,128)(2,1)}, u32[]{:S(2)}) copy-start(bf16[1024,4096]{1,0:T(8,128)(2,1)} %w_ref.7) | copy-start | bytes 25165828
  2.9 37.6 %collective-permute-start.1 = (bf16[768,1024]{1,0:T(8,128)(2,1)S(1)}, bf16[768,1024]{1,0:T(8,128)(2,1)S(1)}, u32[]{:S(2)}, u32[]{:S(2)}) collective-permute-start(bf16[768,1024]{1,0:T(8,128)(2,1)S(1)} %get-tuple-element.78.refs_0_), channel_id=1, source_target_pairs={{0,2},{1,3},{2,0},{3,1},{4,6},{5,7},{6,4},{7,5},{8,10},{9,11},{10,... | collective-permute-start | bytes 4718600 | tf_op jit(solution)/shard_map/ppermute | solution.py:439
  10.7 5.7 %collective-permute-start.2 = (bf16[4,128,128]{2,1,0:T(8,128)(2,1)S(1)}, bf16[4,128,128]{2,1,0:T(8,128)(2,1)S(1)}, u32[]{:S(2)}, u32[]{:S(2)}) collective-permute-start(bf16[4,128,128]{2,1,0:T(8,128)(2,1)S(1)} %get-tuple-element.80), channel_id=1, source_target_pairs={{0,4},{4,0},{8,12},{12,8},{16,20},{20,16},{24,28},{28,24},{1,5},{5... | collective-permute-start | bytes 393224 | tf_op jit(solution)/shard_map/ppermute | solution.py:439
  21.6 6.0 %collective-permute-start.4 = (bf16[4,128,128]{2,1,0:T(8,128)(2,1)S(1)}, bf16[4,128,128]{2,1,0:T(8,128)(2,1)S(1)}, u32[]{:S(2)}, u32[]{:S(2)}) collective-permute-start(bf16[4,128,128]{2,1,0:T(8,128)(2,1)S(1)} %total.4), channel_id=1, source_target_pairs={{0,8},{4,12},{8,16},{12,20},{16,24},{20,28},{1,9},{5,13},{9,17},{1... | collective-permute-start | bytes 393224 | tf_op jit(solution)/shard_map/ppermute | solution.py:443
  27.7 7.9 %collective-permute-start.5 = (bf16[4,128,128]{2,1,0:T(8,128)(2,1)S(1)}, bf16[4,128,128]{2,1,0:T(8,128)(2,1)S(1)}, u32[]{:S(2)}, u32[]{:S(2)}) collective-permute-start(bf16[4,128,128]{2,1,0:T(8,128)(2,1)S(1)} %total.5), channel_id=1, source_target_pairs={{0,16},{4,20},{8,24},{12,28},{1,17},{5,21},{9,25},{13,29},{2,18},{... | collective-permute-start | bytes 393224 | tf_op jit(solution)/shard_map/ppermute | solution.py:443
  40.5 3.4 %collective-permute-start.6 = (bf16[768,1024]{1,0:T(8,128)(2,1)S(1)}, bf16[768,1024]{1,0:T(8,128)(2,1)S(1)}, u32[]{:S(2)}, u32[]{:S(2)}) collective-permute-start(bf16[768,1024]{1,0:T(8,128)(2,1)S(1)} %collective-permute-done.1.refs_0_), channel_id=1, source_target_pairs={{0,1},{1,0},{2,3},{3,2},{4,5},{5,4},{6,7},{7,6},{8,9},{9,8},{10,11... | collective-permute-start | bytes 4718600 | tf_op jit(solution)/shard_map/ppermute | solution.py:439
  40.5 14.3 %collective-permute-start = (bf16[256,1024]{1,0:T(8,128)(2,1)S(1)}, bf16[256,1024]{1,0:T(8,128)(2,1)S(1)}, u32[]{:S(2)}, u32[]{:S(2)}) collective-permute-start(bf16[256,1024]{1,0:T(8,128)(2,1)S(1)} %get-tuple-element.77.refs_1_), channel_id=1, source_target_pairs={{0,2},{1,3},{2,0},{3,1},{4,6},{5,7},{6,4},{7,5},{8,10},{9,11},{10,... | collective-permute-start | bytes 1572872 | tf_op jit(solution)/shard_map/ppermute | solution.py:439
  42.2 8.5 %collective-permute-start.7 = (bf16[4,128,128]{2,1,0:T(8,128)(2,1)S(1)}, bf16[4,128,128]{2,1,0:T(8,128)(2,1)S(1)}, u32[]{:S(2)}, u32[]{:S(2)}) collective-permute-start(bf16[4,128,128]{2,1,0:T(8,128)(2,1)S(1)} %get-tuple-element.96), channel_id=1, source_target_pairs={{0,4},{4,0},{8,12},{12,8},{16,20},{20,16},{24,28},{28,24},{1,5},{5... | collective-permute-start | bytes 393224 | tf_op jit(solution)/shard_map/ppermute | solution.py:439
  54.8 1.9 %collective-permute-start.8 = (bf16[256,1024]{1,0:T(8,128)(2,1)S(1)}, bf16[256,1024]{1,0:T(8,128)(2,1)S(1)}, u32[]{:S(2)}, u32[]{:S(2)}) collective-permute-start(bf16[256,1024]{1,0:T(8,128)(2,1)S(1)} %collective-permute-done.a_ref), channel_id=1, source_target_pairs={{0,1},{1,0},{2,3},{3,2},{4,5},{5,4},{6,7},{7,6},{8,9},{9,8},{10,11... | collective-permute-start | bytes 1572872 | tf_op jit(solution)/shard_map/ppermute | solution.py:439
  58.0 5.6 %collective-permute-start.9 = (bf16[4,128,128]{2,1,0:T(8,128)(2,1)S(1)}, bf16[4,128,128]{2,1,0:T(8,128)(2,1)S(1)}, u32[]{:S(2)}, u32[]{:S(2)}) collective-permute-start(bf16[4,128,128]{2,1,0:T(8,128)(2,1)S(1)} %get-tuple-element.109), channel_id=1, source_target_pairs={{0,4},{4,0},{8,12},{12,8},{16,20},{20,16},{24,28},{28,24},{1,5},{5... | collective-permute-start | bytes 393224 | tf_op jit(solution)/shard_map/ppermute | solution.py:439
  63.6 6.9 %collective-permute-start.10 = (bf16[4,128,128]{2,1,0:T(8,128)(2,1)S(1)}, bf16[4,128,128]{2,1,0:T(8,128)(2,1)S(1)}, u32[]{:S(2)}, u32[]{:S(2)}) collective-permute-start(bf16[4,128,128]{2,1,0:T(8,128)(2,1)S(1)} %total.6), channel_id=1, source_target_pairs={{8,0},{12,4},{16,8},{20,12},{24,16},{28,20},{9,1},{13,5},{17,9},{2... | collective-permute-start | bytes 393224 | tf_op jit(solution)/shard_map/ppermute | solution.py:443
  70.5 9.2 %collective-permute-start.11 = (bf16[4,128,128]{2,1,0:T(8,128)(2,1)S(1)}, bf16[4,128,128]{2,1,0:T(8,128)(2,1)S(1)}, u32[]{:S(2)}, u32[]{:S(2)}) collective-permute-start(bf16[4,128,128]{2,1,0:T(8,128)(2,1)S(1)} %total.7), channel_id=1, source_target_pairs={{16,0},{20,4},{24,8},{28,12},{17,1},{21,5},{25,9},{29,13},{18,2},{... | collective-permute-start | bytes 393224 | tf_op jit(solution)/shard_map/ppermute | solution.py:443
  79.9 5.0 %collective-permute-start.12 = (bf16[4,128,128]{2,1,0:T(8,128)(2,1)S(1)}, bf16[4,128,128]{2,1,0:T(8,128)(2,1)S(1)}, u32[]{:S(2)}, u32[]{:S(2)}) collective-permute-start(bf16[4,128,128]{2,1,0:T(8,128)(2,1)S(1)} %get-tuple-element.123), channel_id=1, source_target_pairs={{0,4},{4,0},{8,12},{12,8},{16,20},{20,16},{24,28},{28,24},{1,5},{5... | collective-permute-start | bytes 393224 | tf_op jit(solution)/shard_map/ppermute | solution.py:439

commit v12 on v11

--- a/solution.py
+++ b/solution.py
@@ -148,9 +148,10 @@
 
 
 def early_kernel(starts, *refs):
-    pieces, (b_ref, w_ref, _, out_ref, token_ref) = refs[: len(starts)], refs[len(starts) :]
+    count = len(starts)
+    pieces, besides, (w_ref, _, out_ref, token_ref) = refs[:count], refs[count:-4], refs[-4:]
     token_ref[...] = jnp.zeros_like(token_ref)
-    features = b_ref.shape[1]
+    features = w_ref.shape[1] // lax.axis_size("head")
     place = lax.axis_index("head")
     first, second = part_of(place, features), part_of(place ^ 1, features)
 
@@ -158,21 +159,23 @@
         tile = part_of(j, PAIR * 128)
         wa, wb = w_ref[tile, first].T, w_ref[tile, second].T
         for start, piece in zip(starts, pieces):
-            rows = slice(start, start + piece.shape[0])
-            out_ref[rows, tile] = dot(piece[...], wa, NN) + dot(b_ref[rows, :], wb, NN)
+            for row in range(0, piece.shape[0], CHUNK):
+                b_ref = besides[(start + row) // CHUNK]
+                product = dot(piece[row : row + CHUNK, :], wa, NN) + dot(b_ref[...], wb, NN)
+                out_ref[start + row : start + row + CHUNK, tile] = product
         return 0
 
     lax.fori_loop(0, out_ref.shape[1] // (PAIR * 128), one_tile, 0)
 
 
-def early(pieces, starts, b, weight, token):
-    tokens = b.shape[0]
+def early(pieces, starts, besides, weight, token):
+    tokens = sum(b.shape[0] for b in besides)
     width = weight.shape[0]
     return call(
         functools.partial(early_kernel, starts),
         "early",
-        [*pieces, b, weight, token],
-        [WHOLE] * (len(pieces) + 2) + [ANYWHERE],
+        [*pieces, *besides, weight, token],
+        [WHOLE] * (len(pieces) + len(besides) + 1) + [ANYWHERE],
         [shape((tokens, width), F32), shape(TOKEN, F32)],
         [WHOLE] * 2,
     )
@@ -497,7 +500,6 @@
     far = 1
     groups = [(1, n - 1), (0, 1)]
     order = Order()
-    beside = swap(d_layer, "head", n_head, far)
     *pieces, order.token = cut(d_layer, groups)
     across = {c: swap(piece, "head", n_head, near) for (c, _), piece in zip(groups, pieces)}
 
@@ -507,6 +509,8 @@
     )
     forward = scan_states([keep], [send], n_ctx, 1, order)
     next(forward)
+    *blocks, order.token = cut(order.tie(d_layer), [(c, 1) for c in range(n)])
+    beside = [swap(one, "head", n_head, far) for one in blocks]
     starts = [c * CHUNK for c, _ in groups]
     part, order.token = early(pieces, starts, beside, out_weight, order.token)
 

time: 88.2 us -> 87.6 us (level)
  waiting for transfers between devices: 26.9 us -> 24.6 us
  Pallas kernels: 36.9 us -> 38.5 us
    ppermute x9 -> x12, waiting for transfers between devices: 16.7 us -> 13.5 us  [swap(): return lax.ppermute(array, axis, [(i, i ^ bit) for i in range(size)])]
    pallas_call x19 -> x20, Pallas kernels: 36.9 us -> 38.5 us  [call(): pl.pallas_call(kernel, in_specs=in_specs, out_specs=out_specs, out_shape=...]
    ppermute x4, waiting for transfers between devices: 10.2 us -> 11.1 us  [shifted(): lax.ppermute(array, 'ctx', [(i, i + step) for i in range(size) if 0 <= i...]
    ppermute x9 -> x12, starting transfers between devices: 11.5 us -> 11.7 us  [swap(): return lax.ppermute(array, axis, [(i, i ^ bit) for i in range(size)])]
  transfers between devices with their start and end apart: 13 -> 16, of which waited for: 11 -> 15; matrix products, arithmetic and copies ran while one was open for 0% -> 0% of each run, Pallas kernels for 37% -> 37%
where the time goes in v12:
time: 87.6 us; the launch traced here: 87.4 us
  Pallas kernels  38.5 us (44%)
  waiting for transfers between devices  24.6 us (28%)
  starting transfers between devices  23.4 us (27%)
  between operations  0.96 us (1%)
    pallas_call x20, Pallas kernels, call(): pl.pallas_call(kernel, in_specs=in_specs, out_specs=out_specs, out_shape=...  38.5 us
    ppermute x12, waiting for transfers between devices, swap(): return lax.ppermute(array, axis, [(i, i ^ bit) for i in range(size)])  13.5 us
    ppermute x12, starting transfers between devices, swap(): return lax.ppermute(array, axis, [(i, i ^ bit) for i in range(size)])  11.7 us
    ppermute x4, starting transfers between devices, shifted(): lax.ppermute(array, 'ctx', [(i, i + step) for i in range(size) if 0 <= i...  11.6 us
    ppermute x4, waiting for transfers between devices, shifted(): lax.ppermute(array, 'ctx', [(i, i + step) for i in range(size) if 0 <= i...  11.1 us
  transfers between devices with their start and end apart: 16, of which 15 were waited for; matrix products, arithmetic and copies ran while one was open for 0% of the time, Pallas kernels for 37%

profile of v12, /device:TPU:0, one launch (start us, length us, event | category | flops | bytes accessed | tf_op | source)
XLA Modules:
  0.0 87.4 jit_solution(11647680877415375511)
XLA Ops:
  0.6 1.6 %cut.2 = (bf16[768,1024]{1,0:T(8,128)(2,1)S(1)}, bf16[256,1024]{1,0:T(8,128)(2,1)S(1)}, f32[8,128]{1,0:T(8,128)S(1)}) custom-call(bf16[1024,1024]{1,0:T(8,128)(2,1)} %source.2), custom_call_target="tpu_custom_call" | custom-call | tf_op jit(solution)/shard_map/cut/pallas_call | solution.py:40
  2.2 3.0 %collective-permute-start.1 = (bf16[768,1024]{1,0:T(8,128)(2,1)S(1)}, bf16[768,1024]{1,0:T(8,128)(2,1)S(1)}, u32[]{:S(2)}, u32[]{:S(2)}) collective-permute-start(bf16[768,1024]{1,0:T(8,128)(2,1)S(1)} %get-tuple-element.82.refs_0_), channel_id=1, source_target_pairs={{0,2},{1,3},{2,0},{3,1},{4,6},{5,7},{6,4},{7,5},{8,10},{9,11},{10,... | collective-permute-start | bytes 4718600 | tf_op jit(solution)/shard_map/ppermute | solution.py:442
  5.2 5.3 %prepare.1 = (bf16[1024,1024]{1,0:T(8,128)(2,1)S(1)}, bf16[1024,1024]{1,0:T(8,128)(2,1)S(1)}, bf16[1024,1024]{1,0:T(8,128)(2,1)S(1)}, bf16[1024,1024]{1,0:T(8,12...) custom-call(bf16[8192,128]{1,0:T(8,128)(2,1)} %bitcast.6, ...), custom_call_target="tpu_custom_call" | custom-call | tf_op jit(solution)/shard_map/prepare/pallas_call | solution.py:40
  10.6 1.6 %collective-permute-start.2 = (bf16[4,128,128]{2,1,0:T(8,128)(2,1)S(1)}, bf16[4,128,128]{2,1,0:T(8,128)(2,1)S(1)}, u32[]{:S(2)}, u32[]{:S(2)}) collective-permute-start(bf16[4,128,128]{2,1,0:T(8,128)(2,1)S(1)} %get-tuple-element.84), channel_id=1, source_target_pairs={{0,4},{4,0},{8,12},{12,8},{16,20},{20,16},{24,28},{28,24},{1,5},{5... | collective-permute-start | bytes 393224 | tf_op jit(solution)/shard_map/ppermute | solution.py:442
  12.2 1.6 %cut.3 = (bf16[256,1024]{1,0:T(8,128)(2,1)S(1)}, bf16[256,1024]{1,0:T(8,128)(2,1)S(1)}, bf16[256,1024]{1,0:T(8,128)(2,1)S(1)}, bf16[256,1024]{1,0:T(8,128)(2,1)S(1)}, f32[8,128]{1,0:T(8,128)S(1)}) custom-call(bf16[1024,1024]{1,0:T(8,128)(2,1)} %source.2), custom_call_target="tpu_custom_call" | custom-call | tf_op jit(solution)/shard_map/cut/pallas_call | solution.py:40
  14.4 1.2 %collective-permute-done.2.refs_1_.came = bf16[4,128,128]{2,1,0:T(8,128)(2,1)S(1)} collective-permute-done((bf16[4,128,128]{2,1,0:T(8,128)(2,1)S(1)}, bf16[4,128,128]{2,1,0:T(8,128)(2,1)S(1)}, u32[]{:S(2)}, u32[]{:S(2)}) %collective-permute-start.2) | collective-permute-done | bytes 131104 | tf_op jit(solution)/shard_map/ppermute | solution.py:442
  18.0 5.1 %early.1 = (f32[1024,1024]{1,0:T(8,128)S(1)}, f32[8,128]{1,0:T(8,128)S(1)}) custom-call(bf16[768,1024]{1,0:T(8,128)(2,1)S(1)} %get-tuple-element.82.refs_0_, bf16[256,1024]{1,0:T(8,128)(2,1)S(1)} %get-tuple-element.81.refs_1_, bf16[256,1024]{1,0:T(8,128)(2,1)S(1)} %collective-permute-done.3.refs_2_, bf16[256,1024]{1,0:T(8,128)(2,1)S(1)} %collective-permute-done.4.refs_3_, ...), custom_call_target="tpu_custom_call" | custom-call | tf_op jit(solution)/shard_map/early/pallas_call | solution.py:40
  23.1 3.5 %collective-permute-start.7 = (bf16[4,128,128]{2,1,0:T(8,128)(2,1)S(1)}, bf16[4,128,128]{2,1,0:T(8,128)(2,1)S(1)}, u32[]{:S(2)}, u32[]{:S(2)}) collective-permute-start(bf16[4,128,128]{2,1,0:T(8,128)(2,1)S(1)} %total.4), channel_id=1, source_target_pairs={{0,8},{4,12},{8,16},{12,20},{16,24},{20,28},{1,9},{5,13},{9,17},{1... | collective-permute-start | bytes 393224 | tf_op jit(solution)/shard_map/ppermute | solution.py:446
  26.6 3.1 %collective-permute-done.7.refs_2_.refs_0_ = bf16[4,128,128]{2,1,0:T(8,128)(2,1)S(1)} collective-permute-done((bf16[4,128,128]{2,1,0:T(8,128)(2,1)S(1)}, bf16[4,128,128]{2,1,0:T(8,128)(2,1)S(1)}, u32[]{:S(2)}, u32[]{:S(2)}) %collective-permute-start.7) | collective-permute-done | bytes 131104 | tf_op jit(solution)/shard_map/ppermute | solution.py:446
  29.7 5.4 %collective-permute-start.8 = (bf16[4,128,128]{2,1,0:T(8,128)(2,1)S(1)}, bf16[4,128,128]{2,1,0:T(8,128)(2,1)S(1)}, u32[]{:S(2)}, u32[]{:S(2)}) collective-permute-start(bf16[4,128,128]{2,1,0:T(8,128)(2,1)S(1)} %total.5), channel_id=1, source_target_pairs={{0,16},{4,20},{8,24},{12,28},{1,17},{5,21},{9,25},{13,29},{2,18},{... | collective-permute-start | bytes 393224 | tf_op jit(solution)/shard_map/ppermute | solution.py:446
  35.1 2.5 %collective-permute-done.8.refs_1_ = bf16[4,128,128]{2,1,0:T(8,128)(2,1)S(1)} collective-permute-done((bf16[4,128,128]{2,1,0:T(8,128)(2,1)S(1)}, bf16[4,128,128]{2,1,0:T(8,128)(2,1)S(1)}, u32[]{:S(2)}, u32[]{:S(2)}) %collective-permute-start.8) | collective-permute-done | bytes 131104 | tf_op jit(solution)/shard_map/ppermute | solution.py:446
  37.7 1.9 %collective-permute-done.1.refs_0_ = bf16[768,1024]{1,0:T(8,128)(2,1)S(1)} collective-permute-done((bf16[768,1024]{1,0:T(8,128)(2,1)S(1)}, bf16[768,1024]{1,0:T(8,128)(2,1)S(1)}, u32[]{:S(2)}, u32[]{:S(2)}) %collective-permute-start.1) | collective-permute-done | bytes 1572896 | tf_op jit(solution)/shard_map/ppermute | solution.py:442
  39.6 1.7 %collective-permute-start = (bf16[256,1024]{1,0:T(8,128)(2,1)S(1)}, bf16[256,1024]{1,0:T(8,128)(2,1)S(1)}, u32[]{:S(2)}, u32[]{:S(2)}) collective-permute-start(bf16[256,1024]{1,0:T(8,128)(2,1)S(1)} %get-tuple-element.81.refs_1_), channel_id=1, source_target_pairs={{0,2},{1,3},{2,0},{3,1},{4,6},{5,7},{6,4},{7,5},{8,10},{9,11},{10,... | collective-permute-start | bytes 1572872 | tf_op jit(solution)/shard_map/ppermute | solution.py:442
  41.4 1.5 %collective-permute-start.10 = (bf16[4,128,128]{2,1,0:T(8,128)(2,1)S(1)}, bf16[4,128,128]{2,1,0:T(8,128)(2,1)S(1)}, u32[]{:S(2)}, u32[]{:S(2)}) collective-permute-start(bf16[4,128,128]{2,1,0:T(8,128)(2,1)S(1)} %get-tuple-element.104), channel_id=1, source_target_pairs={{0,4},{4,0},{8,12},{12,8},{16,20},{20,16},{24,28},{28,24},{1,5},{5... | collective-permute-start | bytes 393224 | tf_op jit(solution)/shard_map/ppermute | solution.py:442
  43.0 6.9 %late.3 = (bf16[768,1024]{1,0:T(8,128)(2,1)S(1)}, f32[8,128]{1,0:T(8,128)S(1)}, f32[3,8,128,128]{3,2,1,0:T(8,128)S(1)}) custom-call(bf16[768,1024]{1,0:T(8,128)(2,1)S(1)} %collective-permute-done.9.b_ref, bf16[1024,4096]{1,0:T(8,128)(2,1)S(1)} %copy-done, f32[1024,1024]{1,0:T(8,128)S(1)} %get-tuple-element.98.part_ref, ...), custom_call_target="tpu_custom_call" | custom-call | tf_op jit(solution)/shard_map/late/pallas_call | solution.py:40
  49.9 2.1 %within.4 = (bf16[2048,128]{1,0:T(8,128)(2,1)S(1)}, bf16[256,1024]{1,0:T(8,128)(2,1)S(1)}, bf16[256,1024]{1,0:T(8,128)(2,1)S(1)}, f32[8,128]{1,0:T(8,128)S(1)}) custom-call(bf16[1024,1024]{1,0:T(8,128)(2,1)S(1)} %get-tuple-element.76.q_ref, bf16[1024,1024]{1,0:T(8,128)(2,1)S(1)} %get-tuple-element.77.k_ref, bf16[1024,1024]{1,0:T(8,128)(2,1)S(1)} %get-tuple-element.78.v_ref, ...), custom_call_target="tpu_custom_call" | custom-call | tf_op jit(solution)/shard_map/within/pallas_call | solution.py:40
  52.0 1.9 %collective-permute-done.a_ref = bf16[256,1024]{1,0:T(8,128)(2,1)S(1)} collective-permute-done((bf16[256,1024]{1,0:T(8,128)(2,1)S(1)}, bf16[256,1024]{1,0:T(8,128)(2,1)S(1)}, u32[]{:S(2)}, u32[]{:S(2)}) %collective-permute-start) | collective-permute-done | bytes 524320 | tf_op jit(solution)/shard_map/ppermute | solution.py:442
  55.9 1.2 %late.4 = (bf16[256,512]{1,0:T(8,128)(2,1)S(1)}, f32[8,128]{1,0:T(8,128)S(1)}, bf16[4,128,128]{2,1,0:T(8,128)(2,1)S(1)}, bf16[1024,256]{1,0:T(8,128)(2,1)S(1)}) custom-call(bf16[256,1024]{1,0:T(8,128)(2,1)S(1)} %collective-permute-done.11.b_ref, bf16[1024,4096]{1,0:T(8,128)(2,1)S(1)} %copy-done, f32[256,1024]{1,0:T(8,128)S(1)} %get-tuple-element.109.part_ref, ...), custom_call_target="tpu_custom_call" | custom-call | tf_op jit(solution)/shard_map/late/pallas_call | solution.py:40
  57.1 1.8 %collective-permute-start.12 = (bf16[4,128,128]{2,1,0:T(8,128)(2,1)S(1)}, bf16[4,128,128]{2,1,0:T(8,128)(2,1)S(1)}, u32[]{:S(2)}, u32[]{:S(2)}) collective-permute-start(bf16[4,128,128]{2,1,0:T(8,128)(2,1)S(1)} %get-tuple-element.117), channel_id=1, source_target_pairs={{0,4},{4,0},{8,12},{12,8},{16,20},{20,16},{24,28},{28,24},{1,5},{5... | collective-permute-start | bytes 393224 | tf_op jit(solution)/shard_map/ppermute | solution.py:442
  58.9 1.2 %late.5 = (bf16[256,512]{1,0:T(8,128)(2,1)S(1)}, f32[8,128]{1,0:T(8,128)S(1)}, bf16[4,128,128]{2,1,0:T(8,128)(2,1)S(1)}) custom-call(bf16[1024,256]{1,0:T(8,128)(2,1)S(1)} %get-tuple-element.112.b_ref, bf16[1024,4096]{1,0:T(8,128)(2,1)S(1)} %copy-done, f32[256,1024]{1,0:T(8,128)S(1)} %get-tuple-element.109.part_ref, ...), custom_call_target="tpu_custom_call" | custom-call | tf_op jit(solution)/shard_map/late/pallas_call | solution.py:40
  60.1 2.6 %collective-permute-done.12.refs_1_.came = bf16[4,128,128]{2,1,0:T(8,128)(2,1)S(1)} collective-permute-done((bf16[4,128,128]{2,1,0:T(8,128)(2,1)S(1)}, bf16[4,128,128]{2,1,0:T(8,128)(2,1)S(1)}, u32[]{:S(2)}, u32[]{:S(2)}) %collective-permute-start.12) | collective-permute-done | bytes 131104 | tf_op jit(solution)/shard_map/ppermute | solution.py:442
  62.7 1.5 %collective-permute-start.13 = (bf16[4,128,128]{2,1,0:T(8,128)(2,1)S(1)}, bf16[4,128,128]{2,1,0:T(8,128)(2,1)S(1)}, u32[]{:S(2)}, u32[]{:S(2)}) collective-permute-start(bf16[4,128,128]{2,1,0:T(8,128)(2,1)S(1)} %total.6), channel_id=1, source_target_pairs={{8,0},{12,4},{16,8},{20,12},{24,16},{28,20},{9,1},{13,5},{17,9},{2... | collective-permute-start | bytes 393224 | tf_op jit(solution)/shard_map/ppermute | solution.py:446
  64.2 2.3 %within.5 = (bf16[2048,128]{1,0:T(8,128)(2,1)S(1)}, bf16[256,1024]{1,0:T(8,128)(2,1)S(1)}, bf16[256,1024]{1,0:T(8,128)(2,1)S(1)}, f32[8,128]{1,0:T(8,128)S(1)}) custom-call(bf16[1024,1024]{1,0:T(8,128)(2,1)S(1)} %get-tuple-element.76.q_ref, bf16[1024,1024]{1,0:T(8,128)(2,1)S(1)} %get-tuple-element.77.k_ref, bf16[1024,1024]{1,0:T(8,128)(2,1)S(1)} %get-tuple-element.78.v_ref, ...), custom_call_target="tpu_custom_call" | custom-call | tf_op jit(solution)/shard_map/within/pallas_call | solution.py:40
  66.6 3.2 %collective-permute-done.13.refs_2_.refs_0_ = bf16[4,128,128]{2,1,0:T(8,128)(2,1)S(1)} collective-permute-done((bf16[4,128,128]{2,1,0:T(8,128)(2,1)S(1)}, bf16[4,128,128]{2,1,0:T(8,128)(2,1)S(1)}, u32[]{:S(2)}, u32[]{:S(2)}) %collective-permute-start.13) | collective-permute-done | bytes 131104 | tf_op jit(solution)/shard_map/ppermute | solution.py:446
  69.8 1.3 %collective-permute-start.14 = (bf16[4,128,128]{2,1,0:T(8,128)(2,1)S(1)}, bf16[4,128,128]{2,1,0:T(8,128)(2,1)S(1)}, u32[]{:S(2)}, u32[]{:S(2)}) collective-permute-start(bf16[4,128,128]{2,1,0:T(8,128)(2,1)S(1)} %total.7), channel_id=1, source_target_pairs={{16,0},{20,4},{24,8},{28,12},{17,1},{21,5},{25,9},{29,13},{18,2},{... | collective-permute-start | bytes 393224 | tf_op jit(solution)/shard_map/ppermute | solution.py:446
  71.1 2.3 %within.6 = (bf16[2048,128]{1,0:T(8,128)(2,1)S(1)}, bf16[256,1024]{1,0:T(8,128)(2,1)S(1)}, bf16[256,1024]{1,0:T(8,128)(2,1)S(1)}, f32[8,128]{1,0:T(8,128)S(1)}) custom-call(bf16[1024,1024]{1,0:T(8,128)(2,1)S(1)} %get-tuple-element.76.q_ref, bf16[1024,1024]{1,0:T(8,128)(2,1)S(1)} %get-tuple-element.77.k_ref, bf16[1024,1024]{1,0:T(8,128)(2,1)S(1)} %get-tuple-element.78.v_ref, ...), custom_call_target="tpu_custom_call" | custom-call | tf_op jit(solution)/shard_map/within/pallas_call | solution.py:40
  73.5 3.5 %within.7 = (bf16[8192,128]{1,0:T(8,128)(2,1)}, bf16[256,1024]{1,0:T(8,128)(2,1)S(1)}, bf16[256,1024]{1,0:T(8,128)(2,1)S(1)}, f32[8,128]{1,0:T(8,128)S(1)}) custom-call(bf16[1024,1024]{1,0:T(8,128)(2,1)S(1)} %get-tuple-element.76.q_ref, bf16[1024,1024]{1,0:T(8,128)(2,1)S(1)} %get-tuple-element.77.k_ref, bf16[1024,1024]{1,0:T(8,128)(2,1)S(1)} %get-tuple-element.78.v_ref, ...), custom_call_target="tpu_custom_call" | custom-call | tf_op jit(solution)/shard_map/within/pallas_call | solution.py:40
  76.9 2.3 %collective-permute-done.14.refs_1_ = bf16[4,128,128]{2,1,0:T(8,128)(2,1)S(1)} collective-permute-done((bf16[4,128,128]{2,1,0:T(8,128)(2,1)S(1)}, bf16[4,128,128]{2,1,0:T(8,128)(2,1)S(1)}, u32[]{:S(2)}, u32[]{:S(2)}) %collective-permute-start.14) | collective-permute-done | bytes 131104 | tf_op jit(solution)/shard_map/ppermute | solution.py:446
  79.3 1.4 %collective-permute-start.15 = (bf16[4,128,128]{2,1,0:T(8,128)(2,1)S(1)}, bf16[4,128,128]{2,1,0:T(8,128)(2,1)S(1)}, u32[]{:S(2)}, u32[]{:S(2)}) collective-permute-start(bf16[4,128,128]{2,1,0:T(8,128)(2,1)S(1)} %get-tuple-element.131), channel_id=1, source_target_pairs={{0,4},{4,0},{8,12},{12,8},{16,20},{20,16},{24,28},{28,24},{1,5},{5... | collective-permute-start | bytes 393224 | tf_op jit(solution)/shard_map/ppermute | solution.py:442
  80.7 1.2 %finish.2 = (f32[8192,128]{1,0:T(8,128)S(1)}, f32[8192,128]{1,0:T(8,128)S(1)}, f32[8,128]{1,0:T(8,128)S(1)}) custom-call(bf16[1024,1024]{1,0:T(8,128)(2,1)S(1)} %get-tuple-element.77.k_ref, bf16[1024,1024]{1,0:T(8,128)(2,1)S(1)} %get-tuple-element.78.v_ref, bf16[4,128,128]{2,1,0:T(8,128)(2,1)S(1)} %get-tuple-element.132.suffix_ref, ...), custom_call_target="tpu_custom_call" | custom-call | tf_op jit(solution)/shard_map/finish/pallas_call | solution.py:40
  82.0 2.4 %collective-permute-done.15.suffix_ref = bf16[4,128,128]{2,1,0:T(8,128)(2,1)S(1)} collective-permute-done((bf16[4,128,128]{2,1,0:T(8,128)(2,1)S(1)}, bf16[4,128,128]{2,1,0:T(8,128)(2,1)S(1)}, u32[]{:S(2)}, u32[]{:S(2)}) %collective-permute-start.15) | collective-permute-done | bytes 131104 | tf_op jit(solution)/shard_map/ppermute | solution.py:442
  84.4 2.9 %finish.3 = (bf16[8192,128]{1,0:T(8,128)(2,1)}, bf16[8192,128]{1,0:T(8,128)(2,1)}, f32[8192,128]{1,0:T(8,128)S(1)}, f32[8192,128]{1,0:T(8,128)S(1)}) custom-call(bf16[1024,1024]{1,0:T(8,128)(2,1)S(1)} %get-tuple-element.77.k_ref, bf16[1024,1024]{1,0:T(8,128)(2,1)S(1)} %get-tuple-element.78.v_ref, ...), custom_call_target="tpu_custom_call", output_to_operand_aliasing={{2}: (12, {}), {3}: (13, {})} | custom-call | tf_op jit(solution)/shard_map/finish/pallas_call | solution.py:40
  (22 shorter events, 5.4 us)
Async XLA Ops:
  2.2 37.4 %collective-permute-start.1 = (bf16[768,1024]{1,0:T(8,128)(2,1)S(1)}, bf16[768,1024]{1,0:T(8,128)(2,1)S(1)}, u32[]{:S(2)}, u32[]{:S(2)}) collective-permute-start(bf16[768,1024]{1,0:T(8,128)(2,1)S(1)} %get-tuple-element.82.refs_0_), channel_id=1, source_target_pairs={{0,2},{1,3},{2,0},{3,1},{4,6},{5,7},{6,4},{7,5},{8,10},{9,11},{10,... | collective-permute-start | bytes 4718600 | tf_op jit(solution)/shard_map/ppermute | solution.py:442
  5.2 12.8 %copy-start = (bf16[1024,4096]{1,0:T(8,128)(2,1)S(1)}, bf16[1024,4096]{1,0:T(8,128)(2,1)}, u32[]{:S(2)}) copy-start(bf16[1024,4096]{1,0:T(8,128)(2,1)} %w_ref.7) | copy-start | bytes 25165828
  10.6 5.0 %collective-permute-start.2 = (bf16[4,128,128]{2,1,0:T(8,128)(2,1)S(1)}, bf16[4,128,128]{2,1,0:T(8,128)(2,1)S(1)}, u32[]{:S(2)}, u32[]{:S(2)}) collective-permute-start(bf16[4,128,128]{2,1,0:T(8,128)(2,1)S(1)} %get-tuple-element.84), channel_id=1, source_target_pairs={{0,4},{4,0},{8,12},{12,8},{16,20},{20,16},{24,28},{28,24},{1,5},{5... | collective-permute-start | bytes 393224 | tf_op jit(solution)/shard_map/ppermute | solution.py:442
  13.7 2.0 %collective-permute-start.3 = (bf16[256,1024]{1,0:T(8,128)(2,1)S(1)}, bf16[256,1024]{1,0:T(8,128)(2,1)S(1)}, u32[]{:S(2)}, u32[]{:S(2)}) collective-permute-start(bf16[256,1024]{1,0:T(8,128)(2,1)S(1)} %get-tuple-element.85), channel_id=1, source_target_pairs={{0,1},{1,0},{2,3},{3,2},{4,5},{5,4},{6,7},{7,6},{8,9},{9,8},{10,11... | collective-permute-start | bytes 1572872 | tf_op jit(solution)/shard_map/ppermute | solution.py:442
  13.8 2.6 %collective-permute-start.4 = (bf16[256,1024]{1,0:T(8,128)(2,1)S(1)}, bf16[256,1024]{1,0:T(8,128)(2,1)S(1)}, u32[]{:S(2)}, u32[]{:S(2)}) collective-permute-start(bf16[256,1024]{1,0:T(8,128)(2,1)S(1)} %get-tuple-element.86), channel_id=1, source_target_pairs={{0,1},{1,0},{2,3},{3,2},{4,5},{5,4},{6,7},{7,6},{8,9},{9,8},{10,11... | collective-permute-start | bytes 1572872 | tf_op jit(solution)/shard_map/ppermute | solution.py:442
  14.3 2.9 %collective-permute-start.5 = (bf16[256,1024]{1,0:T(8,128)(2,1)S(1)}, bf16[256,1024]{1,0:T(8,128)(2,1)S(1)}, u32[]{:S(2)}, u32[]{:S(2)}) collective-permute-start(bf16[256,1024]{1,0:T(8,128)(2,1)S(1)} %get-tuple-element.87), channel_id=1, source_target_pairs={{0,1},{1,0},{2,3},{3,2},{4,5},{5,4},{6,7},{7,6},{8,9},{9,8},{10,11... | collective-permute-start | bytes 1572872 | tf_op jit(solution)/shard_map/ppermute | solution.py:442
  15.6 2.4 %collective-permute-start.6 = (bf16[256,1024]{1,0:T(8,128)(2,1)S(1)}, bf16[256,1024]{1,0:T(8,128)(2,1)S(1)}, u32[]{:S(2)}, u32[]{:S(2)}) collective-permute-start(bf16[256,1024]{1,0:T(8,128)(2,1)S(1)} %get-tuple-element.88), channel_id=1, source_target_pairs={{0,1},{1,0},{2,3},{3,2},{4,5},{5,4},{6,7},{7,6},{8,9},{9,8},{10,11... | collective-permute-start | bytes 1572872 | tf_op jit(solution)/shard_map/ppermute | solution.py:442
  23.1 6.5 %collective-permute-start.7 = (bf16[4,128,128]{2,1,0:T(8,128)(2,1)S(1)}, bf16[4,128,128]{2,1,0:T(8,128)(2,1)S(1)}, u32[]{:S(2)}, u32[]{:S(2)}) collective-permute-start(bf16[4,128,128]{2,1,0:T(8,128)(2,1)S(1)} %total.4), channel_id=1, source_target_pairs={{0,8},{4,12},{8,16},{12,20},{16,24},{20,28},{1,9},{5,13},{9,17},{1... | collective-permute-start | bytes 393224 | tf_op jit(solution)/shard_map/ppermute | solution.py:446
  29.7 7.9 %collective-permute-start.8 = (bf16[4,128,128]{2,1,0:T(8,128)(2,1)S(1)}, bf16[4,128,128]{2,1,0:T(8,128)(2,1)S(1)}, u32[]{:S(2)}, u32[]{:S(2)}) collective-permute-start(bf16[4,128,128]{2,1,0:T(8,128)(2,1)S(1)} %total.5), channel_id=1, source_target_pairs={{0,16},{4,20},{8,24},{12,28},{1,17},{5,21},{9,25},{13,29},{2,18},{... | collective-permute-start | bytes 393224 | tf_op jit(solution)/shard_map/ppermute | solution.py:446
  39.6 3.4 %collective-permute-start.9 = (bf16[768,1024]{1,0:T(8,128)(2,1)S(1)}, bf16[768,1024]{1,0:T(8,128)(2,1)S(1)}, u32[]{:S(2)}, u32[]{:S(2)}) collective-permute-start(bf16[768,1024]{1,0:T(8,128)(2,1)S(1)} %collective-permute-done.1.refs_0_), channel_id=1, source_target_pairs={{0,1},{1,0},{2,3},{3,2},{4,5},{5,4},{6,7},{7,6},{8,9},{9,8},{10,11... | collective-permute-start | bytes 4718600 | tf_op jit(solution)/shard_map/ppermute | solution.py:442
  39.6 14.3 %collective-permute-start = (bf16[256,1024]{1,0:T(8,128)(2,1)S(1)}, bf16[256,1024]{1,0:T(8,128)(2,1)S(1)}, u32[]{:S(2)}, u32[]{:S(2)}) collective-permute-start(bf16[256,1024]{1,0:T(8,128)(2,1)S(1)} %get-tuple-element.81.refs_1_), channel_id=1, source_target_pairs={{0,2},{1,3},{2,0},{3,1},{4,6},{5,7},{6,4},{7,5},{8,10},{9,11},{10,... | collective-permute-start | bytes 1572872 | tf_op jit(solution)/shard_map/ppermute | solution.py:442
  41.4 8.6 %collective-permute-start.10 = (bf16[4,128,128]{2,1,0:T(8,128)(2,1)S(1)}, bf16[4,128,128]{2,1,0:T(8,128)(2,1)S(1)}, u32[]{:S(2)}, u32[]{:S(2)}) collective-permute-start(bf16[4,128,128]{2,1,0:T(8,128)(2,1)S(1)} %get-tuple-element.104), channel_id=1, source_target_pairs={{0,4},{4,0},{8,12},{12,8},{16,20},{20,16},{24,28},{28,24},{1,5},{5... | collective-permute-start | bytes 393224 | tf_op jit(solution)/shard_map/ppermute | solution.py:442
  54.0 1.9 %collective-permute-start.11 = (bf16[256,1024]{1,0:T(8,128)(2,1)S(1)}, bf16[256,1024]{1,0:T(8,128)(2,1)S(1)}, u32[]{:S(2)}, u32[]{:S(2)}) collective-permute-start(bf16[256,1024]{1,0:T(8,128)(2,1)S(1)} %collective-permute-done.a_ref), channel_id=1, source_target_pairs={{0,1},{1,0},{2,3},{3,2},{4,5},{5,4},{6,7},{7,6},{8,9},{9,8},{10,11... | collective-permute-start | bytes 1572872 | tf_op jit(solution)/shard_map/ppermute | solution.py:442
  57.1 5.6 %collective-permute-start.12 = (bf16[4,128,128]{2,1,0:T(8,128)(2,1)S(1)}, bf16[4,128,128]{2,1,0:T(8,128)(2,1)S(1)}, u32[]{:S(2)}, u32[]{:S(2)}) collective-permute-start(bf16[4,128,128]{2,1,0:T(8,128)(2,1)S(1)} %get-tuple-element.117), channel_id=1, source_target_pairs={{0,4},{4,0},{8,12},{12,8},{16,20},{20,16},{24,28},{28,24},{1,5},{5... | collective-permute-start | bytes 393224 | tf_op jit(solution)/shard_map/ppermute | solution.py:442
  62.7 7.0 %collective-permute-start.13 = (bf16[4,128,128]{2,1,0:T(8,128)(2,1)S(1)}, bf16[4,128,128]{2,1,0:T(8,128)(2,1)S(1)}, u32[]{:S(2)}, u32[]{:S(2)}) collective-permute-start(bf16[4,128,128]{2,1,0:T(8,128)(2,1)S(1)} %total.6), channel_id=1, source_target_pairs={{8,0},{12,4},{16,8},{20,12},{24,16},{28,20},{9,1},{13,5},{17,9},{2... | collective-permute-start | bytes 393224 | tf_op jit(solution)/shard_map/ppermute | solution.py:446
  69.8 9.4 %collective-permute-start.14 = (bf16[4,128,128]{2,1,0:T(8,128)(2,1)S(1)}, bf16[4,128,128]{2,1,0:T(8,128)(2,1)S(1)}, u32[]{:S(2)}, u32[]{:S(2)}) collective-permute-start(bf16[4,128,128]{2,1,0:T(8,128)(2,1)S(1)} %total.7), channel_id=1, source_target_pairs={{16,0},{20,4},{24,8},{28,12},{17,1},{21,5},{25,9},{29,13},{18,2},{... | collective-permute-start | bytes 393224 | tf_op jit(solution)/shard_map/ppermute | solution.py:446
  79.3 5.0 %collective-permute-start.15 = (bf16[4,128,128]{2,1,0:T(8,128)(2,1)S(1)}, bf16[4,128,128]{2,1,0:T(8,128)(2,1)S(1)}, u32[]{:S(2)}, u32[]{:S(2)}) collective-permute-start(bf16[4,128,128]{2,1,0:T(8,128)(2,1)S(1)} %get-tuple-element.131), channel_id=1, source_target_pairs={{0,4},{4,0},{8,12},{12,8},{16,20},{20,16},{24,28},{28,24},{1,5},{5... | collective-permute-start | bytes 393224 | tf_op jit(solution)/shard_map/ppermute | solution.py:442

commit v13 on v12

--- a/solution.py
+++ b/solution.py
@@ -75,7 +75,7 @@
         [ANYWHERE],
         [shape((m * CHUNK, features), d_layer.dtype) for _, m in groups] + [shape(TOKEN, F32)],
         [WHOLE] * (len(groups) + 1),
-        [pltpu.SemaphoreType.DMA((d_layer.shape[0] // (CHUNK // 2),))],
+        [pltpu.SemaphoreType.DMA((sum(m for _, m in groups) * 2,))],
     )
 
 
@@ -500,7 +500,7 @@
     far = 1
     groups = [(1, n - 1), (0, 1)]
     order = Order()
-    *pieces, order.token = cut(d_layer, groups)
+    *pieces, order.token = cut(d_layer, groups[:-1])
     across = {c: swap(piece, "head", n_head, near) for (c, _), piece in zip(groups, pieces)}
 
     flat = (tokens * heads, dk)
@@ -511,8 +511,9 @@
     next(forward)
     *blocks, order.token = cut(order.tie(d_layer), [(c, 1) for c in range(n)])
     beside = [swap(one, "head", n_head, far) for one in blocks]
-    starts = [c * CHUNK for c, _ in groups]
-    part, order.token = early(pieces, starts, beside, out_weight, order.token)
+    across[0] = swap(blocks[0], "head", n_head, near)
+    starts = [c * CHUNK for c in range(n)]
+    part, order.token = early(blocks, starts, beside, out_weight, order.token)
 
     prefix = None
     while prefix is None:

time: 87.6 us -> 87.4 us (level)
  no operation moved by 1% of the time
where the time goes in v13:
time: 87.4 us; the launch traced here: 87.2 us
  Pallas kernels  38.3 us (44%)
  waiting for transfers between devices  24.5 us (28%)
  starting transfers between devices  23.4 us (27%)
  between operations  0.96 us (1%)
    pallas_call x20, Pallas kernels, call(): pl.pallas_call(kernel, in_specs=in_specs, out_specs=out_specs, out_shape=...  38.3 us
    ppermute x12, waiting for transfers between devices, swap(): return lax.ppermute(array, axis, [(i, i ^ bit) for i in range(size)])  13.5 us
    ppermute x12, starting transfers between devices, swap(): return lax.ppermute(array, axis, [(i, i ^ bit) for i in range(size)])  11.7 us
    ppermute x4, starting transfers between devices, shifted(): lax.ppermute(array, 'ctx', [(i, i + step) for i in range(size) if 0 <= i...  11.7 us
    ppermute x4, waiting for transfers between devices, shifted(): lax.ppermute(array, 'ctx', [(i, i + step) for i in range(size) if 0 <= i...  11 us
  transfers between devices with their start and end apart: 16, of which 15 were waited for; matrix products, arithmetic and copies ran while one was open for 0% of the time, Pallas kernels for 37%

profile of v13, /device:TPU:0, one launch (start us, length us, event | category | flops | bytes accessed | tf_op | source)
XLA Modules:
  0.0 87.2 jit_solution(1054865862639722893)
XLA Ops:
  0.6 1.4 %cut.2 = (bf16[768,1024]{1,0:T(8,128)(2,1)S(1)}, f32[8,128]{1,0:T(8,128)S(1)}) custom-call(bf16[1024,1024]{1,0:T(8,128)(2,1)} %source.2), custom_call_target="tpu_custom_call" | custom-call | tf_op jit(solution)/shard_map/cut/pallas_call | solution.py:40
  2.0 3.0 %collective-permute-start.1 = (bf16[768,1024]{1,0:T(8,128)(2,1)S(1)}, bf16[768,1024]{1,0:T(8,128)(2,1)S(1)}, u32[]{:S(2)}, u32[]{:S(2)}) collective-permute-start(bf16[768,1024]{1,0:T(8,128)(2,1)S(1)} %get-tuple-element.81), channel_id=1, source_target_pairs={{0,2},{1,3},{2,0},{3,1},{4,6},{5,7},{6,4},{7,5},{8,10},{9,11},{10,... | collective-permute-start | bytes 4718600 | tf_op jit(solution)/shard_map/ppermute | solution.py:442
  5.0 5.4 %prepare.1 = (bf16[1024,1024]{1,0:T(8,128)(2,1)S(1)}, bf16[1024,1024]{1,0:T(8,128)(2,1)S(1)}, bf16[1024,1024]{1,0:T(8,128)(2,1)S(1)}, bf16[1024,1024]{1,0:T(8,12...) custom-call(bf16[8192,128]{1,0:T(8,128)(2,1)} %bitcast.6, ...), custom_call_target="tpu_custom_call" | custom-call | tf_op jit(solution)/shard_map/prepare/pallas_call | solution.py:40
  10.4 1.6 %collective-permute-start.2 = (bf16[4,128,128]{2,1,0:T(8,128)(2,1)S(1)}, bf16[4,128,128]{2,1,0:T(8,128)(2,1)S(1)}, u32[]{:S(2)}, u32[]{:S(2)}) collective-permute-start(bf16[4,128,128]{2,1,0:T(8,128)(2,1)S(1)} %get-tuple-element.83), channel_id=1, source_target_pairs={{0,4},{4,0},{8,12},{12,8},{16,20},{20,16},{24,28},{28,24},{1,5},{5... | collective-permute-start | bytes 393224 | tf_op jit(solution)/shard_map/ppermute | solution.py:442
  12.0 1.6 %cut.3 = (bf16[256,1024]{1,0:T(8,128)(2,1)S(1)}, bf16[256,1024]{1,0:T(8,128)(2,1)S(1)}, bf16[256,1024]{1,0:T(8,128)(2,1)S(1)}, bf16[256,1024]{1,0:T(8,128)(2,1)S(1)}, f32[8,128]{1,0:T(8,128)S(1)}) custom-call(bf16[1024,1024]{1,0:T(8,128)(2,1)} %source.2), custom_call_target="tpu_custom_call" | custom-call | tf_op jit(solution)/shard_map/cut/pallas_call | solution.py:40
  14.2 1.2 %collective-permute-done.2.refs_1_.came = bf16[4,128,128]{2,1,0:T(8,128)(2,1)S(1)} collective-permute-done((bf16[4,128,128]{2,1,0:T(8,128)(2,1)S(1)}, bf16[4,128,128]{2,1,0:T(8,128)(2,1)S(1)}, u32[]{:S(2)}, u32[]{:S(2)}) %collective-permute-start.2) | collective-permute-done | bytes 131104 | tf_op jit(solution)/shard_map/ppermute | solution.py:442
  17.8 5.1 %early.1 = (f32[1024,1024]{1,0:T(8,128)S(1)}, f32[8,128]{1,0:T(8,128)S(1)}) custom-call(bf16[256,1024]{1,0:T(8,128)(2,1)S(1)} %get-tuple-element.80.refs_0_, bf16[256,1024]{1,0:T(8,128)(2,1)S(1)} %get-tuple-element.84.refs_1_, bf16[256,1024]{1,0:T(8,128)(2,1)S(1)} %get-tuple-element.85.refs_2_, bf16[256,1024]{1,0:T(8,128)(2,1)S(1)} %get-tuple-element.86.refs_3_, ...), custom_call_target="tpu_custom_call" | custom-call | tf_op jit(solution)/shard_map/early/pallas_call | solution.py:40
  22.9 3.5 %collective-permute-start.7 = (bf16[4,128,128]{2,1,0:T(8,128)(2,1)S(1)}, bf16[4,128,128]{2,1,0:T(8,128)(2,1)S(1)}, u32[]{:S(2)}, u32[]{:S(2)}) collective-permute-start(bf16[4,128,128]{2,1,0:T(8,128)(2,1)S(1)} %total.4), channel_id=1, source_target_pairs={{0,8},{4,12},{8,16},{12,20},{16,24},{20,28},{1,9},{5,13},{9,17},{1... | collective-permute-start | bytes 393224 | tf_op jit(solution)/shard_map/ppermute | solution.py:446
  26.4 3.0 %collective-permute-done.7.refs_2_.refs_0_ = bf16[4,128,128]{2,1,0:T(8,128)(2,1)S(1)} collective-permute-done((bf16[4,128,128]{2,1,0:T(8,128)(2,1)S(1)}, bf16[4,128,128]{2,1,0:T(8,128)(2,1)S(1)}, u32[]{:S(2)}, u32[]{:S(2)}) %collective-permute-start.7) | collective-permute-done | bytes 131104 | tf_op jit(solution)/shard_map/ppermute | solution.py:446
  29.5 5.4 %collective-permute-start.8 = (bf16[4,128,128]{2,1,0:T(8,128)(2,1)S(1)}, bf16[4,128,128]{2,1,0:T(8,128)(2,1)S(1)}, u32[]{:S(2)}, u32[]{:S(2)}) collective-permute-start(bf16[4,128,128]{2,1,0:T(8,128)(2,1)S(1)} %total.5), channel_id=1, source_target_pairs={{0,16},{4,20},{8,24},{12,28},{1,17},{5,21},{9,25},{13,29},{2,18},{... | collective-permute-start | bytes 393224 | tf_op jit(solution)/shard_map/ppermute | solution.py:446
  34.9 2.5 %collective-permute-done.8.refs_1_ = bf16[4,128,128]{2,1,0:T(8,128)(2,1)S(1)} collective-permute-done((bf16[4,128,128]{2,1,0:T(8,128)(2,1)S(1)}, bf16[4,128,128]{2,1,0:T(8,128)(2,1)S(1)}, u32[]{:S(2)}, u32[]{:S(2)}) %collective-permute-start.8) | collective-permute-done | bytes 131104 | tf_op jit(solution)/shard_map/ppermute | solution.py:446
  37.5 1.9 %collective-permute-done.1.refs_0_ = bf16[768,1024]{1,0:T(8,128)(2,1)S(1)} collective-permute-done((bf16[768,1024]{1,0:T(8,128)(2,1)S(1)}, bf16[768,1024]{1,0:T(8,128)(2,1)S(1)}, u32[]{:S(2)}, u32[]{:S(2)}) %collective-permute-start.1) | collective-permute-done | bytes 1572896 | tf_op jit(solution)/shard_map/ppermute | solution.py:442
  39.4 1.7 %collective-permute-start = (bf16[256,1024]{1,0:T(8,128)(2,1)S(1)}, bf16[256,1024]{1,0:T(8,128)(2,1)S(1)}, u32[]{:S(2)}, u32[]{:S(2)}) collective-permute-start(bf16[256,1024]{1,0:T(8,128)(2,1)S(1)} %get-tuple-element.80.refs_0_), channel_id=1, source_target_pairs={{0,2},{1,3},{2,0},{3,1},{4,6},{5,7},{6,4},{7,5},{8,10},{9,11},{10,... | collective-permute-start | bytes 1572872 | tf_op jit(solution)/shard_map/ppermute | solution.py:442
  41.2 1.5 %collective-permute-start.10 = (bf16[4,128,128]{2,1,0:T(8,128)(2,1)S(1)}, bf16[4,128,128]{2,1,0:T(8,128)(2,1)S(1)}, u32[]{:S(2)}, u32[]{:S(2)}) collective-permute-start(bf16[4,128,128]{2,1,0:T(8,128)(2,1)S(1)} %get-tuple-element.102), channel_id=1, source_target_pairs={{0,4},{4,0},{8,12},{12,8},{16,20},{20,16},{24,28},{28,24},{1,5},{5... | collective-permute-start | bytes 393224 | tf_op jit(solution)/shard_map/ppermute | solution.py:442
  42.8 6.9 %late.3 = (bf16[768,1024]{1,0:T(8,128)(2,1)S(1)}, f32[8,128]{1,0:T(8,128)S(1)}, f32[3,8,128,128]{3,2,1,0:T(8,128)S(1)}) custom-call(bf16[768,1024]{1,0:T(8,128)(2,1)S(1)} %collective-permute-done.9.b_ref, bf16[1024,4096]{1,0:T(8,128)(2,1)S(1)} %copy-done, f32[1024,1024]{1,0:T(8,128)S(1)} %get-tuple-element.96.part_ref, ...), custom_call_target="tpu_custom_call" | custom-call | tf_op jit(solution)/shard_map/late/pallas_call | solution.py:40
  49.7 2.1 %within.4 = (bf16[2048,128]{1,0:T(8,128)(2,1)S(1)}, bf16[256,1024]{1,0:T(8,128)(2,1)S(1)}, bf16[256,1024]{1,0:T(8,128)(2,1)S(1)}, f32[8,128]{1,0:T(8,128)S(1)}) custom-call(bf16[1024,1024]{1,0:T(8,128)(2,1)S(1)} %get-tuple-element.75.q_ref, bf16[1024,1024]{1,0:T(8,128)(2,1)S(1)} %get-tuple-element.76.k_ref, bf16[1024,1024]{1,0:T(8,128)(2,1)S(1)} %get-tuple-element.77.v_ref, ...), custom_call_target="tpu_custom_call" | custom-call | tf_op jit(solution)/shard_map/within/pallas_call | solution.py:40
  51.8 1.9 %collective-permute-done.a_ref = bf16[256,1024]{1,0:T(8,128)(2,1)S(1)} collective-permute-done((bf16[256,1024]{1,0:T(8,128)(2,1)S(1)}, bf16[256,1024]{1,0:T(8,128)(2,1)S(1)}, u32[]{:S(2)}, u32[]{:S(2)}) %collective-permute-start) | collective-permute-done | bytes 524320 | tf_op jit(solution)/shard_map/ppermute | solution.py:442
  55.7 1.2 %late.4 = (bf16[256,512]{1,0:T(8,128)(2,1)S(1)}, f32[8,128]{1,0:T(8,128)S(1)}, bf16[4,128,128]{2,1,0:T(8,128)(2,1)S(1)}, bf16[1024,256]{1,0:T(8,128)(2,1)S(1)}) custom-call(bf16[256,1024]{1,0:T(8,128)(2,1)S(1)} %collective-permute-done.11.b_ref, bf16[1024,4096]{1,0:T(8,128)(2,1)S(1)} %copy-done, f32[256,1024]{1,0:T(8,128)S(1)} %get-tuple-element.107.part_ref, ...), custom_call_target="tpu_custom_call" | custom-call | tf_op jit(solution)/shard_map/late/pallas_call | solution.py:40
  56.9 1.8 %collective-permute-start.12 = (bf16[4,128,128]{2,1,0:T(8,128)(2,1)S(1)}, bf16[4,128,128]{2,1,0:T(8,128)(2,1)S(1)}, u32[]{:S(2)}, u32[]{:S(2)}) collective-permute-start(bf16[4,128,128]{2,1,0:T(8,128)(2,1)S(1)} %get-tuple-element.115), channel_id=1, source_target_pairs={{0,4},{4,0},{8,12},{12,8},{16,20},{20,16},{24,28},{28,24},{1,5},{5... | collective-permute-start | bytes 393224 | tf_op jit(solution)/shard_map/ppermute | solution.py:442
  58.7 1.2 %late.5 = (bf16[256,512]{1,0:T(8,128)(2,1)S(1)}, f32[8,128]{1,0:T(8,128)S(1)}, bf16[4,128,128]{2,1,0:T(8,128)(2,1)S(1)}) custom-call(bf16[1024,256]{1,0:T(8,128)(2,1)S(1)} %get-tuple-element.110.b_ref, bf16[1024,4096]{1,0:T(8,128)(2,1)S(1)} %copy-done, f32[256,1024]{1,0:T(8,128)S(1)} %get-tuple-element.107.part_ref, ...), custom_call_target="tpu_custom_call" | custom-call | tf_op jit(solution)/shard_map/late/pallas_call | solution.py:40
  59.9 2.6 %collective-permute-done.12.refs_1_.came = bf16[4,128,128]{2,1,0:T(8,128)(2,1)S(1)} collective-permute-done((bf16[4,128,128]{2,1,0:T(8,128)(2,1)S(1)}, bf16[4,128,128]{2,1,0:T(8,128)(2,1)S(1)}, u32[]{:S(2)}, u32[]{:S(2)}) %collective-permute-start.12) | collective-permute-done | bytes 131104 | tf_op jit(solution)/shard_map/ppermute | solution.py:442
  62.6 1.5 %collective-permute-start.13 = (bf16[4,128,128]{2,1,0:T(8,128)(2,1)S(1)}, bf16[4,128,128]{2,1,0:T(8,128)(2,1)S(1)}, u32[]{:S(2)}, u32[]{:S(2)}) collective-permute-start(bf16[4,128,128]{2,1,0:T(8,128)(2,1)S(1)} %total.6), channel_id=1, source_target_pairs={{8,0},{12,4},{16,8},{20,12},{24,16},{28,20},{9,1},{13,5},{17,9},{2... | collective-permute-start | bytes 393224 | tf_op jit(solution)/shard_map/ppermute | solution.py:446
  64.1 2.3 %within.5 = (bf16[2048,128]{1,0:T(8,128)(2,1)S(1)}, bf16[256,1024]{1,0:T(8,128)(2,1)S(1)}, bf16[256,1024]{1,0:T(8,128)(2,1)S(1)}, f32[8,128]{1,0:T(8,128)S(1)}) custom-call(bf16[1024,1024]{1,0:T(8,128)(2,1)S(1)} %get-tuple-element.75.q_ref, bf16[1024,1024]{1,0:T(8,128)(2,1)S(1)} %get-tuple-element.76.k_ref, bf16[1024,1024]{1,0:T(8,128)(2,1)S(1)} %get-tuple-element.77.v_ref, ...), custom_call_target="tpu_custom_call" | custom-call | tf_op jit(solution)/shard_map/within/pallas_call | solution.py:40
  66.4 3.2 %collective-permute-done.13.refs_2_.refs_0_ = bf16[4,128,128]{2,1,0:T(8,128)(2,1)S(1)} collective-permute-done((bf16[4,128,128]{2,1,0:T(8,128)(2,1)S(1)}, bf16[4,128,128]{2,1,0:T(8,128)(2,1)S(1)}, u32[]{:S(2)}, u32[]{:S(2)}) %collective-permute-start.13) | collective-permute-done | bytes 131104 | tf_op jit(solution)/shard_map/ppermute | solution.py:446
  69.6 1.3 %collective-permute-start.14 = (bf16[4,128,128]{2,1,0:T(8,128)(2,1)S(1)}, bf16[4,128,128]{2,1,0:T(8,128)(2,1)S(1)}, u32[]{:S(2)}, u32[]{:S(2)}) collective-permute-start(bf16[4,128,128]{2,1,0:T(8,128)(2,1)S(1)} %total.7), channel_id=1, source_target_pairs={{16,0},{20,4},{24,8},{28,12},{17,1},{21,5},{25,9},{29,13},{18,2},{... | collective-permute-start | bytes 393224 | tf_op jit(solution)/shard_map/ppermute | solution.py:446
  70.9 2.3 %within.6 = (bf16[2048,128]{1,0:T(8,128)(2,1)S(1)}, bf16[256,1024]{1,0:T(8,128)(2,1)S(1)}, bf16[256,1024]{1,0:T(8,128)(2,1)S(1)}, f32[8,128]{1,0:T(8,128)S(1)}) custom-call(bf16[1024,1024]{1,0:T(8,128)(2,1)S(1)} %get-tuple-element.75.q_ref, bf16[1024,1024]{1,0:T(8,128)(2,1)S(1)} %get-tuple-element.76.k_ref, bf16[1024,1024]{1,0:T(8,128)(2,1)S(1)} %get-tuple-element.77.v_ref, ...), custom_call_target="tpu_custom_call" | custom-call | tf_op jit(solution)/shard_map/within/pallas_call | solution.py:40
  73.3 3.5 %within.7 = (bf16[8192,128]{1,0:T(8,128)(2,1)}, bf16[256,1024]{1,0:T(8,128)(2,1)S(1)}, bf16[256,1024]{1,0:T(8,128)(2,1)S(1)}, f32[8,128]{1,0:T(8,128)S(1)}) custom-call(bf16[1024,1024]{1,0:T(8,128)(2,1)S(1)} %get-tuple-element.75.q_ref, bf16[1024,1024]{1,0:T(8,128)(2,1)S(1)} %get-tuple-element.76.k_ref, bf16[1024,1024]{1,0:T(8,128)(2,1)S(1)} %get-tuple-element.77.v_ref, ...), custom_call_target="tpu_custom_call" | custom-call | tf_op jit(solution)/shard_map/within/pallas_call | solution.py:40
  76.7 2.3 %collective-permute-done.14.refs_1_ = bf16[4,128,128]{2,1,0:T(8,128)(2,1)S(1)} collective-permute-done((bf16[4,128,128]{2,1,0:T(8,128)(2,1)S(1)}, bf16[4,128,128]{2,1,0:T(8,128)(2,1)S(1)}, u32[]{:S(2)}, u32[]{:S(2)}) %collective-permute-start.14) | collective-permute-done | bytes 131104 | tf_op jit(solution)/shard_map/ppermute | solution.py:446
  79.1 1.4 %collective-permute-start.15 = (bf16[4,128,128]{2,1,0:T(8,128)(2,1)S(1)}, bf16[4,128,128]{2,1,0:T(8,128)(2,1)S(1)}, u32[]{:S(2)}, u32[]{:S(2)}) collective-permute-start(bf16[4,128,128]{2,1,0:T(8,128)(2,1)S(1)} %get-tuple-element.129), channel_id=1, source_target_pairs={{0,4},{4,0},{8,12},{12,8},{16,20},{20,16},{24,28},{28,24},{1,5},{5... | collective-permute-start | bytes 393224 | tf_op jit(solution)/shard_map/ppermute | solution.py:442
  80.6 1.2 %finish.2 = (f32[8192,128]{1,0:T(8,128)S(1)}, f32[8192,128]{1,0:T(8,128)S(1)}, f32[8,128]{1,0:T(8,128)S(1)}) custom-call(bf16[1024,1024]{1,0:T(8,128)(2,1)S(1)} %get-tuple-element.76.k_ref, bf16[1024,1024]{1,0:T(8,128)(2,1)S(1)} %get-tuple-element.77.v_ref, bf16[4,128,128]{2,1,0:T(8,128)(2,1)S(1)} %get-tuple-element.130.suffix_ref, ...), custom_call_target="tpu_custom_call" | custom-call | tf_op jit(solution)/shard_map/finish/pallas_call | solution.py:40
  81.8 2.4 %collective-permute-done.15.suffix_ref = bf16[4,128,128]{2,1,0:T(8,128)(2,1)S(1)} collective-permute-done((bf16[4,128,128]{2,1,0:T(8,128)(2,1)S(1)}, bf16[4,128,128]{2,1,0:T(8,128)(2,1)S(1)}, u32[]{:S(2)}, u32[]{:S(2)}) %collective-permute-start.15) | collective-permute-done | bytes 131104 | tf_op jit(solution)/shard_map/ppermute | solution.py:442
  84.2 2.9 %finish.3 = (bf16[8192,128]{1,0:T(8,128)(2,1)}, bf16[8192,128]{1,0:T(8,128)(2,1)}, f32[8192,128]{1,0:T(8,128)S(1)}, f32[8192,128]{1,0:T(8,128)S(1)}) custom-call(bf16[1024,1024]{1,0:T(8,128)(2,1)S(1)} %get-tuple-element.76.k_ref, bf16[1024,1024]{1,0:T(8,128)(2,1)S(1)} %get-tuple-element.77.v_ref, ...), custom_call_target="tpu_custom_call", output_to_operand_aliasing={{2}: (12, {}), {3}: (13, {})} | custom-call | tf_op jit(solution)/shard_map/finish/pallas_call | solution.py:40
  (22 shorter events, 5.4 us)
Async XLA Ops:
  2.0 37.4 %collective-permute-start.1 = (bf16[768,1024]{1,0:T(8,128)(2,1)S(1)}, bf16[768,1024]{1,0:T(8,128)(2,1)S(1)}, u32[]{:S(2)}, u32[]{:S(2)}) collective-permute-start(bf16[768,1024]{1,0:T(8,128)(2,1)S(1)} %get-tuple-element.81), channel_id=1, source_target_pairs={{0,2},{1,3},{2,0},{3,1},{4,6},{5,7},{6,4},{7,5},{8,10},{9,11},{10,... | collective-permute-start | bytes 4718600 | tf_op jit(solution)/shard_map/ppermute | solution.py:442
  5.0 12.8 %copy-start = (bf16[1024,4096]{1,0:T(8,128)(2,1)S(1)}, bf16[1024,4096]{1,0:T(8,128)(2,1)}, u32[]{:S(2)}) copy-start(bf16[1024,4096]{1,0:T(8,128)(2,1)} %w_ref.7) | copy-start | bytes 25165828
  10.4 5.0 %collective-permute-start.2 = (bf16[4,128,128]{2,1,0:T(8,128)(2,1)S(1)}, bf16[4,128,128]{2,1,0:T(8,128)(2,1)S(1)}, u32[]{:S(2)}, u32[]{:S(2)}) collective-permute-start(bf16[4,128,128]{2,1,0:T(8,128)(2,1)S(1)} %get-tuple-element.83), channel_id=1, source_target_pairs={{0,4},{4,0},{8,12},{12,8},{16,20},{20,16},{24,28},{28,24},{1,5},{5... | collective-permute-start | bytes 393224 | tf_op jit(solution)/shard_map/ppermute | solution.py:442
  13.6 2.0 %collective-permute-start.4 = (bf16[256,1024]{1,0:T(8,128)(2,1)S(1)}, bf16[256,1024]{1,0:T(8,128)(2,1)S(1)}, u32[]{:S(2)}, u32[]{:S(2)}) collective-permute-start(bf16[256,1024]{1,0:T(8,128)(2,1)S(1)} %get-tuple-element.84.refs_1_), channel_id=1, source_target_pairs={{0,1},{1,0},{2,3},{3,2},{4,5},{5,4},{6,7},{7,6},{8,9},{9,8},{10,11... | collective-permute-start | bytes 1572872 | tf_op jit(solution)/shard_map/ppermute | solution.py:442
  13.6 2.6 %collective-permute-start.5 = (bf16[256,1024]{1,0:T(8,128)(2,1)S(1)}, bf16[256,1024]{1,0:T(8,128)(2,1)S(1)}, u32[]{:S(2)}, u32[]{:S(2)}) collective-permute-start(bf16[256,1024]{1,0:T(8,128)(2,1)S(1)} %get-tuple-element.85.refs_2_), channel_id=1, source_target_pairs={{0,1},{1,0},{2,3},{3,2},{4,5},{5,4},{6,7},{7,6},{8,9},{9,8},{10,11... | collective-permute-start | bytes 1572872 | tf_op jit(solution)/shard_map/ppermute | solution.py:442
  14.1 2.9 %collective-permute-start.6 = (bf16[256,1024]{1,0:T(8,128)(2,1)S(1)}, bf16[256,1024]{1,0:T(8,128)(2,1)S(1)}, u32[]{:S(2)}, u32[]{:S(2)}) collective-permute-start(bf16[256,1024]{1,0:T(8,128)(2,1)S(1)} %get-tuple-element.86.refs_3_), channel_id=1, source_target_pairs={{0,1},{1,0},{2,3},{3,2},{4,5},{5,4},{6,7},{7,6},{8,9},{9,8},{10,11... | collective-permute-start | bytes 1572872 | tf_op jit(solution)/shard_map/ppermute | solution.py:442
  15.4 2.4 %collective-permute-start.3 = (bf16[256,1024]{1,0:T(8,128)(2,1)S(1)}, bf16[256,1024]{1,0:T(8,128)(2,1)S(1)}, u32[]{:S(2)}, u32[]{:S(2)}) collective-permute-start(bf16[256,1024]{1,0:T(8,128)(2,1)S(1)} %get-tuple-element.80.refs_0_), channel_id=1, source_target_pairs={{0,1},{1,0},{2,3},{3,2},{4,5},{5,4},{6,7},{7,6},{8,9},{9,8},{10,11... | collective-permute-start | bytes 1572872 | tf_op jit(solution)/shard_map/ppermute | solution.py:442
  22.9 6.5 %collective-permute-start.7 = (bf16[4,128,128]{2,1,0:T(8,128)(2,1)S(1)}, bf16[4,128,128]{2,1,0:T(8,128)(2,1)S(1)}, u32[]{:S(2)}, u32[]{:S(2)}) collective-permute-start(bf16[4,128,128]{2,1,0:T(8,128)(2,1)S(1)} %total.4), channel_id=1, source_target_pairs={{0,8},{4,12},{8,16},{12,20},{16,24},{20,28},{1,9},{5,13},{9,17},{1... | collective-permute-start | bytes 393224 | tf_op jit(solution)/shard_map/ppermute | solution.py:446
  29.5 7.9 %collective-permute-start.8 = (bf16[4,128,128]{2,1,0:T(8,128)(2,1)S(1)}, bf16[4,128,128]{2,1,0:T(8,128)(2,1)S(1)}, u32[]{:S(2)}, u32[]{:S(2)}) collective-permute-start(bf16[4,128,128]{2,1,0:T(8,128)(2,1)S(1)} %total.5), channel_id=1, source_target_pairs={{0,16},{4,20},{8,24},{12,28},{1,17},{5,21},{9,25},{13,29},{2,18},{... | collective-permute-start | bytes 393224 | tf_op jit(solution)/shard_map/ppermute | solution.py:446
  39.4 3.4 %collective-permute-start.9 = (bf16[768,1024]{1,0:T(8,128)(2,1)S(1)}, bf16[768,1024]{1,0:T(8,128)(2,1)S(1)}, u32[]{:S(2)}, u32[]{:S(2)}) collective-permute-start(bf16[768,1024]{1,0:T(8,128)(2,1)S(1)} %collective-permute-done.1.refs_0_), channel_id=1, source_target_pairs={{0,1},{1,0},{2,3},{3,2},{4,5},{5,4},{6,7},{7,6},{8,9},{9,8},{10,11... | collective-permute-start | bytes 4718600 | tf_op jit(solution)/shard_map/ppermute | solution.py:442
  39.4 14.3 %collective-permute-start = (bf16[256,1024]{1,0:T(8,128)(2,1)S(1)}, bf16[256,1024]{1,0:T(8,128)(2,1)S(1)}, u32[]{:S(2)}, u32[]{:S(2)}) collective-permute-start(bf16[256,1024]{1,0:T(8,128)(2,1)S(1)} %get-tuple-element.80.refs_0_), channel_id=1, source_target_pairs={{0,2},{1,3},{2,0},{3,1},{4,6},{5,7},{6,4},{7,5},{8,10},{9,11},{10,... | collective-permute-start | bytes 1572872 | tf_op jit(solution)/shard_map/ppermute | solution.py:442
  41.2 8.5 %collective-permute-start.10 = (bf16[4,128,128]{2,1,0:T(8,128)(2,1)S(1)}, bf16[4,128,128]{2,1,0:T(8,128)(2,1)S(1)}, u32[]{:S(2)}, u32[]{:S(2)}) collective-permute-start(bf16[4,128,128]{2,1,0:T(8,128)(2,1)S(1)} %get-tuple-element.102), channel_id=1, source_target_pairs={{0,4},{4,0},{8,12},{12,8},{16,20},{20,16},{24,28},{28,24},{1,5},{5... | collective-permute-start | bytes 393224 | tf_op jit(solution)/shard_map/ppermute | solution.py:442
  53.8 1.9 %collective-permute-start.11 = (bf16[256,1024]{1,0:T(8,128)(2,1)S(1)}, bf16[256,1024]{1,0:T(8,128)(2,1)S(1)}, u32[]{:S(2)}, u32[]{:S(2)}) collective-permute-start(bf16[256,1024]{1,0:T(8,128)(2,1)S(1)} %collective-permute-done.a_ref), channel_id=1, source_target_pairs={{0,1},{1,0},{2,3},{3,2},{4,5},{5,4},{6,7},{7,6},{8,9},{9,8},{10,11... | collective-permute-start | bytes 1572872 | tf_op jit(solution)/shard_map/ppermute | solution.py:442
  56.9 5.6 %collective-permute-start.12 = (bf16[4,128,128]{2,1,0:T(8,128)(2,1)S(1)}, bf16[4,128,128]{2,1,0:T(8,128)(2,1)S(1)}, u32[]{:S(2)}, u32[]{:S(2)}) collective-permute-start(bf16[4,128,128]{2,1,0:T(8,128)(2,1)S(1)} %get-tuple-element.115), channel_id=1, source_target_pairs={{0,4},{4,0},{8,12},{12,8},{16,20},{20,16},{24,28},{28,24},{1,5},{5... | collective-permute-start | bytes 393224 | tf_op jit(solution)/shard_map/ppermute | solution.py:442
  62.6 7.0 %collective-permute-start.13 = (bf16[4,128,128]{2,1,0:T(8,128)(2,1)S(1)}, bf16[4,128,128]{2,1,0:T(8,128)(2,1)S(1)}, u32[]{:S(2)}, u32[]{:S(2)}) collective-permute-start(bf16[4,128,128]{2,1,0:T(8,128)(2,1)S(1)} %total.6), channel_id=1, source_target_pairs={{8,0},{12,4},{16,8},{20,12},{24,16},{28,20},{9,1},{13,5},{17,9},{2... | collective-permute-start | bytes 393224 | tf_op jit(solution)/shard_map/ppermute | solution.py:446
  69.6 9.4 %collective-permute-start.14 = (bf16[4,128,128]{2,1,0:T(8,128)(2,1)S(1)}, bf16[4,128,128]{2,1,0:T(8,128)(2,1)S(1)}, u32[]{:S(2)}, u32[]{:S(2)}) collective-permute-start(bf16[4,128,128]{2,1,0:T(8,128)(2,1)S(1)} %total.7), channel_id=1, source_target_pairs={{16,0},{20,4},{24,8},{28,12},{17,1},{21,5},{25,9},{29,13},{18,2},{... | collective-permute-start | bytes 393224 | tf_op jit(solution)/shard_map/ppermute | solution.py:446
  79.1 5.0 %collective-permute-start.15 = (bf16[4,128,128]{2,1,0:T(8,128)(2,1)S(1)}, bf16[4,128,128]{2,1,0:T(8,128)(2,1)S(1)}, u32[]{:S(2)}, u32[]{:S(2)}) collective-permute-start(bf16[4,128,128]{2,1,0:T(8,128)(2,1)S(1)} %get-tuple-element.129), channel_id=1, source_target_pairs={{0,4},{4,0},{8,12},{12,8},{16,20},{20,16},{24,28},{28,24},{1,5},{5... | collective-permute-start | bytes 393224 | tf_op jit(solution)/shard_map/ppermute | solution.py:442
